TPU v7x, 32 devices: a whole 2x2x4 slice. The times are simulated.
32 devices in a mesh: tau: 2 (over y), aux: 4 (over z), orb: 2 (over x), sub: 2 (over core).
Axes of the slice: x: 2, y: 2, z: 4, core: 2. Of those that a mesh axis runs over, the one named last changes fastest.
Arguments:
- three_center: float32 [4, 2, 2, 64, 4096], P('aux', 'orb', None, None, 'sub'), may hold values from -6 to 6
- occupied_green: float32 [256, 128], P(('tau', 'orb')), parts along dimension 0, may hold values from -0.5 to 0.5
- virtual_green: float32 [256, 128], P(('tau', 'orb')), parts along dimension 0, may hold values from -0.5 to 0.5
- block_list: int32 [2, 2], P('orb'), may hold values from 0 to 1
Outputs:
- chi_values: float32 [512, 256], P(('tau', 'aux', 'orb', 'sub')), parts along dimension 0
There are 2 independent parts, one for each index of `tau`. A program takes and returns all parts, laid end to end along the dimension named above; an argument that names none is the same for every part. Nothing has to cross between parts.
All inputs are finite; a program needn't handle non-finite values.
Results may differ from a plain program's by a relative error of at most 0.0001.
Values sent between devices are 32-bit elements; how exact they have to be, the bound alone decides.
No kernel may reach another device: no remote copies, remote signals or barrier semaphores. Data moves between devices by JAX's collectives and lax.ppermute only.
A program may use at most 64 MiB of HBM per device.

v0:
```python
import math

import jax
import jax.numpy as jnp
from jax import lax
from jax.sharding import PartitionSpec as P


def local(three_center, occupied_green, virtual_green, block_list):
    slots = three_center.shape[2]
    width = three_center.shape[3]
    columns = three_center.shape[4]
    rows_aux = columns // width
    norb = occupied_green.shape[1]
    nob = norb // width
    own_list = block_list[0]
    flat_tensor = three_center.reshape(slots * width, columns)
    tensors, lists = (
        lax.all_gather(three_center, "orb", axis=1, tiled=True),
        lax.all_gather(block_list, "orb", axis=0, tiled=True),
    )
    virt_full = lax.all_gather(virtual_green, "orb", axis=0, tiled=True)
    occ_sel = jnp.take(occupied_green.reshape(width, nob, width), lists.reshape(-1), axis=1)
    occ_sel = occ_sel.reshape(width, nob, slots, width)
    relayed = jnp.einsum(
        "lnkm,nkmc->lnc",
        occ_sel,
        tensors.reshape(nob, slots, width, columns),
        precision=lax.Precision.HIGHEST,
    ).reshape(width, nob * columns)
    middle_four = relayed.reshape(width, nob, rows_aux, width)
    virt_sel = jnp.take(virt_full.reshape(nob, width, nob, width), own_list, axis=2)
    products = jnp.einsum("lnpw,nwks->kspl", middle_four, virt_sel, precision=lax.Precision.HIGHEST)
    products = products.reshape(slots * width, columns)
    product_moved, tensor_moved = (
        lax.all_to_all(products, ("aux", "sub"), split_axis=0, concat_axis=1, tiled=True),
        lax.all_to_all(flat_tensor, ("aux", "sub"), split_axis=0, concat_axis=1, tiled=True),
    )
    piece_rows = product_moved.shape[0]
    nauxf = product_moved.shape[1] // width
    partial_chi = jnp.einsum(
        "rpl,rql->pq",
        product_moved.reshape(piece_rows, nauxf, width),
        tensor_moved.reshape(piece_rows, nauxf, width),
        precision=lax.Precision.HIGHEST,
    )
    partial_chi = partial_chi * (-2.0 / math.sqrt(norb * slots * width))
    return lax.psum_scatter(partial_chi, ("aux", "orb", "sub"), scatter_dimension=0, tiled=True)


def solution(mesh):
    in_specs = (
        P("aux", "orb", None, None, "sub"),
        P(("tau", "orb"), None),
        P(("tau", "orb"), None),
        P("orb", None),
    )
    out_specs = P(("tau", "aux", "orb", "sub"), None)
    return jax.shard_map(local, mesh=mesh, in_specs=in_specs, out_specs=out_specs, check_vma=False)
```

profile of v0, /device:TPU:0, one launch (start us, length us, event | category | flops | bytes accessed | tf_op | source)
XLA Modules:
  0.0 156.7 jit_solution(10825210243684209781)
XLA Ops:
  6.5 0.0 all-gather.3.cloned.1.call-start
  6.5 0.7 all-gather.3.cloned.1.call-update
  7.3 6.3 %all-to-all-start.1 = ((f32[8,16,2048]{2,1,0:T(8,128)}), f32[8,16,2048]{2,1,0:T(8,128)}, u32[]{:S(2)}, u32[]{:S(2)}) async-start(f32[8,16,2048]{2,1,0:T(8,128)} %bitcast.53), calls=%async_computation.1 | async-start | bytes 2097152 | tf_op jit(solution)/shard_map/all_to_all | solution.py:37
  13.6 0.0 copy-done.2
  13.6 4.2 %all-gather = s32[2,1,2]{2,1,0:T(1,128)S(1)} all-gather(s32[1,1,2]{2,1,0:T(1,128)S(1)} %bitcast.56), channel_id=1, replica_groups=mesh['tau'=2,'aux'=4,'orb'=2,'sub'=2] {'orb'}, dimensions={0}, use_global_device_ids=true | all-gather | bytes 24 | tf_op jit(solution)/shard_map/all_gather | solution.py:20
  17.8 0.5 broadcast.92
  18.3 0.7 reduce.3
  19.0 0.1 reshape.103
  19.1 0.0 copy-done
  19.1 0.1 reshape.102
  19.2 0.0 copy-done.1
  19.2 5.1 %all_gather.9 = f32[128,128]{1,0:T(8,128)S(1)} all-gather(f32[64,128]{1,0:T(8,128)S(1)} %copy-done.1), channel_id=1, replica_groups=mesh['tau'=2,'aux'=4,'orb'=2,'sub'=2] {'orb'}, dimensions={0}, use_global_device_ids=true | all-gather | bytes 98304 | tf_op jit(solution)/shard_map/all_gather | solution.py:22
  24.3 0.1 reshape.101
  24.5 0.6 gather_fusion.1
  25.1 0.6 gather_fusion
  25.7 19.6 %all-gather.3.cloned.1.call-done = f32[1,2,2,64,2048]{4,3,2,0,1:T(8,128)} async-done(((f32[1,1,2,64,2048]{4,3,2,0,1:T(8,128)}), f32[1,2,2,64,2048]{4,3,2,0,1:T(8,128)}) %all-gather.3.cloned.1.call-update) | async-done | bytes 2097168 | tf_op jit(solution)/shard_map/all_gather | solution.py:19
  45.3 3.1 %convolution_bitcast_fusion = f32[64,2,2048]{2,0,1:T(8,128)S(1)} fusion(f32[1,2,2,64,2048]{4,3,2,0,1:T(8,128)} %all-gather.3.cloned.1.call-done, f32[64,2,2,64]{3,0,2,1:T(8,128)S(1)} %bitcast.54, pred[2,2]{1,0:T(4,128)(4,1)S(1)} %compare_and_fusion), kind=kOutput, calls=%fused_computation.2 | convolution fusion | flops 402669568 | bytes 3211268 | tf_op jit(solution)/shard_map/lnkm,nkmc->lnc/dot_general | solution.py:25
  48.3 0.8 reshape_reshape.3
  49.1 4.6 %fusion.4 = f32[2,64,32,64]{3,1,2,0:T(8,128)S(1)} fusion(f32[64,2,32,64]{3,2,0,1:T(8,128)S(1)} %reshape_reshape.3, f32[2,2,64,64]{3,2,1,0:T(8,128)S(1)} %gather_fusion, pred[2]{0:T(512)(128)(4,1)S(1)} %compare_and_fusion.1), kind=kOutput, calls=%fused_computation.7 | convolution fusion | flops 402669568 | bytes 2162690 | tf_op jit(solution)/shard_map/lnpw,nwks->kspl/dot_general | solution.py:33
  53.8 1.2 copy.28
  55.0 1.7 %all_to_all.24 = f32[8,16,2048]{2,1,0:T(8,128)} reshape(f32[2,64,32,64]{3,2,1,0:T(8,128)S(1)} %copy.28) | data formatting | bytes 2097152 | tf_op jit(solution)/shard_map/all_to_all | solution.py:36
  56.7 0.0 all-to-all-done.1
  56.7 4.8 %all-to-all-start = ((f32[8,16,2048]{2,1,0:T(8,128)}), f32[8,16,2048]{2,1,0:T(8,128)}, u32[]{:S(2)}, u32[]{:S(2)}) async-start(f32[8,16,2048]{2,1,0:T(8,128)} %all_to_all.24), calls=%async_computation | async-start | bytes 2097152 | tf_op jit(solution)/shard_map/all_to_all | solution.py:36
  61.5 0.2 reduce-scatter.2.cloned.1.call-start
  61.7 1.8 %copy.30 = f32[16,8,2048]{2,1,0:T(8,128)S(1)} copy(f32[16,8,2048]{2,0,1:T(8,128)} %bitcast.21) | data formatting | bytes 2097152 | tf_op jit(solution)/shard_map/all_to_all | solution.py:37
  63.6 0.8 reshape.106
  64.4 23.8 %all-to-all-done = f32[8,16,2048]{2,1,0:T(8,128)} async-done(((f32[8,16,2048]{2,1,0:T(8,128)}), f32[8,16,2048]{2,1,0:T(8,128)}, u32[]{:S(2)}, u32[]{:S(2)}) %all-to-all-start) | async-done | bytes 1048608 | tf_op jit(solution)/shard_map/all_to_all | solution.py:36
  88.2 1.8 %copy.29 = f32[16,8,2048]{2,1,0:T(8,128)S(1)} copy(f32[16,8,2048]{2,0,1:T(8,128)} %bitcast.19) | data formatting | bytes 2097152 | tf_op jit(solution)/shard_map/all_to_all | solution.py:36
  90.0 2.2 %reshape.105 = f32[16,256,64]{2,1,0:T(8,128)} reshape(f32[16,8,2048]{2,1,0:T(8,128)S(1)} %copy.29) | data formatting | bytes 2097152 | tf_op jit(solution)/shard_map/reshape | solution.py:43
  92.2 4.2 %fusion.7 = f32[256,256]{1,0:T(8,128)} fusion(f32[16,256,64]{2,1,0:T(8,128)} %reshape.105, f32[16,256,64]{2,1,0:T(8,128)S(1)} %reshape.106), kind=kOutput, calls=%fused_computation.9 | convolution fusion | flops 805371904 | bytes 2359296 | tf_op jit(solution)/shard_map/rpl,rql->pq/dot_general | solution.py:41
  96.5 0.0 reduce-scatter.2.cloned.1.call-update
  96.5 53.4 %reduce-scatter.2.cloned.1.call-done = f32[16,256]{1,0:T(8,128)} async-done(((f32[256,256]{1,0:T(8,128)}), f32[16,256]{1,0:T(8,128)}) %reduce-scatter.2.cloned.1.call-update) | async-done | bytes 16400 | tf_op jit(solution)/shard_map/reduce_scatter | solution.py:48
  (11 shorter events, 0.1 us)
Async XLA Ops:
  6.5 7.1 %copy-start.2 = (s32[1,2]{1,0:T(1,128)S(1)}, s32[1,2]{1,0:T(1,128)}, u32[]{:S(2)}) copy-start(s32[1,2]{1,0:T(1,128)} %param.7) | copy-start | bytes 28
  6.5 12.6 %copy-start = (f32[64,128]{1,0:T(8,128)S(1)}, f32[64,128]{1,0:T(8,128)}, u32[]{:S(2)}) copy-start(f32[64,128]{1,0:T(8,128)} %param.5) | copy-start | bytes 98308
  6.5 12.7 %copy-start.1 = (f32[64,128]{1,0:T(8,128)S(1)}, f32[64,128]{1,0:T(8,128)}, u32[]{:S(2)}) copy-start(f32[64,128]{1,0:T(8,128)} %param.6) | copy-start | bytes 98308
  6.5 38.7 %all-gather.3.cloned.1.call-start = ((), (), s32[]{:S(2)}) async-start(), calls=%async_computation.3 | async-start | bytes 3145728 | tf_op jit(solution)/shard_map/all_gather | solution.py:19
  7.3 49.4 %all-to-all-start.1 = ((f32[8,16,2048]{2,1,0:T(8,128)}), f32[8,16,2048]{2,1,0:T(8,128)}, u32[]{:S(2)}, u32[]{:S(2)}) async-start(f32[8,16,2048]{2,1,0:T(8,128)} %bitcast.53), calls=%async_computation.1 | async-start | bytes 2097152 | tf_op jit(solution)/shard_map/all_to_all | solution.py:37
  56.7 31.5 %all-to-all-start = ((f32[8,16,2048]{2,1,0:T(8,128)}), f32[8,16,2048]{2,1,0:T(8,128)}, u32[]{:S(2)}, u32[]{:S(2)}) async-start(f32[8,16,2048]{2,1,0:T(8,128)} %all_to_all.24), calls=%async_computation | async-start | bytes 2097152 | tf_op jit(solution)/shard_map/all_to_all | solution.py:36
  61.5 88.4 %reduce-scatter.2.cloned.1.call-start = ((), (), s32[]{:S(2)}) async-start(), calls=%async_computation.4 | async-start | bytes 278528 | tf_op jit(solution)/shard_map/reduce_scatter | solution.py:48
Sparse Core Ops, SparseCore 0:
  8.9 36.2 all-gather.2
  96.6 53.2 reduce-scatter.1
where the time goes:
time: 157 us
  waiting for transfers between devices  97.5 us (62%)
  between operations  13.5 us (9%)
  local copies, waits for them, and re-layouts  12.4 us (8%)
  matrix products  11.9 us (8%)
  starting transfers between devices  11.4 us (7%)
  blocking collectives  9.31 us (6%)
    reduce_scatter x1, waiting for transfers between devices, local(): lax.psum_scatter(partial_chi, ('aux', 'orb', 'sub'), scatter_dimension=0,...  53.4 us
    all_to_all x1, waiting for transfers between devices, local(): lax.all_to_all(products, ('aux', 'sub'), split_axis=0, concat_axis=1, til...  23.8 us
    all_gather x1, waiting for transfers between devices, local(): lax.all_gather(three_center, 'orb', axis=1, tiled=True)  19.6 us
    all_to_all x1, starting transfers between devices, local(): lax.all_to_all(flat_tensor, ('aux', 'sub'), split_axis=0, concat_axis=1,...  6.34 us
    all_gather x1, blocking collectives, local(): virt_full = lax.all_gather(virtual_green, 'orb', axis=0, tiled=True)  5.1 us
    all_to_all x1, starting transfers between devices, local(): lax.all_to_all(products, ('aux', 'sub'), split_axis=0, concat_axis=1, til...  4.81 us
    dot_general x1, matrix products, local(): jnp.einsum('lnpw,nwks->kspl', middle_four, virt_sel, precision=lax.Precis...  4.63 us
    dot_general x1, matrix products, local(): jnp.einsum('rpl,rql->pq', product_moved.reshape(piece_rows, nauxf, width)...  4.25 us
  transfers between devices with their start and end apart: 4, of which 3 were waited for; matrix products, arithmetic and copies ran while one was open for 10% of the time, Pallas kernels for 0%

commit v1 on v0

v1 whole, which is shorter than its diff:
```python
import math

import jax
import jax.numpy as jnp
from jax import lax
from jax.sharding import PartitionSpec as P

PRECISION = lax.Precision.HIGH


def gather_orb(block, nob):
    if nob == 1:
        return block[None]
    me = lax.axis_index("orb")
    pieces = [block]
    for shift in range(1, nob):
        pairs = [(source, (source - shift) % nob) for source in range(nob)]
        pieces.append(lax.ppermute(block, "orb", pairs))
    stacked = jnp.stack(pieces)
    order = (jnp.arange(nob) - me) % nob
    return jnp.take(stacked, order, axis=0)


def local(three_center, occupied_green, virtual_green, block_list, nob, npieces):
    slots = three_center.shape[2]
    width = three_center.shape[3]
    columns = three_center.shape[4]
    rows_aux = columns // width
    norb = occupied_green.shape[1]
    own_list = block_list[0]
    flat_tensor = three_center.reshape(slots * width, columns)
    listed = jnp.zeros((8, norb), jnp.float32).at[0, :slots].set(own_list.astype(jnp.float32))
    small = lax.all_gather(jnp.concatenate([virtual_green, listed]), "orb", axis=0, tiled=False)
    virt_full = small[:, :width]
    lists = small[:, width, :slots].astype(jnp.int32)
    tensors = gather_orb(flat_tensor, nob)
    tensor_moved = lax.all_to_all(flat_tensor, ("aux", "sub"), split_axis=0, concat_axis=1, tiled=True)
    occ_sel = jnp.take(occupied_green.reshape(width, nob, width), lists.reshape(-1), axis=1)
    occ_sel = occ_sel.reshape(width, nob, slots * width)
    middle = jnp.einsum("lnm,nmc->lnc", occ_sel, tensors, precision=PRECISION)
    middle_four = middle.reshape(width, nob, rows_aux, width)
    virt_sel = jnp.take(virt_full.reshape(nob, width, nob, width), own_list, axis=2)
    products = jnp.einsum("lnpw,nwks->kspl", middle_four, virt_sel, precision=PRECISION)
    products = products.reshape(slots * width, columns)
    product_moved = lax.all_to_all(products, ("aux", "sub"), split_axis=0, concat_axis=1, tiled=True)
    piece_rows = product_moved.shape[0]
    nauxf = product_moved.shape[1] // width
    partial_chi = jnp.einsum(
        "rpl,rql->pq",
        product_moved.reshape(piece_rows, nauxf, width),
        tensor_moved.reshape(piece_rows, nauxf, width),
        precision=PRECISION,
    )
    partial_chi = partial_chi * (-2.0 / math.sqrt(norb * slots * width))
    pieces = npieces
    received = lax.all_to_all(
        partial_chi.reshape(pieces, nauxf // pieces, nauxf), ("aux", "orb", "sub"), split_axis=0, concat_axis=0, tiled=True
    )
    return received.sum(axis=0)


def solution(mesh):
    nob = mesh.shape["orb"]
    npieces = mesh.shape["aux"] * nob * mesh.shape["sub"]
    in_specs = (
        P("aux", "orb", None, None, "sub"),
        P(("tau", "orb"), None),
        P(("tau", "orb"), None),
        P("orb", None),
    )
    out_specs = P(("tau", "aux", "orb", "sub"), None)

    def run(three_center, occupied_green, virtual_green, block_list):
        return local(three_center, occupied_green, virtual_green, block_list, nob, npieces)

    return jax.shard_map(run, mesh=mesh, in_specs=in_specs, out_specs=out_specs, check_vma=False)
```

time: 157 us -> 93.6 us (0.60)
  waiting for transfers between devices: 97.5 us -> 24 us
  blocking collectives: 9.31 us -> 32.5 us
  between operations: 13.5 us -> 0.22 us
  matrix products: 11.9 us -> 6.51 us
  local copies, waits for them, and re-layouts: 12.4 us -> 14.5 us
  starting transfers between devices: 11.4 us -> 13.1 us
    reduce_scatter x1 -> x0, waiting for transfers between devices: 53.4 us -> none  [local(): lax.psum_scatter(partial_chi, ('aux', 'orb', 'sub'), scatter_dimension=0,...]
    all_gather x1 -> x0, waiting for transfers between devices: 19.6 us -> none  [local(): lax.all_gather(three_center, 'orb', axis=1, tiled=True)]
    all_to_all x0 -> x1, blocking collectives: none -> 13.4 us  [local(): lax.all_to_all(partial_chi.reshape(pieces, nauxf // pieces, nauxf), ('aux...]
    all_gather x2 -> x1, blocking collectives: 9.31 us -> 19.1 us  [local(): lax.all_gather(jnp.concatenate([virtual_green, listed]), 'orb', axis=0, t...]
    dot_general x2, matrix products: 7.68 us -> 3.82 us  [the longest x1 2.98 us: local(): jnp.einsum('lnpw,nwks->kspl', middle_four, virt_sel, precision=PRECISION)]
    ppermute x0 -> x1, starting transfers between devices: none -> 3.01 us  [gather_orb(): pieces.append(lax.ppermute(block, 'orb', pairs))]
    gather x0 -> x1, local copies, waits for them, and re-layouts: none -> 2.27 us  [gather_orb(): return jnp.take(stacked, order, axis=0)]
  transfers between devices with their start and end apart: 4 -> 3, of which waited for: 3 -> 1; matrix products, arithmetic and copies ran while one was open for 10% -> 15% of each run, Pallas kernels for 0% -> 0%
where the time goes in v1:
time: 93.6 us; the launch traced here: 93.2 us
  blocking collectives  32.5 us (35%)
  waiting for transfers between devices  24 us (26%)
  local copies, waits for them, and re-layouts  14.5 us (15%)
  starting transfers between devices  13.1 us (14%)
  matrix products  6.51 us (7%)
  other arithmetic  2.25 us (2%)
    all_to_all x1, waiting for transfers between devices, local(): lax.all_to_all(products, ('aux', 'sub'), split_axis=0, concat_axis=1, til...  24 us
    all_gather x1, blocking collectives, local(): lax.all_gather(jnp.concatenate([virtual_green, listed]), 'orb', axis=0, t...  19.1 us
    all_to_all x1, blocking collectives, local(): lax.all_to_all(partial_chi.reshape(pieces, nauxf // pieces, nauxf), ('aux...  13.4 us
    all_to_all x1, starting transfers between devices, local(): lax.all_to_all(products, ('aux', 'sub'), split_axis=0, concat_axis=1, til...  5.13 us
    all_to_all x1, starting transfers between devices, local(): lax.all_to_all(flat_tensor, ('aux', 'sub'), split_axis=0, concat_axis=1,...  5.01 us
    all_to_all x2, local copies, waits for them, and re-layouts, local(): lax.all_to_all(products, ('aux', 'sub'), split_axis=0, concat_axis=1, til...  3.53 us
    ppermute x1, starting transfers between devices, gather_orb(): pieces.append(lax.ppermute(block, 'orb', pairs))  3.01 us
    dot_general x1, matrix products, local(): jnp.einsum('lnpw,nwks->kspl', middle_four, virt_sel, precision=PRECISION)  2.98 us
  transfers between devices with their start and end apart: 3, of which 1 were waited for; matrix products, arithmetic and copies ran while one was open for 15% of the time, Pallas kernels for 0%

profile of v1, /device:TPU:0, one launch (start us, length us, event | category | flops | bytes accessed | tf_op | source)
XLA Modules:
  0.0 93.2 jit_solution(15839882830620461461)
XLA Ops:
  0.0 3.0 %collective-permute-start = (f32[128,2048]{1,0:T(8,128)}, f32[128,2048]{1,0:T(8,128)S(1)}, u32[]{:S(2)}, u32[]{:S(2)}) collective-permute-start(f32[128,2048]{1,0:T(8,128)} %bitcast.53), channel_id=1, source_target_pairs={{0,2},{2,0},{1,3},{3,1},{4,6},{6,4},{5,7},{7,5},{8,10},{10,8},{9,1... | collective-permute-start | bytes 3145736 | tf_op jit(solution)/shard_map/ppermute | solution.py:18
  3.0 5.0 %all-to-all-start.1 = ((f32[8,16,2048]{2,1,0:T(8,128)}), f32[8,16,2048]{2,1,0:T(8,128)}, u32[]{:S(2)}, u32[]{:S(2)}) async-start(f32[8,16,2048]{2,1,0:T(8,128)} %bitcast.54), calls=%async_computation.1 | async-start | bytes 2097152 | tf_op jit(solution)/shard_map/all_to_all | solution.py:37
  8.0 0.0 copy-done.3
  8.1 19.1 %all-gather = f32[144,128]{1,0:T(8,128)S(1)} all-gather(f32[72,128]{1,0:T(8,128)S(1)} %select_maximum_fusion), channel_id=2, replica_groups=mesh['tau'=2,'aux'=4,'orb'=2,'sub'=2] {'orb'}, dimensions={0}, use_global_device_ids=true | all-gather | bytes 110592 | tf_op jit(solution)/shard_map/all_gather | solution.py:33
  27.2 0.1 convert_element_type.27
  27.3 0.0 copy-done.1
  27.3 0.1 reshape.185
  27.4 0.6 gather_fusion.2
  28.0 0.1 copy.32
  28.1 0.1 gather.17
  28.2 0.1 broadcast_in_dim.39
  28.3 0.1 broadcast_in_dim.40
  28.4 0.1 reshape.183
  28.6 0.6 gather_fusion
  29.2 0.0 collective-permute-done
  29.2 1.5 %pad_maximum_fusion = f32[2,128,2048]{2,1,0:T(8,128)} fusion(f32[1,128,2048]{2,1,0:T(8,128)S(1)} %bitcast.57, f32[1,128,2048]{2,1,0:T(8,128)S(1)} %bitcast.55), kind=kLoop, calls=%fused_computation.4 | loop fusion | flops 524288 | bytes 4194304 | tf_op jit(solution)/shard_map/stack | solution.py:19
  30.7 2.3 %gather_fusion.1 = f32[2,128,2048]{2,1,0:T(8,128)S(1)} fusion(f32[2,128,2048]{2,1,0:T(8,128)} %pad_maximum_fusion, s32[1024]{0:T(1024)S(1)} %pad_clamp_fusion.1), kind=kCustom, calls=%fused_computation.1 | custom fusion | bytes 4194312 | tf_op jit(solution)/shard_map/jit(_take)/gather | solution.py:21
  33.0 0.8 convolution_bitcast_fusion
  33.9 0.8 reshape.186
  34.7 3.0 %fusion.4 = f32[2,64,32,64]{3,1,2,0:T(8,128)S(1)} fusion(f32[64,2,32,64]{3,2,0,1:T(8,128)S(1)} %reshape.186, f32[2,2,64,64]{3,2,1,0:T(8,128)S(1)} %gather_fusion, pred[2]{0:T(512)(128)(4,1)S(1)} %compare_and_fusion.2), kind=kOutput, calls=%fused_computation.9 | convolution fusion | flops 201342976 | bytes 2162690 | tf_op jit(solution)/shard_map/lnpw,nwks->kspl/dot_general | solution.py:43
  37.7 1.2 %copy.36 = f32[2,64,32,64]{3,2,1,0:T(8,128)S(1)} copy(f32[2,64,32,64]{3,1,2,0:T(8,128)S(1)} %fusion.4) | data formatting | bytes 2097152 | tf_op jit(solution)/shard_map/lnpw,nwks->kspl/transpose | solution.py:43
  38.9 1.7 %all_to_all.27 = f32[8,16,2048]{2,1,0:T(8,128)} reshape(f32[2,64,32,64]{3,2,1,0:T(8,128)S(1)} %copy.36) | data formatting | bytes 2097152 | tf_op jit(solution)/shard_map/all_to_all | solution.py:45
  40.6 0.0 all-to-all-done.1
  40.6 5.1 %all-to-all-start = ((f32[8,16,2048]{2,1,0:T(8,128)}), f32[8,16,2048]{2,1,0:T(8,128)}, u32[]{:S(2)}, u32[]{:S(2)}) async-start(f32[8,16,2048]{2,1,0:T(8,128)} %all_to_all.27), calls=%async_computation | async-start | bytes 2097152 | tf_op jit(solution)/shard_map/all_to_all | solution.py:45
  45.7 1.8 %copy.38 = f32[16,8,2048]{2,1,0:T(8,128)S(1)} copy(f32[16,8,2048]{2,0,1:T(8,128)} %bitcast.20) | data formatting | bytes 2097152 | tf_op jit(solution)/shard_map/all_to_all | solution.py:37
  47.6 0.8 reshape.188
  48.4 24.0 %all-to-all-done = f32[8,16,2048]{2,1,0:T(8,128)} async-done(((f32[8,16,2048]{2,1,0:T(8,128)}), f32[8,16,2048]{2,1,0:T(8,128)}, u32[]{:S(2)}, u32[]{:S(2)}) %all-to-all-start) | async-done | bytes 1048608 | tf_op jit(solution)/shard_map/all_to_all | solution.py:45
  72.4 1.8 %copy.37 = f32[16,8,2048]{2,1,0:T(8,128)S(1)} copy(f32[16,8,2048]{2,0,1:T(8,128)} %bitcast.18) | data formatting | bytes 2097152 | tf_op jit(solution)/shard_map/all_to_all | solution.py:45
  74.3 2.2 %reshape.187 = f32[16,256,64]{2,1,0:T(8,128)} reshape(f32[16,8,2048]{2,1,0:T(8,128)S(1)} %copy.37) | data formatting | bytes 2097152 | tf_op jit(solution)/shard_map/reshape | solution.py:50
  76.5 2.7 %fusion.7 = f32[256,256]{1,0:T(8,128)S(1)} fusion(f32[16,256,64]{2,1,0:T(8,128)} %reshape.187, f32[16,256,64]{2,1,0:T(8,128)S(1)} %reshape.188), kind=kOutput, calls=%fused_computation.11 | convolution fusion | flops 402718720 | bytes 2359296 | tf_op jit(solution)/shard_map/rpl,rql->pq/dot_general | solution.py:48
  79.2 13.4 %all_to_all.37 = f32[16,16,256]{2,1,0:T(8,128)S(1)} all-to-all(f32[16,16,256]{2,1,0:T(8,128)S(1)} %bitcast.56), channel_id=1, replica_groups=mesh['tau'=2,'aux'=4,'orb'=2,'sub'=2] {'aux','orb','sub'}, dimensions={0} | all-to-all | bytes 524288 | tf_op jit(solution)/shard_map/all_to_all | solution.py:56
  92.6 0.6 reduce_sum.9
  (23 shorter events, 0.2 us)
Async XLA Ops:
  0.0 8.0 %copy-start.3 = (s32[1,2]{1,0:T(1,128)S(1)}, s32[1,2]{1,0:T(1,128)}, u32[]{:S(2)}) copy-start(s32[1,2]{1,0:T(1,128)} %param.9) | copy-start | bytes 28
  0.0 8.0 %copy-start.2 = (f32[64,128]{1,0:T(8,128)S(1)}, f32[64,128]{1,0:T(8,128)}, u32[]{:S(2)}) copy-start(f32[64,128]{1,0:T(8,128)} %param.8) | copy-start | bytes 98308
  0.0 27.3 %copy-start.1 = (f32[64,128]{1,0:T(8,128)S(1)}, f32[64,128]{1,0:T(8,128)}, u32[]{:S(2)}) copy-start(f32[64,128]{1,0:T(8,128)} %param.7) | copy-start | bytes 98308
  0.0 29.2 %collective-permute-start = (f32[128,2048]{1,0:T(8,128)}, f32[128,2048]{1,0:T(8,128)S(1)}, u32[]{:S(2)}, u32[]{:S(2)}) collective-permute-start(f32[128,2048]{1,0:T(8,128)} %bitcast.53), channel_id=1, source_target_pairs={{0,2},{2,0},{1,3},{3,1},{4,6},{6,4},{5,7},{7,5},{8,10},{10,8},{9,1... | collective-permute-start | bytes 3145736 | tf_op jit(solution)/shard_map/ppermute | solution.py:18
  3.0 26.2 %copy-start = (f32[1,1,2,64,2048]{4,3,2,1,0:T(8,128)S(1)}, f32[1,1,2,64,2048]{4,3,2,1,0:T(8,128)}, u32[]{:S(2)}) copy-start(f32[1,1,2,64,2048]{4,3,2,1,0:T(8,128)} %param.6) | copy-start | bytes 3145732
  3.0 37.6 %all-to-all-start.1 = ((f32[8,16,2048]{2,1,0:T(8,128)}), f32[8,16,2048]{2,1,0:T(8,128)}, u32[]{:S(2)}, u32[]{:S(2)}) async-start(f32[8,16,2048]{2,1,0:T(8,128)} %bitcast.54), calls=%async_computation.1 | async-start | bytes 2097152 | tf_op jit(solution)/shard_map/all_to_all | solution.py:37
  40.6 31.8 %all-to-all-start = ((f32[8,16,2048]{2,1,0:T(8,128)}), f32[8,16,2048]{2,1,0:T(8,128)}, u32[]{:S(2)}, u32[]{:S(2)}) async-start(f32[8,16,2048]{2,1,0:T(8,128)} %all_to_all.27), calls=%async_computation | async-start | bytes 2097152 | tf_op jit(solution)/shard_map/all_to_all | solution.py:45

commit v2 on v0

v2 whole, which is shorter than its diff:
```python
import functools
import math

import jax
import jax.numpy as jnp
from jax import lax
from jax.experimental import pallas as pl
from jax.experimental.pallas import tpu as pltpu
from jax.sharding import PartitionSpec as P

VMEM = pl.BlockSpec(memory_space=pltpu.VMEM)
SMEM = pl.BlockSpec(memory_space=pltpu.SMEM)
F32 = jnp.float32
BF16 = jnp.bfloat16
LIST_ROWS = 8
PARAMS = pltpu.CompilerParams(vmem_limit_bytes=48 * 1024 * 1024)


def halves(x):
    high = x.astype(BF16)
    return high, (x - high.astype(F32)).astype(BF16)


def dot(a, b):
    return lax.dot_general(a, b, (((1,), (0,)), ((), ())), preferred_element_type=F32)


def dot_nt(a, b):
    return lax.dot_general(a, b, (((1,), (1,)), ((), ())), preferred_element_type=F32)


def dot_nt3(a, b):
    return dot_nt(a[0], b[0]) + dot_nt(a[0], b[1]) + dot_nt(a[1], b[0])


def prepare(place, tensor_ref, mine_ref, turned, *, share):
    turned[...] = tensor_ref[...].T.reshape(turned.shape)
    start = pl.multiple_of(place[1] * share, share)
    mine_ref[...] = turned[:, pl.ds(start, share), :]


def shifts_of(naux):
    plan = []
    for shift in range(1, naux // 2 + 1):
        if 2 * shift < naux:
            plan.append([(source, (source + shift) % naux) for source in range(naux)])
        else:
            plan.append([(z, z + shift) if z % 2 == 0 else (z + shift, z) for z in range(shift)])
    return plan


def contract(place, greens, *refs, slots, width, share, nob, naux, nt):
    tensors, refs = refs[:nob], refs[nob:]
    mine, refs = refs[:2], refs[2:]
    meets = naux // 2
    pieces_own, refs = refs[:meets], refs[meets:]
    pieces_other, refs = refs[:meets], refs[meets:]
    direct_ref, refs = refs[0], refs[1:]
    back_refs, refs = refs[:meets], refs[meets:]
    acc, spread, side_high, side_low, tensor_high, tensor_low = refs
    me_orb, me_tau, me_sub = place[0], place[1], place[2]
    listed = slots * width
    rows_aux = tensors[0].shape[1] // width
    pairs = rows_aux // 2
    groups = 2 * nt

    def select(block, owner):
        parts = []
        for slot in range(slots):
            entry = greens[0, owner, 2 * width : 2 * width + 1, slot : slot + 1]
            chosen = jnp.zeros((block.shape[0], width), F32)
            for j in range(nob):
                chosen = jnp.where(entry == float(j), block[:, j * width : (j + 1) * width], chosen)
            parts.append(chosen)
        return jnp.concatenate(parts, axis=1)

    for i in range(nob):
        owner = lax.rem(me_orb + i, nob)
        left = []
        for kind in range(2):
            for tau in range(nt):
                start = pl.multiple_of(kind * width + me_tau * share, share)
                left.append(select(greens[tau, me_orb, pl.ds(start, share), :], owner))
        left_high, left_low = halves(jnp.concatenate(left, axis=0))
        high, low = halves(tensors[i][...])
        middle = dot(
            jnp.concatenate([left_high, left_high, left_low], axis=1), jnp.concatenate([high, low, high], axis=0)
        )
        middle_high, middle_low = halves(middle)
        for group in range(groups):
            kind, tau = group // nt, group % nt
            right = select(greens[tau, owner, (1 - kind) * width : (2 - kind) * width, :], me_orb)
            zero = jnp.zeros_like(right)
            right_high, right_low = halves(
                jnp.concatenate(
                    [jnp.concatenate([right, zero], axis=1), jnp.concatenate([zero, right], axis=1)], axis=0
                )
            )

            def stacked(array):
                rows = array[group * share : (group + 1) * share]
                return jnp.concatenate(
                    [rows[:, 2 * width * at : 2 * width * (at + 1)] for at in range(pairs)], axis=0
                )

            rows_high, rows_low = stacked(middle_high), stacked(middle_low)
            result = dot(
                jnp.concatenate([rows_high, rows_high, rows_low], axis=1),
                jnp.concatenate([right_high, right_low, right_high], axis=0),
            )
            if i > 0:
                result = acc[group] + result
            if i < nob - 1:
                acc[group] = result
            else:
                for at in range(pairs):
                    for second in range(2):
                        row = (group * rows_aux + 2 * at + second) * share
                        spread[row : row + share, :] = result[
                            at * share : (at + 1) * share, second * listed : (second + 1) * listed
                        ]

    rows = groups * rows_aux
    for at in range(share):
        high, low = halves(spread[pl.ds(at, rows, stride=share), :])
        side_high[:, at * listed : (at + 1) * listed] = high
        side_low[:, at * listed : (at + 1) * listed] = low
    direct_rows = nt * rows_aux
    side_direct = side_high[:direct_rows], side_low[:direct_rows]
    side_back = side_high[direct_rows:], side_low[direct_rows:]

    blocks = [jnp.zeros((direct_rows, 2 * rows_aux), F32)] * naux
    for shift, sources in enumerate([mine] + list(zip(pieces_own, pieces_other))):
        for which, source in enumerate(sources):
            start = pl.multiple_of(jnp.where(me_sub == which, 0, rows_aux), rows_aux)
            for at in range(share):
                high, low = halves(source[pl.ds(at, rows_aux, stride=share), :])
                tensor_high[shift, pl.ds(start, rows_aux), at * listed : (at + 1) * listed] = high
                tensor_low[shift, pl.ds(start, rows_aux), at * listed : (at + 1) * listed] = low
        tensor = tensor_high[shift], tensor_low[shift]
        blocks[(naux - shift) % naux] = dot_nt3(side_direct, tensor)
        if shift == 0:
            continue
        back = dot_nt3(tensor, side_back)
        parts = []
        for tau in range(nt):
            part = back[:, tau * rows_aux : (tau + 1) * rows_aux]
            zero = jnp.zeros_like(part)
            parts.append(
                jnp.where(
                    me_sub == 0, jnp.concatenate([part, zero], axis=1), jnp.concatenate([zero, part], axis=1)
                )
            )
        back_refs[shift - 1][...] = jnp.concatenate(parts, axis=1)
    direct = jnp.concatenate(blocks, axis=1)
    for tau in range(nt):
        direct_ref[tau] = direct[tau * rows_aux : (tau + 1) * rows_aux]


def assemble(place, direct_ref, *refs):
    back_refs, out_ref = refs[:-1], refs[-1]
    nt, half, _ = direct_ref.shape
    block = back_refs[0].shape[1] // nt
    start = pl.multiple_of(place[2] * half, half)
    for tau in range(nt):
        parts = [ref[:, tau * block : (tau + 1) * block] for ref in back_refs]
        rest = jnp.zeros((block, direct_ref.shape[2] - block * (1 + len(parts))), F32)
        out_ref[tau] = jnp.concatenate([jnp.zeros_like(parts[0])] + parts + [rest], axis=1)
        out_ref[tau, pl.ds(start, half), :] += direct_ref[tau]


def local(three_center, occupied_green, virtual_green, block_list, sizes):
    nt, naux, nob, nsub = sizes
    slots = three_center.shape[2]
    width = three_center.shape[3]
    columns = three_center.shape[4]
    rows_aux = columns // width
    block_aux = rows_aux * nsub
    norb = occupied_green.shape[1]
    listed = slots * width
    share = width // nt
    nauxf = naux * block_aux
    me_orb, me_tau, me_sub, me_aux = (lax.axis_index(axis) for axis in ("orb", "tau", "sub", "aux"))
    place = jnp.stack([me_orb, me_tau, me_sub, me_aux]).astype(jnp.int32)
    tensor = three_center.reshape(listed, columns)

    tensors = [tensor]
    for shift in range(1, nob):
        pairs = [(source, (source - shift) % nob) for source in range(nob)]
        tensors.append(lax.ppermute(tensor, "orb", pairs))

    mine = pl.pallas_call(
        functools.partial(prepare, share=share),
        out_shape=jax.ShapeDtypeStruct((rows_aux, share, listed), F32),
        in_specs=[SMEM, VMEM],
        out_specs=VMEM,
        scratch_shapes=[pltpu.VMEM((rows_aux, width, listed), F32)],
        compiler_params=PARAMS,
        name="prepare",
    )(place, tensor)
    plan = shifts_of(naux)
    pieces = [lax.ppermute(mine, "aux", pairs) for pairs in plan]
    swap = [(source, (source + 1) % nsub) for source in range(nsub)]
    mine_other = lax.ppermute(mine, "sub", swap)

    small = jnp.concatenate(
        [
            occupied_green,
            virtual_green,
            jnp.pad(block_list.astype(F32), ((0, LIST_ROWS - 1), (0, norb - slots))),
        ]
    )
    greens = lax.all_gather(small, ("tau", "orb"), axis=0, tiled=False)
    greens = greens.reshape((nt, nob) + small.shape)

    pieces_other = [lax.ppermute(block, "sub", swap) for block in pieces]
    flat = lambda block: block.reshape(-1, listed)
    groups = 2 * nt
    direct, *backs = pl.pallas_call(
        functools.partial(contract, slots=slots, width=width, share=share, nob=nob, naux=naux, nt=nt),
        out_shape=[jax.ShapeDtypeStruct((nt, rows_aux, nauxf), F32)]
        + [jax.ShapeDtypeStruct((block_aux, nt * block_aux), F32)] * len(plan),
        in_specs=[SMEM] + [VMEM] * (1 + nob + 2 + 2 * len(plan)),
        out_specs=[VMEM] * (1 + len(plan)),
        scratch_shapes=[
            pltpu.VMEM((groups, rows_aux // 2 * share, 2 * listed), F32),
            pltpu.VMEM((groups * rows_aux * share, listed), F32),
            pltpu.VMEM((groups * rows_aux, share * listed), BF16),
            pltpu.VMEM((groups * rows_aux, share * listed), BF16),
            pltpu.VMEM((1 + len(plan), block_aux, share * listed), BF16),
            pltpu.VMEM((1 + len(plan), block_aux, share * listed), BF16),
        ],
        compiler_params=PARAMS,
        name="contract",
    )(place, greens, *tensors, flat(mine), flat(mine_other), *map(flat, pieces), *map(flat, pieces_other))

    returned = [
        lax.ppermute(back, "aux", [(target, source) for source, target in pairs]) for back, pairs in zip(backs, plan)
    ]
    partial_chi = pl.pallas_call(
        assemble,
        out_shape=jax.ShapeDtypeStruct((nt, block_aux, nauxf), F32),
        in_specs=[SMEM] + [VMEM] * (1 + len(plan)),
        out_specs=VMEM,
        compiler_params=PARAMS,
        name="assemble",
    )(place, direct, *returned)
    owners = nt * nob * nsub
    received = lax.all_to_all(
        partial_chi.reshape(owners, nt * block_aux // owners, nauxf),
        ("tau", "orb", "sub"),
        split_axis=0,
        concat_axis=0,
        tiled=True,
    )
    total = received.sum(axis=0) * (-2.0 / math.sqrt(norb * slots * width))
    return jnp.roll(total, me_aux * block_aux, axis=1)


def solution(mesh):
    sizes = tuple(mesh.shape[axis] for axis in ("tau", "aux", "orb", "sub"))
    in_specs = (
        P("aux", "orb", None, None, "sub"),
        P(("tau", "orb"), None),
        P(("tau", "orb"), None),
        P("orb", None),
    )
    out_specs = P(("tau", "aux", "orb", "sub"), None)
    return jax.shard_map(
        functools.partial(local, sizes=sizes), mesh=mesh, in_specs=in_specs, out_specs=out_specs, check_vma=False
    )
```

time: 157 us -> 68.6 us (0.44)
  waiting for transfers between devices: 97.5 us -> 33.4 us
  between operations: 13.5 us -> 0.13 us
  matrix products: 11.9 us -> 0 us
  Pallas kernels: 0 us -> 11.2 us
  local copies, waits for them, and re-layouts: 12.4 us -> 1.24 us
    reduce_scatter x1 -> x0, waiting for transfers between devices: 53.4 us -> none  [local(): lax.psum_scatter(partial_chi, ('aux', 'orb', 'sub'), scatter_dimension=0,...]
    ppermute x0 -> x8, waiting for transfers between devices: none -> 28 us  [the longest x2 22.5 us: local(): pieces = [lax.ppermute(mine, 'aux', pairs) for pairs in plan]]
    all_gather x1 -> x0, waiting for transfers between devices: 19.6 us -> none  [local(): lax.all_gather(three_center, 'orb', axis=1, tiled=True)]
    all_to_all x2 -> x1, waiting for transfers between devices: 23.8 us -> 5.44 us  [local(): lax.all_to_all(partial_chi.reshape(owners, nt * block_aux // owners, naux...]
    dot_general x3 -> x0, matrix products: 11.9 us -> none  [the longest x1 4.63 us: local(): jnp.einsum('lnpw,nwks->kspl', middle_four, virt_sel, precision=lax.Precis...]
    pallas_call x0 -> x3, Pallas kernels: none -> 11.2 us  [the longest x1 9.04 us: local(): pl.pallas_call(functools.partial(contract, slots=slots, width=width, shar...]
    ppermute x0 -> x8, starting transfers between devices: none -> 8.95 us  [the longest x2 6.03 us: local(): pieces = [lax.ppermute(mine, 'aux', pairs) for pairs in plan]]
    all_to_all x2 -> x1, starting transfers between devices: 11.1 us -> 3.37 us  [local(): lax.all_to_all(partial_chi.reshape(owners, nt * block_aux // owners, naux...]
  transfers between devices with their start and end apart: 4 -> 9, of which waited for: 3 -> 5; matrix products, arithmetic and copies ran while one was open for 10% -> 0% of each run, Pallas kernels for 0% -> 0%
where the time goes in v2:
time: 68.6 us; the launch traced here: 68.3 us
  waiting for transfers between devices  33.4 us (49%)
  starting transfers between devices  12.3 us (18%)
  Pallas kernels  11.2 us (16%)
  blocking collectives  9.13 us (13%)
  local copies, waits for them, and re-layouts  1.24 us (2%)
  other arithmetic  0.8 us (1%)
    ppermute x2, waiting for transfers between devices, local(): pieces = [lax.ppermute(mine, 'aux', pairs) for pairs in plan]  22.5 us
    all_gather x1, blocking collectives, local(): greens = lax.all_gather(small, ('tau', 'orb'), axis=0, tiled=False)  9.13 us
    pallas_call x1, Pallas kernels, local(): pl.pallas_call(functools.partial(contract, slots=slots, width=width, shar...  9.04 us
    ppermute x2, starting transfers between devices, local(): pieces = [lax.ppermute(mine, 'aux', pairs) for pairs in plan]  6.03 us
    all_to_all x1, waiting for transfers between devices, local(): lax.all_to_all(partial_chi.reshape(owners, nt * block_aux // owners, naux...  5.44 us
    ppermute x2, waiting for transfers between devices, local(): lax.ppermute(back, 'aux', [(target, source) for source, target in pairs])  5.41 us
    all_to_all x1, starting transfers between devices, local(): lax.all_to_all(partial_chi.reshape(owners, nt * block_aux // owners, naux...  3.37 us
    ppermute x1, starting transfers between devices, local(): tensors.append(lax.ppermute(tensor, 'orb', pairs))  1.56 us
  transfers between devices with their start and end apart: 9, of which 5 were waited for; matrix products, arithmetic and copies ran while one was open for 0% of the time, Pallas kernels for 0%

profile of v2, /device:TPU:0, one launch (start us, length us, event | category | flops | bytes accessed | tf_op | source)
XLA Modules:
  0.0 68.3 jit_solution(16351668977110536125)
XLA Ops:
  0.0 0.1 pad_add_fusion.place
  0.1 0.0 copy-start
  0.1 1.2 %copy-done = f32[1,1,2,64,2048]{4,3,2,1,0:T(8,128)S(1)} copy-done((f32[1,1,2,64,2048]{4,3,2,1,0:T(8,128)S(1)}, f32[1,1,2,64,2048]{4,3,2,1,0:T(8,128)}, u32[]{:S(2)}) %copy-start) | copy-done | bytes 1048600
  1.3 0.0 copy-start.3
  1.3 0.0 copy-start.1
  1.3 0.0 copy-start.2
  1.3 0.9 %prepare.1 = f32[32,32,128]{2,1,0:T(8,128)S(1)} custom-call(s32[4]{0:T(128)S(1)} %pad_add_fusion.place, f32[128,2048]{1,0:T(8,128)S(1)} %bitcast.13), custom_call_target="tpu_custom_call" | custom-call | tf_op jit(solution)/shard_map/prepare/pallas_call | solution.py:192
  2.2 6.0 %collective-permute-start.3 = (f32[32,32,128]{2,1,0:T(8,128)S(1)}, f32[32,32,128]{2,1,0:T(8,128)S(1)}, u32[]{:S(2)}, u32[]{:S(2)}) collective-permute-start(f32[32,32,128]{2,1,0:T(8,128)S(1)} %prepare.1), channel_id=1, source_target_pairs={{0,8},{12,4},{1,9},{13,5},{2,10},{14,6},{3,11},{15,7},{16,24},{28,... | collective-permute-start | bytes 1572872 | tf_op jit(solution)/shard_map/ppermute | solution.py:202
  8.2 0.1 collective-permute-start.2
  8.3 1.6 %collective-permute-start = (f32[128,2048]{1,0:T(8,128)S(1)}, f32[128,2048]{1,0:T(8,128)S(1)}, u32[]{:S(2)}, u32[]{:S(2)}) collective-permute-start(f32[128,2048]{1,0:T(8,128)S(1)} %bitcast.14), channel_id=1, source_target_pairs={{0,2},{2,0},{1,3},{3,1},{4,6},{6,4},{5,7},{7,5},{8,10},{10,8},{9,1... | collective-permute-start | bytes 3145736 | tf_op jit(solution)/shard_map/ppermute | solution.py:190
  9.8 0.0 collective-permute-start.1
  9.8 10.7 %collective-permute-done.3 = f32[32,32,128]{2,1,0:T(8,128)S(1)} collective-permute-done((f32[32,32,128]{2,1,0:T(8,128)S(1)}, f32[32,32,128]{2,1,0:T(8,128)S(1)}, u32[]{:S(2)}, u32[]{:S(2)}) %collective-permute-start.3) | collective-permute-done | bytes 524320 | tf_op jit(solution)/shard_map/ppermute | solution.py:202
  20.5 0.0 collective-permute-start.5
  20.5 11.9 %collective-permute-done.2 = f32[32,32,128]{2,1,0:T(8,128)S(1)} collective-permute-done((f32[32,32,128]{2,1,0:T(8,128)S(1)}, f32[32,32,128]{2,1,0:T(8,128)S(1)}, u32[]{:S(2)}, u32[]{:S(2)}) %collective-permute-start.2) | collective-permute-done | bytes 524320 | tf_op jit(solution)/shard_map/ppermute | solution.py:202
  32.4 0.0 collective-permute-start.4
  32.4 0.0 copy-done.3
  32.4 0.0 copy-done.1
  32.4 0.0 copy-done.2
  32.4 9.1 %all-gather = f32[544,128]{1,0:T(8,128)S(1)} all-gather(f32[136,128]{1,0:T(8,128)S(1)} %select_maximum_fusion), channel_id=2, replica_groups=mesh['tau'=2,'aux'=4,'orb'=2,'sub'=2] {'tau','orb'}, dimensions={0}, use_global_device_ids=true | all-gather | bytes 348160 | tf_op jit(solution)/shard_map/all_gather | solution.py:213
  41.6 0.0 collective-permute-done.1
  41.6 0.0 collective-permute-done.5
  41.6 0.0 collective-permute-done.4
  41.6 0.0 collective-permute-done.refs_1_
  41.6 9.0 %contract.1 = (f32[2,32,256]{2,1,0:T(8,128)S(1)}, f32[64,128]{1,0:T(8,128)S(1)}, f32[64,128]{1,0:T(8,128)S(1)}) custom-call(s32[4]{0:T(128)S(1)} %pad_add_fusion.place, f32[2,2,136,128]{3,2,1,0:T(8,128)S(1)} %bitcast.17, f32[128,2048]{1,0:T(8,128)S(1)} %bitcast.15, f32[128,2048]{1,0:T(8,128)S(1)} %collective-permute-done.refs_1_, f32[1024,128]{1,0:T(8,128)S(1)} %bitcast.16, ...), custom_call_target="tpu_custom_call" | custom-call | tf_op jit(solution)/shard_map/contract/pallas_call | solution.py:219
  50.6 0.1 collective-permute-start.6
  50.7 1.3 %collective-permute-start.7 = (f32[64,128]{1,0:T(8,128)S(1)}, f32[64,128]{1,0:T(8,128)S(1)}, u32[]{:S(2)}, u32[]{:S(2)}) collective-permute-start(f32[64,128]{1,0:T(8,128)S(1)} %get-tuple-element.10), channel_id=1, source_target_pairs={{8,0},{4,12},{9,1},{5,13},{10,2},{6,14},{11,3},{7,15},{24,16},{20,... | collective-permute-start | bytes 98312 | tf_op jit(solution)/shard_map/ppermute | solution.py:238
  52.0 2.6 %collective-permute-done.6.refs_0_ = f32[64,128]{1,0:T(8,128)S(1)} collective-permute-done((f32[64,128]{1,0:T(8,128)S(1)}, f32[64,128]{1,0:T(8,128)S(1)}, u32[]{:S(2)}, u32[]{:S(2)}) %collective-permute-start.6) | collective-permute-done | bytes 32800 | tf_op jit(solution)/shard_map/ppermute | solution.py:238
  54.6 2.8 %collective-permute-done.7.refs_1_ = f32[64,128]{1,0:T(8,128)S(1)} collective-permute-done((f32[64,128]{1,0:T(8,128)S(1)}, f32[64,128]{1,0:T(8,128)S(1)}, u32[]{:S(2)}, u32[]{:S(2)}) %collective-permute-start.7) | collective-permute-done | bytes 32800 | tf_op jit(solution)/shard_map/ppermute | solution.py:238
  57.4 1.3 %assemble.1 = f32[2,64,256]{2,1,0:T(8,128)} custom-call(s32[4]{0:T(128)S(1)} %pad_add_fusion.place, f32[2,32,256]{2,1,0:T(8,128)S(1)} %get-tuple-element.8.direct_ref, f32[64,128]{1,0:T(8,128)S(1)} %collective-permute-done.6.refs_0_, f32[64,128]{1,0:T(8,128)S(1)} %collective-permute-done.7.refs_1_), custom_call_target="tpu_custom_call" | custom-call | tf_op jit(solution)/shard_map/assemble/pallas_call | solution.py:240
  58.7 3.4 %all-to-all-start = ((f32[8,16,256]{2,1,0:T(8,128)}), f32[8,16,256]{2,1,0:T(8,128)S(1)}, u32[]{:S(2)}, u32[]{:S(2)}) async-start(f32[8,16,256]{2,1,0:T(8,128)} %bitcast.12), calls=%async_computation | async-start | bytes 262144 | tf_op jit(solution)/shard_map/all_to_all | solution.py:249
  62.1 5.4 %all-to-all-done = f32[8,16,256]{2,1,0:T(8,128)S(1)} async-done(((f32[8,16,256]{2,1,0:T(8,128)}), f32[8,16,256]{2,1,0:T(8,128)S(1)}, u32[]{:S(2)}, u32[]{:S(2)}) %all-to-all-start) | async-done | bytes 131104 | tf_op jit(solution)/shard_map/all_to_all | solution.py:249
  67.6 0.7 %fusion = f32[16,256]{1,0:T(8,128)} fusion(s32[]{:T(128)S(6)} %select_n.14, f32[16,256]{1,0:T(8,128)S(1)} %broadcast_multiply_fusion), kind=kLoop, calls=%fused_computation.4 | loop fusion | flops 4096 | bytes 32772 | tf_op jit(solution)/shard_map/jit(_roll_dynamic)/concatenate | solution.py:257
  (4 shorter events, 0.0 us)
Async XLA Ops:
  0.1 1.2 %copy-start = (f32[1,1,2,64,2048]{4,3,2,1,0:T(8,128)S(1)}, f32[1,1,2,64,2048]{4,3,2,1,0:T(8,128)}, u32[]{:S(2)}) copy-start(f32[1,1,2,64,2048]{4,3,2,1,0:T(8,128)} %param.4) | copy-start | bytes 3145732
  1.3 31.1 %copy-start.3 = (s32[1,2]{1,0:T(1,128)S(1)}, s32[1,2]{1,0:T(1,128)}, u32[]{:S(2)}) copy-start(s32[1,2]{1,0:T(1,128)} %param.7) | copy-start | bytes 28
  1.3 31.1 %copy-start.1 = (f32[64,128]{1,0:T(8,128)S(1)}, f32[64,128]{1,0:T(8,128)}, u32[]{:S(2)}) copy-start(f32[64,128]{1,0:T(8,128)} %param.6) | copy-start | bytes 98308
  1.3 31.1 %copy-start.2 = (f32[64,128]{1,0:T(8,128)S(1)}, f32[64,128]{1,0:T(8,128)}, u32[]{:S(2)}) copy-start(f32[64,128]{1,0:T(8,128)} %param.5) | copy-start | bytes 98308
  2.2 18.3 %collective-permute-start.3 = (f32[32,32,128]{2,1,0:T(8,128)S(1)}, f32[32,32,128]{2,1,0:T(8,128)S(1)}, u32[]{:S(2)}, u32[]{:S(2)}) collective-permute-start(f32[32,32,128]{2,1,0:T(8,128)S(1)} %prepare.1), channel_id=1, source_target_pairs={{0,8},{12,4},{1,9},{13,5},{2,10},{14,6},{3,11},{15,7},{16,24},{28,... | collective-permute-start | bytes 1572872 | tf_op jit(solution)/shard_map/ppermute | solution.py:202
  8.2 24.2 %collective-permute-start.2 = (f32[32,32,128]{2,1,0:T(8,128)S(1)}, f32[32,32,128]{2,1,0:T(8,128)S(1)}, u32[]{:S(2)}, u32[]{:S(2)}) collective-permute-start(f32[32,32,128]{2,1,0:T(8,128)S(1)} %prepare.1), channel_id=1, source_target_pairs={{0,4},{4,8},{8,12},{12,0},{1,5},{5,9},{9,13},{13,1},{2,6},{6,10},{... | collective-permute-start | bytes 1572872 | tf_op jit(solution)/shard_map/ppermute | solution.py:202
  8.3 33.3 %collective-permute-start = (f32[128,2048]{1,0:T(8,128)S(1)}, f32[128,2048]{1,0:T(8,128)S(1)}, u32[]{:S(2)}, u32[]{:S(2)}) collective-permute-start(f32[128,2048]{1,0:T(8,128)S(1)} %bitcast.14), channel_id=1, source_target_pairs={{0,2},{2,0},{1,3},{3,1},{4,6},{6,4},{5,7},{7,5},{8,10},{10,8},{9,1... | collective-permute-start | bytes 3145736 | tf_op jit(solution)/shard_map/ppermute | solution.py:190
  9.8 31.7 %collective-permute-start.1 = (f32[32,32,128]{2,1,0:T(8,128)S(1)}, f32[32,32,128]{2,1,0:T(8,128)S(1)}, u32[]{:S(2)}, u32[]{:S(2)}) collective-permute-start(f32[32,32,128]{2,1,0:T(8,128)S(1)} %prepare.1), channel_id=1, source_target_pairs={{0,1},{1,0},{2,3},{3,2},{4,5},{5,4},{6,7},{7,6},{8,9},{9,8},{10,11... | collective-permute-start | bytes 1572872 | tf_op jit(solution)/shard_map/ppermute | solution.py:204
  20.5 21.1 %collective-permute-start.5 = (f32[32,32,128]{2,1,0:T(8,128)S(1)}, f32[32,32,128]{2,1,0:T(8,128)S(1)}, u32[]{:S(2)}, u32[]{:S(2)}) collective-permute-start(f32[32,32,128]{2,1,0:T(8,128)S(1)} %collective-permute-done.3), channel_id=1, source_target_pairs={{0,1},{1,0},{2,3},{3,2},{4,5},{5,4},{6,7},{7,6},{8,9},{9,8},{10,11... | collective-permute-start | bytes 1572872 | tf_op jit(solution)/shard_map/ppermute | solution.py:216
  32.4 9.2 %collective-permute-start.4 = (f32[32,32,128]{2,1,0:T(8,128)S(1)}, f32[32,32,128]{2,1,0:T(8,128)S(1)}, u32[]{:S(2)}, u32[]{:S(2)}) collective-permute-start(f32[32,32,128]{2,1,0:T(8,128)S(1)} %collective-permute-done.2), channel_id=1, source_target_pairs={{0,1},{1,0},{2,3},{3,2},{4,5},{5,4},{6,7},{7,6},{8,9},{9,8},{10,11... | collective-permute-start | bytes 1572872 | tf_op jit(solution)/shard_map/ppermute | solution.py:216
  50.6 4.0 %collective-permute-start.6 = (f32[64,128]{1,0:T(8,128)S(1)}, f32[64,128]{1,0:T(8,128)S(1)}, u32[]{:S(2)}, u32[]{:S(2)}) collective-permute-start(f32[64,128]{1,0:T(8,128)S(1)} %get-tuple-element.9), channel_id=1, source_target_pairs={{4,0},{8,4},{12,8},{0,12},{5,1},{9,5},{13,9},{1,13},{6,2},{10,6},{... | collective-permute-start | bytes 98312 | tf_op jit(solution)/shard_map/ppermute | solution.py:238
  50.7 6.7 %collective-permute-start.7 = (f32[64,128]{1,0:T(8,128)S(1)}, f32[64,128]{1,0:T(8,128)S(1)}, u32[]{:S(2)}, u32[]{:S(2)}) collective-permute-start(f32[64,128]{1,0:T(8,128)S(1)} %get-tuple-element.10), channel_id=1, source_target_pairs={{8,0},{4,12},{9,1},{5,13},{10,2},{6,14},{11,3},{7,15},{24,16},{20,... | collective-permute-start | bytes 98312 | tf_op jit(solution)/shard_map/ppermute | solution.py:238
  58.7 8.8 %all-to-all-start = ((f32[8,16,256]{2,1,0:T(8,128)}), f32[8,16,256]{2,1,0:T(8,128)S(1)}, u32[]{:S(2)}, u32[]{:S(2)}) async-start(f32[8,16,256]{2,1,0:T(8,128)} %bitcast.12), calls=%async_computation | async-start | bytes 262144 | tf_op jit(solution)/shard_map/all_to_all | solution.py:249

commit v3 on v0

v3 whole, which is shorter than its diff:
```python
import functools
import math

import jax
import jax.numpy as jnp
from jax import lax
from jax.experimental import pallas as pl
from jax.experimental.pallas import tpu as pltpu
from jax.sharding import PartitionSpec as P

VMEM = pl.BlockSpec(memory_space=pltpu.VMEM)
SMEM = pl.BlockSpec(memory_space=pltpu.SMEM)
F32 = jnp.float32
BF16 = jnp.bfloat16
LIST_ROWS = 8
PARAMS = pltpu.CompilerParams(vmem_limit_bytes=48 * 1024 * 1024)


def halves(x):
    high = x.astype(BF16)
    return high, (x - high.astype(F32)).astype(BF16)


def dot(a, b):
    return lax.dot_general(a, b, (((1,), (0,)), ((), ())), preferred_element_type=F32)


def dot_nt(a, b):
    return lax.dot_general(a, b, (((1,), (1,)), ((), ())), preferred_element_type=F32)


def dot_nt3(a, b):
    return dot_nt(a[0], b[0]) + dot_nt(a[0], b[1]) + dot_nt(a[1], b[0])


def ring(count, shift):
    return [((target + shift) % count, target) for target in range(count)]


def prepare(place, tensor_ref, token_ref, mine_ref, part_ref, common_ref, turned, *, share):
    part = part_ref.shape[0]
    common = common_ref.shape[0]
    start = pl.multiple_of(place[1] * (part + common), 8)
    part_ref[...] = tensor_ref[pl.ds(start, part), :]
    common_ref[...] = tensor_ref[part : part + common, :]
    turned[...] = tensor_ref[...].T.reshape(turned.shape)
    start = pl.multiple_of(place[1] * share, share)
    mine_ref[...] = turned[:, pl.ds(start, share), :]


def after(block, *tokens):
    return pl.pallas_call(
        lambda *refs: None,
        out_shape=jax.ShapeDtypeStruct(block.shape, block.dtype),
        in_specs=[pl.BlockSpec(memory_space=pl.ANY)] * (1 + len(tokens)),
        out_specs=pl.BlockSpec(memory_space=pl.ANY),
        input_output_aliases={0: 0},
        name="after",
    )(block, *tokens)


def shifts_of(naux):
    plan = []
    for shift in range(1, naux // 2 + 1):
        if 2 * shift < naux:
            plan.append([(source, (source + shift) % naux) for source in range(naux)])
        else:
            plan.append([(z, z + shift) if z % 2 == 0 else (z + shift, z) for z in range(shift)])
    return plan


def select(block, list_rows, slots, width):
    parts = []
    for slot in range(slots):
        entry = list_rows[:1, slot : slot + 1]
        chosen = jnp.zeros((block.shape[0], width), F32)
        for j in range(block.shape[1] // width):
            chosen = jnp.where(entry == float(j), block[:, j * width : (j + 1) * width], chosen)
        parts.append(chosen)
    return jnp.concatenate(parts, axis=1)


def mix(place, greens, i, tensor, slots, width, share):
    nt = greens.shape[0]
    pairs = tensor.shape[1] // (2 * width)
    near_list, far_list = greens[0, 0, 2 * width :, :], greens[0, i, 2 * width :, :]
    which = [lax.rem(tau + nt - place[1], nt) for tau in range(nt)]
    left = []
    for kind in range(2):
        for tau in range(nt):
            start = pl.multiple_of(kind * width + place[1] * share, share)
            left.append(select(greens[which[tau], 0, pl.ds(start, share), :], far_list, slots, width))
    left_high, left_low = halves(jnp.concatenate(left, axis=0))
    high, low = halves(tensor[...])
    middle = dot(
        jnp.concatenate([left_high, left_high, left_low], axis=1), jnp.concatenate([high, low, high], axis=0)
    )
    middle_high, middle_low = halves(middle)
    results = []
    for group in range(2 * nt):
        kind, tau = group // nt, group % nt
        right = select(greens[which[tau], i, (1 - kind) * width : (2 - kind) * width, :], near_list, slots, width)
        zero = jnp.zeros_like(right)
        right_high, right_low = halves(
            jnp.concatenate([jnp.concatenate([right, zero], axis=1), jnp.concatenate([zero, right], axis=1)], axis=0)
        )

        def stacked(array):
            rows = array[group * share : (group + 1) * share]
            return jnp.concatenate([rows[:, 2 * width * at : 2 * width * (at + 1)] for at in range(pairs)], axis=0)

        rows_high, rows_low = stacked(middle_high), stacked(middle_low)
        results.append(
            dot(
                jnp.concatenate([rows_high, rows_high, rows_low], axis=1),
                jnp.concatenate([right_high, right_low, right_high], axis=0),
            )
        )
    return results


def first(place, greens, tensor, acc, *, slots, width, share):
    for group, result in enumerate(mix(place, greens, 0, tensor, slots, width, share)):
        acc[group] = result


def second(place, greens, acc, *refs, slots, width, share):
    refs, (side_high, side_low, spread, tensor) = refs[:-4], refs[-4:]
    listed = slots * width
    groups, tall, _ = acc.shape
    pairs = tall // share
    terms = []
    for i in range(len(refs) // 3):
        direct, shared, over_tau = refs[3 * i : 3 * i + 3]
        part, common = direct.shape[0], shared.shape[0]
        for which, block in enumerate((direct, over_tau)):
            start = jnp.where(place[1] == which, 0, part + common)
            tensor[pl.ds(pl.multiple_of(start, 8), part), :] = block[...]
        tensor[part : part + common, :] = shared[...]
        terms.append(mix(place, greens, 1 + i, tensor, slots, width, share))
    for group in range(groups):
        result = acc[group]
        for term in terms:
            result = result + term[group]
        for at in range(pairs):
            for place_in in range(2):
                row = (group * 2 * pairs + 2 * at + place_in) * share
                spread[row : row + share, :] = result[
                    at * share : (at + 1) * share, place_in * listed : (place_in + 1) * listed
                ]
    rows = groups * 2 * pairs
    for at in range(share):
        high, low = halves(spread[pl.ds(at, rows, stride=share), :])
        side_high[:, at * listed : (at + 1) * listed] = high
        side_low[:, at * listed : (at + 1) * listed] = low


def meet(place, side_high, side_low, own, other, *refs, share, nt):
    outs, (tensor_high, tensor_low) = refs[:-2], refs[-2:]
    listed = own.shape[1]
    rows_aux = own.shape[0] // share
    for which, source in enumerate((own, other)):
        start = pl.multiple_of(jnp.where(place[2] == which, 0, rows_aux), rows_aux)
        for at in range(share):
            high, low = halves(source[pl.ds(at, rows_aux, stride=share), :])
            tensor_high[pl.ds(start, rows_aux), at * listed : (at + 1) * listed] = high
            tensor_low[pl.ds(start, rows_aux), at * listed : (at + 1) * listed] = low
    tensor = tensor_high[...], tensor_low[...]
    rows = nt * rows_aux
    if len(outs) == 2:
        back = dot_nt3(tensor, (side_high[rows:], side_low[rows:]))
        parts = []
        for tau in range(nt):
            part = back[:, tau * rows_aux : (tau + 1) * rows_aux]
            zero = jnp.zeros_like(part)
            parts.append(
                jnp.where(
                    place[2] == 0, jnp.concatenate([part, zero], axis=1), jnp.concatenate([zero, part], axis=1)
                )
            )
        outs[1][...] = jnp.concatenate(parts, axis=1)
    outs[0][...] = dot_nt3((side_high[:rows], side_low[:rows]), tensor)


def assemble(place, *refs, naux, nt):
    refs, out_ref = refs[:-1], refs[-1]
    meets = naux // 2
    directs, backs = refs[: 1 + meets], refs[1 + meets :]
    block = directs[0].shape[1]
    half = directs[0].shape[0] // nt
    start = pl.multiple_of(place[2] * half, half)
    for tau in range(nt):
        here = [jnp.zeros((half, block), F32)] * naux
        for shift, ref in enumerate(directs):
            here[(naux - shift) % naux] = ref[tau * half : (tau + 1) * half, :]
        there = [jnp.zeros((block, block), F32)] * naux
        for shift, ref in enumerate(backs, 1):
            there[shift] = ref[:, tau * block : (tau + 1) * block]
        out_ref[tau] = jnp.concatenate(there, axis=1)
        out_ref[tau, pl.ds(start, half), :] += jnp.concatenate(here, axis=1)


def local(three_center, occupied_green, virtual_green, block_list, sizes):
    nt, naux, nob, nsub = sizes
    slots = three_center.shape[2]
    width = three_center.shape[3]
    columns = three_center.shape[4]
    rows_aux = columns // width
    block_aux = rows_aux * nsub
    norb = occupied_green.shape[1]
    listed = slots * width
    share = width // nt
    nauxf = naux * block_aux
    me_orb, me_tau, me_sub, me_aux = (lax.axis_index(axis) for axis in ("orb", "tau", "sub", "aux"))
    place = jnp.stack([me_orb, me_tau, me_sub, me_aux]).astype(jnp.int32)
    tensor = three_center.reshape(listed, columns)

    small = jnp.concatenate(
        [
            occupied_green,
            virtual_green,
            jnp.pad(block_list.astype(F32), ((0, LIST_ROWS - 1), (0, norb - slots))),
        ]
    )
    row = jnp.stack([small] + [lax.ppermute(small, "orb", ring(nob, shift)) for shift in range(1, nob)])
    greens = jnp.stack([row] + [lax.ppermute(row, "tau", ring(nt, shift)) for shift in range(1, nt)])

    part = listed // 3 // 8 * 8
    common = listed - 2 * part
    mine, part_own, common_own = pl.pallas_call(
        functools.partial(prepare, share=share),
        out_shape=[
            jax.ShapeDtypeStruct(shape, F32)
            for shape in ((rows_aux, share, listed), (part, columns), (common, columns))
        ],
        in_specs=[SMEM, VMEM, pl.BlockSpec(memory_space=pl.ANY)],
        out_specs=[VMEM] * 3,
        scratch_shapes=[pltpu.VMEM((rows_aux, width, listed), F32)],
        compiler_params=PARAMS,
        name="prepare",
    )(place, tensor, row)
    tensors = []
    for shift in range(1, nob):
        direct = after(lax.ppermute(part_own, "orb", ring(nob, shift)), greens)
        over_tau = lax.ppermute(direct, "tau", ring(nt, 1))
        tensors += [direct, lax.ppermute(common_own, "orb", ring(nob, shift)), over_tau]
    plan = shifts_of(naux)
    pieces = [lax.ppermute(mine, "aux", pairs) for pairs in plan]
    swap = ring(nsub, 1)
    mine_other = lax.ppermute(mine, "sub", swap)
    def call(kernel, outs, scratch, flops, *arguments, **options):
        shapes = [jax.ShapeDtypeStruct(shape, kind) for shape, kind in outs]
        size = sum(4 * math.prod(x.shape) for x in arguments)
        return pl.pallas_call(
            functools.partial(kernel, **options),
            out_shape=shapes,
            in_specs=[SMEM] + [VMEM] * len(arguments),
            out_specs=[VMEM] * len(shapes),
            scratch_shapes=[pltpu.VMEM(shape, kind) for shape, kind in scratch],
            compiler_params=PARAMS,
            cost_estimate=pl.CostEstimate(flops=flops, bytes_accessed=size, transcendentals=0),
            name=kernel.__name__,
        )(place, *arguments)

    groups = 2 * nt
    work = 6 * groups * share * columns * listed * 3
    rows = groups * rows_aux
    depth = share * listed
    options = dict(slots=slots, width=width, share=share)
    (acc,) = call(
        first, [((groups, rows_aux // 2 * share, 2 * listed), F32)], [], work, greens, tensor, **options
    )
    side = call(
        second,
        [((rows, depth), BF16)] * 2,
        [((rows * share, listed), F32), ((listed, columns), F32)],
        work * (nob - 1),
        greens,
        acc,
        *tensors,
        **options,
    )
    tokens = [(tensors[-1], mine_other)] + [(side[0],)] * (len(plan) - 1)
    pieces = [after(block, *token) for block, token in zip(pieces, tokens)]
    pieces_other = [lax.ppermute(block, "sub", swap) for block in pieces]
    flat = lambda block: block.reshape(-1, listed)
    turned = [((block_aux, depth), BF16)] * 2
    shape_direct = ((nt * rows_aux, block_aux), F32)
    shape_back = ((block_aux, nt * block_aux), F32)
    work = 6 * rows * block_aux * depth
    (direct,) = call(
        meet, [shape_direct], turned, work, *side, flat(mine), flat(mine_other), share=share, nt=nt
    )
    directs, returned = [direct], []
    for own, other, pairs in zip(pieces, pieces_other, plan):
        direct, back = call(
            meet, [shape_direct, shape_back], turned, work, *side, flat(own), flat(other), share=share, nt=nt
        )
        directs.append(direct)
        returned.append(lax.ppermute(back, "aux", [(target, source) for source, target in pairs]))
    (partial_chi,) = call(
        assemble, [((nt, block_aux, nauxf), F32)], [], 0, *directs, *returned, naux=naux, nt=nt
    )
    owners = nt * nob * nsub
    received = lax.all_to_all(
        partial_chi.reshape(owners, nt * block_aux // owners, nauxf),
        ("tau", "orb", "sub"),
        split_axis=0,
        concat_axis=0,
        tiled=True,
    )
    total = received.sum(axis=0) * (-2.0 / math.sqrt(norb * slots * width))
    return jnp.roll(total, me_aux * block_aux, axis=1)


def solution(mesh):
    sizes = tuple(mesh.shape[axis] for axis in ("tau", "aux", "orb", "sub"))
    in_specs = (
        P("aux", "orb", None, None, "sub"),
        P(("tau", "orb"), None),
        P(("tau", "orb"), None),
        P("orb", None),
    )
    out_specs = P(("tau", "aux", "orb", "sub"), None)
    return jax.shard_map(
        functools.partial(local, sizes=sizes), mesh=mesh, in_specs=in_specs, out_specs=out_specs, check_vma=False
    )
```

time: 157 us -> 63.2 us (0.40)
  waiting for transfers between devices: 97.5 us -> 21.5 us
  Pallas kernels: 0 us -> 15.4 us
  between operations: 13.5 us -> 0.2 us
  matrix products: 11.9 us -> 0 us
  blocking collectives: 9.31 us -> 0 us
  local copies, waits for them, and re-layouts: 12.4 us -> 4.7 us
  starting transfers between devices: 11.4 us -> 17.9 us
  other arithmetic: 0.7 us -> 2.99 us
    reduce_scatter x1 -> x0, waiting for transfers between devices: 53.4 us -> none  [local(): lax.psum_scatter(partial_chi, ('aux', 'orb', 'sub'), scatter_dimension=0,...]
    all_gather x1 -> x0, waiting for transfers between devices: 19.6 us -> none  [local(): lax.all_gather(three_center, 'orb', axis=1, tiled=True)]
    all_to_all x2 -> x1, waiting for transfers between devices: 23.8 us -> 5.44 us  [local(): lax.all_to_all(partial_chi.reshape(owners, nt * block_aux // owners, naux...]
    ppermute x0 -> x12, waiting for transfers between devices: none -> 16.1 us  [the longest x1 6.5 us: local(): lax.ppermute(common_own, 'orb', ring(nob, shift))]
    pallas_call x0 -> x10, Pallas kernels: none -> 15.4 us  [the longest x6 13.7 us: call(): pl.pallas_call(functools.partial(kernel, **options), out_shape=shapes, in...]
    ppermute x0 -> x12, starting transfers between devices: none -> 14.5 us  [the longest x2 5.29 us: local(): pieces = [lax.ppermute(mine, 'aux', pairs) for pairs in plan]]
    dot_general x3 -> x0, matrix products: 11.9 us -> none  [the longest x1 4.63 us: local(): jnp.einsum('lnpw,nwks->kspl', middle_four, virt_sel, precision=lax.Precis...]
    all_gather x2 -> x0, blocking collectives: 9.31 us -> none  [the longest x1 5.1 us: local(): virt_full = lax.all_gather(virtual_green, 'orb', axis=0, tiled=True)]
  transfers between devices with their start and end apart: 4 -> 13, of which waited for: 3 -> 7; matrix products, arithmetic and copies ran while one was open for 10% -> 1% of each run, Pallas kernels for 0% -> 20%
where the time goes in v3:
time: 63.2 us; the launch traced here: 62.7 us
  waiting for transfers between devices  21.5 us (34%)
  starting transfers between devices  17.9 us (28%)
  Pallas kernels  15.4 us (24%)
  local copies, waits for them, and re-layouts  4.7 us (7%)
  other arithmetic  2.99 us (5%)
    pallas_call x6, Pallas kernels, call(): pl.pallas_call(functools.partial(kernel, **options), out_shape=shapes, in...  13.7 us
    ppermute x1, waiting for transfers between devices, local(): lax.ppermute(common_own, 'orb', ring(nob, shift))  6.5 us
    all_to_all x1, waiting for transfers between devices, local(): lax.all_to_all(partial_chi.reshape(owners, nt * block_aux // owners, naux...  5.44 us
    ppermute x2, waiting for transfers between devices, local(): pieces = [lax.ppermute(mine, 'aux', pairs) for pairs in plan]  5.35 us
    ppermute x2, starting transfers between devices, local(): pieces = [lax.ppermute(mine, 'aux', pairs) for pairs in plan]  5.29 us
    unnamed x24, local copies, waits for them, and re-layouts  4.7 us
    all_to_all x1, starting transfers between devices, local(): lax.all_to_all(partial_chi.reshape(owners, nt * block_aux // owners, naux...  3.37 us
    ppermute x1, starting transfers between devices, local(): lax.ppermute(small, 'orb', ring(nob, shift))  3 us
  transfers between devices with their start and end apart: 13, of which 7 were waited for; matrix products, arithmetic and copies ran while one was open for 1% of the time, Pallas kernels for 20%

profile of v3, /device:TPU:0, one launch (start us, length us, event | category | flops | bytes accessed | tf_op | source)
XLA Modules:
  0.0 62.7 jit_solution(88569703685240516)
XLA Ops:
  0.0 0.7 %convert_element_type.5 = f32[1,2]{1,0:T(1,128)S(1)} convert(s32[1,2]{1,0:T(1,128)} %param.7) | non-fusion elementwise | flops 2 | bytes 16 | tf_op jit(solution)/shard_map/convert_element_type | solution.py:222
  0.7 0.8 %fusion.2 = (f32[1,136,128]{2,1,0:T(8,128)S(1)}, f32[136,128]{1,0:T(8,128)S(1)}) fusion(f32[1,2]{1,0:T(1,128)S(1)} %convert_element_type.5, f32[64,128]{1,0:T(8,128)} %param.6, f32[64,128]{1,0:T(8,128)} %param.5), kind=kLoop, calls=%fused_computation.10 | loop fusion | flops 69632 | bytes 204808 | tf_op jit(solution)/shard_map/stack | solution.py:225
  1.4 3.0 %collective-permute-start = (f32[136,128]{1,0:T(8,128)S(1)}, f32[136,128]{1,0:T(8,128)S(1)}, u32[]{:S(2)}, u32[]{:S(2)}) collective-permute-start(f32[136,128]{1,0:T(8,128)S(1)} %get-tuple-element.26), channel_id=1, source_target_pairs={{2,0},{0,2},{3,1},{1,3},{6,4},{4,6},{7,5},{5,7},{10,8},{8,10},{11,... | collective-permute-start | bytes 208904 | tf_op jit(solution)/shard_map/ppermute | solution.py:225
  4.4 0.1 pad_add_fusion.place
  4.5 2.2 %collective-permute-done = f32[136,128]{1,0:T(8,128)S(1)} collective-permute-done((f32[136,128]{1,0:T(8,128)S(1)}, f32[136,128]{1,0:T(8,128)S(1)}, u32[]{:S(2)}, u32[]{:S(2)}) %collective-permute-start) | collective-permute-done | bytes 69664 | tf_op jit(solution)/shard_map/ppermute | solution.py:225
  6.8 1.2 %copy-done.3 = f32[1,1,2,64,2048]{4,3,2,1,0:T(8,128)S(1)} copy-done((f32[1,1,2,64,2048]{4,3,2,1,0:T(8,128)S(1)}, f32[1,1,2,64,2048]{4,3,2,1,0:T(8,128)}, u32[]{:S(2)}) %copy-start.3) | copy-done | bytes 1048600
  8.0 1.8 %prepare.1 = (f32[32,32,128]{2,1,0:T(8,128)}, f32[40,2048]{1,0:T(8,128)S(1)}, f32[48,2048]{1,0:T(8,128)}) custom-call(s32[4]{0:T(128)S(1)} %pad_add_fusion.place, f32[128,2048]{1,0:T(8,128)S(1)} %bitcast.18, f32[2,136,128]{2,1,0:T(8,128)S(1)} %get-tuple-element.24.token_ref), custom_call_target="tpu_custom_call" | custom-call | tf_op jit(solution)/shard_map/prepare/pallas_call | solution.py:230
  9.8 2.0 %collective-permute-start.2 = (f32[40,2048]{1,0:T(8,128)S(1)}, f32[40,2048]{1,0:T(8,128)S(1)}, u32[]{:S(2)}, u32[]{:S(2)}) collective-permute-start(f32[40,2048]{1,0:T(8,128)S(1)} %get-tuple-element.14), channel_id=1, source_target_pairs={{2,0},{0,2},{3,1},{1,3},{6,4},{4,6},{7,5},{5,7},{10,8},{8,10},{11,... | collective-permute-start | bytes 983048 | tf_op jit(solution)/shard_map/ppermute | solution.py:244
  11.8 1.5 %collective-permute-start.1 = (f32[2,136,128]{2,1,0:T(8,128)S(1)}, f32[2,136,128]{2,1,0:T(8,128)S(1)}, u32[]{:S(2)}, u32[]{:S(2)}) collective-permute-start(f32[2,136,128]{2,1,0:T(8,128)S(1)} %get-tuple-element.24.token_ref), channel_id=1, source_target_pairs={{16,0},{0,16},{17,1},{1,17},{18,2},{2,18},{19,3},{3,19},{20,4},{4,... | collective-permute-start | bytes 417800 | tf_op jit(solution)/shard_map/ppermute | solution.py:226
  13.3 5.3 %collective-permute-start.8 = (f32[32,32,128]{2,1,0:T(8,128)}, f32[32,32,128]{2,1,0:T(8,128)}, u32[]{:S(2)}, u32[]{:S(2)}) collective-permute-start(f32[32,32,128]{2,1,0:T(8,128)} %get-tuple-element.18), channel_id=1, source_target_pairs={{0,8},{12,4},{1,9},{13,5},{2,10},{14,6},{3,11},{15,7},{16,24},{28,... | collective-permute-start | bytes 1572872 | tf_op jit(solution)/shard_map/ppermute | solution.py:248
  18.6 0.6 collective-permute-start.3
  19.2 0.7 %pad_maximum_fusion.greens.refs_1_ = f32[2,2,136,128]{3,2,1,0:T(8,128)} fusion(f32[1,2,136,128]{3,2,1,0:T(8,128)S(1)} %bitcast.23, f32[1,2,136,128]{3,2,1,0:T(8,128)S(1)} %get-tuple-element.23), kind=kLoop, calls=%fused_computation | loop fusion | flops 69632 | bytes 557056 | tf_op jit(solution)/shard_map/stack | solution.py:226
  19.9 0.7 %copy-done.9 = f32[40,2048]{1,0:T(8,128)} copy-done((f32[40,2048]{1,0:T(8,128)}, f32[40,2048]{1,0:T(8,128)S(1)}, u32[]{:S(2)}) %copy-start.9) | copy-done | bytes 327704
  20.7 0.5 collective-permute-start.4
  21.2 1.0 %copy-done.2 = f32[2,2,136,128]{3,2,1,0:T(8,128)S(1)} copy-done((f32[2,2,136,128]{3,2,1,0:T(8,128)S(1)}, f32[2,2,136,128]{3,2,1,0:T(8,128)}, u32[]{:S(2)}) %copy-start.2) | copy-done | bytes 278552
  22.1 1.7 %first.1.acc = f32[4,512,256]{2,1,0:T(8,128)S(1)} custom-call(s32[4]{0:T(128)S(1)} %pad_add_fusion.place, f32[2,2,136,128]{3,2,1,0:T(8,128)S(1)} %copy-done.2, f32[128,2048]{1,0:T(8,128)S(1)} %bitcast.19), custom_call_target="tpu_custom_call" | custom-call | flops 603979776 | bytes 1327104 | tf_op jit(solution)/shard_map/first/pallas_call | solution.py:254
  23.8 6.5 %collective-permute-done.3.refs_1_ = f32[48,2048]{1,0:T(8,128)S(1)} collective-permute-done((f32[48,2048]{1,0:T(8,128)}, f32[48,2048]{1,0:T(8,128)S(1)}, u32[]{:S(2)}, u32[]{:S(2)}) %collective-permute-start.3) | collective-permute-done | bytes 393248 | tf_op jit(solution)/shard_map/ppermute | solution.py:246
  30.3 0.3 collective-permute-done.4.refs_2_.refs_1_
  30.6 3.4 %second.1 = (bf16[128,4096]{1,0:T(8,128)(2,1)S(1)}, bf16[128,4096]{1,0:T(8,128)(2,1)S(1)}) custom-call(s32[4]{0:T(128)S(1)} %pad_add_fusion.place, f32[2,2,136,128]{3,2,1,0:T(8,128)S(1)} %copy-done.2, f32[4,512,256]{2,1,0:T(8,128)S(1)} %first.1.acc, f32[40,2048]{1,0:T(8,128)S(1)} %copy-done.10, f32[48,2048]{1,0:T(8,128)S(1)} %collective-permute-done.3.refs_1_, ...), custom_call_target="tpu_custom_call" | custom-call | flops 603979776 | bytes 3424256 | tf_op jit(solution)/shard_map/second/pallas_call | solution.py:254
  34.1 1.0 %copy-done = bf16[128,4096]{1,0:T(8,128)(2,1)} copy-done((bf16[128,4096]{1,0:T(8,128)(2,1)}, bf16[128,4096]{1,0:T(8,128)(2,1)S(1)}, u32[]{:S(2)}) %copy-start) | copy-done | bytes 1048600
  35.1 5.3 %collective-permute-done.6.refs_0_ = f32[32,32,128]{2,1,0:T(8,128)S(1)} collective-permute-done((f32[32,32,128]{2,1,0:T(8,128)}, f32[32,32,128]{2,1,0:T(8,128)S(1)}, u32[]{:S(2)}, u32[]{:S(2)}) %collective-permute-start.6) | collective-permute-done | bytes 524320 | tf_op jit(solution)/shard_map/ppermute | solution.py:248
  40.5 0.8 %copy-done.7 = f32[32,32,128]{2,1,0:T(8,128)} copy-done((f32[32,32,128]{2,1,0:T(8,128)}, f32[32,32,128]{2,1,0:T(8,128)S(1)}, u32[]{:S(2)}) %copy-start.7) | copy-done | bytes 524312
  41.3 2.9 %meet.5 = (f32[64,64]{1,0:T(8,128)S(1)}, f32[64,128]{1,0:T(8,128)S(1)}) custom-call(s32[4]{0:T(128)S(1)} %pad_add_fusion.place, bf16[128,4096]{1,0:T(8,128)(2,1)S(1)} %copy-done.1, bf16[128,4096]{1,0:T(8,128)(2,1)S(1)} %get-tuple-element.17.side_low, f32[1024,128]{1,0:T(8,128)} %bitcast.13.own, f32[1024,128]{1,0:T(8,128)} %bitcast.14.other), custom_call_target="tpu_custom_call" | custom-call | flops 201326592 | bytes 5242880 | tf_op jit(solution)/shard_map/meet/pallas_call | solution.py:254
  44.2 1.4 %collective-permute-start.11 = (f32[64,128]{1,0:T(8,128)S(1)}, f32[64,128]{1,0:T(8,128)S(1)}, u32[]{:S(2)}, u32[]{:S(2)}) collective-permute-start(f32[64,128]{1,0:T(8,128)S(1)} %get-tuple-element.22), channel_id=1, source_target_pairs={{8,0},{4,12},{9,1},{5,13},{10,2},{6,14},{11,3},{7,15},{24,16},{20,... | collective-permute-start | bytes 98312 | tf_op jit(solution)/shard_map/ppermute | solution.py:300
  45.7 2.2 %meet.4 = (f32[64,64]{1,0:T(8,128)S(1)}, f32[64,128]{1,0:T(8,128)S(1)}) custom-call(s32[4]{0:T(128)S(1)} %pad_add_fusion.place, bf16[128,4096]{1,0:T(8,128)(2,1)S(1)} %copy-done.1, bf16[128,4096]{1,0:T(8,128)(2,1)S(1)} %get-tuple-element.17.side_low, f32[1024,128]{1,0:T(8,128)S(1)} %bitcast.21, f32[1024,128]{1,0:T(8,128)S(1)} %bitcast.22), custom_call_target="tpu_custom_call" | custom-call | flops 201326592 | bytes 5242880 | tf_op jit(solution)/shard_map/meet/pallas_call | solution.py:254
  48.0 2.2 %meet.3.refs_0_ = f32[64,64]{1,0:T(8,128)S(1)} custom-call(s32[4]{0:T(128)S(1)} %pad_add_fusion.place, bf16[128,4096]{1,0:T(8,128)(2,1)S(1)} %copy-done.1, bf16[128,4096]{1,0:T(8,128)(2,1)S(1)} %get-tuple-element.17.side_low, f32[1024,128]{1,0:T(8,128)} %bitcast.9.own, f32[1024,128]{1,0:T(8,128)S(1)} %bitcast.20), custom_call_target="tpu_custom_call" | custom-call | flops 201326592 | bytes 5242880 | tf_op jit(solution)/shard_map/meet/pallas_call | solution.py:254
  50.2 0.9 %collective-permute-done.11.refs_4_ = f32[64,128]{1,0:T(8,128)S(1)} collective-permute-done((f32[64,128]{1,0:T(8,128)S(1)}, f32[64,128]{1,0:T(8,128)S(1)}, u32[]{:S(2)}, u32[]{:S(2)}) %collective-permute-start.11) | collective-permute-done | bytes 32800 | tf_op jit(solution)/shard_map/ppermute | solution.py:300
  51.1 0.8 %collective-permute-done.10.refs_3_ = f32[64,128]{1,0:T(8,128)S(1)} collective-permute-done((f32[64,128]{1,0:T(8,128)S(1)}, f32[64,128]{1,0:T(8,128)S(1)}, u32[]{:S(2)}, u32[]{:S(2)}) %collective-permute-start.10) | collective-permute-done | bytes 32800 | tf_op jit(solution)/shard_map/ppermute | solution.py:300
  51.9 1.3 %assemble.1 = f32[2,64,256]{2,1,0:T(8,128)} custom-call(s32[4]{0:T(128)S(1)} %pad_add_fusion.place, f32[64,64]{1,0:T(8,128)S(1)} %meet.3.refs_0_, f32[64,64]{1,0:T(8,128)S(1)} %get-tuple-element.19.refs_1_, f32[64,64]{1,0:T(8,128)S(1)} %get-tuple-element.20.refs_2_, f32[64,128]{1,0:T(8,128)S(1)} %collective-permute-done.10.refs_3_, ...), custom_call_target="tpu_custom_call" | custom-call | bytes 114688 | tf_op jit(solution)/shard_map/assemble/pallas_call | solution.py:254
  53.1 3.4 %all-to-all-start = ((f32[8,16,256]{2,1,0:T(8,128)}), f32[8,16,256]{2,1,0:T(8,128)S(1)}, u32[]{:S(2)}, u32[]{:S(2)}) async-start(f32[8,16,256]{2,1,0:T(8,128)} %bitcast.15), calls=%async_computation | async-start | bytes 262144 | tf_op jit(solution)/shard_map/all_to_all | solution.py:305
  56.5 5.4 %all-to-all-done = f32[8,16,256]{2,1,0:T(8,128)S(1)} async-done(((f32[8,16,256]{2,1,0:T(8,128)}), f32[8,16,256]{2,1,0:T(8,128)S(1)}, u32[]{:S(2)}, u32[]{:S(2)}) %all-to-all-start) | async-done | bytes 131104 | tf_op jit(solution)/shard_map/all_to_all | solution.py:305
  62.0 0.7 %fusion = f32[16,256]{1,0:T(8,128)} fusion(s32[]{:T(128)S(6)} %select_n.14, f32[16,256]{1,0:T(8,128)S(1)} %broadcast_multiply_fusion), kind=kLoop, calls=%fused_computation.6 | loop fusion | flops 4096 | bytes 32772 | tf_op jit(solution)/shard_map/jit(_roll_dynamic)/concatenate | solution.py:313
  (36 shorter events, 0.2 us)
Async XLA Ops:
  1.4 5.3 %collective-permute-start = (f32[136,128]{1,0:T(8,128)S(1)}, f32[136,128]{1,0:T(8,128)S(1)}, u32[]{:S(2)}, u32[]{:S(2)}) collective-permute-start(f32[136,128]{1,0:T(8,128)S(1)} %get-tuple-element.26), channel_id=1, source_target_pairs={{2,0},{0,2},{3,1},{1,3},{6,4},{4,6},{7,5},{5,7},{10,8},{8,10},{11,... | collective-permute-start | bytes 208904 | tf_op jit(solution)/shard_map/ppermute | solution.py:225
  6.8 1.2 %copy-start.3 = (f32[1,1,2,64,2048]{4,3,2,1,0:T(8,128)S(1)}, f32[1,1,2,64,2048]{4,3,2,1,0:T(8,128)}, u32[]{:S(2)}) copy-start(f32[1,1,2,64,2048]{4,3,2,1,0:T(8,128)} %param.4) | copy-start | bytes 3145732
  8.0 13.2 %copy-start.4 = (f32[1,1,2,64,2048]{4,3,2,1,0:T(8,128)S(1)}, f32[1,1,2,64,2048]{4,3,2,1,0:T(8,128)}, u32[]{:S(2)}) copy-start(f32[1,1,2,64,2048]{4,3,2,1,0:T(8,128)} %param.4) | copy-start | bytes 3145732
  9.8 10.2 %collective-permute-start.2 = (f32[40,2048]{1,0:T(8,128)S(1)}, f32[40,2048]{1,0:T(8,128)S(1)}, u32[]{:S(2)}, u32[]{:S(2)}) collective-permute-start(f32[40,2048]{1,0:T(8,128)S(1)} %get-tuple-element.14), channel_id=1, source_target_pairs={{2,0},{0,2},{3,1},{1,3},{6,4},{4,6},{7,5},{5,7},{10,8},{8,10},{11,... | collective-permute-start | bytes 983048 | tf_op jit(solution)/shard_map/ppermute | solution.py:244
  11.8 6.8 %collective-permute-start.1 = (f32[2,136,128]{2,1,0:T(8,128)S(1)}, f32[2,136,128]{2,1,0:T(8,128)S(1)}, u32[]{:S(2)}, u32[]{:S(2)}) collective-permute-start(f32[2,136,128]{2,1,0:T(8,128)S(1)} %get-tuple-element.24.token_ref), channel_id=1, source_target_pairs={{16,0},{0,16},{17,1},{1,17},{18,2},{2,18},{19,3},{3,19},{20,4},{4,... | collective-permute-start | bytes 417800 | tf_op jit(solution)/shard_map/ppermute | solution.py:226
  13.3 21.7 %collective-permute-start.8 = (f32[32,32,128]{2,1,0:T(8,128)}, f32[32,32,128]{2,1,0:T(8,128)}, u32[]{:S(2)}, u32[]{:S(2)}) collective-permute-start(f32[32,32,128]{2,1,0:T(8,128)} %get-tuple-element.18), channel_id=1, source_target_pairs={{0,8},{12,4},{1,9},{13,5},{2,10},{14,6},{3,11},{15,7},{16,24},{28,... | collective-permute-start | bytes 1572872 | tf_op jit(solution)/shard_map/ppermute | solution.py:248
  18.6 16.5 %collective-permute-start.5 = (f32[32,32,128]{2,1,0:T(8,128)}, f32[32,32,128]{2,1,0:T(8,128)S(1)}, u32[]{:S(2)}, u32[]{:S(2)}) collective-permute-start(f32[32,32,128]{2,1,0:T(8,128)} %get-tuple-element.18), channel_id=1, source_target_pairs={{1,0},{0,1},{3,2},{2,3},{5,4},{4,5},{7,6},{6,7},{9,8},{8,9},{11,10... | collective-permute-start | bytes 1572872 | tf_op jit(solution)/shard_map/ppermute | solution.py:250
  18.6 21.9 %collective-permute-start.6 = (f32[32,32,128]{2,1,0:T(8,128)}, f32[32,32,128]{2,1,0:T(8,128)S(1)}, u32[]{:S(2)}, u32[]{:S(2)}) collective-permute-start(f32[32,32,128]{2,1,0:T(8,128)} %get-tuple-element.18), channel_id=1, source_target_pairs={{0,4},{4,8},{8,12},{12,0},{1,5},{5,9},{9,13},{13,1},{2,6},{6,10},{... | collective-permute-start | bytes 1572872 | tf_op jit(solution)/shard_map/ppermute | solution.py:248
  18.6 11.7 %collective-permute-start.3 = (f32[48,2048]{1,0:T(8,128)}, f32[48,2048]{1,0:T(8,128)S(1)}, u32[]{:S(2)}, u32[]{:S(2)}) collective-permute-start(f32[48,2048]{1,0:T(8,128)} %get-tuple-element.15), channel_id=1, source_target_pairs={{2,0},{0,2},{3,1},{1,3},{6,4},{4,6},{7,5},{5,7},{10,8},{8,10},{11,... | collective-permute-start | bytes 1179656 | tf_op jit(solution)/shard_map/ppermute | solution.py:246
  19.9 0.7 %copy-start.9 = (f32[40,2048]{1,0:T(8,128)}, f32[40,2048]{1,0:T(8,128)S(1)}, u32[]{:S(2)}) copy-start(f32[40,2048]{1,0:T(8,128)S(1)} %collective-permute-done.2.refs_0_) | copy-start | bytes 983044
  20.7 10.0 %collective-permute-start.4 = (f32[40,2048]{1,0:T(8,128)}, f32[40,2048]{1,0:T(8,128)S(1)}, u32[]{:S(2)}, u32[]{:S(2)}) collective-permute-start(f32[40,2048]{1,0:T(8,128)} %after.3.refs_0_), channel_id=1, source_target_pairs={{16,0},{0,16},{17,1},{1,17},{18,2},{2,18},{19,3},{3,19},{20,4},{4,... | collective-permute-start | bytes 983048 | tf_op jit(solution)/shard_map/ppermute | solution.py:245
  21.2 1.0 %copy-start.2 = (f32[2,2,136,128]{3,2,1,0:T(8,128)S(1)}, f32[2,2,136,128]{3,2,1,0:T(8,128)}, u32[]{:S(2)}) copy-start(f32[2,2,136,128]{3,2,1,0:T(8,128)} %pad_maximum_fusion.greens.refs_1_) | copy-start | bytes 835588
  22.1 8.5 %copy-start.10 = (f32[40,2048]{1,0:T(8,128)S(1)}, f32[40,2048]{1,0:T(8,128)}, u32[]{:S(2)}) copy-start(f32[40,2048]{1,0:T(8,128)} %after.3.refs_0_) | copy-start | bytes 983044
  30.6 4.4 %copy-start.11 = (f32[40,2048]{1,0:T(8,128)}, f32[40,2048]{1,0:T(8,128)S(1)}, u32[]{:S(2)}) copy-start(f32[40,2048]{1,0:T(8,128)S(1)} %collective-permute-done.4.refs_2_.refs_1_) | copy-start | bytes 983044
  34.0 1.0 %copy-start = (bf16[128,4096]{1,0:T(8,128)(2,1)}, bf16[128,4096]{1,0:T(8,128)(2,1)S(1)}, u32[]{:S(2)}) copy-start(bf16[128,4096]{1,0:T(8,128)(2,1)S(1)} %get-tuple-element.16.side_high.refs_1_) | copy-start | bytes 3145732
  35.0 6.3 %copy-start.1 = (bf16[128,4096]{1,0:T(8,128)(2,1)S(1)}, bf16[128,4096]{1,0:T(8,128)(2,1)}, u32[]{:S(2)}) copy-start(bf16[128,4096]{1,0:T(8,128)(2,1)} %copy-done) | copy-start | bytes 3145732
  35.0 6.3 %collective-permute-start.9 = (f32[32,32,128]{2,1,0:T(8,128)}, f32[32,32,128]{2,1,0:T(8,128)}, u32[]{:S(2)}, u32[]{:S(2)}) collective-permute-start(f32[32,32,128]{2,1,0:T(8,128)} %after.5), channel_id=1, source_target_pairs={{1,0},{0,1},{3,2},{2,3},{5,4},{4,5},{7,6},{6,7},{9,8},{8,9},{11,10... | collective-permute-start | bytes 1572872 | tf_op jit(solution)/shard_map/ppermute | solution.py:285
  35.1 5.4 %copy-start.5 = (f32[32,32,128]{2,1,0:T(8,128)}, f32[32,32,128]{2,1,0:T(8,128)S(1)}, u32[]{:S(2)}) copy-start(f32[32,32,128]{2,1,0:T(8,128)S(1)} %collective-permute-done.5.refs_2_) | copy-start | bytes 1572868
  40.5 0.8 %copy-start.7 = (f32[32,32,128]{2,1,0:T(8,128)}, f32[32,32,128]{2,1,0:T(8,128)S(1)}, u32[]{:S(2)}) copy-start(f32[32,32,128]{2,1,0:T(8,128)S(1)} %collective-permute-done.6.refs_0_) | copy-start | bytes 1572868
  41.3 4.4 %copy-start.8 = (f32[32,32,128]{2,1,0:T(8,128)S(1)}, f32[32,32,128]{2,1,0:T(8,128)}, u32[]{:S(2)}) copy-start(f32[32,32,128]{2,1,0:T(8,128)} %after.4) | copy-start | bytes 1572868
  41.3 4.3 %collective-permute-start.7 = (f32[32,32,128]{2,1,0:T(8,128)}, f32[32,32,128]{2,1,0:T(8,128)S(1)}, u32[]{:S(2)}, u32[]{:S(2)}) collective-permute-start(f32[32,32,128]{2,1,0:T(8,128)} %after.4), channel_id=1, source_target_pairs={{1,0},{0,1},{3,2},{2,3},{5,4},{4,5},{7,6},{6,7},{9,8},{8,9},{11,10... | collective-permute-start | bytes 1572872 | tf_op jit(solution)/shard_map/ppermute | solution.py:285
  44.2 3.7 %copy-start.6 = (f32[32,32,128]{2,1,0:T(8,128)S(1)}, f32[32,32,128]{2,1,0:T(8,128)}, u32[]{:S(2)}) copy-start(f32[32,32,128]{2,1,0:T(8,128)} %copy-done.5) | copy-start | bytes 1572868
  44.2 6.8 %collective-permute-start.11 = (f32[64,128]{1,0:T(8,128)S(1)}, f32[64,128]{1,0:T(8,128)S(1)}, u32[]{:S(2)}, u32[]{:S(2)}) collective-permute-start(f32[64,128]{1,0:T(8,128)S(1)} %get-tuple-element.22), channel_id=1, source_target_pairs={{8,0},{4,12},{9,1},{5,13},{10,2},{6,14},{11,3},{7,15},{24,16},{20,... | collective-permute-start | bytes 98312 | tf_op jit(solution)/shard_map/ppermute | solution.py:300
  47.9 4.0 %collective-permute-start.10 = (f32[64,128]{1,0:T(8,128)S(1)}, f32[64,128]{1,0:T(8,128)S(1)}, u32[]{:S(2)}, u32[]{:S(2)}) collective-permute-start(f32[64,128]{1,0:T(8,128)S(1)} %get-tuple-element.21), channel_id=1, source_target_pairs={{4,0},{8,4},{12,8},{0,12},{5,1},{9,5},{13,9},{1,13},{6,2},{10,6},{... | collective-permute-start | bytes 98312 | tf_op jit(solution)/shard_map/ppermute | solution.py:300
  53.1 8.8 %all-to-all-start = ((f32[8,16,256]{2,1,0:T(8,128)}), f32[8,16,256]{2,1,0:T(8,128)S(1)}, u32[]{:S(2)}, u32[]{:S(2)}) async-start(f32[8,16,256]{2,1,0:T(8,128)} %bitcast.15), calls=%async_computation | async-start | bytes 262144 | tf_op jit(solution)/shard_map/all_to_all | solution.py:305

commit v4 on v3

v4 whole, which is shorter than its diff:
```python
import functools
import math

import jax
import jax.numpy as jnp
from jax import lax
from jax.experimental import pallas as pl
from jax.experimental.pallas import tpu as pltpu
from jax.sharding import PartitionSpec as P

VMEM = pl.BlockSpec(memory_space=pltpu.VMEM)
SMEM = pl.BlockSpec(memory_space=pltpu.SMEM)
F32 = jnp.float32
BF16 = jnp.bfloat16
LIST_ROWS = 8
MIB = 1024 * 1024


def halves(x):
    high = x.astype(BF16)
    return high, (x - high.astype(F32)).astype(BF16)


def dot(a, b):
    return lax.dot_general(a, b, (((1,), (0,)), ((), ())), preferred_element_type=F32)


def dot_nt(a, b):
    return lax.dot_general(a, b, (((1,), (1,)), ((), ())), preferred_element_type=F32)


def ring(count, shift):
    return [((target + shift) % count, target) for target in range(count)]


def prepare(place, tensor, occupied, virtual, listed_ref, mine, small, turned, *, share):
    width, norb = occupied.shape
    turned[...] = tensor[...].T.reshape(turned.shape)
    start = pl.multiple_of(place[1] * share, share)
    mine[...] = turned[:, pl.ds(start, share), :]
    small[:width, :] = occupied[...]
    small[width : 2 * width, :] = virtual[...]
    entries = listed_ref[...].astype(F32)
    lanes = lax.broadcasted_iota(jnp.int32, (LIST_ROWS, norb), 1)
    rows = jnp.zeros((LIST_ROWS, norb), F32)
    for slot in range(entries.shape[1]):
        rows = jnp.where(lanes == slot, entries[:, slot : slot + 1], rows)
    small[2 * width :, :] = rows


def hold(block, *refs):
    refs[-1][...] = block[...]


def after(block, *tokens):
    return pl.pallas_call(
        hold,
        out_shape=jax.ShapeDtypeStruct(block.shape, block.dtype),
        in_specs=[VMEM] * (1 + len(tokens)),
        out_specs=VMEM,
        name="hold",
    )(block, *tokens)


def shifts_of(naux):
    plan = []
    for shift in range(1, naux // 2 + 1):
        if 2 * shift < naux:
            plan.append([(source, (source + shift) % naux) for source in range(naux)])
        else:
            plan.append([(z, z + shift) if z % 2 == 0 else (z + shift, z) for z in range(shift)])
    return plan


def select(block, list_rows, slots, width):
    parts = []
    for slot in range(slots):
        entry = list_rows[:1, slot : slot + 1]
        chosen = jnp.zeros((block.shape[0], width), F32)
        for j in range(block.shape[1] // width):
            chosen = jnp.where(entry == float(j), block[:, j * width : (j + 1) * width], chosen)
        parts.append(chosen)
    return jnp.concatenate(parts, axis=1)


def mix(place, near, far, tensor, slots, width, share):
    nt = near.shape[0]
    pairs = tensor.shape[1] // (2 * width)
    near_list, far_list = near[0, 2 * width :, :], far[0, 2 * width :, :]
    which = [lax.rem(tau + nt - place[1], nt) for tau in range(nt)]
    left = []
    for kind in range(2):
        for tau in range(nt):
            start = pl.multiple_of(kind * width + place[1] * share, share)
            left.append(select(near[which[tau], pl.ds(start, share), :], far_list, slots, width))
    left_high, left_low = halves(jnp.concatenate(left, axis=0))
    high, low = halves(tensor[...])
    middle = dot(
        jnp.concatenate([left_high, left_high, left_low], axis=1), jnp.concatenate([high, low, high], axis=0)
    )
    middle_high, middle_low = halves(middle)
    results = []
    for group in range(2 * nt):
        kind, tau = group // nt, group % nt
        right = select(far[which[tau], (1 - kind) * width : (2 - kind) * width, :], near_list, slots, width)
        zero = jnp.zeros_like(right)
        right_high, right_low = halves(
            jnp.concatenate([jnp.concatenate([right, zero], axis=1), jnp.concatenate([zero, right], axis=1)], axis=0)
        )

        def stacked(array):
            rows = array[group * share : (group + 1) * share]
            return jnp.concatenate([rows[:, 2 * width * at : 2 * width * (at + 1)] for at in range(pairs)], axis=0)

        rows_high, rows_low = stacked(middle_high), stacked(middle_low)
        results.append(
            dot(
                jnp.concatenate([rows_high, rows_high, rows_low], axis=1),
                jnp.concatenate([right_high, right_low, right_high], axis=0),
            )
        )
    return results


def first(place, near, tensor, acc, token, *, slots, width, share):
    token[...] = jnp.zeros_like(token)
    for group, result in enumerate(mix(place, near, near, tensor, slots, width, share)):
        acc[group] = result


def second(place, near, acc, *refs, slots, width, share):
    refs, (sides, token, spread) = refs[:-3], refs[-3:]
    tensors, fars = refs[: len(refs) // 2], refs[len(refs) // 2 :]
    token[...] = jnp.zeros_like(token)
    listed = slots * width
    groups, tall, _ = acc.shape
    pairs = tall // share
    total = [acc[group] for group in range(groups)]
    for tensor, far in zip(tensors, fars):
        term = mix(place, near, far, tensor, slots, width, share)
        total = [x + y for x, y in zip(total, term)]
    for group in range(groups):
        for at in range(pairs):
            for place_in in range(2):
                row = (group * 2 * pairs + 2 * at + place_in) * share
                spread[row : row + share, :] = total[group][
                    at * share : (at + 1) * share, place_in * listed : (place_in + 1) * listed
                ]
    rows = groups * 2 * pairs
    for at in range(share):
        high, low = halves(spread[pl.ds(at, rows, stride=share), :])
        sides[:rows, at * listed : (at + 1) * listed] = high
        sides[rows:, at * listed : (at + 1) * listed] = low


def meet(place, sides, own, other, *refs, share, nt, given):
    outs, tensor = refs[given:-1], refs[-1]
    listed = own.shape[1]
    rows_aux = own.shape[0] // share
    block = 2 * rows_aux
    for which, source in enumerate((own, other)):
        start = pl.multiple_of(jnp.where(place[2] == which, 0, rows_aux), rows_aux)
        for at in range(share):
            high, low = halves(source[pl.ds(at, rows_aux, stride=share), :])
            tensor[pl.ds(start, rows_aux), at * listed : (at + 1) * listed] = high
            tensor[pl.ds(block + start, rows_aux), at * listed : (at + 1) * listed] = low
    product = dot_nt(sides[...], tensor[...])
    product = product[:, :block] + product[:, block:]
    product = product[: 2 * nt * rows_aux] + product[2 * nt * rows_aux :]
    outs[0][...] = product[: nt * rows_aux]
    if len(outs) == 2:
        back = product[nt * rows_aux :].T
        parts = []
        for tau in range(nt):
            part = back[:, tau * rows_aux : (tau + 1) * rows_aux]
            zero = jnp.zeros_like(part)
            parts.append(
                jnp.where(
                    place[2] == 0, jnp.concatenate([part, zero], axis=1), jnp.concatenate([zero, part], axis=1)
                )
            )
        outs[1][...] = jnp.concatenate(parts, axis=1)


def assemble(place, *refs, naux, nt):
    refs, out_ref = refs[:-1], refs[-1]
    meets = naux // 2
    directs, backs = refs[: 1 + meets], refs[1 + meets :]
    block = directs[0].shape[1]
    half = directs[0].shape[0] // nt
    start = pl.multiple_of(place[2] * half, half)
    for tau in range(nt):
        here = [jnp.zeros((half, block), F32)] * naux
        for shift, ref in enumerate(directs):
            here[(naux - shift) % naux] = ref[tau * half : (tau + 1) * half, :]
        there = [jnp.zeros((block, block), F32)] * naux
        for shift, ref in enumerate(backs, 1):
            there[shift] = ref[:, tau * block : (tau + 1) * block]
        out_ref[tau] = jnp.concatenate(there, axis=1)
        out_ref[tau, pl.ds(start, half), :] += jnp.concatenate(here, axis=1)


def finish(place, received, out_ref, *, scale):
    total = received[0]
    for i in range(1, received.shape[0]):
        total = total + received[i]
    block = place[4]
    out_ref[...] = pltpu.roll(total * scale, place[3] * block, 1)


def local(three_center, occupied_green, virtual_green, block_list, sizes):
    nt, naux, nob, nsub = sizes
    slots = three_center.shape[2]
    width = three_center.shape[3]
    columns = three_center.shape[4]
    rows_aux = columns // width
    block_aux = rows_aux * nsub
    norb = occupied_green.shape[1]
    listed = slots * width
    share = width // nt
    nauxf = naux * block_aux
    me_orb, me_tau, me_sub, me_aux = (lax.axis_index(axis) for axis in ("orb", "tau", "sub", "aux"))
    place = jnp.stack([me_orb, me_tau, me_sub, me_aux, block_aux]).astype(jnp.int32)
    tensor = three_center.reshape(listed, columns)
    limit = 24 + 3 * max(nob - 2, 0)

    def call(kernel, outs, scratch, flops, *arguments, **options):
        shapes = [jax.ShapeDtypeStruct(shape, kind) for shape, kind in outs]
        size = sum(4 * math.prod(x.shape) for x in arguments)
        return pl.pallas_call(
            functools.partial(kernel, **options),
            out_shape=shapes,
            in_specs=[SMEM] + [VMEM] * len(arguments),
            out_specs=[VMEM] * len(shapes),
            scratch_shapes=[pltpu.VMEM(shape, kind) for shape, kind in scratch],
            compiler_params=pltpu.CompilerParams(vmem_limit_bytes=limit * MIB),
            cost_estimate=pl.CostEstimate(flops=flops, bytes_accessed=size, transcendentals=0),
            name=kernel.__name__,
        )(place, *arguments)

    tensors = [lax.ppermute(tensor, "orb", ring(nob, shift)) for shift in range(1, nob)]
    mine, small = call(
        prepare,
        [((rows_aux, share, listed), F32), ((2 * width + LIST_ROWS, norb), F32)],
        [((rows_aux, width, listed), F32)],
        0,
        tensor,
        occupied_green,
        virtual_green,
        block_list,
        share=share,
    )
    plan = shifts_of(naux)
    pieces = [lax.ppermute(mine, "aux", pairs) for pairs in plan]
    swap = ring(nsub, 1)
    mine_other = lax.ppermute(mine, "sub", swap)
    near = jnp.stack([small] + [lax.ppermute(small, "tau", ring(nt, shift)) for shift in range(1, nt)])
    fars = [lax.ppermute(near, "orb", ring(nob, shift)) for shift in range(1, nob)]

    groups = 2 * nt
    work = 6 * groups * share * columns * listed * 3
    rows = groups * rows_aux
    depth = share * listed
    options = dict(slots=slots, width=width, share=share)
    acc, token = call(
        first,
        [((groups, rows_aux // 2 * share, 2 * listed), F32), ((8, 128), F32)],
        [],
        work,
        near,
        tensor,
        **options,
    )
    sides, token_late = call(
        second,
        [((2 * rows, depth), BF16), ((8, 128), F32)],
        [((rows * share, listed), F32)],
        work * (nob - 1),
        near,
        acc,
        *tensors,
        *fars,
        **options,
    )
    tokens = [(token, mine_other) + tuple(fars[-1:])] + [(token_late,)] * (len(plan) - 1)
    pieces = [after(block, *token) for block, token in zip(pieces, tokens)]
    others = [lax.ppermute(block, "sub", swap) for block in pieces]
    flat = lambda block: block.reshape(-1, listed)
    turned = [((2 * block_aux, depth), BF16)]
    shape_direct = ((nt * rows_aux, block_aux), F32)
    shape_back = ((block_aux, nt * block_aux), F32)
    work = 16 * rows * block_aux * depth
    options = dict(share=share, nt=nt)
    (direct,) = call(meet, [shape_direct], turned, work, sides, flat(mine), flat(mine_other), given=0, **options)
    directs, returned = [direct], []
    for own, other, pairs in zip(pieces, others, plan):
        direct, back = call(meet, [shape_direct, shape_back], turned, work, sides, flat(own), flat(other), given=0, **options)
        directs.append(direct)
        returned.append(lax.ppermute(back, "aux", [(target, source) for source, target in pairs]))
    (partial_chi,) = call(assemble, [((nt, block_aux, nauxf), F32)], [], 0, *directs, *returned, naux=naux, nt=nt)
    owners = nt * nob * nsub
    received = lax.all_to_all(
        partial_chi.reshape(owners, nt * block_aux // owners, nauxf),
        ("tau", "orb", "sub"),
        split_axis=0,
        concat_axis=0,
        tiled=True,
    )
    (chi,) = call(
        finish,
        [((nt * block_aux // owners, nauxf), F32)],
        [],
        0,
        received,
        scale=-2.0 / math.sqrt(norb * slots * width),
    )
    return chi


def solution(mesh):
    sizes = tuple(mesh.shape[axis] for axis in ("tau", "aux", "orb", "sub"))
    in_specs = (
        P("aux", "orb", None, None, "sub"),
        P(("tau", "orb"), None),
        P(("tau", "orb"), None),
        P("orb", None),
    )
    out_specs = P(("tau", "aux", "orb", "sub"), None)
    return jax.shard_map(
        functools.partial(local, sizes=sizes), mesh=mesh, in_specs=in_specs, out_specs=out_specs, check_vma=False
    )
```

time: 63.2 us -> 70 us (1.11)
  waiting for transfers between devices: 21.5 us -> 11.6 us
  blocking collectives: 0 us -> 9.08 us
  local copies, waits for them, and re-layouts: 4.7 us -> 12.9 us
  other arithmetic: 2.99 us -> 0.02 us
  Pallas kernels: 15.4 us -> 18 us
    all_to_all x0 -> x1, blocking collectives: none -> 9.08 us  [local(): lax.all_to_all(partial_chi.reshape(owners, nt * block_aux // owners, naux...]
    unnamed x24 -> x36, local copies, waits for them, and re-layouts: 4.7 us -> 12.9 us
    all_to_all x1 -> x0, waiting for transfers between devices: 5.44 us -> none  [local(): lax.all_to_all(partial_chi.reshape(owners, nt * block_aux // owners, naux...]
    ppermute x2, waiting for transfers between devices: 5.35 us -> 0.01 us  [local(): pieces = [lax.ppermute(mine, 'aux', pairs) for pairs in plan]]
    ppermute x2, starting transfers between devices: 1.48 us -> 5.18 us  [local(): lax.ppermute(back, 'aux', [(target, source) for source, target in pairs])]
    all_to_all x1 -> x0, starting transfers between devices: 3.37 us -> none  [local(): lax.all_to_all(partial_chi.reshape(owners, nt * block_aux // owners, naux...]
    pallas_call x4 -> x2, Pallas kernels: 1.77 us -> 3.97 us  [after(): pl.pallas_call(hold, out_shape=jax.ShapeDtypeStruct(block.shape, block.dt...]
    ppermute x7 -> x5, starting transfers between devices: 7.72 us -> 5.56 us  [the longest x1 2.94 us: local(): lax.ppermute(tensor, 'orb', ring(nob, shift))]
  transfers between devices with their start and end apart: 13 -> 10, of which waited for: 7 -> 3; matrix products, arithmetic and copies ran while one was open for 1% -> 0% of each run, Pallas kernels for 20% -> 23%
where the time goes in v4:
time: 70 us; the launch traced here: 69.5 us
  Pallas kernels  18 us (26%)
  starting transfers between devices  17.7 us (25%)
  local copies, waits for them, and re-layouts  12.9 us (18%)
  waiting for transfers between devices  11.6 us (17%)
  blocking collectives  9.08 us (13%)
    pallas_call x8, Pallas kernels, call(): pl.pallas_call(functools.partial(kernel, **options), out_shape=shapes, in...  14 us
    unnamed x36, local copies, waits for them, and re-layouts  12.9 us
    all_to_all x1, blocking collectives, local(): lax.all_to_all(partial_chi.reshape(owners, nt * block_aux // owners, naux...  9.08 us
    ppermute x2, starting transfers between devices, local(): pieces = [lax.ppermute(mine, 'aux', pairs) for pairs in plan]  6.91 us
    ppermute x2, starting transfers between devices, local(): lax.ppermute(back, 'aux', [(target, source) for source, target in pairs])  5.18 us
    ppermute x1, waiting for transfers between devices, local(): lax.ppermute(near, 'orb', ring(nob, shift))  5.15 us
    pallas_call x2, Pallas kernels, after(): pl.pallas_call(hold, out_shape=jax.ShapeDtypeStruct(block.shape, block.dt...  3.97 us
    ppermute x2, waiting for transfers between devices, local(): lax.ppermute(back, 'aux', [(target, source) for source, target in pairs])  3.61 us
  transfers between devices with their start and end apart: 10, of which 3 were waited for; matrix products, arithmetic and copies ran while one was open for 0% of the time, Pallas kernels for 23%

profile of v4, /device:TPU:0, one launch (start us, length us, event | category | flops | bytes accessed | tf_op | source)
XLA Modules:
  0.0 69.5 jit_solution(4350067298757759276)
XLA Ops:
  0.0 2.9 %collective-permute-start.1 = (f32[128,2048]{1,0:T(8,128)}, f32[128,2048]{1,0:T(8,128)S(1)}, u32[]{:S(2)}, u32[]{:S(2)}) collective-permute-start(f32[128,2048]{1,0:T(8,128)} %bitcast.17), channel_id=1, source_target_pairs={{2,0},{0,2},{3,1},{1,3},{6,4},{4,6},{7,5},{5,7},{10,8},{8,10},{11,... | collective-permute-start | bytes 3145736 | tf_op jit(solution)/shard_map/ppermute | solution.py:241
  3.0 1.2 %copy-done.6 = f32[1,1,2,64,2048]{4,3,2,1,0:T(8,128)S(1)} copy-done((f32[1,1,2,64,2048]{4,3,2,1,0:T(8,128)S(1)}, f32[1,1,2,64,2048]{4,3,2,1,0:T(8,128)}, u32[]{:S(2)}) %copy-start.6) | copy-done | bytes 1048600
  4.3 0.8 %copy-done.12 = f32[64,128]{1,0:T(8,128)S(1)} copy-done((f32[64,128]{1,0:T(8,128)S(1)}, f32[64,128]{1,0:T(8,128)}, u32[]{:S(2)}) %copy-start.12) | copy-done | bytes 32792
  5.0 0.8 %copy-done.13 = f32[64,128]{1,0:T(8,128)S(1)} copy-done((f32[64,128]{1,0:T(8,128)S(1)}, f32[64,128]{1,0:T(8,128)}, u32[]{:S(2)}) %copy-start.13) | copy-done | bytes 32792
  5.8 0.7 copy-done.16
  6.4 0.9 %prepare.1 = (f32[32,32,128]{2,1,0:T(8,128)S(1)}, f32[136,128]{1,0:T(8,128)S(1)}) custom-call(s32[5]{0:T(128)S(1)} %stack.28.place, f32[128,2048]{1,0:T(8,128)S(1)} %bitcast.18, f32[64,128]{1,0:T(8,128)S(1)} %copy-done.12, f32[64,128]{1,0:T(8,128)S(1)} %copy-done.13, s32[1,2]{1,0:T(1,128)S(1)} %copy-done.16), custom_call_target="tpu_custom_call" | custom-call | bytes 1114120 | tf_op jit(solution)/shard_map/prepare/pallas_call | solution.py:230
  7.4 1.6 %collective-permute-start.4 = (f32[32,32,128]{2,1,0:T(8,128)S(1)}, f32[32,32,128]{2,1,0:T(8,128)S(1)}, u32[]{:S(2)}, u32[]{:S(2)}) collective-permute-start(f32[32,32,128]{2,1,0:T(8,128)S(1)} %get-tuple-element.18), channel_id=1, source_target_pairs={{0,4},{4,8},{8,12},{12,0},{1,5},{5,9},{9,13},{13,1},{2,6},{6,10},{... | collective-permute-start | bytes 1572872 | tf_op jit(solution)/shard_map/ppermute | solution.py:254
  9.0 5.3 %collective-permute-start.6 = (f32[32,32,128]{2,1,0:T(8,128)S(1)}, f32[32,32,128]{2,1,0:T(8,128)}, u32[]{:S(2)}, u32[]{:S(2)}) collective-permute-start(f32[32,32,128]{2,1,0:T(8,128)S(1)} %get-tuple-element.18), channel_id=1, source_target_pairs={{0,8},{12,4},{1,9},{13,5},{2,10},{14,6},{3,11},{15,7},{16,24},{28,... | collective-permute-start | bytes 1572872 | tf_op jit(solution)/shard_map/ppermute | solution.py:254
  14.3 1.5 %collective-permute-start = (f32[136,128]{1,0:T(8,128)S(1)}, f32[136,128]{1,0:T(8,128)S(1)}, u32[]{:S(2)}, u32[]{:S(2)}) collective-permute-start(f32[136,128]{1,0:T(8,128)S(1)} %get-tuple-element.15), channel_id=1, source_target_pairs={{16,0},{0,16},{17,1},{1,17},{18,2},{2,18},{19,3},{3,19},{20,4},{4,... | collective-permute-start | bytes 208904 | tf_op jit(solution)/shard_map/ppermute | solution.py:257
  15.8 2.8 %collective-permute-done = f32[136,128]{1,0:T(8,128)S(1)} collective-permute-done((f32[136,128]{1,0:T(8,128)S(1)}, f32[136,128]{1,0:T(8,128)S(1)}, u32[]{:S(2)}, u32[]{:S(2)}) %collective-permute-start) | collective-permute-done | bytes 69664 | tf_op jit(solution)/shard_map/ppermute | solution.py:257
  18.7 0.6 collective-permute-start.2
  19.3 1.2 %copy-done.7 = f32[1,1,2,64,2048]{4,3,2,1,0:T(8,128)S(1)} copy-done((f32[1,1,2,64,2048]{4,3,2,1,0:T(8,128)S(1)}, f32[1,1,2,64,2048]{4,3,2,1,0:T(8,128)}, u32[]{:S(2)}) %copy-start.7) | copy-done | bytes 1048600
  20.5 1.7 %first.1 = (f32[4,512,256]{2,1,0:T(8,128)S(1)}, f32[8,128]{1,0:T(8,128)S(1)}) custom-call(s32[5]{0:T(128)S(1)} %stack.28.place, f32[2,136,128]{2,1,0:T(8,128)S(1)} %pad_maximum_fusion.near, f32[128,2048]{1,0:T(8,128)S(1)} %bitcast.19), custom_call_target="tpu_custom_call" | custom-call | flops 603979776 | bytes 1187840 | tf_op jit(solution)/shard_map/first/pallas_call | solution.py:230
  22.2 1.4 %copy-done = f32[4,512,256]{2,1,0:T(8,128)} copy-done((f32[4,512,256]{2,1,0:T(8,128)}, f32[4,512,256]{2,1,0:T(8,128)S(1)}, u32[]{:S(2)}) %copy-start) | copy-done | bytes 2097176
  24.1 5.2 %collective-permute-done.2.refs_1_.refs_2_ = f32[2,136,128]{2,1,0:T(8,128)S(1)} collective-permute-done((f32[2,136,128]{2,1,0:T(8,128)S(1)}, f32[2,136,128]{2,1,0:T(8,128)S(1)}, u32[]{:S(2)}, u32[]{:S(2)}) %collective-permute-start.2) | collective-permute-done | bytes 139296 | tf_op jit(solution)/shard_map/ppermute | solution.py:258
  29.3 0.6 copy-done.10
  30.3 2.1 %hold.2 = f32[32,32,128]{2,1,0:T(8,128)} custom-call(f32[32,32,128]{2,1,0:T(8,128)} %copy-done.17, f32[8,128]{1,0:T(8,128)} %copy-done.14, f32[32,32,128]{2,1,0:T(8,128)} %copy-done.2, f32[2,136,128]{2,1,0:T(8,128)} %copy-done.10), custom_call_target="tpu_custom_call" | custom-call | tf_op jit(solution)/shard_map/hold/pallas_call | solution.py:56
  32.4 1.0 %copy-done.8 = f32[128,2048]{1,0:T(8,128)} copy-done((f32[128,2048]{1,0:T(8,128)}, f32[128,2048]{1,0:T(8,128)S(1)}, u32[]{:S(2)}) %copy-start.8) | copy-done | bytes 1048600
  33.4 1.6 %copy-done.1 = f32[4,512,256]{2,1,0:T(8,128)S(1)} copy-done((f32[4,512,256]{2,1,0:T(8,128)S(1)}, f32[4,512,256]{2,1,0:T(8,128)}, u32[]{:S(2)}) %copy-start.1) | copy-done | bytes 2097176
  35.0 1.2 %copy-done.9 = f32[128,2048]{1,0:T(8,128)S(1)} copy-done((f32[128,2048]{1,0:T(8,128)S(1)}, f32[128,2048]{1,0:T(8,128)}, u32[]{:S(2)}) %copy-start.9) | copy-done | bytes 1048600
  36.2 0.9 %copy-done.11 = f32[2,136,128]{2,1,0:T(8,128)S(1)} copy-done((f32[2,136,128]{2,1,0:T(8,128)S(1)}, f32[2,136,128]{2,1,0:T(8,128)}, u32[]{:S(2)}) %copy-start.11) | copy-done | bytes 139288
  37.1 3.3 %second.1 = (bf16[256,4096]{1,0:T(8,128)(2,1)S(1)}, f32[8,128]{1,0:T(8,128)S(1)}) custom-call(s32[5]{0:T(128)S(1)} %stack.28.place, f32[2,136,128]{2,1,0:T(8,128)S(1)} %pad_maximum_fusion.near, f32[4,512,256]{2,1,0:T(8,128)S(1)} %copy-done.1, f32[128,2048]{1,0:T(8,128)S(1)} %copy-done.9, f32[2,136,128]{2,1,0:T(8,128)S(1)} %copy-done.11), custom_call_target="tpu_custom_call" | custom-call | flops 603979776 | bytes 3424256 | tf_op jit(solution)/shard_map/second/pallas_call | solution.py:230
  41.0 1.9 %hold.3 = f32[32,32,128]{2,1,0:T(8,128)} custom-call(f32[32,32,128]{2,1,0:T(8,128)} %collective-permute-done.6.block, f32[8,128]{1,0:T(8,128)} %copy-done.15), custom_call_target="tpu_custom_call" | custom-call | tf_op jit(solution)/shard_map/hold/pallas_call | solution.py:56
  43.4 2.5 %meet.4 = (f32[64,64]{1,0:T(8,128)S(1)}, f32[64,128]{1,0:T(8,128)S(1)}) custom-call(s32[5]{0:T(128)S(1)} %stack.28.place, bf16[256,4096]{1,0:T(8,128)(2,1)S(1)} %get-tuple-element.17.sides, f32[1024,128]{1,0:T(8,128)S(1)} %bitcast.15, f32[1024,128]{1,0:T(8,128)} %bitcast.10.other), custom_call_target="tpu_custom_call" | custom-call | flops 536870912 | bytes 5242880 | tf_op jit(solution)/shard_map/meet/pallas_call | solution.py:230
  45.9 3.9 %collective-permute-start.8 = (f32[64,128]{1,0:T(8,128)S(1)}, f32[64,128]{1,0:T(8,128)S(1)}, u32[]{:S(2)}, u32[]{:S(2)}) collective-permute-start(f32[64,128]{1,0:T(8,128)S(1)} %get-tuple-element.23), channel_id=1, source_target_pairs={{4,0},{8,4},{12,8},{0,12},{5,1},{9,5},{13,9},{1,13},{6,2},{10,6},{... | collective-permute-start | bytes 98312 | tf_op jit(solution)/shard_map/ppermute | solution.py:299
  49.8 2.0 %meet.5 = (f32[64,64]{1,0:T(8,128)S(1)}, f32[64,128]{1,0:T(8,128)S(1)}) custom-call(s32[5]{0:T(128)S(1)} %stack.28.place, bf16[256,4096]{1,0:T(8,128)(2,1)S(1)} %get-tuple-element.17.sides, f32[1024,128]{1,0:T(8,128)S(1)} %bitcast.16, f32[1024,128]{1,0:T(8,128)S(1)} %bitcast.22), custom_call_target="tpu_custom_call" | custom-call | flops 536870912 | bytes 5242880 | tf_op jit(solution)/shard_map/meet/pallas_call | solution.py:230
  51.8 1.3 %collective-permute-start.9 = (f32[64,128]{1,0:T(8,128)S(1)}, f32[64,128]{1,0:T(8,128)S(1)}, u32[]{:S(2)}, u32[]{:S(2)}) collective-permute-start(f32[64,128]{1,0:T(8,128)S(1)} %get-tuple-element.24), channel_id=1, source_target_pairs={{8,0},{4,12},{9,1},{5,13},{10,2},{6,14},{11,3},{7,15},{24,16},{20,... | collective-permute-start | bytes 98312 | tf_op jit(solution)/shard_map/ppermute | solution.py:299
  53.1 1.8 %meet.3.refs_0_ = f32[64,64]{1,0:T(8,128)S(1)} custom-call(s32[5]{0:T(128)S(1)} %stack.28.place, bf16[256,4096]{1,0:T(8,128)(2,1)S(1)} %get-tuple-element.17.sides, f32[1024,128]{1,0:T(8,128)S(1)} %bitcast.21, f32[1024,128]{1,0:T(8,128)S(1)} %bitcast.14), custom_call_target="tpu_custom_call" | custom-call | flops 536870912 | bytes 5242880 | tf_op jit(solution)/shard_map/meet/pallas_call | solution.py:230
  54.9 3.6 %collective-permute-done.9.refs_4_ = f32[64,128]{1,0:T(8,128)S(1)} collective-permute-done((f32[64,128]{1,0:T(8,128)S(1)}, f32[64,128]{1,0:T(8,128)S(1)}, u32[]{:S(2)}, u32[]{:S(2)}) %collective-permute-start.9) | collective-permute-done | bytes 32800 | tf_op jit(solution)/shard_map/ppermute | solution.py:299
  58.5 0.6 assemble.1
  59.2 9.1 %all_to_all.5.received = f32[8,16,256]{2,1,0:T(8,128)S(1)} all-to-all(f32[8,16,256]{2,1,0:T(8,128)S(1)} %bitcast.20), channel_id=1, replica_groups=mesh['tau'=2,'aux'=4,'orb'=2,'sub'=2] {'tau','orb','sub'}, dimensions={0} | all-to-all | bytes 262144 | tf_op jit(solution)/shard_map/all_to_all | solution.py:302
  68.2 1.2 %finish.1 = f32[16,256]{1,0:T(8,128)} custom-call(s32[5]{0:T(128)S(1)} %stack.28.place, f32[8,16,256]{2,1,0:T(8,128)S(1)} %all_to_all.5.received), custom_call_target="tpu_custom_call" | custom-call | bytes 131072 | tf_op jit(solution)/shard_map/finish/pallas_call | solution.py:230
  (37 shorter events, 2.3 us)
Async XLA Ops:
  0.0 32.4 %collective-permute-start.1 = (f32[128,2048]{1,0:T(8,128)}, f32[128,2048]{1,0:T(8,128)S(1)}, u32[]{:S(2)}, u32[]{:S(2)}) collective-permute-start(f32[128,2048]{1,0:T(8,128)} %bitcast.17), channel_id=1, source_target_pairs={{2,0},{0,2},{3,1},{1,3},{6,4},{4,6},{7,5},{5,7},{10,8},{8,10},{11,... | collective-permute-start | bytes 3145736 | tf_op jit(solution)/shard_map/ppermute | solution.py:241
  3.0 1.2 %copy-start.6 = (f32[1,1,2,64,2048]{4,3,2,1,0:T(8,128)S(1)}, f32[1,1,2,64,2048]{4,3,2,1,0:T(8,128)}, u32[]{:S(2)}) copy-start(f32[1,1,2,64,2048]{4,3,2,1,0:T(8,128)} %param.4) | copy-start | bytes 3145732
  4.2 0.8 %copy-start.12 = (f32[64,128]{1,0:T(8,128)S(1)}, f32[64,128]{1,0:T(8,128)}, u32[]{:S(2)}) copy-start(f32[64,128]{1,0:T(8,128)} %occupied.1) | copy-start | bytes 98308
  5.0 0.8 %copy-start.13 = (f32[64,128]{1,0:T(8,128)S(1)}, f32[64,128]{1,0:T(8,128)}, u32[]{:S(2)}) copy-start(f32[64,128]{1,0:T(8,128)} %virtual.1) | copy-start | bytes 98308
  5.8 0.7 copy-start.16
  7.3 22.0 %collective-permute-start.3 = (f32[32,32,128]{2,1,0:T(8,128)S(1)}, f32[32,32,128]{2,1,0:T(8,128)S(1)}, u32[]{:S(2)}, u32[]{:S(2)}) collective-permute-start(f32[32,32,128]{2,1,0:T(8,128)S(1)} %get-tuple-element.18), channel_id=1, source_target_pairs={{1,0},{0,1},{3,2},{2,3},{5,4},{4,5},{7,6},{6,7},{9,8},{8,9},{11,10... | collective-permute-start | bytes 1572872 | tf_op jit(solution)/shard_map/ppermute | solution.py:256
  7.4 21.9 %collective-permute-start.4 = (f32[32,32,128]{2,1,0:T(8,128)S(1)}, f32[32,32,128]{2,1,0:T(8,128)S(1)}, u32[]{:S(2)}, u32[]{:S(2)}) collective-permute-start(f32[32,32,128]{2,1,0:T(8,128)S(1)} %get-tuple-element.18), channel_id=1, source_target_pairs={{0,4},{4,8},{8,12},{12,0},{1,5},{5,9},{9,13},{13,1},{2,6},{6,10},{... | collective-permute-start | bytes 1572872 | tf_op jit(solution)/shard_map/ppermute | solution.py:254
  9.0 31.9 %collective-permute-start.6 = (f32[32,32,128]{2,1,0:T(8,128)S(1)}, f32[32,32,128]{2,1,0:T(8,128)}, u32[]{:S(2)}, u32[]{:S(2)}) collective-permute-start(f32[32,32,128]{2,1,0:T(8,128)S(1)} %get-tuple-element.18), channel_id=1, source_target_pairs={{0,8},{12,4},{1,9},{13,5},{2,10},{14,6},{3,11},{15,7},{16,24},{28,... | collective-permute-start | bytes 1572872 | tf_op jit(solution)/shard_map/ppermute | solution.py:254
  14.3 4.3 %collective-permute-start = (f32[136,128]{1,0:T(8,128)S(1)}, f32[136,128]{1,0:T(8,128)S(1)}, u32[]{:S(2)}, u32[]{:S(2)}) collective-permute-start(f32[136,128]{1,0:T(8,128)S(1)} %get-tuple-element.15), channel_id=1, source_target_pairs={{16,0},{0,16},{17,1},{1,17},{18,2},{2,18},{19,3},{3,19},{20,4},{4,... | collective-permute-start | bytes 208904 | tf_op jit(solution)/shard_map/ppermute | solution.py:257
  18.7 10.6 %collective-permute-start.2 = (f32[2,136,128]{2,1,0:T(8,128)S(1)}, f32[2,136,128]{2,1,0:T(8,128)S(1)}, u32[]{:S(2)}, u32[]{:S(2)}) collective-permute-start(f32[2,136,128]{2,1,0:T(8,128)S(1)} %pad_maximum_fusion.near), channel_id=1, source_target_pairs={{2,0},{0,2},{3,1},{1,3},{6,4},{4,6},{7,5},{5,7},{10,8},{8,10},{11,... | collective-permute-start | bytes 417800 | tf_op jit(solution)/shard_map/ppermute | solution.py:258
  19.3 1.2 %copy-start.7 = (f32[1,1,2,64,2048]{4,3,2,1,0:T(8,128)S(1)}, f32[1,1,2,64,2048]{4,3,2,1,0:T(8,128)}, u32[]{:S(2)}) copy-start(f32[1,1,2,64,2048]{4,3,2,1,0:T(8,128)} %param.4) | copy-start | bytes 3145732
  22.2 1.4 %copy-start = (f32[4,512,256]{2,1,0:T(8,128)}, f32[4,512,256]{2,1,0:T(8,128)S(1)}, u32[]{:S(2)}) copy-start(f32[4,512,256]{2,1,0:T(8,128)S(1)} %get-tuple-element.16.acc) | copy-start | bytes 6291460
  23.5 0.6 copy-start.14
  29.3 0.7 copy-start.10
  29.3 0.9 %copy-start.2 = (f32[32,32,128]{2,1,0:T(8,128)}, f32[32,32,128]{2,1,0:T(8,128)S(1)}, u32[]{:S(2)}) copy-start(f32[32,32,128]{2,1,0:T(8,128)S(1)} %collective-permute-done.3.refs_1_) | copy-start | bytes 1572868
  29.3 1.0 %copy-start.17 = (f32[32,32,128]{2,1,0:T(8,128)}, f32[32,32,128]{2,1,0:T(8,128)S(1)}, u32[]{:S(2)}) copy-start(f32[32,32,128]{2,1,0:T(8,128)S(1)} %collective-permute-done.4.block) | copy-start | bytes 1572868
  32.4 11.0 %collective-permute-start.5 = (f32[32,32,128]{2,1,0:T(8,128)}, f32[32,32,128]{2,1,0:T(8,128)}, u32[]{:S(2)}, u32[]{:S(2)}) collective-permute-start(f32[32,32,128]{2,1,0:T(8,128)} %hold.2), channel_id=1, source_target_pairs={{1,0},{0,1},{3,2},{2,3},{5,4},{4,5},{7,6},{6,7},{9,8},{8,9},{11,10... | collective-permute-start | bytes 1572872 | tf_op jit(solution)/shard_map/ppermute | solution.py:287
  32.4 1.0 %copy-start.8 = (f32[128,2048]{1,0:T(8,128)}, f32[128,2048]{1,0:T(8,128)S(1)}, u32[]{:S(2)}) copy-start(f32[128,2048]{1,0:T(8,128)S(1)} %collective-permute-done.1.refs_0_) | copy-start | bytes 3145732
  33.4 1.6 %copy-start.1 = (f32[4,512,256]{2,1,0:T(8,128)S(1)}, f32[4,512,256]{2,1,0:T(8,128)}, u32[]{:S(2)}) copy-start(f32[4,512,256]{2,1,0:T(8,128)} %copy-done) | copy-start | bytes 6291460
  35.0 1.2 %copy-start.9 = (f32[128,2048]{1,0:T(8,128)S(1)}, f32[128,2048]{1,0:T(8,128)}, u32[]{:S(2)}) copy-start(f32[128,2048]{1,0:T(8,128)} %copy-done.8) | copy-start | bytes 3145732
  36.2 0.9 %copy-start.11 = (f32[2,136,128]{2,1,0:T(8,128)S(1)}, f32[2,136,128]{2,1,0:T(8,128)}, u32[]{:S(2)}) copy-start(f32[2,136,128]{2,1,0:T(8,128)} %copy-done.10) | copy-start | bytes 417796
  37.1 6.3 %copy-start.4 = (f32[32,32,128]{2,1,0:T(8,128)S(1)}, f32[32,32,128]{2,1,0:T(8,128)}, u32[]{:S(2)}) copy-start(f32[32,32,128]{2,1,0:T(8,128)} %hold.2) | copy-start | bytes 1572868
  40.4 0.6 copy-start.15
  42.9 6.9 %copy-start.5 = (f32[32,32,128]{2,1,0:T(8,128)S(1)}, f32[32,32,128]{2,1,0:T(8,128)}, u32[]{:S(2)}) copy-start(f32[32,32,128]{2,1,0:T(8,128)} %hold.3) | copy-start | bytes 1572868
  42.9 6.9 %collective-permute-start.7 = (f32[32,32,128]{2,1,0:T(8,128)}, f32[32,32,128]{2,1,0:T(8,128)S(1)}, u32[]{:S(2)}, u32[]{:S(2)}) collective-permute-start(f32[32,32,128]{2,1,0:T(8,128)} %hold.3), channel_id=1, source_target_pairs={{1,0},{0,1},{3,2},{2,3},{5,4},{4,5},{7,6},{6,7},{9,8},{8,9},{11,10... | collective-permute-start | bytes 1572872 | tf_op jit(solution)/shard_map/ppermute | solution.py:287
  45.9 7.2 %copy-start.3 = (f32[32,32,128]{2,1,0:T(8,128)S(1)}, f32[32,32,128]{2,1,0:T(8,128)}, u32[]{:S(2)}) copy-start(f32[32,32,128]{2,1,0:T(8,128)} %copy-done.2) | copy-start | bytes 1572868
  45.9 9.0 %collective-permute-start.8 = (f32[64,128]{1,0:T(8,128)S(1)}, f32[64,128]{1,0:T(8,128)S(1)}, u32[]{:S(2)}, u32[]{:S(2)}) collective-permute-start(f32[64,128]{1,0:T(8,128)S(1)} %get-tuple-element.23), channel_id=1, source_target_pairs={{4,0},{8,4},{12,8},{0,12},{5,1},{9,5},{13,9},{1,13},{6,2},{10,6},{... | collective-permute-start | bytes 98312 | tf_op jit(solution)/shard_map/ppermute | solution.py:299
  51.8 6.7 %collective-permute-start.9 = (f32[64,128]{1,0:T(8,128)S(1)}, f32[64,128]{1,0:T(8,128)S(1)}, u32[]{:S(2)}, u32[]{:S(2)}) collective-permute-start(f32[64,128]{1,0:T(8,128)S(1)} %get-tuple-element.24), channel_id=1, source_target_pairs={{8,0},{4,12},{9,1},{5,13},{10,2},{6,14},{11,3},{7,15},{24,16},{20,... | collective-permute-start | bytes 98312 | tf_op jit(solution)/shard_map/ppermute | solution.py:299

commit v5 on v4

--- a/solution.py
+++ b/solution.py
@@ -9,6 +9,8 @@
 from jax.sharding import PartitionSpec as P
 
 VMEM = pl.BlockSpec(memory_space=pltpu.VMEM)
+ANY = pl.BlockSpec(memory_space=pl.ANY)
+HBM = pl.BlockSpec(memory_space=pltpu.HBM)
 SMEM = pl.BlockSpec(memory_space=pltpu.SMEM)
 F32 = jnp.float32
 BF16 = jnp.bfloat16
@@ -33,32 +35,46 @@
     return [((target + shift) % count, target) for target in range(count)]
 
 
-def prepare(place, tensor, occupied, virtual, listed_ref, mine, small, turned, *, share):
+def prepare(place, tensor_ref, occupied, virtual, listed_ref, tensor, mine, small, entries, turned, sems, *, share):
     width, norb = occupied.shape
-    turned[...] = tensor[...].T.reshape(turned.shape)
-    start = pl.multiple_of(place[1] * share, share)
-    mine[...] = turned[:, pl.ds(start, share), :]
-    small[:width, :] = occupied[...]
-    small[width : 2 * width, :] = virtual[...]
-    entries = listed_ref[...].astype(F32)
+    chunks = sems.shape[0] - 3
+    columns = tensor.shape[1] // chunks
+    some = columns // width
+    loads = [
+        pltpu.make_async_copy(
+            tensor_ref.at[:, pl.ds(i * columns, columns)], tensor.at[:, pl.ds(i * columns, columns)], sems.at[i]
+        )
+        for i in range(chunks)
+    ]
+    loads.append(pltpu.make_async_copy(occupied, small.at[pl.ds(0, width), :], sems.at[chunks]))
+    loads.append(pltpu.make_async_copy(virtual, small.at[pl.ds(width, width), :], sems.at[chunks + 1]))
+    loads.append(pltpu.make_async_copy(listed_ref, entries, sems.at[chunks + 2]))
+    for load in loads:
+        load.start()
+    start = place[1] * share
+    for i in range(chunks):
+        loads[i].wait()
+        turned[...] = tensor[:, i * columns : (i + 1) * columns].T
+        for at in range(share):
+            mine[at, i * some : (i + 1) * some, :] = turned[pl.ds(start + at, some, stride=width), :]
+    for load in loads[chunks:]:
+        load.wait()
     lanes = lax.broadcasted_iota(jnp.int32, (LIST_ROWS, norb), 1)
     rows = jnp.zeros((LIST_ROWS, norb), F32)
     for slot in range(entries.shape[1]):
-        rows = jnp.where(lanes == slot, entries[:, slot : slot + 1], rows)
+        rows = jnp.where(lanes == slot, entries[:, slot : slot + 1].astype(F32), rows)
     small[2 * width :, :] = rows
-
-
-def hold(block, *refs):
-    refs[-1][...] = block[...]
 
 
 def after(block, *tokens):
     return pl.pallas_call(
-        hold,
+        lambda *refs: None,
         out_shape=jax.ShapeDtypeStruct(block.shape, block.dtype),
-        in_specs=[VMEM] * (1 + len(tokens)),
-        out_specs=VMEM,
-        name="hold",
+        in_specs=[ANY] * (1 + len(tokens)),
+        out_specs=ANY,
+        input_output_aliases={0: 0},
+        compiler_params=pltpu.CompilerParams(vmem_limit_bytes=MIB),
+        name="after",
     )(block, *tokens)
 
 
@@ -161,7 +177,7 @@
     for which, source in enumerate((own, other)):
         start = pl.multiple_of(jnp.where(place[2] == which, 0, rows_aux), rows_aux)
         for at in range(share):
-            high, low = halves(source[pl.ds(at, rows_aux, stride=share), :])
+            high, low = halves(source[at * rows_aux : (at + 1) * rows_aux, :])
             tensor[pl.ds(start, rows_aux), at * listed : (at + 1) * listed] = high
             tensor[pl.ds(block + start, rows_aux), at * listed : (at + 1) * listed] = low
     product = dot_nt(sides[...], tensor[...])
@@ -200,14 +216,6 @@
         out_ref[tau, pl.ds(start, half), :] += jnp.concatenate(here, axis=1)
 
 
-def finish(place, received, out_ref, *, scale):
-    total = received[0]
-    for i in range(1, received.shape[0]):
-        total = total + received[i]
-    block = place[4]
-    out_ref[...] = pltpu.roll(total * scale, place[3] * block, 1)
-
-
 def local(three_center, occupied_green, virtual_green, block_list, sizes):
     nt, naux, nob, nsub = sizes
     slots = three_center.shape[2]
@@ -220,7 +228,7 @@
     share = width // nt
     nauxf = naux * block_aux
     me_orb, me_tau, me_sub, me_aux = (lax.axis_index(axis) for axis in ("orb", "tau", "sub", "aux"))
-    place = jnp.stack([me_orb, me_tau, me_sub, me_aux, block_aux]).astype(jnp.int32)
+    place = jnp.stack([me_orb, me_tau, me_sub, me_aux]).astype(jnp.int32)
     tensor = three_center.reshape(listed, columns)
     limit = 24 + 3 * max(nob - 2, 0)
 
@@ -239,17 +247,23 @@
         )(place, *arguments)
 
     tensors = [lax.ppermute(tensor, "orb", ring(nob, shift)) for shift in range(1, nob)]
-    mine, small = call(
-        prepare,
-        [((rows_aux, share, listed), F32), ((2 * width + LIST_ROWS, norb), F32)],
-        [((rows_aux, width, listed), F32)],
-        0,
-        tensor,
-        occupied_green,
-        virtual_green,
-        block_list,
-        share=share,
-    )
+    chunks = 4
+    held, mine, small = pl.pallas_call(
+        functools.partial(prepare, share=share),
+        out_shape=[
+            jax.ShapeDtypeStruct(shape, F32)
+            for shape in ((listed, columns), (share, rows_aux, listed), (2 * width + LIST_ROWS, norb))
+        ],
+        in_specs=[SMEM] + [HBM] * 4,
+        out_specs=[VMEM] * 3,
+        scratch_shapes=[
+            pltpu.VMEM(block_list.shape, jnp.int32),
+            pltpu.VMEM((columns // chunks, listed), F32),
+            pltpu.SemaphoreType.DMA((chunks + 3,)),
+        ],
+        compiler_params=pltpu.CompilerParams(vmem_limit_bytes=limit * MIB),
+        name="prepare",
+    )(place, tensor, occupied_green, virtual_green, block_list)
     plan = shifts_of(naux)
     pieces = [lax.ppermute(mine, "aux", pairs) for pairs in plan]
     swap = ring(nsub, 1)
@@ -268,7 +282,7 @@
         [],
         work,
         near,
-        tensor,
+        held,
         **options,
     )
     sides, token_late = call(
@@ -306,15 +320,8 @@
         concat_axis=0,
         tiled=True,
     )
-    (chi,) = call(
-        finish,
-        [((nt * block_aux // owners, nauxf), F32)],
-        [],
-        0,
-        received,
-        scale=-2.0 / math.sqrt(norb * slots * width),
-    )
-    return chi
+    total = received.sum(axis=0) * (-2.0 / math.sqrt(norb * slots * width))
+    return jnp.roll(total, me_aux * block_aux, axis=1)
 
 
 def solution(mesh):

time: 70 us -> 58.9 us (0.84)
  local copies, waits for them, and re-layouts: 12.9 us -> 3.4 us
  waiting for transfers between devices: 11.6 us -> 20.8 us
  blocking collectives: 9.08 us -> 0 us
  Pallas kernels: 18 us -> 12.7 us
  starting transfers between devices: 17.7 us -> 20.7 us
  other arithmetic: 0.02 us -> 0.8 us
    unnamed x36 -> x8, local copies, waits for them, and re-layouts: 12.9 us -> 3.4 us
    all_to_all x1 -> x0, blocking collectives: 9.08 us -> none  [local(): lax.all_to_all(partial_chi.reshape(owners, nt * block_aux // owners, naux...]
    all_to_all x0 -> x1, waiting for transfers between devices: none -> 5.53 us  [local(): lax.all_to_all(partial_chi.reshape(owners, nt * block_aux // owners, naux...]
    all_to_all x0 -> x1, starting transfers between devices: none -> 3.73 us  [local(): lax.all_to_all(partial_chi.reshape(owners, nt * block_aux // owners, naux...]
    ppermute x1, waiting for transfers between devices: 5.15 us -> 8.25 us  [local(): lax.ppermute(near, 'orb', ring(nob, shift))]
    pallas_call x8 -> x6, Pallas kernels: 14 us -> 11 us  [call(): pl.pallas_call(functools.partial(kernel, **options), out_shape=shapes, in...]
    pallas_call x2 -> x3, Pallas kernels: 3.97 us -> 1.7 us  [the longest x1 1.7 us: local(): pl.pallas_call(functools.partial(prepare, share=share), out_shape=[jax.Sh...]
    ppermute x2, starting transfers between devices: 6.91 us -> 6.14 us  [local(): pieces = [lax.ppermute(mine, 'aux', pairs) for pairs in plan]]
  transfers between devices with their start and end apart: 10 -> 11, of which waited for: 3 -> 5; matrix products, arithmetic and copies ran while one was open for 0% -> 0% of each run, Pallas kernels for 23% -> 20%
where the time goes in v5:
time: 58.9 us; the launch traced here: 58.5 us
  waiting for transfers between devices  20.8 us (35%)
  starting transfers between devices  20.7 us (35%)
  Pallas kernels  12.7 us (22%)
  local copies, waits for them, and re-layouts  3.4 us (6%)
  other arithmetic  0.8 us (1%)
    pallas_call x6, Pallas kernels, call(): pl.pallas_call(functools.partial(kernel, **options), out_shape=shapes, in...  11 us
    ppermute x1, waiting for transfers between devices, local(): lax.ppermute(near, 'orb', ring(nob, shift))  8.25 us
    ppermute x2, starting transfers between devices, local(): pieces = [lax.ppermute(mine, 'aux', pairs) for pairs in plan]  6.14 us
    all_to_all x1, waiting for transfers between devices, local(): lax.all_to_all(partial_chi.reshape(owners, nt * block_aux // owners, naux...  5.53 us
    ppermute x2, starting transfers between devices, local(): lax.ppermute(back, 'aux', [(target, source) for source, target in pairs])  5.19 us
    ppermute x2, waiting for transfers between devices, local(): lax.ppermute(back, 'aux', [(target, source) for source, target in pairs])  3.97 us
    all_to_all x1, starting transfers between devices, local(): lax.all_to_all(partial_chi.reshape(owners, nt * block_aux // owners, naux...  3.73 us
    unnamed x8, local copies, waits for them, and re-layouts  3.4 us
  transfers between devices with their start and end apart: 11, of which 5 were waited for; matrix products, arithmetic and copies ran while one was open for 0% of the time, Pallas kernels for 20%

profile of v5, /device:TPU:0, one launch (start us, length us, event | category | flops | bytes accessed | tf_op | source)
XLA Modules:
  0.0 58.5 jit_solution(14148918673400820917)
XLA Ops:
  0.0 2.9 %collective-permute-start.1 = (f32[128,2048]{1,0:T(8,128)}, f32[128,2048]{1,0:T(8,128)S(1)}, u32[]{:S(2)}, u32[]{:S(2)}) collective-permute-start(f32[128,2048]{1,0:T(8,128)} %bitcast.17), channel_id=1, source_target_pairs={{2,0},{0,2},{3,1},{1,3},{6,4},{4,6},{7,5},{5,7},{10,8},{8,10},{11,... | collective-permute-start | bytes 3145736 | tf_op jit(solution)/shard_map/ppermute | solution.py:249
  2.9 0.1 pad_add_fusion.place
  3.0 1.2 %copy-done = f32[1,1,2,64,2048]{4,3,2,1,0:T(8,128)S(1)} copy-done((f32[1,1,2,64,2048]{4,3,2,1,0:T(8,128)S(1)}, f32[1,1,2,64,2048]{4,3,2,1,0:T(8,128)}, u32[]{:S(2)}) %copy-start) | copy-done | bytes 1048600
  4.2 0.8 %copy-done.1 = f32[64,128]{1,0:T(8,128)S(1)} copy-done((f32[64,128]{1,0:T(8,128)S(1)}, f32[64,128]{1,0:T(8,128)}, u32[]{:S(2)}) %copy-start.1) | copy-done | bytes 32792
  5.0 0.8 %copy-done.2 = f32[64,128]{1,0:T(8,128)S(1)} copy-done((f32[64,128]{1,0:T(8,128)S(1)}, f32[64,128]{1,0:T(8,128)}, u32[]{:S(2)}) %copy-start.2) | copy-done | bytes 32792
  5.8 0.7 %copy-done.3 = s32[1,2]{1,0:T(1,128)S(1)} copy-done((s32[1,2]{1,0:T(1,128)S(1)}, s32[1,2]{1,0:T(1,128)}, u32[]{:S(2)}) %copy-start.3) | copy-done | bytes 32
  6.4 1.7 %prepare.1 = (f32[128,2048]{1,0:T(8,128)S(1)}, f32[32,32,128]{2,1,0:T(8,128)S(1)}, f32[136,128]{1,0:T(8,128)S(1)}) custom-call(s32[4]{0:T(128)S(1)} %pad_add_fusion.place, f32[128,2048]{1,0:T(8,128)S(1)} %bitcast.18, f32[64,128]{1,0:T(8,128)S(1)} %copy-done.1, f32[64,128]{1,0:T(8,128)S(1)} %copy-done.2, s32[1,2]{1,0:T(1,128)S(1)} %copy-done.3), custom_call_target="tpu_custom_call" | custom-call | tf_op jit(solution)/shard_map/prepare/pallas_call | solution.py:251
  8.1 0.1 collective-permute-start.3
  8.2 1.6 %collective-permute-start.4 = (f32[32,32,128]{2,1,0:T(8,128)S(1)}, f32[32,32,128]{2,1,0:T(8,128)S(1)}, u32[]{:S(2)}, u32[]{:S(2)}) collective-permute-start(f32[32,32,128]{2,1,0:T(8,128)S(1)} %get-tuple-element.20), channel_id=1, source_target_pairs={{0,4},{4,8},{8,12},{12,0},{1,5},{5,9},{9,13},{13,1},{2,6},{6,10},{... | collective-permute-start | bytes 1572872 | tf_op jit(solution)/shard_map/ppermute | solution.py:268
  9.8 4.5 %collective-permute-start.6 = (f32[32,32,128]{2,1,0:T(8,128)S(1)}, f32[32,32,128]{2,1,0:T(8,128)S(1)}, u32[]{:S(2)}, u32[]{:S(2)}) collective-permute-start(f32[32,32,128]{2,1,0:T(8,128)S(1)} %get-tuple-element.20), channel_id=1, source_target_pairs={{0,8},{12,4},{1,9},{13,5},{2,10},{14,6},{3,11},{15,7},{16,24},{28,... | collective-permute-start | bytes 1572872 | tf_op jit(solution)/shard_map/ppermute | solution.py:268
  14.4 1.6 %collective-permute-start = (f32[136,128]{1,0:T(8,128)S(1)}, f32[136,128]{1,0:T(8,128)S(1)}, u32[]{:S(2)}, u32[]{:S(2)}) collective-permute-start(f32[136,128]{1,0:T(8,128)S(1)} %get-tuple-element.16), channel_id=1, source_target_pairs={{16,0},{0,16},{17,1},{1,17},{18,2},{2,18},{19,3},{3,19},{20,4},{4,... | collective-permute-start | bytes 208904 | tf_op jit(solution)/shard_map/ppermute | solution.py:271
  15.9 2.8 %collective-permute-done = f32[136,128]{1,0:T(8,128)S(1)} collective-permute-done((f32[136,128]{1,0:T(8,128)S(1)}, f32[136,128]{1,0:T(8,128)S(1)}, u32[]{:S(2)}, u32[]{:S(2)}) %collective-permute-start) | collective-permute-done | bytes 69664 | tf_op jit(solution)/shard_map/ppermute | solution.py:271
  18.7 0.6 %collective-permute-start.2 = (f32[2,136,128]{2,1,0:T(8,128)S(1)}, f32[2,136,128]{2,1,0:T(8,128)S(1)}, u32[]{:S(2)}, u32[]{:S(2)}) collective-permute-start(f32[2,136,128]{2,1,0:T(8,128)S(1)} %pad_maximum_fusion.near), channel_id=1, source_target_pairs={{2,0},{0,2},{3,1},{1,3},{6,4},{4,6},{7,5},{5,7},{10,8},{8,10},{11,... | collective-permute-start | bytes 417800 | tf_op jit(solution)/shard_map/ppermute | solution.py:272
  19.3 1.7 %first.1 = (f32[4,512,256]{2,1,0:T(8,128)S(1)}, f32[8,128]{1,0:T(8,128)S(1)}) custom-call(s32[4]{0:T(128)S(1)} %pad_add_fusion.place, f32[2,136,128]{2,1,0:T(8,128)S(1)} %pad_maximum_fusion.near, f32[128,2048]{1,0:T(8,128)S(1)} %get-tuple-element.17.tensor), custom_call_target="tpu_custom_call" | custom-call | flops 603979776 | bytes 1187840 | tf_op jit(solution)/shard_map/first/pallas_call | solution.py:238
  21.0 8.2 %collective-permute-done.2.refs_1_.refs_3_ = f32[2,136,128]{2,1,0:T(8,128)S(1)} collective-permute-done((f32[2,136,128]{2,1,0:T(8,128)S(1)}, f32[2,136,128]{2,1,0:T(8,128)S(1)}, u32[]{:S(2)}, u32[]{:S(2)}) %collective-permute-start.2) | collective-permute-done | bytes 139296 | tf_op jit(solution)/shard_map/ppermute | solution.py:272
  29.3 0.0 collective-permute-done.3.refs_2_
  29.3 0.0 collective-permute-done.4.refs_0_
  29.3 0.1 collective-permute-start.5
  29.4 0.0 collective-permute-done.1.refs_0_
  29.4 3.3 %second.1 = (bf16[256,4096]{1,0:T(8,128)(2,1)S(1)}, f32[8,128]{1,0:T(8,128)S(1)}) custom-call(s32[4]{0:T(128)S(1)} %pad_add_fusion.place, f32[2,136,128]{2,1,0:T(8,128)S(1)} %pad_maximum_fusion.near, f32[4,512,256]{2,1,0:T(8,128)S(1)} %get-tuple-element.18.acc, f32[128,2048]{1,0:T(8,128)S(1)} %collective-permute-done.1.refs_0_, ...), custom_call_target="tpu_custom_call" | custom-call | flops 603979776 | bytes 3424256 | tf_op jit(solution)/shard_map/second/pallas_call | solution.py:238
  32.7 0.2 collective-permute-done.6.refs_0_
  32.9 0.4 collective-permute-start.7
  33.3 1.6 %meet.4 = (f32[64,64]{1,0:T(8,128)S(1)}, f32[64,128]{1,0:T(8,128)S(1)}) custom-call(s32[4]{0:T(128)S(1)} %pad_add_fusion.place, bf16[256,4096]{1,0:T(8,128)(2,1)S(1)} %get-tuple-element.19.sides, f32[1024,128]{1,0:T(8,128)S(1)} %bitcast.16, f32[1024,128]{1,0:T(8,128)S(1)} %bitcast.20), custom_call_target="tpu_custom_call" | custom-call | flops 536870912 | bytes 5242880 | tf_op jit(solution)/shard_map/meet/pallas_call | solution.py:238
  34.9 3.9 %collective-permute-start.8 = (f32[64,128]{1,0:T(8,128)S(1)}, f32[64,128]{1,0:T(8,128)S(1)}, u32[]{:S(2)}, u32[]{:S(2)}) collective-permute-start(f32[64,128]{1,0:T(8,128)S(1)} %get-tuple-element.25), channel_id=1, source_target_pairs={{4,0},{8,4},{12,8},{0,12},{5,1},{9,5},{13,9},{1,13},{6,2},{10,6},{... | collective-permute-start | bytes 98312 | tf_op jit(solution)/shard_map/ppermute | solution.py:313
  38.8 1.6 %meet.5 = (f32[64,64]{1,0:T(8,128)S(1)}, f32[64,128]{1,0:T(8,128)S(1)}) custom-call(s32[4]{0:T(128)S(1)} %pad_add_fusion.place, bf16[256,4096]{1,0:T(8,128)(2,1)S(1)} %get-tuple-element.19.sides, f32[1024,128]{1,0:T(8,128)S(1)} %bitcast.15, f32[1024,128]{1,0:T(8,128)S(1)} %bitcast.21), custom_call_target="tpu_custom_call" | custom-call | flops 536870912 | bytes 5242880 | tf_op jit(solution)/shard_map/meet/pallas_call | solution.py:238
  40.5 1.3 %collective-permute-start.9 = (f32[64,128]{1,0:T(8,128)S(1)}, f32[64,128]{1,0:T(8,128)S(1)}, u32[]{:S(2)}, u32[]{:S(2)}) collective-permute-start(f32[64,128]{1,0:T(8,128)S(1)} %get-tuple-element.26), channel_id=1, source_target_pairs={{8,0},{4,12},{9,1},{5,13},{10,2},{6,14},{11,3},{7,15},{24,16},{20,... | collective-permute-start | bytes 98312 | tf_op jit(solution)/shard_map/ppermute | solution.py:313
  41.8 1.4 %meet.3.refs_0_ = f32[64,64]{1,0:T(8,128)S(1)} custom-call(s32[4]{0:T(128)S(1)} %pad_add_fusion.place, bf16[256,4096]{1,0:T(8,128)(2,1)S(1)} %get-tuple-element.19.sides, f32[1024,128]{1,0:T(8,128)S(1)} %bitcast.19, f32[1024,128]{1,0:T(8,128)S(1)} %bitcast.14), custom_call_target="tpu_custom_call" | custom-call | flops 536870912 | bytes 5242880 | tf_op jit(solution)/shard_map/meet/pallas_call | solution.py:238
  43.2 4.0 %collective-permute-done.9.refs_4_ = f32[64,128]{1,0:T(8,128)S(1)} collective-permute-done((f32[64,128]{1,0:T(8,128)S(1)}, f32[64,128]{1,0:T(8,128)S(1)}, u32[]{:S(2)}, u32[]{:S(2)}) %collective-permute-start.9) | collective-permute-done | bytes 32800 | tf_op jit(solution)/shard_map/ppermute | solution.py:313
  47.2 1.3 %assemble.1 = f32[2,64,256]{2,1,0:T(8,128)} custom-call(s32[4]{0:T(128)S(1)} %pad_add_fusion.place, f32[64,64]{1,0:T(8,128)S(1)} %meet.3.refs_0_, f32[64,64]{1,0:T(8,128)S(1)} %get-tuple-element.22.refs_1_, f32[64,64]{1,0:T(8,128)S(1)} %get-tuple-element.24.refs_2_, f32[64,128]{1,0:T(8,128)S(1)} %collective-permute-done.8.refs_3_, ...), custom_call_target="tpu_custom_call" | custom-call | bytes 114688 | tf_op jit(solution)/shard_map/assemble/pallas_call | solution.py:238
  48.5 3.7 %all-to-all-start = ((f32[8,16,256]{2,1,0:T(8,128)}), f32[8,16,256]{2,1,0:T(8,128)S(1)}, u32[]{:S(2)}, u32[]{:S(2)}) async-start(f32[8,16,256]{2,1,0:T(8,128)} %bitcast.13), calls=%async_computation | async-start | bytes 262144 | tf_op jit(solution)/shard_map/all_to_all | solution.py:316
  52.2 5.5 %all-to-all-done = f32[8,16,256]{2,1,0:T(8,128)S(1)} async-done(((f32[8,16,256]{2,1,0:T(8,128)}), f32[8,16,256]{2,1,0:T(8,128)S(1)}, u32[]{:S(2)}, u32[]{:S(2)}) %all-to-all-start) | async-done | bytes 131104 | tf_op jit(solution)/shard_map/all_to_all | solution.py:316
  57.8 0.7 %fusion = f32[16,256]{1,0:T(8,128)} fusion(s32[]{:T(128)S(6)} %select_n.14, f32[16,256]{1,0:T(8,128)S(1)} %broadcast_multiply_fusion), kind=kLoop, calls=%fused_computation.3 | loop fusion | flops 4096 | bytes 32772 | tf_op jit(solution)/shard_map/jit(_roll_dynamic)/concatenate | solution.py:324
  (12 shorter events, 0.0 us)
Async XLA Ops:
  0.0 29.4 %collective-permute-start.1 = (f32[128,2048]{1,0:T(8,128)}, f32[128,2048]{1,0:T(8,128)S(1)}, u32[]{:S(2)}, u32[]{:S(2)}) collective-permute-start(f32[128,2048]{1,0:T(8,128)} %bitcast.17), channel_id=1, source_target_pairs={{2,0},{0,2},{3,1},{1,3},{6,4},{4,6},{7,5},{5,7},{10,8},{8,10},{11,... | collective-permute-start | bytes 3145736 | tf_op jit(solution)/shard_map/ppermute | solution.py:249
  3.0 1.2 %copy-start = (f32[1,1,2,64,2048]{4,3,2,1,0:T(8,128)S(1)}, f32[1,1,2,64,2048]{4,3,2,1,0:T(8,128)}, u32[]{:S(2)}) copy-start(f32[1,1,2,64,2048]{4,3,2,1,0:T(8,128)} %param.4) | copy-start | bytes 3145732
  4.2 0.8 %copy-start.1 = (f32[64,128]{1,0:T(8,128)S(1)}, f32[64,128]{1,0:T(8,128)}, u32[]{:S(2)}) copy-start(f32[64,128]{1,0:T(8,128)} %occupied.1) | copy-start | bytes 98308
  5.0 0.8 %copy-start.2 = (f32[64,128]{1,0:T(8,128)S(1)}, f32[64,128]{1,0:T(8,128)}, u32[]{:S(2)}) copy-start(f32[64,128]{1,0:T(8,128)} %virtual.1) | copy-start | bytes 98308
  5.8 0.7 %copy-start.3 = (s32[1,2]{1,0:T(1,128)S(1)}, s32[1,2]{1,0:T(1,128)}, u32[]{:S(2)}) copy-start(s32[1,2]{1,0:T(1,128)} %listed_ref.1) | copy-start | bytes 28
  8.1 21.2 %collective-permute-start.3 = (f32[32,32,128]{2,1,0:T(8,128)S(1)}, f32[32,32,128]{2,1,0:T(8,128)S(1)}, u32[]{:S(2)}, u32[]{:S(2)}) collective-permute-start(f32[32,32,128]{2,1,0:T(8,128)S(1)} %get-tuple-element.20), channel_id=1, source_target_pairs={{1,0},{0,1},{3,2},{2,3},{5,4},{4,5},{7,6},{6,7},{9,8},{8,9},{11,10... | collective-permute-start | bytes 1572872 | tf_op jit(solution)/shard_map/ppermute | solution.py:270
  8.2 21.1 %collective-permute-start.4 = (f32[32,32,128]{2,1,0:T(8,128)S(1)}, f32[32,32,128]{2,1,0:T(8,128)S(1)}, u32[]{:S(2)}, u32[]{:S(2)}) collective-permute-start(f32[32,32,128]{2,1,0:T(8,128)S(1)} %get-tuple-element.20), channel_id=1, source_target_pairs={{0,4},{4,8},{8,12},{12,0},{1,5},{5,9},{9,13},{13,1},{2,6},{6,10},{... | collective-permute-start | bytes 1572872 | tf_op jit(solution)/shard_map/ppermute | solution.py:268
  9.8 23.1 %collective-permute-start.6 = (f32[32,32,128]{2,1,0:T(8,128)S(1)}, f32[32,32,128]{2,1,0:T(8,128)S(1)}, u32[]{:S(2)}, u32[]{:S(2)}) collective-permute-start(f32[32,32,128]{2,1,0:T(8,128)S(1)} %get-tuple-element.20), channel_id=1, source_target_pairs={{0,8},{12,4},{1,9},{13,5},{2,10},{14,6},{3,11},{15,7},{16,24},{28,... | collective-permute-start | bytes 1572872 | tf_op jit(solution)/shard_map/ppermute | solution.py:268
  14.4 4.4 %collective-permute-start = (f32[136,128]{1,0:T(8,128)S(1)}, f32[136,128]{1,0:T(8,128)S(1)}, u32[]{:S(2)}, u32[]{:S(2)}) collective-permute-start(f32[136,128]{1,0:T(8,128)S(1)} %get-tuple-element.16), channel_id=1, source_target_pairs={{16,0},{0,16},{17,1},{1,17},{18,2},{2,18},{19,3},{3,19},{20,4},{4,... | collective-permute-start | bytes 208904 | tf_op jit(solution)/shard_map/ppermute | solution.py:271
  18.7 10.5 %collective-permute-start.2 = (f32[2,136,128]{2,1,0:T(8,128)S(1)}, f32[2,136,128]{2,1,0:T(8,128)S(1)}, u32[]{:S(2)}, u32[]{:S(2)}) collective-permute-start(f32[2,136,128]{2,1,0:T(8,128)S(1)} %pad_maximum_fusion.near), channel_id=1, source_target_pairs={{2,0},{0,2},{3,1},{1,3},{6,4},{4,6},{7,5},{5,7},{10,8},{8,10},{11,... | collective-permute-start | bytes 417800 | tf_op jit(solution)/shard_map/ppermute | solution.py:272
  29.3 4.0 %collective-permute-start.5 = (f32[32,32,128]{2,1,0:T(8,128)S(1)}, f32[32,32,128]{2,1,0:T(8,128)S(1)}, u32[]{:S(2)}, u32[]{:S(2)}) collective-permute-start(f32[32,32,128]{2,1,0:T(8,128)S(1)} %after.2), channel_id=1, source_target_pairs={{1,0},{0,1},{3,2},{2,3},{5,4},{4,5},{7,6},{6,7},{9,8},{8,9},{11,10... | collective-permute-start | bytes 1572872 | tf_op jit(solution)/shard_map/ppermute | solution.py:301
  32.9 5.9 %collective-permute-start.7 = (f32[32,32,128]{2,1,0:T(8,128)S(1)}, f32[32,32,128]{2,1,0:T(8,128)S(1)}, u32[]{:S(2)}, u32[]{:S(2)}) collective-permute-start(f32[32,32,128]{2,1,0:T(8,128)S(1)} %after.3), channel_id=1, source_target_pairs={{1,0},{0,1},{3,2},{2,3},{5,4},{4,5},{7,6},{6,7},{9,8},{8,9},{11,10... | collective-permute-start | bytes 1572872 | tf_op jit(solution)/shard_map/ppermute | solution.py:301
  34.9 8.3 %collective-permute-start.8 = (f32[64,128]{1,0:T(8,128)S(1)}, f32[64,128]{1,0:T(8,128)S(1)}, u32[]{:S(2)}, u32[]{:S(2)}) collective-permute-start(f32[64,128]{1,0:T(8,128)S(1)} %get-tuple-element.25), channel_id=1, source_target_pairs={{4,0},{8,4},{12,8},{0,12},{5,1},{9,5},{13,9},{1,13},{6,2},{10,6},{... | collective-permute-start | bytes 98312 | tf_op jit(solution)/shard_map/ppermute | solution.py:313
  40.5 6.7 %collective-permute-start.9 = (f32[64,128]{1,0:T(8,128)S(1)}, f32[64,128]{1,0:T(8,128)S(1)}, u32[]{:S(2)}, u32[]{:S(2)}) collective-permute-start(f32[64,128]{1,0:T(8,128)S(1)} %get-tuple-element.26), channel_id=1, source_target_pairs={{8,0},{4,12},{9,1},{5,13},{10,2},{6,14},{11,3},{7,15},{24,16},{20,... | collective-permute-start | bytes 98312 | tf_op jit(solution)/shard_map/ppermute | solution.py:313
  48.5 9.3 %all-to-all-start = ((f32[8,16,256]{2,1,0:T(8,128)}), f32[8,16,256]{2,1,0:T(8,128)S(1)}, u32[]{:S(2)}, u32[]{:S(2)}) async-start(f32[8,16,256]{2,1,0:T(8,128)} %bitcast.13), calls=%async_computation | async-start | bytes 262144 | tf_op jit(solution)/shard_map/all_to_all | solution.py:316

commit v6 on v5

--- a/solution.py
+++ b/solution.py
@@ -35,35 +35,12 @@
     return [((target + shift) % count, target) for target in range(count)]
 
 
-def prepare(place, tensor_ref, occupied, virtual, listed_ref, tensor, mine, small, entries, turned, sems, *, share):
-    width, norb = occupied.shape
-    chunks = sems.shape[0] - 3
-    columns = tensor.shape[1] // chunks
-    some = columns // width
-    loads = [
-        pltpu.make_async_copy(
-            tensor_ref.at[:, pl.ds(i * columns, columns)], tensor.at[:, pl.ds(i * columns, columns)], sems.at[i]
-        )
-        for i in range(chunks)
-    ]
-    loads.append(pltpu.make_async_copy(occupied, small.at[pl.ds(0, width), :], sems.at[chunks]))
-    loads.append(pltpu.make_async_copy(virtual, small.at[pl.ds(width, width), :], sems.at[chunks + 1]))
-    loads.append(pltpu.make_async_copy(listed_ref, entries, sems.at[chunks + 2]))
-    for load in loads:
-        load.start()
+def prepare(place, tensor, mine, turned, *, share):
+    some = mine.shape[1]
+    turned[...] = tensor[...].T
     start = place[1] * share
-    for i in range(chunks):
-        loads[i].wait()
-        turned[...] = tensor[:, i * columns : (i + 1) * columns].T
-        for at in range(share):
-            mine[at, i * some : (i + 1) * some, :] = turned[pl.ds(start + at, some, stride=width), :]
-    for load in loads[chunks:]:
-        load.wait()
-    lanes = lax.broadcasted_iota(jnp.int32, (LIST_ROWS, norb), 1)
-    rows = jnp.zeros((LIST_ROWS, norb), F32)
-    for slot in range(entries.shape[1]):
-        rows = jnp.where(lanes == slot, entries[:, slot : slot + 1].astype(F32), rows)
-    small[2 * width :, :] = rows
+    for at in range(share):
+        mine[at] = turned[pl.ds(start + at, some, stride=turned.shape[0] // some), :]
 
 
 def after(block, *tokens):
@@ -169,8 +146,8 @@
         sides[rows:, at * listed : (at + 1) * listed] = low
 
 
-def meet(place, sides, own, other, *refs, share, nt, given):
-    outs, tensor = refs[given:-1], refs[-1]
+def meet(place, sides, own, other, *refs, share, nt):
+    outs, tensor = refs[:-1], refs[-1]
     listed = own.shape[1]
     rows_aux = own.shape[0] // share
     block = 2 * rows_aux
@@ -200,8 +177,8 @@
 
 def assemble(place, *refs, naux, nt):
     refs, out_ref = refs[:-1], refs[-1]
-    meets = naux // 2
-    directs, backs = refs[: 1 + meets], refs[1 + meets :]
+    count = naux // 2
+    directs, backs = refs[:count], refs[count:]
     block = directs[0].shape[1]
     half = directs[0].shape[0] // nt
     start = pl.multiple_of(place[2] * half, half)
@@ -214,6 +191,19 @@
             there[shift] = ref[:, tau * block : (tau + 1) * block]
         out_ref[tau] = jnp.concatenate(there, axis=1)
         out_ref[tau, pl.ds(start, half), :] += jnp.concatenate(here, axis=1)
+
+
+def complete(place, early, direct, back, out_ref):
+    nt, block, wide = early.shape
+    half = direct.shape[0] // nt
+    naux = wide // block
+    last = naux // 2
+    start = pl.multiple_of(place[2] * half, half)
+    for tau in range(nt):
+        out_ref[tau] = early[tau]
+        out_ref[tau, :, last * block : (last + 1) * block] += back[:, tau * block : (tau + 1) * block]
+        at = (naux - last) * block
+        out_ref[tau, pl.ds(start, half), at : at + block] += direct[tau * half : (tau + 1) * half, :]
 
 
 def local(three_center, occupied_green, virtual_green, block_list, sizes):
@@ -247,29 +237,25 @@
         )(place, *arguments)
 
     tensors = [lax.ppermute(tensor, "orb", ring(nob, shift)) for shift in range(1, nob)]
-    chunks = 4
-    held, mine, small = pl.pallas_call(
-        functools.partial(prepare, share=share),
-        out_shape=[
-            jax.ShapeDtypeStruct(shape, F32)
-            for shape in ((listed, columns), (share, rows_aux, listed), (2 * width + LIST_ROWS, norb))
-        ],
-        in_specs=[SMEM] + [HBM] * 4,
-        out_specs=[VMEM] * 3,
-        scratch_shapes=[
-            pltpu.VMEM(block_list.shape, jnp.int32),
-            pltpu.VMEM((columns // chunks, listed), F32),
-            pltpu.SemaphoreType.DMA((chunks + 3,)),
-        ],
-        compiler_params=pltpu.CompilerParams(vmem_limit_bytes=limit * MIB),
-        name="prepare",
-    )(place, tensor, occupied_green, virtual_green, block_list)
+    (mine,) = call(
+        prepare, [((share, rows_aux, listed), F32)], [((columns, listed), F32)], 0, tensor, share=share
+    )
     plan = shifts_of(naux)
     pieces = [lax.ppermute(mine, "aux", pairs) for pairs in plan]
     swap = ring(nsub, 1)
     mine_other = lax.ppermute(mine, "sub", swap)
+    small = jnp.concatenate(
+        [
+            occupied_green,
+            virtual_green,
+            jnp.pad(block_list.astype(F32), ((0, LIST_ROWS - 1), (0, norb - slots))),
+        ]
+    )
     near = jnp.stack([small] + [lax.ppermute(small, "tau", ring(nt, shift)) for shift in range(1, nt)])
-    fars = [lax.ppermute(near, "orb", ring(nob, shift)) for shift in range(1, nob)]
+    fars = []
+    for shift in range(1, nob):
+        pairs = [(a * nsub + c, b * nsub + (c + 1) % nsub) for a, b in ring(nob, shift) for c in range(nsub)]
+        fars.append(lax.ppermute(near, ("orb", "sub"), pairs))
 
     groups = 2 * nt
     work = 6 * groups * share * columns * listed * 3
@@ -282,7 +268,7 @@
         [],
         work,
         near,
-        held,
+        tensor,
         **options,
     )
     sides, token_late = call(
@@ -305,13 +291,15 @@
     shape_back = ((block_aux, nt * block_aux), F32)
     work = 16 * rows * block_aux * depth
     options = dict(share=share, nt=nt)
-    (direct,) = call(meet, [shape_direct], turned, work, sides, flat(mine), flat(mine_other), given=0, **options)
+    (direct,) = call(meet, [shape_direct], turned, work, sides, flat(mine), flat(mine_other), **options)
     directs, returned = [direct], []
     for own, other, pairs in zip(pieces, others, plan):
-        direct, back = call(meet, [shape_direct, shape_back], turned, work, sides, flat(own), flat(other), given=0, **options)
+        direct, back = call(meet, [shape_direct, shape_back], turned, work, sides, flat(own), flat(other), **options)
         directs.append(direct)
         returned.append(lax.ppermute(back, "aux", [(target, source) for source, target in pairs]))
-    (partial_chi,) = call(assemble, [((nt, block_aux, nauxf), F32)], [], 0, *directs, *returned, naux=naux, nt=nt)
+    shape = ((nt, block_aux, nauxf), F32)
+    (early,) = call(assemble, [shape], [], 0, *directs[:-1], *returned[:-1], naux=naux, nt=nt)
+    (partial_chi,) = call(complete, [shape], [], 0, early, directs[-1], returned[-1])
     owners = nt * nob * nsub
     received = lax.all_to_all(
         partial_chi.reshape(owners, nt * block_aux // owners, nauxf),

time: 58.9 us -> 58.2 us (0.988)
  other arithmetic: 0.8 us -> 2.25 us
  waiting for transfers between devices: 20.8 us -> 19.7 us
  local copies, waits for them, and re-layouts: 3.4 us -> 2.45 us
    pallas_call x6 -> x8, Pallas kernels: 11 us -> 12.8 us  [call(): pl.pallas_call(functools.partial(kernel, **options), out_shape=shapes, in...]
    pallas_call x1 -> x0, Pallas kernels: 1.7 us -> none  [local(): pl.pallas_call(functools.partial(prepare, share=share), out_shape=[jax.Sh...]
    unnamed x8 -> x4, local copies, waits for them, and re-layouts: 3.4 us -> 2.45 us
    another operation x1 -> x2, other arithmetic: 0.01 us -> 0.8 us  [local(): jnp.stack([small] + [lax.ppermute(small, 'tau', ring(nt, shift)) for shif...]
    convert_element_type x0 -> x1, other arithmetic: none -> 0.66 us  [local(): block_list.astype(F32)]
    ppermute x2, waiting for transfers between devices: 3.97 us -> 3.33 us  [local(): lax.ppermute(back, 'aux', [(target, source) for source, target in pairs])]
  transfers between devices with their start and end apart: 11 -> 11, of which waited for: 5 -> 4; matrix products, arithmetic and copies ran while one was open for 0% -> 3% of each run, Pallas kernels for 20% -> 20%
where the time goes in v6:
time: 58.2 us; the launch traced here: 57.8 us
  starting transfers between devices  20.4 us (35%)
  waiting for transfers between devices  19.7 us (34%)
  Pallas kernels  12.8 us (22%)
  local copies, waits for them, and re-layouts  2.45 us (4%)
  other arithmetic  2.25 us (4%)
    pallas_call x8, Pallas kernels, call(): pl.pallas_call(functools.partial(kernel, **options), out_shape=shapes, in...  12.8 us
    ppermute x1, waiting for transfers between devices, local(): fars.append(lax.ppermute(near, ('orb', 'sub'), pairs))  8.06 us
    ppermute x2, starting transfers between devices, local(): pieces = [lax.ppermute(mine, 'aux', pairs) for pairs in plan]  6.14 us
    all_to_all x1, waiting for transfers between devices, local(): lax.all_to_all(partial_chi.reshape(owners, nt * block_aux // owners, naux...  5.53 us
    ppermute x2, starting transfers between devices, local(): lax.ppermute(back, 'aux', [(target, source) for source, target in pairs])  5.21 us
    all_to_all x1, starting transfers between devices, local(): lax.all_to_all(partial_chi.reshape(owners, nt * block_aux // owners, naux...  3.72 us
    ppermute x2, waiting for transfers between devices, local(): lax.ppermute(back, 'aux', [(target, source) for source, target in pairs])  3.33 us
    ppermute x1, starting transfers between devices, local(): lax.ppermute(tensor, 'orb', ring(nob, shift))  2.94 us
  transfers between devices with their start and end apart: 11, of which 4 were waited for; matrix products, arithmetic and copies ran while one was open for 3% of the time, Pallas kernels for 20%

profile of v6, /device:TPU:0, one launch (start us, length us, event | category | flops | bytes accessed | tf_op | source)
XLA Modules:
  0.0 57.8 jit_solution(2300163608162783381)
XLA Ops:
  0.0 2.9 %collective-permute-start.1 = (f32[128,2048]{1,0:T(8,128)}, f32[128,2048]{1,0:T(8,128)S(1)}, u32[]{:S(2)}, u32[]{:S(2)}) collective-permute-start(f32[128,2048]{1,0:T(8,128)} %bitcast.19), channel_id=1, source_target_pairs={{2,0},{0,2},{3,1},{1,3},{6,4},{4,6},{7,5},{5,7},{10,8},{8,10},{11,... | collective-permute-start | bytes 3145736 | tf_op jit(solution)/shard_map/ppermute | solution.py:239
  2.9 0.1 pad_add_fusion.place
  3.0 1.2 %copy-done = f32[1,1,2,64,2048]{4,3,2,1,0:T(8,128)S(1)} copy-done((f32[1,1,2,64,2048]{4,3,2,1,0:T(8,128)S(1)}, f32[1,1,2,64,2048]{4,3,2,1,0:T(8,128)}, u32[]{:S(2)}) %copy-start) | copy-done | bytes 1048600
  4.2 1.2 %prepare.1 = f32[32,32,128]{2,1,0:T(8,128)S(1)} custom-call(s32[4]{0:T(128)S(1)} %pad_add_fusion.place, f32[128,2048]{1,0:T(8,128)S(1)} %bitcast.20), custom_call_target="tpu_custom_call" | custom-call | bytes 1048576 | tf_op jit(solution)/shard_map/prepare/pallas_call | solution.py:228
  5.4 0.1 collective-permute-start.3
  5.5 1.6 %collective-permute-start.4 = (f32[32,32,128]{2,1,0:T(8,128)S(1)}, f32[32,32,128]{2,1,0:T(8,128)S(1)}, u32[]{:S(2)}, u32[]{:S(2)}) collective-permute-start(f32[32,32,128]{2,1,0:T(8,128)S(1)} %prepare.1), channel_id=1, source_target_pairs={{0,4},{4,8},{8,12},{12,0},{1,5},{5,9},{9,13},{13,1},{2,6},{6,10},{... | collective-permute-start | bytes 1572872 | tf_op jit(solution)/shard_map/ppermute | solution.py:244
  7.1 4.5 %collective-permute-start.7 = (f32[32,32,128]{2,1,0:T(8,128)S(1)}, f32[32,32,128]{2,1,0:T(8,128)S(1)}, u32[]{:S(2)}, u32[]{:S(2)}) collective-permute-start(f32[32,32,128]{2,1,0:T(8,128)S(1)} %prepare.1), channel_id=1, source_target_pairs={{0,8},{12,4},{1,9},{13,5},{2,10},{14,6},{3,11},{15,7},{16,24},{28,... | collective-permute-start | bytes 1572872 | tf_op jit(solution)/shard_map/ppermute | solution.py:244
  11.7 0.7 %convert_element_type.5 = f32[1,2]{1,0:T(1,128)S(1)} convert(s32[1,2]{1,0:T(1,128)} %param.7) | non-fusion elementwise | flops 2 | bytes 16 | tf_op jit(solution)/shard_map/convert_element_type | solution.py:251
  12.3 0.8 %fusion.1 = (f32[1,136,128]{2,1,0:T(8,128)S(1)}, f32[136,128]{1,0:T(8,128)S(1)}) fusion(f32[1,2]{1,0:T(1,128)S(1)} %convert_element_type.5, f32[64,128]{1,0:T(8,128)} %param.6, f32[64,128]{1,0:T(8,128)} %param.5), kind=kLoop, calls=%fused_computation.8 | loop fusion | flops 69632 | bytes 204808 | tf_op jit(solution)/shard_map/stack | solution.py:254
  13.1 1.6 %collective-permute-start = (f32[136,128]{1,0:T(8,128)S(1)}, f32[136,128]{1,0:T(8,128)S(1)}, u32[]{:S(2)}, u32[]{:S(2)}) collective-permute-start(f32[136,128]{1,0:T(8,128)S(1)} %get-tuple-element.22), channel_id=1, source_target_pairs={{16,0},{0,16},{17,1},{1,17},{18,2},{2,18},{19,3},{3,19},{20,4},{4,... | collective-permute-start | bytes 208904 | tf_op jit(solution)/shard_map/ppermute | solution.py:254
  14.7 2.8 %collective-permute-done = f32[136,128]{1,0:T(8,128)S(1)} collective-permute-done((f32[136,128]{1,0:T(8,128)S(1)}, f32[136,128]{1,0:T(8,128)S(1)}, u32[]{:S(2)}, u32[]{:S(2)}) %collective-permute-start) | collective-permute-done | bytes 69664 | tf_op jit(solution)/shard_map/ppermute | solution.py:254
  17.5 0.1 collective-permute-start.2
  17.6 0.0 copy-start.1
  17.6 1.2 %copy-done.1 = f32[1,1,2,64,2048]{4,3,2,1,0:T(8,128)S(1)} copy-done((f32[1,1,2,64,2048]{4,3,2,1,0:T(8,128)S(1)}, f32[1,1,2,64,2048]{4,3,2,1,0:T(8,128)}, u32[]{:S(2)}) %copy-start.1) | copy-done | bytes 1048600
  18.8 1.7 %first.1 = (f32[4,512,256]{2,1,0:T(8,128)S(1)}, f32[8,128]{1,0:T(8,128)S(1)}) custom-call(s32[4]{0:T(128)S(1)} %pad_add_fusion.place, f32[2,136,128]{2,1,0:T(8,128)S(1)} %pad_maximum_fusion.near, f32[128,2048]{1,0:T(8,128)S(1)} %bitcast.21), custom_call_target="tpu_custom_call" | custom-call | flops 603979776 | bytes 1187840 | tf_op jit(solution)/shard_map/first/pallas_call | solution.py:228
  20.5 8.1 %collective-permute-done.2.refs_1_.refs_3_ = f32[2,136,128]{2,1,0:T(8,128)S(1)} collective-permute-done((f32[2,136,128]{2,1,0:T(8,128)S(1)}, f32[2,136,128]{2,1,0:T(8,128)S(1)}, u32[]{:S(2)}, u32[]{:S(2)}) %collective-permute-start.2) | collective-permute-done | bytes 139296 | tf_op jit(solution)/shard_map/ppermute | solution.py:258
  28.6 0.0 collective-permute-done.3.refs_2_
  28.6 0.6 %collective-permute-start.5 = (f32[32,32,128]{2,1,0:T(8,128)S(1)}, f32[32,32,128]{2,1,0:T(8,128)S(1)}, u32[]{:S(2)}, u32[]{:S(2)}) collective-permute-start(f32[32,32,128]{2,1,0:T(8,128)S(1)} %after.2), channel_id=1, source_target_pairs={{1,0},{0,1},{3,2},{2,3},{5,4},{4,5},{7,6},{6,7},{9,8},{8,9},{11,10... | collective-permute-start | bytes 1572872 | tf_op jit(solution)/shard_map/ppermute | solution.py:287
  29.2 0.0 collective-permute-done.1.refs_0_
  29.2 3.3 %second.1 = (bf16[256,4096]{1,0:T(8,128)(2,1)S(1)}, f32[8,128]{1,0:T(8,128)S(1)}) custom-call(s32[4]{0:T(128)S(1)} %pad_add_fusion.place, f32[2,136,128]{2,1,0:T(8,128)S(1)} %pad_maximum_fusion.near, f32[4,512,256]{2,1,0:T(8,128)S(1)} %get-tuple-element.13.acc, f32[128,2048]{1,0:T(8,128)S(1)} %collective-permute-done.1.refs_0_, ...), custom_call_target="tpu_custom_call" | custom-call | flops 603979776 | bytes 3424256 | tf_op jit(solution)/shard_map/second/pallas_call | solution.py:228
  32.5 0.1 collective-permute-start.8
  32.6 1.6 %meet.4 = (f32[64,64]{1,0:T(8,128)S(1)}, f32[64,128]{1,0:T(8,128)S(1)}) custom-call(s32[4]{0:T(128)S(1)} %pad_add_fusion.place, bf16[256,4096]{1,0:T(8,128)(2,1)S(1)} %get-tuple-element.14.sides, f32[1024,128]{1,0:T(8,128)S(1)} %bitcast.18, f32[1024,128]{1,0:T(8,128)S(1)} %bitcast.22), custom_call_target="tpu_custom_call" | custom-call | flops 536870912 | bytes 5242880 | tf_op jit(solution)/shard_map/meet/pallas_call | solution.py:228
  34.3 3.9 %collective-permute-start.6 = (f32[64,128]{1,0:T(8,128)S(1)}, f32[64,128]{1,0:T(8,128)S(1)}, u32[]{:S(2)}, u32[]{:S(2)}) collective-permute-start(f32[64,128]{1,0:T(8,128)S(1)} %get-tuple-element.17), channel_id=1, source_target_pairs={{4,0},{8,4},{12,8},{0,12},{5,1},{9,5},{13,9},{1,13},{6,2},{10,6},{... | collective-permute-start | bytes 98312 | tf_op jit(solution)/shard_map/ppermute | solution.py:299
  38.2 1.6 %meet.5 = (f32[64,64]{1,0:T(8,128)S(1)}, f32[64,128]{1,0:T(8,128)S(1)}) custom-call(s32[4]{0:T(128)S(1)} %pad_add_fusion.place, bf16[256,4096]{1,0:T(8,128)(2,1)S(1)} %get-tuple-element.14.sides, f32[1024,128]{1,0:T(8,128)S(1)} %bitcast.17, f32[1024,128]{1,0:T(8,128)S(1)} %bitcast.23), custom_call_target="tpu_custom_call" | custom-call | flops 536870912 | bytes 5242880 | tf_op jit(solution)/shard_map/meet/pallas_call | solution.py:228
  39.8 1.3 %collective-permute-start.9 = (f32[64,128]{1,0:T(8,128)S(1)}, f32[64,128]{1,0:T(8,128)S(1)}, u32[]{:S(2)}, u32[]{:S(2)}) collective-permute-start(f32[64,128]{1,0:T(8,128)S(1)} %get-tuple-element.20), channel_id=1, source_target_pairs={{8,0},{4,12},{9,1},{5,13},{10,2},{6,14},{11,3},{7,15},{24,16},{20,... | collective-permute-start | bytes 98312 | tf_op jit(solution)/shard_map/ppermute | solution.py:299
  41.1 1.4 %meet.3.refs_0_ = f32[64,64]{1,0:T(8,128)S(1)} custom-call(s32[4]{0:T(128)S(1)} %pad_add_fusion.place, bf16[256,4096]{1,0:T(8,128)(2,1)S(1)} %get-tuple-element.14.sides, f32[1024,128]{1,0:T(8,128)S(1)} %bitcast.15, f32[1024,128]{1,0:T(8,128)S(1)} %bitcast.16), custom_call_target="tpu_custom_call" | custom-call | flops 536870912 | bytes 5242880 | tf_op jit(solution)/shard_map/meet/pallas_call | solution.py:228
  42.6 0.6 %assemble.1.early = f32[2,64,256]{2,1,0:T(8,128)S(1)} custom-call(s32[4]{0:T(128)S(1)} %pad_add_fusion.place, f32[64,64]{1,0:T(8,128)S(1)} %meet.3.refs_0_, f32[64,64]{1,0:T(8,128)S(1)} %get-tuple-element.16.refs_1_, f32[64,128]{1,0:T(8,128)S(1)} %collective-permute-done.6.refs_2_), custom_call_target="tpu_custom_call" | custom-call | bytes 65536 | tf_op jit(solution)/shard_map/assemble/pallas_call | solution.py:228
  43.2 3.3 %collective-permute-done.9.back = f32[64,128]{1,0:T(8,128)S(1)} collective-permute-done((f32[64,128]{1,0:T(8,128)S(1)}, f32[64,128]{1,0:T(8,128)S(1)}, u32[]{:S(2)}, u32[]{:S(2)}) %collective-permute-start.9) | collective-permute-done | bytes 32800 | tf_op jit(solution)/shard_map/ppermute | solution.py:299
  46.5 1.3 %complete.1 = f32[2,64,256]{2,1,0:T(8,128)} custom-call(s32[4]{0:T(128)S(1)} %pad_add_fusion.place, f32[2,64,256]{2,1,0:T(8,128)S(1)} %assemble.1.early, f32[64,64]{1,0:T(8,128)S(1)} %get-tuple-element.19.direct, f32[64,128]{1,0:T(8,128)S(1)} %collective-permute-done.9.back), custom_call_target="tpu_custom_call" | custom-call | bytes 180224 | tf_op jit(solution)/shard_map/complete/pallas_call | solution.py:228
  47.8 3.7 %all-to-all-start = ((f32[8,16,256]{2,1,0:T(8,128)}), f32[8,16,256]{2,1,0:T(8,128)S(1)}, u32[]{:S(2)}, u32[]{:S(2)}) async-start(f32[8,16,256]{2,1,0:T(8,128)} %bitcast.13), calls=%async_computation | async-start | bytes 262144 | tf_op jit(solution)/shard_map/all_to_all | solution.py:304
  51.5 5.5 %all-to-all-done = f32[8,16,256]{2,1,0:T(8,128)S(1)} async-done(((f32[8,16,256]{2,1,0:T(8,128)}), f32[8,16,256]{2,1,0:T(8,128)S(1)}, u32[]{:S(2)}, u32[]{:S(2)}) %all-to-all-start) | async-done | bytes 131104 | tf_op jit(solution)/shard_map/all_to_all | solution.py:304
  57.1 0.7 %fusion = f32[16,256]{1,0:T(8,128)} fusion(s32[]{:T(128)S(6)} %select_n.14, f32[16,256]{1,0:T(8,128)S(1)} %broadcast_multiply_fusion), kind=kLoop, calls=%fused_computation.5 | loop fusion | flops 4096 | bytes 32772 | tf_op jit(solution)/shard_map/jit(_roll_dynamic)/concatenate | solution.py:312
  (11 shorter events, 0.1 us)
Async XLA Ops:
  0.0 29.2 %collective-permute-start.1 = (f32[128,2048]{1,0:T(8,128)}, f32[128,2048]{1,0:T(8,128)S(1)}, u32[]{:S(2)}, u32[]{:S(2)}) collective-permute-start(f32[128,2048]{1,0:T(8,128)} %bitcast.19), channel_id=1, source_target_pairs={{2,0},{0,2},{3,1},{1,3},{6,4},{4,6},{7,5},{5,7},{10,8},{8,10},{11,... | collective-permute-start | bytes 3145736 | tf_op jit(solution)/shard_map/ppermute | solution.py:239
  3.0 1.2 %copy-start = (f32[1,1,2,64,2048]{4,3,2,1,0:T(8,128)S(1)}, f32[1,1,2,64,2048]{4,3,2,1,0:T(8,128)}, u32[]{:S(2)}) copy-start(f32[1,1,2,64,2048]{4,3,2,1,0:T(8,128)} %param.4) | copy-start | bytes 3145732
  5.4 23.1 %collective-permute-start.3 = (f32[32,32,128]{2,1,0:T(8,128)S(1)}, f32[32,32,128]{2,1,0:T(8,128)S(1)}, u32[]{:S(2)}, u32[]{:S(2)}) collective-permute-start(f32[32,32,128]{2,1,0:T(8,128)S(1)} %prepare.1), channel_id=1, source_target_pairs={{1,0},{0,1},{3,2},{2,3},{5,4},{4,5},{7,6},{6,7},{9,8},{8,9},{11,10... | collective-permute-start | bytes 1572872 | tf_op jit(solution)/shard_map/ppermute | solution.py:246
  5.5 23.1 %collective-permute-start.4 = (f32[32,32,128]{2,1,0:T(8,128)S(1)}, f32[32,32,128]{2,1,0:T(8,128)S(1)}, u32[]{:S(2)}, u32[]{:S(2)}) collective-permute-start(f32[32,32,128]{2,1,0:T(8,128)S(1)} %prepare.1), channel_id=1, source_target_pairs={{0,4},{4,8},{8,12},{12,0},{1,5},{5,9},{9,13},{13,1},{2,6},{6,10},{... | collective-permute-start | bytes 1572872 | tf_op jit(solution)/shard_map/ppermute | solution.py:244
  7.1 25.4 %collective-permute-start.7 = (f32[32,32,128]{2,1,0:T(8,128)S(1)}, f32[32,32,128]{2,1,0:T(8,128)S(1)}, u32[]{:S(2)}, u32[]{:S(2)}) collective-permute-start(f32[32,32,128]{2,1,0:T(8,128)S(1)} %prepare.1), channel_id=1, source_target_pairs={{0,8},{12,4},{1,9},{13,5},{2,10},{14,6},{3,11},{15,7},{16,24},{28,... | collective-permute-start | bytes 1572872 | tf_op jit(solution)/shard_map/ppermute | solution.py:244
  13.1 4.4 %collective-permute-start = (f32[136,128]{1,0:T(8,128)S(1)}, f32[136,128]{1,0:T(8,128)S(1)}, u32[]{:S(2)}, u32[]{:S(2)}) collective-permute-start(f32[136,128]{1,0:T(8,128)S(1)} %get-tuple-element.22), channel_id=1, source_target_pairs={{16,0},{0,16},{17,1},{1,17},{18,2},{2,18},{19,3},{3,19},{20,4},{4,... | collective-permute-start | bytes 208904 | tf_op jit(solution)/shard_map/ppermute | solution.py:254
  17.5 11.1 %collective-permute-start.2 = (f32[2,136,128]{2,1,0:T(8,128)S(1)}, f32[2,136,128]{2,1,0:T(8,128)S(1)}, u32[]{:S(2)}, u32[]{:S(2)}) collective-permute-start(f32[2,136,128]{2,1,0:T(8,128)S(1)} %pad_maximum_fusion.near), channel_id=1, source_target_pairs={{2,1},{3,0},{0,3},{1,2},{6,5},{7,4},{4,7},{5,6},{10,9},{11,8},{8,1... | collective-permute-start | bytes 417800 | tf_op jit(solution)/shard_map/ppermute | solution.py:258
  17.6 1.2 %copy-start.1 = (f32[1,1,2,64,2048]{4,3,2,1,0:T(8,128)S(1)}, f32[1,1,2,64,2048]{4,3,2,1,0:T(8,128)}, u32[]{:S(2)}) copy-start(f32[1,1,2,64,2048]{4,3,2,1,0:T(8,128)} %param.4) | copy-start | bytes 3145732
  28.6 4.0 %collective-permute-start.5 = (f32[32,32,128]{2,1,0:T(8,128)S(1)}, f32[32,32,128]{2,1,0:T(8,128)S(1)}, u32[]{:S(2)}, u32[]{:S(2)}) collective-permute-start(f32[32,32,128]{2,1,0:T(8,128)S(1)} %after.2), channel_id=1, source_target_pairs={{1,0},{0,1},{3,2},{2,3},{5,4},{4,5},{7,6},{6,7},{9,8},{8,9},{11,10... | collective-permute-start | bytes 1572872 | tf_op jit(solution)/shard_map/ppermute | solution.py:287
  32.5 5.7 %collective-permute-start.8 = (f32[32,32,128]{2,1,0:T(8,128)S(1)}, f32[32,32,128]{2,1,0:T(8,128)S(1)}, u32[]{:S(2)}, u32[]{:S(2)}) collective-permute-start(f32[32,32,128]{2,1,0:T(8,128)S(1)} %after.3), channel_id=1, source_target_pairs={{1,0},{0,1},{3,2},{2,3},{5,4},{4,5},{7,6},{6,7},{9,8},{8,9},{11,10... | collective-permute-start | bytes 1572872 | tf_op jit(solution)/shard_map/ppermute | solution.py:287
  34.3 8.3 %collective-permute-start.6 = (f32[64,128]{1,0:T(8,128)S(1)}, f32[64,128]{1,0:T(8,128)S(1)}, u32[]{:S(2)}, u32[]{:S(2)}) collective-permute-start(f32[64,128]{1,0:T(8,128)S(1)} %get-tuple-element.17), channel_id=1, source_target_pairs={{4,0},{8,4},{12,8},{0,12},{5,1},{9,5},{13,9},{1,13},{6,2},{10,6},{... | collective-permute-start | bytes 98312 | tf_op jit(solution)/shard_map/ppermute | solution.py:299
  39.8 6.7 %collective-permute-start.9 = (f32[64,128]{1,0:T(8,128)S(1)}, f32[64,128]{1,0:T(8,128)S(1)}, u32[]{:S(2)}, u32[]{:S(2)}) collective-permute-start(f32[64,128]{1,0:T(8,128)S(1)} %get-tuple-element.20), channel_id=1, source_target_pairs={{8,0},{4,12},{9,1},{5,13},{10,2},{6,14},{11,3},{7,15},{24,16},{20,... | collective-permute-start | bytes 98312 | tf_op jit(solution)/shard_map/ppermute | solution.py:299
  47.8 9.2 %all-to-all-start = ((f32[8,16,256]{2,1,0:T(8,128)}), f32[8,16,256]{2,1,0:T(8,128)S(1)}, u32[]{:S(2)}, u32[]{:S(2)}) async-start(f32[8,16,256]{2,1,0:T(8,128)} %bitcast.13), calls=%async_computation | async-start | bytes 262144 | tf_op jit(solution)/shard_map/all_to_all | solution.py:304

commit v7 on v6

--- a/solution.py
+++ b/solution.py
@@ -293,10 +293,10 @@
     options = dict(share=share, nt=nt)
     (direct,) = call(meet, [shape_direct], turned, work, sides, flat(mine), flat(mine_other), **options)
     directs, returned = [direct], []
-    for own, other, pairs in zip(pieces, others, plan):
+    for own, other in zip(pieces, others):
         direct, back = call(meet, [shape_direct, shape_back], turned, work, sides, flat(own), flat(other), **options)
         directs.append(direct)
-        returned.append(lax.ppermute(back, "aux", [(target, source) for source, target in pairs]))
+        returned.append(lax.ppermute(back, "aux", ring(naux, len(directs) - 1)))
     shape = ((nt, block_aux, nauxf), F32)
     (early,) = call(assemble, [shape], [], 0, *directs[:-1], *returned[:-1], naux=naux, nt=nt)
     (partial_chi,) = call(complete, [shape], [], 0, early, directs[-1], returned[-1])

time: 58.2 us -> 56.3 us (0.967)
  waiting for transfers between devices: 19.7 us -> 18 us
    ppermute x2, waiting for transfers between devices: 3.33 us -> 1.61 us  [local(): returned.append(lax.ppermute(back, 'aux', ring(naux, len(directs) - 1)))]
  transfers between devices with their start and end apart: 11 -> 11, of which waited for: 4 -> 4; matrix products, arithmetic and copies ran while one was open for 3% -> 3% of each run, Pallas kernels for 20% -> 21%
where the time goes in v7:
time: 56.3 us; the launch traced here: 56 us
  starting transfers between devices  20.3 us (36%)
  waiting for transfers between devices  18 us (32%)
  Pallas kernels  12.8 us (23%)
  local copies, waits for them, and re-layouts  2.45 us (4%)
  other arithmetic  2.25 us (4%)
    pallas_call x8, Pallas kernels, call(): pl.pallas_call(functools.partial(kernel, **options), out_shape=shapes, in...  12.8 us
    ppermute x1, waiting for transfers between devices, local(): fars.append(lax.ppermute(near, ('orb', 'sub'), pairs))  8.06 us
    ppermute x2, starting transfers between devices, local(): pieces = [lax.ppermute(mine, 'aux', pairs) for pairs in plan]  6.14 us
    all_to_all x1, waiting for transfers between devices, local(): lax.all_to_all(partial_chi.reshape(owners, nt * block_aux // owners, naux...  5.53 us
    ppermute x2, starting transfers between devices, local(): returned.append(lax.ppermute(back, 'aux', ring(naux, len(directs) - 1)))  5.11 us
    all_to_all x1, starting transfers between devices, local(): lax.all_to_all(partial_chi.reshape(owners, nt * block_aux // owners, naux...  3.72 us
    ppermute x1, starting transfers between devices, local(): lax.ppermute(tensor, 'orb', ring(nob, shift))  2.94 us
    ppermute x1, waiting for transfers between devices, local(): lax.ppermute(small, 'tau', ring(nt, shift))  2.79 us
  transfers between devices with their start and end apart: 11, of which 4 were waited for; matrix products, arithmetic and copies ran while one was open for 3% of the time, Pallas kernels for 21%

profile of v7, /device:TPU:0, one launch (start us, length us, event | category | flops | bytes accessed | tf_op | source)
XLA Modules:
  0.0 56.0 jit_solution(14008072188816900952)
XLA Ops:
  0.0 2.9 %collective-permute-start.1 = (f32[128,2048]{1,0:T(8,128)}, f32[128,2048]{1,0:T(8,128)S(1)}, u32[]{:S(2)}, u32[]{:S(2)}) collective-permute-start(f32[128,2048]{1,0:T(8,128)} %bitcast.19), channel_id=1, source_target_pairs={{2,0},{0,2},{3,1},{1,3},{6,4},{4,6},{7,5},{5,7},{10,8},{8,10},{11,... | collective-permute-start | bytes 3145736 | tf_op jit(solution)/shard_map/ppermute | solution.py:239
  2.9 0.1 pad_add_fusion.place
  3.0 1.2 %copy-done = f32[1,1,2,64,2048]{4,3,2,1,0:T(8,128)S(1)} copy-done((f32[1,1,2,64,2048]{4,3,2,1,0:T(8,128)S(1)}, f32[1,1,2,64,2048]{4,3,2,1,0:T(8,128)}, u32[]{:S(2)}) %copy-start) | copy-done | bytes 1048600
  4.2 1.2 %prepare.1 = f32[32,32,128]{2,1,0:T(8,128)S(1)} custom-call(s32[4]{0:T(128)S(1)} %pad_add_fusion.place, f32[128,2048]{1,0:T(8,128)S(1)} %bitcast.20), custom_call_target="tpu_custom_call" | custom-call | bytes 1048576 | tf_op jit(solution)/shard_map/prepare/pallas_call | solution.py:228
  5.4 0.1 collective-permute-start.3
  5.5 1.6 %collective-permute-start.4 = (f32[32,32,128]{2,1,0:T(8,128)S(1)}, f32[32,32,128]{2,1,0:T(8,128)S(1)}, u32[]{:S(2)}, u32[]{:S(2)}) collective-permute-start(f32[32,32,128]{2,1,0:T(8,128)S(1)} %prepare.1), channel_id=1, source_target_pairs={{0,4},{4,8},{8,12},{12,0},{1,5},{5,9},{9,13},{13,1},{2,6},{6,10},{... | collective-permute-start | bytes 1572872 | tf_op jit(solution)/shard_map/ppermute | solution.py:244
  7.1 4.5 %collective-permute-start.7 = (f32[32,32,128]{2,1,0:T(8,128)S(1)}, f32[32,32,128]{2,1,0:T(8,128)S(1)}, u32[]{:S(2)}, u32[]{:S(2)}) collective-permute-start(f32[32,32,128]{2,1,0:T(8,128)S(1)} %prepare.1), channel_id=1, source_target_pairs={{0,8},{12,4},{1,9},{13,5},{2,10},{14,6},{3,11},{15,7},{16,24},{28,... | collective-permute-start | bytes 1572872 | tf_op jit(solution)/shard_map/ppermute | solution.py:244
  11.7 0.7 %convert_element_type.5 = f32[1,2]{1,0:T(1,128)S(1)} convert(s32[1,2]{1,0:T(1,128)} %param.7) | non-fusion elementwise | flops 2 | bytes 16 | tf_op jit(solution)/shard_map/convert_element_type | solution.py:251
  12.3 0.8 %fusion.1 = (f32[1,136,128]{2,1,0:T(8,128)S(1)}, f32[136,128]{1,0:T(8,128)S(1)}) fusion(f32[1,2]{1,0:T(1,128)S(1)} %convert_element_type.5, f32[64,128]{1,0:T(8,128)} %param.6, f32[64,128]{1,0:T(8,128)} %param.5), kind=kLoop, calls=%fused_computation.8 | loop fusion | flops 69632 | bytes 204808 | tf_op jit(solution)/shard_map/stack | solution.py:254
  13.1 1.6 %collective-permute-start = (f32[136,128]{1,0:T(8,128)S(1)}, f32[136,128]{1,0:T(8,128)S(1)}, u32[]{:S(2)}, u32[]{:S(2)}) collective-permute-start(f32[136,128]{1,0:T(8,128)S(1)} %get-tuple-element.22), channel_id=1, source_target_pairs={{16,0},{0,16},{17,1},{1,17},{18,2},{2,18},{19,3},{3,19},{20,4},{4,... | collective-permute-start | bytes 208904 | tf_op jit(solution)/shard_map/ppermute | solution.py:254
  14.7 2.8 %collective-permute-done = f32[136,128]{1,0:T(8,128)S(1)} collective-permute-done((f32[136,128]{1,0:T(8,128)S(1)}, f32[136,128]{1,0:T(8,128)S(1)}, u32[]{:S(2)}, u32[]{:S(2)}) %collective-permute-start) | collective-permute-done | bytes 69664 | tf_op jit(solution)/shard_map/ppermute | solution.py:254
  17.5 0.1 collective-permute-start.2
  17.6 0.0 copy-start.1
  17.6 1.2 %copy-done.1 = f32[1,1,2,64,2048]{4,3,2,1,0:T(8,128)S(1)} copy-done((f32[1,1,2,64,2048]{4,3,2,1,0:T(8,128)S(1)}, f32[1,1,2,64,2048]{4,3,2,1,0:T(8,128)}, u32[]{:S(2)}) %copy-start.1) | copy-done | bytes 1048600
  18.8 1.7 %first.1 = (f32[4,512,256]{2,1,0:T(8,128)S(1)}, f32[8,128]{1,0:T(8,128)S(1)}) custom-call(s32[4]{0:T(128)S(1)} %pad_add_fusion.place, f32[2,136,128]{2,1,0:T(8,128)S(1)} %pad_maximum_fusion.near, f32[128,2048]{1,0:T(8,128)S(1)} %bitcast.21), custom_call_target="tpu_custom_call" | custom-call | flops 603979776 | bytes 1187840 | tf_op jit(solution)/shard_map/first/pallas_call | solution.py:228
  20.5 8.1 %collective-permute-done.2.refs_1_.refs_3_ = f32[2,136,128]{2,1,0:T(8,128)S(1)} collective-permute-done((f32[2,136,128]{2,1,0:T(8,128)S(1)}, f32[2,136,128]{2,1,0:T(8,128)S(1)}, u32[]{:S(2)}, u32[]{:S(2)}) %collective-permute-start.2) | collective-permute-done | bytes 139296 | tf_op jit(solution)/shard_map/ppermute | solution.py:258
  28.6 0.0 collective-permute-done.3.refs_2_
  28.6 0.6 %collective-permute-start.5 = (f32[32,32,128]{2,1,0:T(8,128)S(1)}, f32[32,32,128]{2,1,0:T(8,128)S(1)}, u32[]{:S(2)}, u32[]{:S(2)}) collective-permute-start(f32[32,32,128]{2,1,0:T(8,128)S(1)} %after.2), channel_id=1, source_target_pairs={{1,0},{0,1},{3,2},{2,3},{5,4},{4,5},{7,6},{6,7},{9,8},{8,9},{11,10... | collective-permute-start | bytes 1572872 | tf_op jit(solution)/shard_map/ppermute | solution.py:287
  29.2 0.0 collective-permute-done.1.refs_0_
  29.2 3.3 %second.1 = (bf16[256,4096]{1,0:T(8,128)(2,1)S(1)}, f32[8,128]{1,0:T(8,128)S(1)}) custom-call(s32[4]{0:T(128)S(1)} %pad_add_fusion.place, f32[2,136,128]{2,1,0:T(8,128)S(1)} %pad_maximum_fusion.near, f32[4,512,256]{2,1,0:T(8,128)S(1)} %get-tuple-element.13.acc, f32[128,2048]{1,0:T(8,128)S(1)} %collective-permute-done.1.refs_0_, ...), custom_call_target="tpu_custom_call" | custom-call | flops 603979776 | bytes 3424256 | tf_op jit(solution)/shard_map/second/pallas_call | solution.py:228
  32.5 0.1 collective-permute-start.8
  32.6 1.6 %meet.4 = (f32[64,64]{1,0:T(8,128)S(1)}, f32[64,128]{1,0:T(8,128)S(1)}) custom-call(s32[4]{0:T(128)S(1)} %pad_add_fusion.place, bf16[256,4096]{1,0:T(8,128)(2,1)S(1)} %get-tuple-element.14.sides, f32[1024,128]{1,0:T(8,128)S(1)} %bitcast.18, f32[1024,128]{1,0:T(8,128)S(1)} %bitcast.22), custom_call_target="tpu_custom_call" | custom-call | flops 536870912 | bytes 5242880 | tf_op jit(solution)/shard_map/meet/pallas_call | solution.py:228
  34.3 3.9 %collective-permute-start.6 = (f32[64,128]{1,0:T(8,128)S(1)}, f32[64,128]{1,0:T(8,128)S(1)}, u32[]{:S(2)}, u32[]{:S(2)}) collective-permute-start(f32[64,128]{1,0:T(8,128)S(1)} %get-tuple-element.17), channel_id=1, source_target_pairs={{4,0},{8,4},{12,8},{0,12},{5,1},{9,5},{13,9},{1,13},{6,2},{10,6},{... | collective-permute-start | bytes 98312 | tf_op jit(solution)/shard_map/ppermute | solution.py:299
  38.2 1.6 %meet.5 = (f32[64,64]{1,0:T(8,128)S(1)}, f32[64,128]{1,0:T(8,128)S(1)}) custom-call(s32[4]{0:T(128)S(1)} %pad_add_fusion.place, bf16[256,4096]{1,0:T(8,128)(2,1)S(1)} %get-tuple-element.14.sides, f32[1024,128]{1,0:T(8,128)S(1)} %bitcast.17, f32[1024,128]{1,0:T(8,128)S(1)} %bitcast.23), custom_call_target="tpu_custom_call" | custom-call | flops 536870912 | bytes 5242880 | tf_op jit(solution)/shard_map/meet/pallas_call | solution.py:228
  39.8 1.2 %collective-permute-start.9 = (f32[64,128]{1,0:T(8,128)S(1)}, f32[64,128]{1,0:T(8,128)S(1)}, u32[]{:S(2)}, u32[]{:S(2)}) collective-permute-start(f32[64,128]{1,0:T(8,128)S(1)} %get-tuple-element.20), channel_id=1, source_target_pairs={{8,0},{12,4},{0,8},{4,12},{9,1},{13,5},{1,9},{5,13},{10,2},{14,6},... | collective-permute-start | bytes 98312 | tf_op jit(solution)/shard_map/ppermute | solution.py:299
  41.0 1.4 %meet.3.refs_0_ = f32[64,64]{1,0:T(8,128)S(1)} custom-call(s32[4]{0:T(128)S(1)} %pad_add_fusion.place, bf16[256,4096]{1,0:T(8,128)(2,1)S(1)} %get-tuple-element.14.sides, f32[1024,128]{1,0:T(8,128)S(1)} %bitcast.15, f32[1024,128]{1,0:T(8,128)S(1)} %bitcast.16), custom_call_target="tpu_custom_call" | custom-call | flops 536870912 | bytes 5242880 | tf_op jit(solution)/shard_map/meet/pallas_call | solution.py:228
  42.5 0.6 %assemble.1.early = f32[2,64,256]{2,1,0:T(8,128)S(1)} custom-call(s32[4]{0:T(128)S(1)} %pad_add_fusion.place, f32[64,64]{1,0:T(8,128)S(1)} %meet.3.refs_0_, f32[64,64]{1,0:T(8,128)S(1)} %get-tuple-element.16.refs_1_, f32[64,128]{1,0:T(8,128)S(1)} %collective-permute-done.6.refs_2_), custom_call_target="tpu_custom_call" | custom-call | bytes 65536 | tf_op jit(solution)/shard_map/assemble/pallas_call | solution.py:228
  43.1 1.6 %collective-permute-done.9.back = f32[64,128]{1,0:T(8,128)S(1)} collective-permute-done((f32[64,128]{1,0:T(8,128)S(1)}, f32[64,128]{1,0:T(8,128)S(1)}, u32[]{:S(2)}, u32[]{:S(2)}) %collective-permute-start.9) | collective-permute-done | bytes 32800 | tf_op jit(solution)/shard_map/ppermute | solution.py:299
  44.7 1.3 %complete.1 = f32[2,64,256]{2,1,0:T(8,128)} custom-call(s32[4]{0:T(128)S(1)} %pad_add_fusion.place, f32[2,64,256]{2,1,0:T(8,128)S(1)} %assemble.1.early, f32[64,64]{1,0:T(8,128)S(1)} %get-tuple-element.19.direct, f32[64,128]{1,0:T(8,128)S(1)} %collective-permute-done.9.back), custom_call_target="tpu_custom_call" | custom-call | bytes 180224 | tf_op jit(solution)/shard_map/complete/pallas_call | solution.py:228
  46.0 3.7 %all-to-all-start = ((f32[8,16,256]{2,1,0:T(8,128)}), f32[8,16,256]{2,1,0:T(8,128)S(1)}, u32[]{:S(2)}, u32[]{:S(2)}) async-start(f32[8,16,256]{2,1,0:T(8,128)} %bitcast.13), calls=%async_computation | async-start | bytes 262144 | tf_op jit(solution)/shard_map/all_to_all | solution.py:304
  49.7 5.5 %all-to-all-done = f32[8,16,256]{2,1,0:T(8,128)S(1)} async-done(((f32[8,16,256]{2,1,0:T(8,128)}), f32[8,16,256]{2,1,0:T(8,128)S(1)}, u32[]{:S(2)}, u32[]{:S(2)}) %all-to-all-start) | async-done | bytes 131104 | tf_op jit(solution)/shard_map/all_to_all | solution.py:304
  55.3 0.7 %fusion = f32[16,256]{1,0:T(8,128)} fusion(s32[]{:T(128)S(6)} %select_n.14, f32[16,256]{1,0:T(8,128)S(1)} %broadcast_multiply_fusion), kind=kLoop, calls=%fused_computation.5 | loop fusion | flops 4096 | bytes 32772 | tf_op jit(solution)/shard_map/jit(_roll_dynamic)/concatenate | solution.py:312
  (11 shorter events, 0.1 us)
Async XLA Ops:
  0.0 29.2 %collective-permute-start.1 = (f32[128,2048]{1,0:T(8,128)}, f32[128,2048]{1,0:T(8,128)S(1)}, u32[]{:S(2)}, u32[]{:S(2)}) collective-permute-start(f32[128,2048]{1,0:T(8,128)} %bitcast.19), channel_id=1, source_target_pairs={{2,0},{0,2},{3,1},{1,3},{6,4},{4,6},{7,5},{5,7},{10,8},{8,10},{11,... | collective-permute-start | bytes 3145736 | tf_op jit(solution)/shard_map/ppermute | solution.py:239
  3.0 1.2 %copy-start = (f32[1,1,2,64,2048]{4,3,2,1,0:T(8,128)S(1)}, f32[1,1,2,64,2048]{4,3,2,1,0:T(8,128)}, u32[]{:S(2)}) copy-start(f32[1,1,2,64,2048]{4,3,2,1,0:T(8,128)} %param.4) | copy-start | bytes 3145732
  5.4 23.1 %collective-permute-start.3 = (f32[32,32,128]{2,1,0:T(8,128)S(1)}, f32[32,32,128]{2,1,0:T(8,128)S(1)}, u32[]{:S(2)}, u32[]{:S(2)}) collective-permute-start(f32[32,32,128]{2,1,0:T(8,128)S(1)} %prepare.1), channel_id=1, source_target_pairs={{1,0},{0,1},{3,2},{2,3},{5,4},{4,5},{7,6},{6,7},{9,8},{8,9},{11,10... | collective-permute-start | bytes 1572872 | tf_op jit(solution)/shard_map/ppermute | solution.py:246
  5.5 23.1 %collective-permute-start.4 = (f32[32,32,128]{2,1,0:T(8,128)S(1)}, f32[32,32,128]{2,1,0:T(8,128)S(1)}, u32[]{:S(2)}, u32[]{:S(2)}) collective-permute-start(f32[32,32,128]{2,1,0:T(8,128)S(1)} %prepare.1), channel_id=1, source_target_pairs={{0,4},{4,8},{8,12},{12,0},{1,5},{5,9},{9,13},{13,1},{2,6},{6,10},{... | collective-permute-start | bytes 1572872 | tf_op jit(solution)/shard_map/ppermute | solution.py:244
  7.1 25.4 %collective-permute-start.7 = (f32[32,32,128]{2,1,0:T(8,128)S(1)}, f32[32,32,128]{2,1,0:T(8,128)S(1)}, u32[]{:S(2)}, u32[]{:S(2)}) collective-permute-start(f32[32,32,128]{2,1,0:T(8,128)S(1)} %prepare.1), channel_id=1, source_target_pairs={{0,8},{12,4},{1,9},{13,5},{2,10},{14,6},{3,11},{15,7},{16,24},{28,... | collective-permute-start | bytes 1572872 | tf_op jit(solution)/shard_map/ppermute | solution.py:244
  13.1 4.4 %collective-permute-start = (f32[136,128]{1,0:T(8,128)S(1)}, f32[136,128]{1,0:T(8,128)S(1)}, u32[]{:S(2)}, u32[]{:S(2)}) collective-permute-start(f32[136,128]{1,0:T(8,128)S(1)} %get-tuple-element.22), channel_id=1, source_target_pairs={{16,0},{0,16},{17,1},{1,17},{18,2},{2,18},{19,3},{3,19},{20,4},{4,... | collective-permute-start | bytes 208904 | tf_op jit(solution)/shard_map/ppermute | solution.py:254
  17.5 11.1 %collective-permute-start.2 = (f32[2,136,128]{2,1,0:T(8,128)S(1)}, f32[2,136,128]{2,1,0:T(8,128)S(1)}, u32[]{:S(2)}, u32[]{:S(2)}) collective-permute-start(f32[2,136,128]{2,1,0:T(8,128)S(1)} %pad_maximum_fusion.near), channel_id=1, source_target_pairs={{2,1},{3,0},{0,3},{1,2},{6,5},{7,4},{4,7},{5,6},{10,9},{11,8},{8,1... | collective-permute-start | bytes 417800 | tf_op jit(solution)/shard_map/ppermute | solution.py:258
  17.6 1.2 %copy-start.1 = (f32[1,1,2,64,2048]{4,3,2,1,0:T(8,128)S(1)}, f32[1,1,2,64,2048]{4,3,2,1,0:T(8,128)}, u32[]{:S(2)}) copy-start(f32[1,1,2,64,2048]{4,3,2,1,0:T(8,128)} %param.4) | copy-start | bytes 3145732
  28.6 4.0 %collective-permute-start.5 = (f32[32,32,128]{2,1,0:T(8,128)S(1)}, f32[32,32,128]{2,1,0:T(8,128)S(1)}, u32[]{:S(2)}, u32[]{:S(2)}) collective-permute-start(f32[32,32,128]{2,1,0:T(8,128)S(1)} %after.2), channel_id=1, source_target_pairs={{1,0},{0,1},{3,2},{2,3},{5,4},{4,5},{7,6},{6,7},{9,8},{8,9},{11,10... | collective-permute-start | bytes 1572872 | tf_op jit(solution)/shard_map/ppermute | solution.py:287
  32.5 5.7 %collective-permute-start.8 = (f32[32,32,128]{2,1,0:T(8,128)S(1)}, f32[32,32,128]{2,1,0:T(8,128)S(1)}, u32[]{:S(2)}, u32[]{:S(2)}) collective-permute-start(f32[32,32,128]{2,1,0:T(8,128)S(1)} %after.3), channel_id=1, source_target_pairs={{1,0},{0,1},{3,2},{2,3},{5,4},{4,5},{7,6},{6,7},{9,8},{8,9},{11,10... | collective-permute-start | bytes 1572872 | tf_op jit(solution)/shard_map/ppermute | solution.py:287
  34.3 8.2 %collective-permute-start.6 = (f32[64,128]{1,0:T(8,128)S(1)}, f32[64,128]{1,0:T(8,128)S(1)}, u32[]{:S(2)}, u32[]{:S(2)}) collective-permute-start(f32[64,128]{1,0:T(8,128)S(1)} %get-tuple-element.17), channel_id=1, source_target_pairs={{4,0},{8,4},{12,8},{0,12},{5,1},{9,5},{13,9},{1,13},{6,2},{10,6},{... | collective-permute-start | bytes 98312 | tf_op jit(solution)/shard_map/ppermute | solution.py:299
  39.8 4.9 %collective-permute-start.9 = (f32[64,128]{1,0:T(8,128)S(1)}, f32[64,128]{1,0:T(8,128)S(1)}, u32[]{:S(2)}, u32[]{:S(2)}) collective-permute-start(f32[64,128]{1,0:T(8,128)S(1)} %get-tuple-element.20), channel_id=1, source_target_pairs={{8,0},{12,4},{0,8},{4,12},{9,1},{13,5},{1,9},{5,13},{10,2},{14,6},... | collective-permute-start | bytes 98312 | tf_op jit(solution)/shard_map/ppermute | solution.py:299
  46.0 9.2 %all-to-all-start = ((f32[8,16,256]{2,1,0:T(8,128)}), f32[8,16,256]{2,1,0:T(8,128)S(1)}, u32[]{:S(2)}, u32[]{:S(2)}) async-start(f32[8,16,256]{2,1,0:T(8,128)} %bitcast.13), calls=%async_computation | async-start | bytes 262144 | tf_op jit(solution)/shard_map/all_to_all | solution.py:304

commit v8 on v7

--- a/solution.py
+++ b/solution.py
@@ -76,7 +76,7 @@
     return jnp.concatenate(parts, axis=1)
 
 
-def mix(place, near, far, tensor, slots, width, share):
+def mix(place, near, far, tensor, rows, slots, width, share):
     nt = near.shape[0]
     pairs = tensor.shape[1] // (2 * width)
     near_list, far_list = near[0, 2 * width :, :], far[0, 2 * width :, :]
@@ -91,7 +91,11 @@
     middle = dot(
         jnp.concatenate([left_high, left_high, left_low], axis=1), jnp.concatenate([high, low, high], axis=0)
     )
-    middle_high, middle_low = halves(middle)
+    for group in range(2 * nt):
+        for at in range(pairs):
+            rows[(group * pairs + at) * share : (group * pairs + at + 1) * share, :] = middle[
+                group * share : (group + 1) * share, 2 * width * at : 2 * width * (at + 1)
+            ]
     results = []
     for group in range(2 * nt):
         kind, tau = group // nt, group % nt
@@ -101,11 +105,11 @@
             jnp.concatenate([jnp.concatenate([right, zero], axis=1), jnp.concatenate([zero, right], axis=1)], axis=0)
         )
 
-        def stacked(array):
-            rows = array[group * share : (group + 1) * share]
-            return jnp.concatenate([rows[:, 2 * width * at : 2 * width * (at + 1)] for at in range(pairs)], axis=0)
-
-        rows_high, rows_low = stacked(middle_high), stacked(middle_low)
+        rows_high, rows_low = halves(
+            jnp.concatenate(
+                [rows[pl.ds(group * pairs * share + at, pairs, stride=share), :] for at in range(share)], axis=0
+            )
+        )
         results.append(
             dot(
                 jnp.concatenate([rows_high, rows_high, rows_low], axis=1),
@@ -115,14 +119,14 @@
     return results
 
 
-def first(place, near, tensor, acc, token, *, slots, width, share):
+def first(place, near, tensor, acc, token, rows, *, slots, width, share):
     token[...] = jnp.zeros_like(token)
-    for group, result in enumerate(mix(place, near, near, tensor, slots, width, share)):
+    for group, result in enumerate(mix(place, near, near, tensor, rows, slots, width, share)):
         acc[group] = result
 
 
 def second(place, near, acc, *refs, slots, width, share):
-    refs, (sides, token, spread) = refs[:-3], refs[-3:]
+    refs, (sides, token, rows) = refs[:-3], refs[-3:]
     tensors, fars = refs[: len(refs) // 2], refs[len(refs) // 2 :]
     token[...] = jnp.zeros_like(token)
     listed = slots * width
@@ -130,24 +134,22 @@
     pairs = tall // share
     total = [acc[group] for group in range(groups)]
     for tensor, far in zip(tensors, fars):
-        term = mix(place, near, far, tensor, slots, width, share)
+        term = mix(place, near, far, tensor, rows, slots, width, share)
         total = [x + y for x, y in zip(total, term)]
     for group in range(groups):
-        for at in range(pairs):
-            for place_in in range(2):
-                row = (group * 2 * pairs + 2 * at + place_in) * share
-                spread[row : row + share, :] = total[group][
-                    at * share : (at + 1) * share, place_in * listed : (place_in + 1) * listed
-                ]
-    rows = groups * 2 * pairs
-    for at in range(share):
-        high, low = halves(spread[pl.ds(at, rows, stride=share), :])
-        sides[:rows, at * listed : (at + 1) * listed] = high
-        sides[rows:, at * listed : (at + 1) * listed] = low
+        high, low = halves(total[group])
+        for odd in range(2):
+            row = (2 * group + odd) * pairs
+            for at in range(share):
+                for part, array in enumerate((high, low)):
+                    sides[
+                        part * 2 * groups * pairs + row : part * 2 * groups * pairs + row + pairs,
+                        at * listed : (at + 1) * listed,
+                    ] = array[at * pairs : (at + 1) * pairs, odd * listed : (odd + 1) * listed]
 
 
 def meet(place, sides, own, other, *refs, share, nt):
-    outs, tensor = refs[:-1], refs[-1]
+    outs, (tensor, ordered) = refs[:-2], refs[-2:]
     listed = own.shape[1]
     rows_aux = own.shape[0] // share
     block = 2 * rows_aux
@@ -157,12 +159,17 @@
             high, low = halves(source[at * rows_aux : (at + 1) * rows_aux, :])
             tensor[pl.ds(start, rows_aux), at * listed : (at + 1) * listed] = high
             tensor[pl.ds(block + start, rows_aux), at * listed : (at + 1) * listed] = low
-    product = dot_nt(sides[...], tensor[...])
-    product = product[:, :block] + product[:, block:]
-    product = product[: 2 * nt * rows_aux] + product[2 * nt * rows_aux :]
-    outs[0][...] = product[: nt * rows_aux]
+    product = dot_nt(tensor[...], sides[...])
+    product = product[:block] + product[block:]
+    product = (product[:, : 2 * nt * rows_aux] + product[:, 2 * nt * rows_aux :]).T
+    pairs = rows_aux // 2
+    for group in range(2 * nt):
+        for odd in range(2):
+            at = (2 * group + odd) * pairs
+            ordered[pl.ds(group * rows_aux + odd, pairs, stride=2), :] = product[at : at + pairs]
+    outs[0][...] = ordered[: nt * rows_aux, :]
     if len(outs) == 2:
-        back = product[nt * rows_aux :].T
+        back = ordered[nt * rows_aux :, :].T
         parts = []
         for tau in range(nt):
             part = back[:, tau * rows_aux : (tau + 1) * rows_aux]
@@ -198,12 +205,17 @@
     half = direct.shape[0] // nt
     naux = wide // block
     last = naux // 2
-    start = pl.multiple_of(place[2] * half, half)
     for tau in range(nt):
-        out_ref[tau] = early[tau]
-        out_ref[tau, :, last * block : (last + 1) * block] += back[:, tau * block : (tau + 1) * block]
-        at = (naux - last) * block
-        out_ref[tau, pl.ds(start, half), at : at + block] += direct[tau * half : (tau + 1) * half, :]
+        here = direct[tau * half : (tau + 1) * half, :]
+        zero = jnp.zeros_like(here)
+        here = jnp.where(
+            place[2] == 0, jnp.concatenate([here, zero], axis=0), jnp.concatenate([zero, here], axis=0)
+        )
+        parts = [jnp.zeros((block, block), F32)] * naux
+        parts[last] = back[:, tau * block : (tau + 1) * block]
+        parts[(naux - last) % naux] = parts[(naux - last) % naux] + here
+        total = early[tau] + jnp.concatenate(parts, axis=1)
+        out_ref[tau] = pltpu.roll(total, place[3] * block, 1)
 
 
 def local(three_center, occupied_green, virtual_green, block_list, sizes):
@@ -265,7 +277,7 @@
     acc, token = call(
         first,
         [((groups, rows_aux // 2 * share, 2 * listed), F32), ((8, 128), F32)],
-        [],
+        [((groups * rows_aux // 2 * share, 2 * width), F32)],
         work,
         near,
         tensor,
@@ -274,7 +286,7 @@
     sides, token_late = call(
         second,
         [((2 * rows, depth), BF16), ((8, 128), F32)],
-        [((rows * share, listed), F32)],
+        [((groups * rows_aux // 2 * share, 2 * width), F32)],
         work * (nob - 1),
         near,
         acc,
@@ -286,7 +298,7 @@
     pieces = [after(block, *token) for block, token in zip(pieces, tokens)]
     others = [lax.ppermute(block, "sub", swap) for block in pieces]
     flat = lambda block: block.reshape(-1, listed)
-    turned = [((2 * block_aux, depth), BF16)]
+    turned = [((2 * block_aux, depth), BF16), ((rows, block_aux), F32)]
     shape_direct = ((nt * rows_aux, block_aux), F32)
     shape_back = ((block_aux, nt * block_aux), F32)
     work = 16 * rows * block_aux * depth
@@ -308,8 +320,7 @@
         concat_axis=0,
         tiled=True,
     )
-    total = received.sum(axis=0) * (-2.0 / math.sqrt(norb * slots * width))
-    return jnp.roll(total, me_aux * block_aux, axis=1)
+    return received.sum(axis=0) * (-2.0 / math.sqrt(norb * slots * width))
 
 
 def solution(mesh):

time: 56.3 us -> 54.5 us (0.968)
  blocking collectives: 0 us -> 9.04 us
  waiting for transfers between devices: 18 us -> 12.1 us
  starting transfers between devices: 20.3 us -> 16.6 us
  Pallas kernels: 12.8 us -> 11.7 us
    all_to_all x0 -> x1, blocking collectives: none -> 9.04 us  [local(): lax.all_to_all(partial_chi.reshape(owners, nt * block_aux // owners, naux...]
    all_to_all x1 -> x0, waiting for transfers between devices: 5.53 us -> none  [local(): lax.all_to_all(partial_chi.reshape(owners, nt * block_aux // owners, naux...]
    all_to_all x1 -> x0, starting transfers between devices: 3.72 us -> none  [local(): lax.all_to_all(partial_chi.reshape(owners, nt * block_aux // owners, naux...]
    pallas_call x8, Pallas kernels: 12.8 us -> 11.7 us  [call(): pl.pallas_call(functools.partial(kernel, **options), out_shape=shapes, in...]
    concatenate x1 -> x0, other arithmetic: 0.7 us -> none  [local(): return jnp.roll(total, me_aux * block_aux, axis=1)]
    mul x1, other arithmetic: 0.01 us -> 0.61 us  [local(): return received.sum(axis=0) * (-2.0 / math.sqrt(norb * slots * width))]
  transfers between devices with their start and end apart: 11 -> 10, of which waited for: 4 -> 3; matrix products, arithmetic and copies ran while one was open for 3% -> 3% of each run, Pallas kernels for 21% -> 20%
where the time goes in v8:
time: 54.5 us; the launch traced here: 54.2 us
  starting transfers between devices  16.6 us (30%)
  waiting for transfers between devices  12.1 us (22%)
  Pallas kernels  11.7 us (21%)
  blocking collectives  9.04 us (17%)
  local copies, waits for them, and re-layouts  2.45 us (4%)
  other arithmetic  2.16 us (4%)
    pallas_call x8, Pallas kernels, call(): pl.pallas_call(functools.partial(kernel, **options), out_shape=shapes, in...  11.7 us
    all_to_all x1, blocking collectives, local(): lax.all_to_all(partial_chi.reshape(owners, nt * block_aux // owners, naux...  9.04 us
    ppermute x1, waiting for transfers between devices, local(): fars.append(lax.ppermute(near, ('orb', 'sub'), pairs))  7.73 us
    ppermute x2, starting transfers between devices, local(): pieces = [lax.ppermute(mine, 'aux', pairs) for pairs in plan]  6.14 us
    ppermute x2, starting transfers between devices, local(): returned.append(lax.ppermute(back, 'aux', ring(naux, len(directs) - 1)))  5.11 us
    ppermute x1, starting transfers between devices, local(): lax.ppermute(tensor, 'orb', ring(nob, shift))  2.94 us
    ppermute x1, waiting for transfers between devices, local(): lax.ppermute(small, 'tau', ring(nt, shift))  2.79 us
    unnamed x4, local copies, waits for them, and re-layouts  2.45 us
  transfers between devices with their start and end apart: 10, of which 3 were waited for; matrix products, arithmetic and copies ran while one was open for 3% of the time, Pallas kernels for 20%

profile of v8, /device:TPU:0, one launch (start us, length us, event | category | flops | bytes accessed | tf_op | source)
XLA Modules:
  0.0 54.2 jit_solution(15219999628845448983)
XLA Ops:
  0.0 2.9 %collective-permute-start.1 = (f32[128,2048]{1,0:T(8,128)}, f32[128,2048]{1,0:T(8,128)S(1)}, u32[]{:S(2)}, u32[]{:S(2)}) collective-permute-start(f32[128,2048]{1,0:T(8,128)} %bitcast.19), channel_id=1, source_target_pairs={{2,0},{0,2},{3,1},{1,3},{6,4},{4,6},{7,5},{5,7},{10,8},{8,10},{11,... | collective-permute-start | bytes 3145736 | tf_op jit(solution)/shard_map/ppermute | solution.py:251
  2.9 0.1 pad_add_fusion.place
  3.0 1.2 %copy-done = f32[1,1,2,64,2048]{4,3,2,1,0:T(8,128)S(1)} copy-done((f32[1,1,2,64,2048]{4,3,2,1,0:T(8,128)S(1)}, f32[1,1,2,64,2048]{4,3,2,1,0:T(8,128)}, u32[]{:S(2)}) %copy-start) | copy-done | bytes 1048600
  4.2 1.2 %prepare.1 = f32[32,32,128]{2,1,0:T(8,128)S(1)} custom-call(s32[4]{0:T(128)S(1)} %pad_add_fusion.place, f32[128,2048]{1,0:T(8,128)S(1)} %bitcast.20), custom_call_target="tpu_custom_call" | custom-call | bytes 1048576 | tf_op jit(solution)/shard_map/prepare/pallas_call | solution.py:240
  5.4 0.1 collective-permute-start.3
  5.5 1.6 %collective-permute-start.4 = (f32[32,32,128]{2,1,0:T(8,128)S(1)}, f32[32,32,128]{2,1,0:T(8,128)S(1)}, u32[]{:S(2)}, u32[]{:S(2)}) collective-permute-start(f32[32,32,128]{2,1,0:T(8,128)S(1)} %prepare.1), channel_id=1, source_target_pairs={{0,4},{4,8},{8,12},{12,0},{1,5},{5,9},{9,13},{13,1},{2,6},{6,10},{... | collective-permute-start | bytes 1572872 | tf_op jit(solution)/shard_map/ppermute | solution.py:256
  7.1 4.5 %collective-permute-start.7 = (f32[32,32,128]{2,1,0:T(8,128)S(1)}, f32[32,32,128]{2,1,0:T(8,128)S(1)}, u32[]{:S(2)}, u32[]{:S(2)}) collective-permute-start(f32[32,32,128]{2,1,0:T(8,128)S(1)} %prepare.1), channel_id=1, source_target_pairs={{0,8},{12,4},{1,9},{13,5},{2,10},{14,6},{3,11},{15,7},{16,24},{28,... | collective-permute-start | bytes 1572872 | tf_op jit(solution)/shard_map/ppermute | solution.py:256
  11.7 0.7 %convert_element_type.5 = f32[1,2]{1,0:T(1,128)S(1)} convert(s32[1,2]{1,0:T(1,128)} %param.7) | non-fusion elementwise | flops 2 | bytes 16 | tf_op jit(solution)/shard_map/convert_element_type | solution.py:263
  12.3 0.8 %fusion = (f32[1,136,128]{2,1,0:T(8,128)S(1)}, f32[136,128]{1,0:T(8,128)S(1)}) fusion(f32[1,2]{1,0:T(1,128)S(1)} %convert_element_type.5, f32[64,128]{1,0:T(8,128)} %param.6, f32[64,128]{1,0:T(8,128)} %param.5), kind=kLoop, calls=%fused_computation.5 | loop fusion | flops 69632 | bytes 204808 | tf_op jit(solution)/shard_map/stack | solution.py:266
  13.1 1.6 %collective-permute-start = (f32[136,128]{1,0:T(8,128)S(1)}, f32[136,128]{1,0:T(8,128)S(1)}, u32[]{:S(2)}, u32[]{:S(2)}) collective-permute-start(f32[136,128]{1,0:T(8,128)S(1)} %get-tuple-element.22), channel_id=1, source_target_pairs={{16,0},{0,16},{17,1},{1,17},{18,2},{2,18},{19,3},{3,19},{20,4},{4,... | collective-permute-start | bytes 208904 | tf_op jit(solution)/shard_map/ppermute | solution.py:266
  14.7 2.8 %collective-permute-done = f32[136,128]{1,0:T(8,128)S(1)} collective-permute-done((f32[136,128]{1,0:T(8,128)S(1)}, f32[136,128]{1,0:T(8,128)S(1)}, u32[]{:S(2)}, u32[]{:S(2)}) %collective-permute-start) | collective-permute-done | bytes 69664 | tf_op jit(solution)/shard_map/ppermute | solution.py:266
  17.5 0.1 collective-permute-start.2
  17.6 0.0 copy-start.1
  17.6 1.2 %copy-done.1 = f32[1,1,2,64,2048]{4,3,2,1,0:T(8,128)S(1)} copy-done((f32[1,1,2,64,2048]{4,3,2,1,0:T(8,128)S(1)}, f32[1,1,2,64,2048]{4,3,2,1,0:T(8,128)}, u32[]{:S(2)}) %copy-start.1) | copy-done | bytes 1048600
  18.8 2.0 %first.1 = (f32[4,512,256]{2,1,0:T(8,128)S(1)}, f32[8,128]{1,0:T(8,128)S(1)}) custom-call(s32[4]{0:T(128)S(1)} %pad_add_fusion.place, f32[2,136,128]{2,1,0:T(8,128)S(1)} %pad_maximum_fusion.near, f32[128,2048]{1,0:T(8,128)S(1)} %bitcast.21), custom_call_target="tpu_custom_call" | custom-call | flops 603979776 | bytes 1187840 | tf_op jit(solution)/shard_map/first/pallas_call | solution.py:240
  20.8 7.7 %collective-permute-done.2.refs_1_.refs_3_ = f32[2,136,128]{2,1,0:T(8,128)S(1)} collective-permute-done((f32[2,136,128]{2,1,0:T(8,128)S(1)}, f32[2,136,128]{2,1,0:T(8,128)S(1)}, u32[]{:S(2)}, u32[]{:S(2)}) %collective-permute-start.2) | collective-permute-done | bytes 139296 | tf_op jit(solution)/shard_map/ppermute | solution.py:270
  28.6 0.0 collective-permute-done.3.refs_2_
  28.6 0.0 collective-permute-done.4.refs_0_
  28.6 0.6 %collective-permute-start.5 = (f32[32,32,128]{2,1,0:T(8,128)S(1)}, f32[32,32,128]{2,1,0:T(8,128)S(1)}, u32[]{:S(2)}, u32[]{:S(2)}) collective-permute-start(f32[32,32,128]{2,1,0:T(8,128)S(1)} %after.2), channel_id=1, source_target_pairs={{1,0},{0,1},{3,2},{2,3},{5,4},{4,5},{7,6},{6,7},{9,8},{8,9},{11,10... | collective-permute-start | bytes 1572872 | tf_op jit(solution)/shard_map/ppermute | solution.py:299
  29.2 2.3 %second.1 = (bf16[256,4096]{1,0:T(8,128)(2,1)S(1)}, f32[8,128]{1,0:T(8,128)S(1)}) custom-call(s32[4]{0:T(128)S(1)} %pad_add_fusion.place, f32[2,136,128]{2,1,0:T(8,128)S(1)} %pad_maximum_fusion.near, f32[4,512,256]{2,1,0:T(8,128)S(1)} %get-tuple-element.13.acc, f32[128,2048]{1,0:T(8,128)S(1)} %collective-permute-done.1.refs_0_, ...), custom_call_target="tpu_custom_call" | custom-call | flops 603979776 | bytes 3424256 | tf_op jit(solution)/shard_map/second/pallas_call | solution.py:240
  31.5 0.0 collective-permute-done.7.refs_0_
  31.5 0.1 collective-permute-start.8
  31.6 1.7 %meet.4 = (f32[64,64]{1,0:T(8,128)S(1)}, f32[64,128]{1,0:T(8,128)S(1)}) custom-call(s32[4]{0:T(128)S(1)} %pad_add_fusion.place, bf16[256,4096]{1,0:T(8,128)(2,1)S(1)} %get-tuple-element.14.sides, f32[1024,128]{1,0:T(8,128)S(1)} %bitcast.18, f32[1024,128]{1,0:T(8,128)S(1)} %bitcast.23), custom_call_target="tpu_custom_call" | custom-call | flops 536870912 | bytes 5242880 | tf_op jit(solution)/shard_map/meet/pallas_call | solution.py:240
  33.3 3.9 %collective-permute-start.6 = (f32[64,128]{1,0:T(8,128)S(1)}, f32[64,128]{1,0:T(8,128)S(1)}, u32[]{:S(2)}, u32[]{:S(2)}) collective-permute-start(f32[64,128]{1,0:T(8,128)S(1)} %get-tuple-element.17), channel_id=1, source_target_pairs={{4,0},{8,4},{12,8},{0,12},{5,1},{9,5},{13,9},{1,13},{6,2},{10,6},{... | collective-permute-start | bytes 98312 | tf_op jit(solution)/shard_map/ppermute | solution.py:311
  37.2 1.7 %meet.5 = (f32[64,64]{1,0:T(8,128)S(1)}, f32[64,128]{1,0:T(8,128)S(1)}) custom-call(s32[4]{0:T(128)S(1)} %pad_add_fusion.place, bf16[256,4096]{1,0:T(8,128)(2,1)S(1)} %get-tuple-element.14.sides, f32[1024,128]{1,0:T(8,128)S(1)} %bitcast.17, f32[1024,128]{1,0:T(8,128)S(1)} %bitcast.24), custom_call_target="tpu_custom_call" | custom-call | flops 536870912 | bytes 5242880 | tf_op jit(solution)/shard_map/meet/pallas_call | solution.py:240
  38.9 1.2 %collective-permute-start.9 = (f32[64,128]{1,0:T(8,128)S(1)}, f32[64,128]{1,0:T(8,128)S(1)}, u32[]{:S(2)}, u32[]{:S(2)}) collective-permute-start(f32[64,128]{1,0:T(8,128)S(1)} %get-tuple-element.20), channel_id=1, source_target_pairs={{8,0},{12,4},{0,8},{4,12},{9,1},{13,5},{1,9},{5,13},{10,2},{14,6},... | collective-permute-start | bytes 98312 | tf_op jit(solution)/shard_map/ppermute | solution.py:311
  40.1 1.5 %meet.3.refs_0_ = f32[64,64]{1,0:T(8,128)S(1)} custom-call(s32[4]{0:T(128)S(1)} %pad_add_fusion.place, bf16[256,4096]{1,0:T(8,128)(2,1)S(1)} %get-tuple-element.14.sides, f32[1024,128]{1,0:T(8,128)S(1)} %bitcast.15, f32[1024,128]{1,0:T(8,128)S(1)} %bitcast.16), custom_call_target="tpu_custom_call" | custom-call | flops 536870912 | bytes 5242880 | tf_op jit(solution)/shard_map/meet/pallas_call | solution.py:240
  41.6 0.6 %assemble.1.early = f32[2,64,256]{2,1,0:T(8,128)S(1)} custom-call(s32[4]{0:T(128)S(1)} %pad_add_fusion.place, f32[64,64]{1,0:T(8,128)S(1)} %meet.3.refs_0_, f32[64,64]{1,0:T(8,128)S(1)} %get-tuple-element.16.refs_1_, f32[64,128]{1,0:T(8,128)S(1)} %collective-permute-done.6.refs_2_), custom_call_target="tpu_custom_call" | custom-call | bytes 65536 | tf_op jit(solution)/shard_map/assemble/pallas_call | solution.py:240
  42.2 1.6 %collective-permute-done.9.back = f32[64,128]{1,0:T(8,128)S(1)} collective-permute-done((f32[64,128]{1,0:T(8,128)S(1)}, f32[64,128]{1,0:T(8,128)S(1)}, u32[]{:S(2)}, u32[]{:S(2)}) %collective-permute-start.9) | collective-permute-done | bytes 32800 | tf_op jit(solution)/shard_map/ppermute | solution.py:311
  43.8 0.8 %complete.1 = f32[2,64,256]{2,1,0:T(8,128)S(1)} custom-call(s32[4]{0:T(128)S(1)} %pad_add_fusion.place, f32[2,64,256]{2,1,0:T(8,128)S(1)} %assemble.1.early, f32[64,64]{1,0:T(8,128)S(1)} %get-tuple-element.19.direct, f32[64,128]{1,0:T(8,128)S(1)} %collective-permute-done.9.back), custom_call_target="tpu_custom_call" | custom-call | bytes 180224 | tf_op jit(solution)/shard_map/complete/pallas_call | solution.py:240
  44.6 9.0 %all_to_all.5 = f32[8,16,256]{2,1,0:T(8,128)S(1)} all-to-all(f32[8,16,256]{2,1,0:T(8,128)S(1)} %bitcast.22), channel_id=1, replica_groups=mesh['tau'=2,'aux'=4,'orb'=2,'sub'=2] {'tau','orb','sub'}, dimensions={0} | all-to-all | bytes 262144 | tf_op jit(solution)/shard_map/all_to_all | solution.py:316
  53.6 0.6 %broadcast_multiply_fusion = f32[16,256]{1,0:T(8,128)} fusion(f32[16,256]{1,0:T(8,128)S(1)} %reduce_sum.9), kind=kLoop, calls=%fused_computation.3 | loop fusion | flops 4096 | bytes 32768 | tf_op jit(solution)/shard_map/mul | solution.py:323
  (9 shorter events, 0.0 us)
Async XLA Ops:
  0.0 29.2 %collective-permute-start.1 = (f32[128,2048]{1,0:T(8,128)}, f32[128,2048]{1,0:T(8,128)S(1)}, u32[]{:S(2)}, u32[]{:S(2)}) collective-permute-start(f32[128,2048]{1,0:T(8,128)} %bitcast.19), channel_id=1, source_target_pairs={{2,0},{0,2},{3,1},{1,3},{6,4},{4,6},{7,5},{5,7},{10,8},{8,10},{11,... | collective-permute-start | bytes 3145736 | tf_op jit(solution)/shard_map/ppermute | solution.py:251
  3.0 1.2 %copy-start = (f32[1,1,2,64,2048]{4,3,2,1,0:T(8,128)S(1)}, f32[1,1,2,64,2048]{4,3,2,1,0:T(8,128)}, u32[]{:S(2)}) copy-start(f32[1,1,2,64,2048]{4,3,2,1,0:T(8,128)} %param.4) | copy-start | bytes 3145732
  5.4 23.1 %collective-permute-start.3 = (f32[32,32,128]{2,1,0:T(8,128)S(1)}, f32[32,32,128]{2,1,0:T(8,128)S(1)}, u32[]{:S(2)}, u32[]{:S(2)}) collective-permute-start(f32[32,32,128]{2,1,0:T(8,128)S(1)} %prepare.1), channel_id=1, source_target_pairs={{1,0},{0,1},{3,2},{2,3},{5,4},{4,5},{7,6},{6,7},{9,8},{8,9},{11,10... | collective-permute-start | bytes 1572872 | tf_op jit(solution)/shard_map/ppermute | solution.py:258
  5.5 23.1 %collective-permute-start.4 = (f32[32,32,128]{2,1,0:T(8,128)S(1)}, f32[32,32,128]{2,1,0:T(8,128)S(1)}, u32[]{:S(2)}, u32[]{:S(2)}) collective-permute-start(f32[32,32,128]{2,1,0:T(8,128)S(1)} %prepare.1), channel_id=1, source_target_pairs={{0,4},{4,8},{8,12},{12,0},{1,5},{5,9},{9,13},{13,1},{2,6},{6,10},{... | collective-permute-start | bytes 1572872 | tf_op jit(solution)/shard_map/ppermute | solution.py:256
  7.1 24.3 %collective-permute-start.7 = (f32[32,32,128]{2,1,0:T(8,128)S(1)}, f32[32,32,128]{2,1,0:T(8,128)S(1)}, u32[]{:S(2)}, u32[]{:S(2)}) collective-permute-start(f32[32,32,128]{2,1,0:T(8,128)S(1)} %prepare.1), channel_id=1, source_target_pairs={{0,8},{12,4},{1,9},{13,5},{2,10},{14,6},{3,11},{15,7},{16,24},{28,... | collective-permute-start | bytes 1572872 | tf_op jit(solution)/shard_map/ppermute | solution.py:256
  13.1 4.4 %collective-permute-start = (f32[136,128]{1,0:T(8,128)S(1)}, f32[136,128]{1,0:T(8,128)S(1)}, u32[]{:S(2)}, u32[]{:S(2)}) collective-permute-start(f32[136,128]{1,0:T(8,128)S(1)} %get-tuple-element.22), channel_id=1, source_target_pairs={{16,0},{0,16},{17,1},{1,17},{18,2},{2,18},{19,3},{3,19},{20,4},{4,... | collective-permute-start | bytes 208904 | tf_op jit(solution)/shard_map/ppermute | solution.py:266
  17.5 11.1 %collective-permute-start.2 = (f32[2,136,128]{2,1,0:T(8,128)S(1)}, f32[2,136,128]{2,1,0:T(8,128)S(1)}, u32[]{:S(2)}, u32[]{:S(2)}) collective-permute-start(f32[2,136,128]{2,1,0:T(8,128)S(1)} %pad_maximum_fusion.near), channel_id=1, source_target_pairs={{2,1},{3,0},{0,3},{1,2},{6,5},{7,4},{4,7},{5,6},{10,9},{11,8},{8,1... | collective-permute-start | bytes 417800 | tf_op jit(solution)/shard_map/ppermute | solution.py:270
  17.6 1.2 %copy-start.1 = (f32[1,1,2,64,2048]{4,3,2,1,0:T(8,128)S(1)}, f32[1,1,2,64,2048]{4,3,2,1,0:T(8,128)}, u32[]{:S(2)}) copy-start(f32[1,1,2,64,2048]{4,3,2,1,0:T(8,128)} %param.4) | copy-start | bytes 3145732
  28.6 3.0 %collective-permute-start.5 = (f32[32,32,128]{2,1,0:T(8,128)S(1)}, f32[32,32,128]{2,1,0:T(8,128)S(1)}, u32[]{:S(2)}, u32[]{:S(2)}) collective-permute-start(f32[32,32,128]{2,1,0:T(8,128)S(1)} %after.2), channel_id=1, source_target_pairs={{1,0},{0,1},{3,2},{2,3},{5,4},{4,5},{7,6},{6,7},{9,8},{8,9},{11,10... | collective-permute-start | bytes 1572872 | tf_op jit(solution)/shard_map/ppermute | solution.py:299
  31.5 5.7 %collective-permute-start.8 = (f32[32,32,128]{2,1,0:T(8,128)S(1)}, f32[32,32,128]{2,1,0:T(8,128)S(1)}, u32[]{:S(2)}, u32[]{:S(2)}) collective-permute-start(f32[32,32,128]{2,1,0:T(8,128)S(1)} %after.3), channel_id=1, source_target_pairs={{1,0},{0,1},{3,2},{2,3},{5,4},{4,5},{7,6},{6,7},{9,8},{8,9},{11,10... | collective-permute-start | bytes 1572872 | tf_op jit(solution)/shard_map/ppermute | solution.py:299
  33.3 8.3 %collective-permute-start.6 = (f32[64,128]{1,0:T(8,128)S(1)}, f32[64,128]{1,0:T(8,128)S(1)}, u32[]{:S(2)}, u32[]{:S(2)}) collective-permute-start(f32[64,128]{1,0:T(8,128)S(1)} %get-tuple-element.17), channel_id=1, source_target_pairs={{4,0},{8,4},{12,8},{0,12},{5,1},{9,5},{13,9},{1,13},{6,2},{10,6},{... | collective-permute-start | bytes 98312 | tf_op jit(solution)/shard_map/ppermute | solution.py:311
  38.9 4.9 %collective-permute-start.9 = (f32[64,128]{1,0:T(8,128)S(1)}, f32[64,128]{1,0:T(8,128)S(1)}, u32[]{:S(2)}, u32[]{:S(2)}) collective-permute-start(f32[64,128]{1,0:T(8,128)S(1)} %get-tuple-element.20), channel_id=1, source_target_pairs={{8,0},{12,4},{0,8},{4,12},{9,1},{13,5},{1,9},{5,13},{10,2},{14,6},... | collective-permute-start | bytes 98312 | tf_op jit(solution)/shard_map/ppermute | solution.py:311

commit v9 on v8

--- a/solution.py
+++ b/solution.py
@@ -148,28 +148,33 @@
                     ] = array[at * pairs : (at + 1) * pairs, odd * listed : (odd + 1) * listed]
 
 
-def meet(place, sides, own, other, *refs, share, nt):
-    outs, (tensor, ordered) = refs[:-2], refs[-2:]
-    listed = own.shape[1]
-    rows_aux = own.shape[0] // share
+def meet(place, sides, *refs, share, nt):
+    refs, (tensor, ordered) = refs[:-2], refs[-2:]
+    count = (len(refs) + 1) // 4
+    pieces, directs, backs = refs[: 2 * count], refs[2 * count : 3 * count], refs[3 * count :]
+    listed = pieces[0].shape[1]
+    rows_aux = pieces[0].shape[0] // share
     block = 2 * rows_aux
-    for which, source in enumerate((own, other)):
-        start = pl.multiple_of(jnp.where(place[2] == which, 0, rows_aux), rows_aux)
-        for at in range(share):
-            high, low = halves(source[at * rows_aux : (at + 1) * rows_aux, :])
-            tensor[pl.ds(start, rows_aux), at * listed : (at + 1) * listed] = high
-            tensor[pl.ds(block + start, rows_aux), at * listed : (at + 1) * listed] = low
-    product = dot_nt(tensor[...], sides[...])
-    product = product[:block] + product[block:]
-    product = (product[:, : 2 * nt * rows_aux] + product[:, 2 * nt * rows_aux :]).T
+    for i in range(count):
+        for which, source in enumerate(pieces[2 * i : 2 * i + 2]):
+            start = pl.multiple_of(jnp.where(place[2] == which, 0, rows_aux), rows_aux)
+            for at in range(share):
+                high, low = halves(source[at * rows_aux : (at + 1) * rows_aux, :])
+                tensor[pl.ds(2 * i * block + start, rows_aux), at * listed : (at + 1) * listed] = high
+                tensor[pl.ds((2 * i + 1) * block + start, rows_aux), at * listed : (at + 1) * listed] = low
+    products = dot_nt(tensor[...], sides[...])
     pairs = rows_aux // 2
-    for group in range(2 * nt):
-        for odd in range(2):
-            at = (2 * group + odd) * pairs
-            ordered[pl.ds(group * rows_aux + odd, pairs, stride=2), :] = product[at : at + pairs]
-    outs[0][...] = ordered[: nt * rows_aux, :]
-    if len(outs) == 2:
-        back = ordered[nt * rows_aux :, :].T
+    for i in range(count):
+        product = products[2 * i * block : (2 * i + 1) * block] + products[(2 * i + 1) * block : 2 * (i + 1) * block]
+        product = (product[:, : 2 * nt * rows_aux] + product[:, 2 * nt * rows_aux :]).T
+        for group in range(2 * nt):
+            for odd in range(2):
+                at = (2 * group + odd) * pairs
+                ordered[i, pl.ds(group * rows_aux + odd, pairs, stride=2), :] = product[at : at + pairs]
+        directs[i][...] = ordered[i, : nt * rows_aux, :]
+        if i == 0:
+            continue
+        back = ordered[i, nt * rows_aux :, :].T
         parts = []
         for tau in range(nt):
             part = back[:, tau * rows_aux : (tau + 1) * rows_aux]
@@ -179,41 +184,32 @@
                     place[2] == 0, jnp.concatenate([part, zero], axis=1), jnp.concatenate([zero, part], axis=1)
                 )
             )
-        outs[1][...] = jnp.concatenate(parts, axis=1)
+        backs[i - 1][...] = jnp.concatenate(parts, axis=1)
 
 
 def assemble(place, *refs, naux, nt):
-    refs, out_ref = refs[:-1], refs[-1]
-    count = naux // 2
-    directs, backs = refs[:count], refs[count:]
+    directs, out_ref = refs[:-1], refs[-1]
     block = directs[0].shape[1]
     half = directs[0].shape[0] // nt
-    start = pl.multiple_of(place[2] * half, half)
     for tau in range(nt):
         here = [jnp.zeros((half, block), F32)] * naux
         for shift, ref in enumerate(directs):
             here[(naux - shift) % naux] = ref[tau * half : (tau + 1) * half, :]
-        there = [jnp.zeros((block, block), F32)] * naux
-        for shift, ref in enumerate(backs, 1):
-            there[shift] = ref[:, tau * block : (tau + 1) * block]
-        out_ref[tau] = jnp.concatenate(there, axis=1)
-        out_ref[tau, pl.ds(start, half), :] += jnp.concatenate(here, axis=1)
-
-
-def complete(place, early, direct, back, out_ref):
-    nt, block, wide = early.shape
-    half = direct.shape[0] // nt
-    naux = wide // block
-    last = naux // 2
-    for tau in range(nt):
-        here = direct[tau * half : (tau + 1) * half, :]
+        here = jnp.concatenate(here, axis=1)
         zero = jnp.zeros_like(here)
-        here = jnp.where(
+        out_ref[tau] = jnp.where(
             place[2] == 0, jnp.concatenate([here, zero], axis=0), jnp.concatenate([zero, here], axis=0)
         )
+
+
+def complete(place, early, *refs):
+    backs, out_ref = refs[:-1], refs[-1]
+    nt, block, wide = early.shape
+    naux = wide // block
+    for tau in range(nt):
         parts = [jnp.zeros((block, block), F32)] * naux
-        parts[last] = back[:, tau * block : (tau + 1) * block]
-        parts[(naux - last) % naux] = parts[(naux - last) % naux] + here
+        for shift, ref in enumerate(backs, 1):
+            parts[shift] = ref[:, tau * block : (tau + 1) * block]
         total = early[tau] + jnp.concatenate(parts, axis=1)
         out_ref[tau] = pltpu.roll(total, place[3] * block, 1)
 
@@ -294,24 +290,26 @@
         *fars,
         **options,
     )
-    tokens = [(token, mine_other) + tuple(fars[-1:])] + [(token_late,)] * (len(plan) - 1)
-    pieces = [after(block, *token) for block, token in zip(pieces, tokens)]
+    pieces = [after(block, token_late, mine_other) for block in pieces]
     others = [lax.ppermute(block, "sub", swap) for block in pieces]
     flat = lambda block: block.reshape(-1, listed)
-    turned = [((2 * block_aux, depth), BF16), ((rows, block_aux), F32)]
-    shape_direct = ((nt * rows_aux, block_aux), F32)
-    shape_back = ((block_aux, nt * block_aux), F32)
-    work = 16 * rows * block_aux * depth
-    options = dict(share=share, nt=nt)
-    (direct,) = call(meet, [shape_direct], turned, work, sides, flat(mine), flat(mine_other), **options)
-    directs, returned = [direct], []
-    for own, other in zip(pieces, others):
-        direct, back = call(meet, [shape_direct, shape_back], turned, work, sides, flat(own), flat(other), **options)
-        directs.append(direct)
-        returned.append(lax.ppermute(back, "aux", ring(naux, len(directs) - 1)))
+    count = 1 + len(plan)
+    work = 16 * rows * block_aux * depth * count
+    blocks = [flat(x) for pair in zip([mine] + pieces, [mine_other] + others) for x in pair]
+    results = call(
+        meet,
+        [((nt * rows_aux, block_aux), F32)] * count + [((block_aux, nt * block_aux), F32)] * (count - 1),
+        [((2 * count * block_aux, depth), BF16), ((count, rows, block_aux), F32)],
+        work,
+        sides,
+        *blocks,
+        share=share,
+        nt=nt,
+    )
+    returned = [lax.ppermute(back, "aux", ring(naux, i)) for i, back in enumerate(results[count:], 1)]
     shape = ((nt, block_aux, nauxf), F32)
-    (early,) = call(assemble, [shape], [], 0, *directs[:-1], *returned[:-1], naux=naux, nt=nt)
-    (partial_chi,) = call(complete, [shape], [], 0, early, directs[-1], returned[-1])
+    (early,) = call(assemble, [shape], [], 0, *results[:count], naux=naux, nt=nt)
+    (partial_chi,) = call(complete, [shape], [], 0, early, *returned)
     owners = nt * nob * nsub
     received = lax.all_to_all(
         partial_chi.reshape(owners, nt * block_aux // owners, nauxf),

time: 54.5 us -> 55.6 us (1.020)
  waiting for transfers between devices: 12.1 us -> 19.5 us
  starting transfers between devices: 16.6 us -> 12.4 us
  Pallas kernels: 11.7 us -> 9.63 us
    ppermute x2, waiting for transfers between devices: 0.01 us -> 3.06 us  [local(): pieces = [lax.ppermute(mine, 'aux', pairs) for pairs in plan]]
    ppermute x2, starting transfers between devices: 5.11 us -> 2.24 us  [local(): lax.ppermute(back, 'aux', ring(naux, i))]
    pallas_call x8 -> x6, Pallas kernels: 11.7 us -> 9.63 us  [call(): pl.pallas_call(functools.partial(kernel, **options), out_shape=shapes, in...]
    ppermute x2, waiting for transfers between devices: 0.01 us -> 1.91 us  [local(): others = [lax.ppermute(block, 'sub', swap) for block in pieces]]
    ppermute x2, starting transfers between devices: 6.14 us -> 4.58 us  [local(): pieces = [lax.ppermute(mine, 'aux', pairs) for pairs in plan]]
    ppermute x2, waiting for transfers between devices: 1.56 us -> 2.91 us  [local(): lax.ppermute(back, 'aux', ring(naux, i))]
    ppermute x1, waiting for transfers between devices: 7.73 us -> 8.79 us  [local(): fars.append(lax.ppermute(near, ('orb', 'sub'), pairs))]
  transfers between devices with their start and end apart: 10 -> 10, of which waited for: 3 -> 6; matrix products, arithmetic and copies ran while one was open for 3% -> 3% of each run, Pallas kernels for 20% -> 12%
where the time goes in v9:
time: 55.6 us; the launch traced here: 55.2 us
  waiting for transfers between devices  19.5 us (35%)
  starting transfers between devices  12.4 us (22%)
  Pallas kernels  9.63 us (17%)
  blocking collectives  9.05 us (16%)
  local copies, waits for them, and re-layouts  2.45 us (4%)
  other arithmetic  2.15 us (4%)
    pallas_call x6, Pallas kernels, call(): pl.pallas_call(functools.partial(kernel, **options), out_shape=shapes, in...  9.63 us
    all_to_all x1, blocking collectives, local(): lax.all_to_all(partial_chi.reshape(owners, nt * block_aux // owners, naux...  9.05 us
    ppermute x1, waiting for transfers between devices, local(): fars.append(lax.ppermute(near, ('orb', 'sub'), pairs))  8.79 us
    ppermute x2, starting transfers between devices, local(): pieces = [lax.ppermute(mine, 'aux', pairs) for pairs in plan]  4.58 us
    ppermute x2, waiting for transfers between devices, local(): pieces = [lax.ppermute(mine, 'aux', pairs) for pairs in plan]  3.06 us
    ppermute x1, starting transfers between devices, local(): lax.ppermute(tensor, 'orb', ring(nob, shift))  2.94 us
    ppermute x2, waiting for transfers between devices, local(): lax.ppermute(back, 'aux', ring(naux, i))  2.91 us
    ppermute x1, waiting for transfers between devices, local(): lax.ppermute(small, 'tau', ring(nt, shift))  2.79 us
  transfers between devices with their start and end apart: 10, of which 6 were waited for; matrix products, arithmetic and copies ran while one was open for 3% of the time, Pallas kernels for 12%

profile of v9, /device:TPU:0, one launch (start us, length us, event | category | flops | bytes accessed | tf_op | source)
XLA Modules:
  0.0 55.2 jit_solution(7661523658446898735)
XLA Ops:
  0.0 2.9 %collective-permute-start.1 = (f32[128,2048]{1,0:T(8,128)}, f32[128,2048]{1,0:T(8,128)S(1)}, u32[]{:S(2)}, u32[]{:S(2)}) collective-permute-start(f32[128,2048]{1,0:T(8,128)} %bitcast.16), channel_id=1, source_target_pairs={{2,0},{0,2},{3,1},{1,3},{6,4},{4,6},{7,5},{5,7},{10,8},{8,10},{11,... | collective-permute-start | bytes 3145736 | tf_op jit(solution)/shard_map/ppermute | solution.py:247
  2.9 0.1 pad_add_fusion.place
  3.0 1.2 %copy-done = f32[1,1,2,64,2048]{4,3,2,1,0:T(8,128)S(1)} copy-done((f32[1,1,2,64,2048]{4,3,2,1,0:T(8,128)S(1)}, f32[1,1,2,64,2048]{4,3,2,1,0:T(8,128)}, u32[]{:S(2)}) %copy-start) | copy-done | bytes 1048600
  4.2 1.2 %prepare.1 = f32[32,32,128]{2,1,0:T(8,128)S(1)} custom-call(s32[4]{0:T(128)S(1)} %pad_add_fusion.place, f32[128,2048]{1,0:T(8,128)S(1)} %bitcast.17), custom_call_target="tpu_custom_call" | custom-call | bytes 1048576 | tf_op jit(solution)/shard_map/prepare/pallas_call | solution.py:236
  5.4 0.1 collective-permute-start.3
  5.5 4.5 %collective-permute-start.6 = (f32[32,32,128]{2,1,0:T(8,128)S(1)}, f32[32,32,128]{2,1,0:T(8,128)S(1)}, u32[]{:S(2)}, u32[]{:S(2)}) collective-permute-start(f32[32,32,128]{2,1,0:T(8,128)S(1)} %prepare.1), channel_id=1, source_target_pairs={{0,8},{12,4},{1,9},{13,5},{2,10},{14,6},{3,11},{15,7},{16,24},{28,... | collective-permute-start | bytes 1572872 | tf_op jit(solution)/shard_map/ppermute | solution.py:252
  10.0 0.1 collective-permute-start.4
  10.1 0.7 %convert_element_type.5 = f32[1,2]{1,0:T(1,128)S(1)} convert(s32[1,2]{1,0:T(1,128)} %param.7) | non-fusion elementwise | flops 2 | bytes 16 | tf_op jit(solution)/shard_map/convert_element_type | solution.py:259
  10.8 0.8 %fusion = (f32[1,136,128]{2,1,0:T(8,128)S(1)}, f32[136,128]{1,0:T(8,128)S(1)}) fusion(f32[1,2]{1,0:T(1,128)S(1)} %convert_element_type.5, f32[64,128]{1,0:T(8,128)} %param.6, f32[64,128]{1,0:T(8,128)} %param.5), kind=kLoop, calls=%fused_computation.5 | loop fusion | flops 69632 | bytes 204808 | tf_op jit(solution)/shard_map/stack | solution.py:262
  11.5 1.6 %collective-permute-start = (f32[136,128]{1,0:T(8,128)S(1)}, f32[136,128]{1,0:T(8,128)S(1)}, u32[]{:S(2)}, u32[]{:S(2)}) collective-permute-start(f32[136,128]{1,0:T(8,128)S(1)} %get-tuple-element.22), channel_id=1, source_target_pairs={{16,0},{0,16},{17,1},{1,17},{18,2},{2,18},{19,3},{3,19},{20,4},{4,... | collective-permute-start | bytes 208904 | tf_op jit(solution)/shard_map/ppermute | solution.py:262
  13.1 2.8 %collective-permute-done = f32[136,128]{1,0:T(8,128)S(1)} collective-permute-done((f32[136,128]{1,0:T(8,128)S(1)}, f32[136,128]{1,0:T(8,128)S(1)}, u32[]{:S(2)}, u32[]{:S(2)}) %collective-permute-start) | collective-permute-done | bytes 69664 | tf_op jit(solution)/shard_map/ppermute | solution.py:262
  15.9 0.1 collective-permute-start.2
  16.0 0.0 copy-start.1
  16.0 1.2 %copy-done.1 = f32[1,1,2,64,2048]{4,3,2,1,0:T(8,128)S(1)} copy-done((f32[1,1,2,64,2048]{4,3,2,1,0:T(8,128)S(1)}, f32[1,1,2,64,2048]{4,3,2,1,0:T(8,128)}, u32[]{:S(2)}) %copy-start.1) | copy-done | bytes 1048600
  17.2 2.5 %first.1 = (f32[4,512,256]{2,1,0:T(8,128)S(1)}, f32[8,128]{1,0:T(8,128)}) custom-call(s32[4]{0:T(128)S(1)} %pad_add_fusion.place, f32[2,136,128]{2,1,0:T(8,128)S(1)} %pad_maximum_fusion.near, f32[128,2048]{1,0:T(8,128)S(1)} %bitcast.18), custom_call_target="tpu_custom_call" | custom-call | flops 603979776 | bytes 1187840 | tf_op jit(solution)/shard_map/first/pallas_call | solution.py:236
  19.8 8.8 %collective-permute-done.2.refs_1_ = f32[2,136,128]{2,1,0:T(8,128)S(1)} collective-permute-done((f32[2,136,128]{2,1,0:T(8,128)S(1)}, f32[2,136,128]{2,1,0:T(8,128)S(1)}, u32[]{:S(2)}, u32[]{:S(2)}) %collective-permute-start.2) | collective-permute-done | bytes 139296 | tf_op jit(solution)/shard_map/ppermute | solution.py:266
  28.6 0.0 collective-permute-done.1.refs_0_
  28.6 2.3 %second.1 = (bf16[256,4096]{1,0:T(8,128)(2,1)S(1)}, f32[8,128]{1,0:T(8,128)S(1)}) custom-call(s32[4]{0:T(128)S(1)} %pad_add_fusion.place, f32[2,136,128]{2,1,0:T(8,128)S(1)} %pad_maximum_fusion.near, f32[4,512,256]{2,1,0:T(8,128)S(1)} %get-tuple-element.13.acc, f32[128,2048]{1,0:T(8,128)S(1)} %collective-permute-done.1.refs_0_, ...), custom_call_target="tpu_custom_call" | custom-call | flops 603979776 | bytes 3424256 | tf_op jit(solution)/shard_map/second/pallas_call | solution.py:236
  30.9 0.0 collective-permute-done.3.refs_2_
  30.9 0.9 %collective-permute-start.7 = (f32[32,32,128]{2,1,0:T(8,128)S(1)}, f32[32,32,128]{2,1,0:T(8,128)S(1)}, u32[]{:S(2)}, u32[]{:S(2)}) collective-permute-start(f32[32,32,128]{2,1,0:T(8,128)S(1)} %after.3), channel_id=1, source_target_pairs={{1,0},{0,1},{3,2},{2,3},{5,4},{4,5},{7,6},{6,7},{9,8},{8,9},{11,10... | collective-permute-start | bytes 1572872 | tf_op jit(solution)/shard_map/ppermute | solution.py:294
  31.8 3.1 %collective-permute-done.4.refs_0_ = f32[32,32,128]{2,1,0:T(8,128)S(1)} collective-permute-done((f32[32,32,128]{2,1,0:T(8,128)S(1)}, f32[32,32,128]{2,1,0:T(8,128)S(1)}, u32[]{:S(2)}, u32[]{:S(2)}) %collective-permute-start.4) | collective-permute-done | bytes 524320 | tf_op jit(solution)/shard_map/ppermute | solution.py:252
  34.9 0.0 collective-permute-start.5
  34.9 1.9 %collective-permute-done.5 = f32[32,32,128]{2,1,0:T(8,128)S(1)} collective-permute-done((f32[32,32,128]{2,1,0:T(8,128)S(1)}, f32[32,32,128]{2,1,0:T(8,128)S(1)}, u32[]{:S(2)}, u32[]{:S(2)}) %collective-permute-start.5) | collective-permute-done | bytes 524320 | tf_op jit(solution)/shard_map/ppermute | solution.py:294
  36.8 2.3 %meet.1 = (f32[64,64]{1,0:T(8,128)S(1)}, f32[64,64]{1,0:T(8,128)S(1)}, f32[64,64]{1,0:T(8,128)S(1)}, f32[64,128]{1,0:T(8,128)S(1)}, f32[64,128]{1,0:T(8,128)S(1)}) custom-call(s32[4]{0:T(128)S(1)} %pad_add_fusion.place, bf16[256,4096]{1,0:T(8,128)(2,1)S(1)} %get-tuple-element.14.sides, f32[1024,128]{1,0:T(8,128)S(1)} %bitcast.22, f32[1024,128]{1,0:T(8,128)S(1)} %bitcast.15, ...), custom_call_target="tpu_custom_call" | custom-call | flops 1610612736 | bytes 7340032 | tf_op jit(solution)/shard_map/meet/pallas_call | solution.py:236
  39.1 0.9 %collective-permute-start.8 = (f32[64,128]{1,0:T(8,128)S(1)}, f32[64,128]{1,0:T(8,128)S(1)}, u32[]{:S(2)}, u32[]{:S(2)}) collective-permute-start(f32[64,128]{1,0:T(8,128)S(1)} %get-tuple-element.19), channel_id=1, source_target_pairs={{4,0},{8,4},{12,8},{0,12},{5,1},{9,5},{13,9},{1,13},{6,2},{10,6},{... | collective-permute-start | bytes 98312 | tf_op jit(solution)/shard_map/ppermute | solution.py:309
  40.1 1.3 %collective-permute-start.9 = (f32[64,128]{1,0:T(8,128)S(1)}, f32[64,128]{1,0:T(8,128)S(1)}, u32[]{:S(2)}, u32[]{:S(2)}) collective-permute-start(f32[64,128]{1,0:T(8,128)S(1)} %get-tuple-element.20), channel_id=1, source_target_pairs={{8,0},{12,4},{0,8},{4,12},{9,1},{13,5},{1,9},{5,13},{10,2},{14,6},... | collective-permute-start | bytes 98312 | tf_op jit(solution)/shard_map/ppermute | solution.py:309
  41.4 0.6 %assemble.1.early = f32[2,64,256]{2,1,0:T(8,128)S(1)} custom-call(s32[4]{0:T(128)S(1)} %pad_add_fusion.place, f32[64,64]{1,0:T(8,128)S(1)} %get-tuple-element.16.refs_0_, f32[64,64]{1,0:T(8,128)S(1)} %get-tuple-element.17.refs_1_, f32[64,64]{1,0:T(8,128)S(1)} %get-tuple-element.18.refs_2_), custom_call_target="tpu_custom_call" | custom-call | bytes 49152 | tf_op jit(solution)/shard_map/assemble/pallas_call | solution.py:236
  42.0 1.1 %collective-permute-done.8.refs_0_ = f32[64,128]{1,0:T(8,128)S(1)} collective-permute-done((f32[64,128]{1,0:T(8,128)S(1)}, f32[64,128]{1,0:T(8,128)S(1)}, u32[]{:S(2)}, u32[]{:S(2)}) %collective-permute-start.8) | collective-permute-done | bytes 32800 | tf_op jit(solution)/shard_map/ppermute | solution.py:309
  43.1 1.8 %collective-permute-done.9.refs_1_ = f32[64,128]{1,0:T(8,128)S(1)} collective-permute-done((f32[64,128]{1,0:T(8,128)S(1)}, f32[64,128]{1,0:T(8,128)S(1)}, u32[]{:S(2)}, u32[]{:S(2)}) %collective-permute-start.9) | collective-permute-done | bytes 32800 | tf_op jit(solution)/shard_map/ppermute | solution.py:309
  44.9 0.7 %complete.1 = f32[2,64,256]{2,1,0:T(8,128)S(1)} custom-call(s32[4]{0:T(128)S(1)} %pad_add_fusion.place, f32[2,64,256]{2,1,0:T(8,128)S(1)} %assemble.1.early, f32[64,128]{1,0:T(8,128)S(1)} %collective-permute-done.8.refs_0_, f32[64,128]{1,0:T(8,128)S(1)} %collective-permute-done.9.refs_1_), custom_call_target="tpu_custom_call" | custom-call | bytes 196608 | tf_op jit(solution)/shard_map/complete/pallas_call | solution.py:236
  45.6 9.0 %all_to_all.5 = f32[8,16,256]{2,1,0:T(8,128)S(1)} all-to-all(f32[8,16,256]{2,1,0:T(8,128)S(1)} %bitcast.21), channel_id=1, replica_groups=mesh['tau'=2,'aux'=4,'orb'=2,'sub'=2] {'tau','orb','sub'}, dimensions={0} | all-to-all | bytes 262144 | tf_op jit(solution)/shard_map/all_to_all | solution.py:314
  54.6 0.6 %broadcast_multiply_fusion = f32[16,256]{1,0:T(8,128)} fusion(f32[16,256]{1,0:T(8,128)S(1)} %reduce_sum.9), kind=kLoop, calls=%fused_computation.3 | loop fusion | flops 4096 | bytes 32768 | tf_op jit(solution)/shard_map/mul | solution.py:321
  (7 shorter events, 0.0 us)
Async XLA Ops:
  0.0 28.6 %collective-permute-start.1 = (f32[128,2048]{1,0:T(8,128)}, f32[128,2048]{1,0:T(8,128)S(1)}, u32[]{:S(2)}, u32[]{:S(2)}) collective-permute-start(f32[128,2048]{1,0:T(8,128)} %bitcast.16), channel_id=1, source_target_pairs={{2,0},{0,2},{3,1},{1,3},{6,4},{4,6},{7,5},{5,7},{10,8},{8,10},{11,... | collective-permute-start | bytes 3145736 | tf_op jit(solution)/shard_map/ppermute | solution.py:247
  3.0 1.2 %copy-start = (f32[1,1,2,64,2048]{4,3,2,1,0:T(8,128)S(1)}, f32[1,1,2,64,2048]{4,3,2,1,0:T(8,128)}, u32[]{:S(2)}) copy-start(f32[1,1,2,64,2048]{4,3,2,1,0:T(8,128)} %param.4) | copy-start | bytes 3145732
  5.4 25.4 %collective-permute-start.3 = (f32[32,32,128]{2,1,0:T(8,128)S(1)}, f32[32,32,128]{2,1,0:T(8,128)S(1)}, u32[]{:S(2)}, u32[]{:S(2)}) collective-permute-start(f32[32,32,128]{2,1,0:T(8,128)S(1)} %prepare.1), channel_id=1, source_target_pairs={{1,0},{0,1},{3,2},{2,3},{5,4},{4,5},{7,6},{6,7},{9,8},{8,9},{11,10... | collective-permute-start | bytes 1572872 | tf_op jit(solution)/shard_map/ppermute | solution.py:254
  5.5 25.4 %collective-permute-start.6 = (f32[32,32,128]{2,1,0:T(8,128)S(1)}, f32[32,32,128]{2,1,0:T(8,128)S(1)}, u32[]{:S(2)}, u32[]{:S(2)}) collective-permute-start(f32[32,32,128]{2,1,0:T(8,128)S(1)} %prepare.1), channel_id=1, source_target_pairs={{0,8},{12,4},{1,9},{13,5},{2,10},{14,6},{3,11},{15,7},{16,24},{28,... | collective-permute-start | bytes 1572872 | tf_op jit(solution)/shard_map/ppermute | solution.py:252
  10.0 24.8 %collective-permute-start.4 = (f32[32,32,128]{2,1,0:T(8,128)S(1)}, f32[32,32,128]{2,1,0:T(8,128)S(1)}, u32[]{:S(2)}, u32[]{:S(2)}) collective-permute-start(f32[32,32,128]{2,1,0:T(8,128)S(1)} %prepare.1), channel_id=1, source_target_pairs={{0,4},{4,8},{8,12},{12,0},{1,5},{5,9},{9,13},{13,1},{2,6},{6,10},{... | collective-permute-start | bytes 1572872 | tf_op jit(solution)/shard_map/ppermute | solution.py:252
  11.5 4.4 %collective-permute-start = (f32[136,128]{1,0:T(8,128)S(1)}, f32[136,128]{1,0:T(8,128)S(1)}, u32[]{:S(2)}, u32[]{:S(2)}) collective-permute-start(f32[136,128]{1,0:T(8,128)S(1)} %get-tuple-element.22), channel_id=1, source_target_pairs={{16,0},{0,16},{17,1},{1,17},{18,2},{2,18},{19,3},{3,19},{20,4},{4,... | collective-permute-start | bytes 208904 | tf_op jit(solution)/shard_map/ppermute | solution.py:262
  15.9 12.6 %collective-permute-start.2 = (f32[2,136,128]{2,1,0:T(8,128)S(1)}, f32[2,136,128]{2,1,0:T(8,128)S(1)}, u32[]{:S(2)}, u32[]{:S(2)}) collective-permute-start(f32[2,136,128]{2,1,0:T(8,128)S(1)} %pad_maximum_fusion.near), channel_id=1, source_target_pairs={{2,1},{3,0},{0,3},{1,2},{6,5},{7,4},{4,7},{5,6},{10,9},{11,8},{8,1... | collective-permute-start | bytes 417800 | tf_op jit(solution)/shard_map/ppermute | solution.py:266
  16.0 1.2 %copy-start.1 = (f32[1,1,2,64,2048]{4,3,2,1,0:T(8,128)S(1)}, f32[1,1,2,64,2048]{4,3,2,1,0:T(8,128)}, u32[]{:S(2)}) copy-start(f32[1,1,2,64,2048]{4,3,2,1,0:T(8,128)} %param.4) | copy-start | bytes 3145732
  30.9 4.0 %collective-permute-start.7 = (f32[32,32,128]{2,1,0:T(8,128)S(1)}, f32[32,32,128]{2,1,0:T(8,128)S(1)}, u32[]{:S(2)}, u32[]{:S(2)}) collective-permute-start(f32[32,32,128]{2,1,0:T(8,128)S(1)} %after.3), channel_id=1, source_target_pairs={{1,0},{0,1},{3,2},{2,3},{5,4},{4,5},{7,6},{6,7},{9,8},{8,9},{11,10... | collective-permute-start | bytes 1572872 | tf_op jit(solution)/shard_map/ppermute | solution.py:294
  34.9 1.9 %collective-permute-start.5 = (f32[32,32,128]{2,1,0:T(8,128)S(1)}, f32[32,32,128]{2,1,0:T(8,128)S(1)}, u32[]{:S(2)}, u32[]{:S(2)}) collective-permute-start(f32[32,32,128]{2,1,0:T(8,128)S(1)} %after.2), channel_id=1, source_target_pairs={{1,0},{0,1},{3,2},{2,3},{5,4},{4,5},{7,6},{6,7},{9,8},{8,9},{11,10... | collective-permute-start | bytes 1572872 | tf_op jit(solution)/shard_map/ppermute | solution.py:294
  39.1 4.0 %collective-permute-start.8 = (f32[64,128]{1,0:T(8,128)S(1)}, f32[64,128]{1,0:T(8,128)S(1)}, u32[]{:S(2)}, u32[]{:S(2)}) collective-permute-start(f32[64,128]{1,0:T(8,128)S(1)} %get-tuple-element.19), channel_id=1, source_target_pairs={{4,0},{8,4},{12,8},{0,12},{5,1},{9,5},{13,9},{1,13},{6,2},{10,6},{... | collective-permute-start | bytes 98312 | tf_op jit(solution)/shard_map/ppermute | solution.py:309
  40.1 4.8 %collective-permute-start.9 = (f32[64,128]{1,0:T(8,128)S(1)}, f32[64,128]{1,0:T(8,128)S(1)}, u32[]{:S(2)}, u32[]{:S(2)}) collective-permute-start(f32[64,128]{1,0:T(8,128)S(1)} %get-tuple-element.20), channel_id=1, source_target_pairs={{8,0},{12,4},{0,8},{4,12},{9,1},{13,5},{1,9},{5,13},{10,2},{14,6},... | collective-permute-start | bytes 98312 | tf_op jit(solution)/shard_map/ppermute | solution.py:309

commit v10 on v9

--- a/solution.py
+++ b/solution.py
@@ -148,70 +148,61 @@
                     ] = array[at * pairs : (at + 1) * pairs, odd * listed : (odd + 1) * listed]
 
 
-def meet(place, sides, *refs, share, nt):
-    refs, (tensor, ordered) = refs[:-2], refs[-2:]
-    count = (len(refs) + 1) // 4
-    pieces, directs, backs = refs[: 2 * count], refs[2 * count : 3 * count], refs[3 * count :]
+def meet(place, sides, *refs, share, nt, naux):
+    pieces, (out_ref, tensor, ordered) = refs[:-3], refs[-3:]
+    count = len(pieces) // 2
     listed = pieces[0].shape[1]
-    rows_aux = pieces[0].shape[0] // share
-    block = 2 * rows_aux
+    half = pieces[0].shape[0] // share
+    block = 2 * half
     for i in range(count):
         for which, source in enumerate(pieces[2 * i : 2 * i + 2]):
-            start = pl.multiple_of(jnp.where(place[2] == which, 0, rows_aux), rows_aux)
+            start = pl.multiple_of(jnp.where(place[2] == which, 0, half), half)
             for at in range(share):
-                high, low = halves(source[at * rows_aux : (at + 1) * rows_aux, :])
-                tensor[pl.ds(2 * i * block + start, rows_aux), at * listed : (at + 1) * listed] = high
-                tensor[pl.ds((2 * i + 1) * block + start, rows_aux), at * listed : (at + 1) * listed] = low
+                high, low = halves(source[at * half : (at + 1) * half, :])
+                tensor[pl.ds(2 * i * block + start, half), at * listed : (at + 1) * listed] = high
+                tensor[pl.ds((2 * i + 1) * block + start, half), at * listed : (at + 1) * listed] = low
     products = dot_nt(tensor[...], sides[...])
-    pairs = rows_aux // 2
+    pairs = half // 2
     for i in range(count):
         product = products[2 * i * block : (2 * i + 1) * block] + products[(2 * i + 1) * block : 2 * (i + 1) * block]
-        product = (product[:, : 2 * nt * rows_aux] + product[:, 2 * nt * rows_aux :]).T
+        product = (product[:, : 2 * nt * half] + product[:, 2 * nt * half :]).T
         for group in range(2 * nt):
             for odd in range(2):
                 at = (2 * group + odd) * pairs
-                ordered[i, pl.ds(group * rows_aux + odd, pairs, stride=2), :] = product[at : at + pairs]
-        directs[i][...] = ordered[i, : nt * rows_aux, :]
-        if i == 0:
-            continue
-        back = ordered[i, nt * rows_aux :, :].T
-        parts = []
-        for tau in range(nt):
-            part = back[:, tau * rows_aux : (tau + 1) * rows_aux]
-            zero = jnp.zeros_like(part)
-            parts.append(
-                jnp.where(
-                    place[2] == 0, jnp.concatenate([part, zero], axis=1), jnp.concatenate([zero, part], axis=1)
-                )
-            )
-        backs[i - 1][...] = jnp.concatenate(parts, axis=1)
-
-
-def assemble(place, *refs, naux, nt):
-    directs, out_ref = refs[:-1], refs[-1]
-    block = directs[0].shape[1]
-    half = directs[0].shape[0] // nt
+                ordered[i, pl.ds(group * half + odd, pairs, stride=2), :] = product[at : at + pairs]
+
+    def at_sub(x, axis):
+        zero = jnp.zeros_like(x)
+        return jnp.where(
+            place[2] == 0, jnp.concatenate([x, zero], axis=axis), jnp.concatenate([zero, x], axis=axis)
+        )
+
+    wide = naux * block
     for tau in range(nt):
         here = [jnp.zeros((half, block), F32)] * naux
-        for shift, ref in enumerate(directs):
-            here[(naux - shift) % naux] = ref[tau * half : (tau + 1) * half, :]
-        here = jnp.concatenate(here, axis=1)
-        zero = jnp.zeros_like(here)
-        out_ref[tau] = jnp.where(
-            place[2] == 0, jnp.concatenate([here, zero], axis=0), jnp.concatenate([zero, here], axis=0)
-        )
-
-
-def complete(place, early, *refs):
-    backs, out_ref = refs[:-1], refs[-1]
-    nt, block, wide = early.shape
-    naux = wide // block
-    for tau in range(nt):
-        parts = [jnp.zeros((block, block), F32)] * naux
-        for shift, ref in enumerate(backs, 1):
-            parts[shift] = ref[:, tau * block : (tau + 1) * block]
-        total = early[tau] + jnp.concatenate(parts, axis=1)
-        out_ref[tau] = pltpu.roll(total, place[3] * block, 1)
+        for shift in range(count):
+            here[(naux - shift) % naux] = ordered[shift, tau * half : (tau + 1) * half, :]
+        here = pltpu.roll(jnp.concatenate(here, axis=1), place[3] * block, 1)
+        out_ref[tau, :, :wide] = at_sub(here, 0)
+        rest = [
+            at_sub(ordered[shift, (nt + tau) * half : (nt + tau + 1) * half, :].T, 1) for shift in range(1, count)
+        ]
+        padding = out_ref.shape[2] - wide - block * len(rest)
+        if padding:
+            rest.append(jnp.zeros((block, padding), F32))
+        out_ref[tau, :, wide:] = jnp.concatenate(rest, axis=1)
+
+
+def add(place, received, *outs, block):
+    total = received[0]
+    for i in range(1, received.shape[0]):
+        total = total + received[i]
+    rows, wide = outs[0].shape
+    outs[0][...] = total[:, :wide]
+    for shift, out in enumerate(outs[1:]):
+        back = total[:, wide + shift * block : wide + (shift + 1) * block]
+        back = jnp.concatenate([back, jnp.zeros((rows, wide - block), F32)], axis=1)
+        out[...] = pltpu.roll(back, place[3] * block, 1)
 
 
 def local(three_center, occupied_green, virtual_green, block_list, sizes):
@@ -290,35 +281,40 @@
         *fars,
         **options,
     )
-    pieces = [after(block, token_late, mine_other) for block in pieces]
+    held = []
+    for block in pieces:
+        held.append(after(block, token_late, mine_other, *held[-1:]))
+    pieces = held
     others = [lax.ppermute(block, "sub", swap) for block in pieces]
     flat = lambda block: block.reshape(-1, listed)
     count = 1 + len(plan)
     work = 16 * rows * block_aux * depth * count
     blocks = [flat(x) for pair in zip([mine] + pieces, [mine_other] + others) for x in pair]
-    results = call(
+    wide = nauxf + -(-len(plan) * block_aux // 128) * 128
+    (partial_chi,) = call(
         meet,
-        [((nt * rows_aux, block_aux), F32)] * count + [((block_aux, nt * block_aux), F32)] * (count - 1),
+        [((nt, block_aux, wide), F32)],
         [((2 * count * block_aux, depth), BF16), ((count, rows, block_aux), F32)],
         work,
         sides,
         *blocks,
         share=share,
         nt=nt,
-    )
-    returned = [lax.ppermute(back, "aux", ring(naux, i)) for i, back in enumerate(results[count:], 1)]
-    shape = ((nt, block_aux, nauxf), F32)
-    (early,) = call(assemble, [shape], [], 0, *results[:count], naux=naux, nt=nt)
-    (partial_chi,) = call(complete, [shape], [], 0, early, *returned)
+        naux=naux,
+    )
     owners = nt * nob * nsub
+    own_rows = nt * block_aux // owners
     received = lax.all_to_all(
-        partial_chi.reshape(owners, nt * block_aux // owners, nauxf),
+        partial_chi.reshape(owners, own_rows, wide),
         ("tau", "orb", "sub"),
         split_axis=0,
         concat_axis=0,
         tiled=True,
     )
-    return received.sum(axis=0) * (-2.0 / math.sqrt(norb * slots * width))
+    chi, *backs = call(add, [((own_rows, nauxf), F32)] * count, [], 0, received, block=block_aux)
+    for shift, back in enumerate(backs, 1):
+        chi = chi + lax.ppermute(back, "aux", ring(naux, shift))
+    return chi * (-2.0 / math.sqrt(norb * slots * width))
 
 
 def solution(mesh):

time: 55.6 us -> 56.1 us (level)
  starting transfers between devices: 12.4 us -> 15.1 us
  waiting for transfers between devices: 19.5 us -> 16.9 us
  blocking collectives: 9.05 us -> 10 us
    ppermute x2, waiting for transfers between devices: 3.06 us -> 0.01 us  [local(): pieces = [lax.ppermute(mine, 'aux', pairs) for pairs in plan]]
    ppermute x2, waiting for transfers between devices: 2.91 us -> 4.63 us  [local(): chi = chi + lax.ppermute(back, 'aux', ring(naux, shift))]
    ppermute x2, starting transfers between devices: 4.58 us -> 6.14 us  [local(): pieces = [lax.ppermute(mine, 'aux', pairs) for pairs in plan]]
    ppermute x1, waiting for transfers between devices: 8.79 us -> 7.23 us  [local(): fars.append(lax.ppermute(near, ('orb', 'sub'), pairs))]
    ppermute x2, starting transfers between devices: 2.24 us -> 3.6 us  [local(): chi = chi + lax.ppermute(back, 'aux', ring(naux, shift))]
    all_to_all x1, blocking collectives: 9.05 us -> 10 us  [local(): lax.all_to_all(partial_chi.reshape(owners, own_rows, wide), ('tau', 'orb'...]
    pallas_call x6 -> x5, Pallas kernels: 9.63 us -> 9.12 us  [call(): pl.pallas_call(functools.partial(kernel, **options), out_shape=shapes, in...]
  transfers between devices with their start and end apart: 10 -> 10, of which waited for: 6 -> 6; matrix products, arithmetic and copies ran while one was open for 3% -> 3% of each run, Pallas kernels for 12% -> 11%
where the time goes in v10:
time: 56.1 us; the launch traced here: 55.8 us
  waiting for transfers between devices  16.9 us (30%)
  starting transfers between devices  15.1 us (27%)
  blocking collectives  10 us (18%)
  Pallas kernels  9.13 us (16%)
  local copies, waits for them, and re-layouts  2.45 us (4%)
  other arithmetic  2.14 us (4%)
    all_to_all x1, blocking collectives, local(): lax.all_to_all(partial_chi.reshape(owners, own_rows, wide), ('tau', 'orb'...  10 us
    pallas_call x5, Pallas kernels, call(): pl.pallas_call(functools.partial(kernel, **options), out_shape=shapes, in...  9.12 us
    ppermute x1, waiting for transfers between devices, local(): fars.append(lax.ppermute(near, ('orb', 'sub'), pairs))  7.23 us
    ppermute x2, starting transfers between devices, local(): pieces = [lax.ppermute(mine, 'aux', pairs) for pairs in plan]  6.14 us
    ppermute x2, waiting for transfers between devices, local(): chi = chi + lax.ppermute(back, 'aux', ring(naux, shift))  4.63 us
    ppermute x2, starting transfers between devices, local(): chi = chi + lax.ppermute(back, 'aux', ring(naux, shift))  3.6 us
    ppermute x1, starting transfers between devices, local(): lax.ppermute(tensor, 'orb', ring(nob, shift))  2.94 us
    ppermute x1, waiting for transfers between devices, local(): lax.ppermute(small, 'tau', ring(nt, shift))  2.79 us
  transfers between devices with their start and end apart: 10, of which 6 were waited for; matrix products, arithmetic and copies ran while one was open for 3% of the time, Pallas kernels for 11%

profile of v10, /device:TPU:0, one launch (start us, length us, event | category | flops | bytes accessed | tf_op | source)
XLA Modules:
  0.0 55.8 jit_solution(8397106381186795278)
XLA Ops:
  0.0 2.9 %collective-permute-start.1 = (f32[128,2048]{1,0:T(8,128)}, f32[128,2048]{1,0:T(8,128)S(1)}, u32[]{:S(2)}, u32[]{:S(2)}) collective-permute-start(f32[128,2048]{1,0:T(8,128)} %bitcast.17), channel_id=1, source_target_pairs={{2,0},{0,2},{3,1},{1,3},{6,4},{4,6},{7,5},{5,7},{10,8},{8,10},{11,... | collective-permute-start | bytes 3145736 | tf_op jit(solution)/shard_map/ppermute | solution.py:238
  2.9 0.1 pad_add_fusion.place
  3.0 1.2 %copy-done = f32[1,1,2,64,2048]{4,3,2,1,0:T(8,128)S(1)} copy-done((f32[1,1,2,64,2048]{4,3,2,1,0:T(8,128)S(1)}, f32[1,1,2,64,2048]{4,3,2,1,0:T(8,128)}, u32[]{:S(2)}) %copy-start) | copy-done | bytes 1048600
  4.2 1.2 %prepare.1 = f32[32,32,128]{2,1,0:T(8,128)S(1)} custom-call(s32[4]{0:T(128)S(1)} %pad_add_fusion.place, f32[128,2048]{1,0:T(8,128)S(1)} %bitcast.18), custom_call_target="tpu_custom_call" | custom-call | bytes 1048576 | tf_op jit(solution)/shard_map/prepare/pallas_call | solution.py:227
  5.4 0.1 collective-permute-start.3
  5.5 1.6 %collective-permute-start.4 = (f32[32,32,128]{2,1,0:T(8,128)S(1)}, f32[32,32,128]{2,1,0:T(8,128)S(1)}, u32[]{:S(2)}, u32[]{:S(2)}) collective-permute-start(f32[32,32,128]{2,1,0:T(8,128)S(1)} %prepare.1), channel_id=1, source_target_pairs={{0,4},{4,8},{8,12},{12,0},{1,5},{5,9},{9,13},{13,1},{2,6},{6,10},{... | collective-permute-start | bytes 1572872 | tf_op jit(solution)/shard_map/ppermute | solution.py:243
  7.1 4.5 %collective-permute-start.6 = (f32[32,32,128]{2,1,0:T(8,128)S(1)}, f32[32,32,128]{2,1,0:T(8,128)S(1)}, u32[]{:S(2)}, u32[]{:S(2)}) collective-permute-start(f32[32,32,128]{2,1,0:T(8,128)S(1)} %prepare.1), channel_id=1, source_target_pairs={{0,8},{12,4},{1,9},{13,5},{2,10},{14,6},{3,11},{15,7},{16,24},{28,... | collective-permute-start | bytes 1572872 | tf_op jit(solution)/shard_map/ppermute | solution.py:243
  11.7 0.7 %convert_element_type.5 = f32[1,2]{1,0:T(1,128)S(1)} convert(s32[1,2]{1,0:T(1,128)} %param.7) | non-fusion elementwise | flops 2 | bytes 16 | tf_op jit(solution)/shard_map/convert_element_type | solution.py:250
  12.3 0.8 %fusion = (f32[1,136,128]{2,1,0:T(8,128)S(1)}, f32[136,128]{1,0:T(8,128)S(1)}) fusion(f32[1,2]{1,0:T(1,128)S(1)} %convert_element_type.5, f32[64,128]{1,0:T(8,128)} %param.6, f32[64,128]{1,0:T(8,128)} %param.5), kind=kLoop, calls=%fused_computation.5 | loop fusion | flops 69632 | bytes 204808 | tf_op jit(solution)/shard_map/stack | solution.py:253
  13.1 1.6 %collective-permute-start = (f32[136,128]{1,0:T(8,128)S(1)}, f32[136,128]{1,0:T(8,128)S(1)}, u32[]{:S(2)}, u32[]{:S(2)}) collective-permute-start(f32[136,128]{1,0:T(8,128)S(1)} %get-tuple-element.18), channel_id=1, source_target_pairs={{16,0},{0,16},{17,1},{1,17},{18,2},{2,18},{19,3},{3,19},{20,4},{4,... | collective-permute-start | bytes 208904 | tf_op jit(solution)/shard_map/ppermute | solution.py:253
  14.7 2.8 %collective-permute-done = f32[136,128]{1,0:T(8,128)S(1)} collective-permute-done((f32[136,128]{1,0:T(8,128)S(1)}, f32[136,128]{1,0:T(8,128)S(1)}, u32[]{:S(2)}, u32[]{:S(2)}) %collective-permute-start) | collective-permute-done | bytes 69664 | tf_op jit(solution)/shard_map/ppermute | solution.py:253
  17.5 0.1 collective-permute-start.2
  17.6 0.0 copy-start.1
  17.6 1.2 %copy-done.1 = f32[1,1,2,64,2048]{4,3,2,1,0:T(8,128)S(1)} copy-done((f32[1,1,2,64,2048]{4,3,2,1,0:T(8,128)S(1)}, f32[1,1,2,64,2048]{4,3,2,1,0:T(8,128)}, u32[]{:S(2)}) %copy-start.1) | copy-done | bytes 1048600
  18.8 2.5 %first.1 = (f32[4,512,256]{2,1,0:T(8,128)S(1)}, f32[8,128]{1,0:T(8,128)}) custom-call(s32[4]{0:T(128)S(1)} %pad_add_fusion.place, f32[2,136,128]{2,1,0:T(8,128)S(1)} %pad_maximum_fusion.near, f32[128,2048]{1,0:T(8,128)S(1)} %bitcast.19), custom_call_target="tpu_custom_call" | custom-call | flops 603979776 | bytes 1187840 | tf_op jit(solution)/shard_map/first/pallas_call | solution.py:227
  21.3 7.2 %collective-permute-done.2.refs_1_ = f32[2,136,128]{2,1,0:T(8,128)S(1)} collective-permute-done((f32[2,136,128]{2,1,0:T(8,128)S(1)}, f32[2,136,128]{2,1,0:T(8,128)S(1)}, u32[]{:S(2)}, u32[]{:S(2)}) %collective-permute-start.2) | collective-permute-done | bytes 139296 | tf_op jit(solution)/shard_map/ppermute | solution.py:257
  28.6 0.0 collective-permute-done.1.refs_0_
  28.6 2.3 %second.1 = (bf16[256,4096]{1,0:T(8,128)(2,1)S(1)}, f32[8,128]{1,0:T(8,128)S(1)}) custom-call(s32[4]{0:T(128)S(1)} %pad_add_fusion.place, f32[2,136,128]{2,1,0:T(8,128)S(1)} %pad_maximum_fusion.near, f32[4,512,256]{2,1,0:T(8,128)S(1)} %get-tuple-element.11.acc, f32[128,2048]{1,0:T(8,128)S(1)} %collective-permute-done.1.refs_0_, ...), custom_call_target="tpu_custom_call" | custom-call | flops 603979776 | bytes 3424256 | tf_op jit(solution)/shard_map/second/pallas_call | solution.py:227
  30.9 0.0 collective-permute-done.3.refs_2_
  30.9 0.0 collective-permute-done.6.refs_0_
  30.9 0.6 %collective-permute-start.7 = (f32[32,32,128]{2,1,0:T(8,128)S(1)}, f32[32,32,128]{2,1,0:T(8,128)S(1)}, u32[]{:S(2)}, u32[]{:S(2)}) collective-permute-start(f32[32,32,128]{2,1,0:T(8,128)S(1)} %after.3), channel_id=1, source_target_pairs={{1,0},{0,1},{3,2},{2,3},{5,4},{4,5},{7,6},{6,7},{9,8},{8,9},{11,10... | collective-permute-start | bytes 1572872 | tf_op jit(solution)/shard_map/ppermute | solution.py:288
  31.5 0.1 collective-permute-start.5
  31.6 1.5 %collective-permute-done.7 = f32[32,32,128]{2,1,0:T(8,128)S(1)} collective-permute-done((f32[32,32,128]{2,1,0:T(8,128)S(1)}, f32[32,32,128]{2,1,0:T(8,128)S(1)}, u32[]{:S(2)}, u32[]{:S(2)}) %collective-permute-start.7) | collective-permute-done | bytes 524320 | tf_op jit(solution)/shard_map/ppermute | solution.py:288
  33.1 0.7 %collective-permute-done.5 = f32[32,32,128]{2,1,0:T(8,128)S(1)} collective-permute-done((f32[32,32,128]{2,1,0:T(8,128)S(1)}, f32[32,32,128]{2,1,0:T(8,128)S(1)}, u32[]{:S(2)}, u32[]{:S(2)}) %collective-permute-start.5) | collective-permute-done | bytes 524320 | tf_op jit(solution)/shard_map/ppermute | solution.py:288
  33.8 2.5 %meet.1 = f32[2,64,384]{2,1,0:T(8,128)S(1)} custom-call(s32[4]{0:T(128)S(1)} %pad_add_fusion.place, bf16[256,4096]{1,0:T(8,128)(2,1)S(1)} %get-tuple-element.12.sides, f32[1024,128]{1,0:T(8,128)S(1)} %bitcast.20, f32[1024,128]{1,0:T(8,128)S(1)} %bitcast.15, f32[1024,128]{1,0:T(8,128)S(1)} %bitcast.16, f32[1024,128]{1,0:T(8,128)S(1)} %bitcast.24, ...), custom_call_target="tpu_custom_call" | custom-call | flops 1610612736 | bytes 7340032 | tf_op jit(solution)/shard_map/meet/pallas_call | solution.py:227
  36.3 10.0 %all_to_all.5.received = f32[8,16,384]{2,1,0:T(8,128)S(1)} all-to-all(f32[8,16,384]{2,1,0:T(8,128)S(1)} %bitcast.22), channel_id=1, replica_groups=mesh['tau'=2,'aux'=4,'orb'=2,'sub'=2] {'tau','orb','sub'}, dimensions={0} | all-to-all | bytes 393216 | tf_op jit(solution)/shard_map/all_to_all | solution.py:307
  46.3 0.7 %add.19 = (f32[16,256]{1,0:T(8,128)S(1)}, f32[16,256]{1,0:T(8,128)S(1)}, f32[16,256]{1,0:T(8,128)S(1)}) custom-call(s32[4]{0:T(128)S(1)} %pad_add_fusion.place, f32[8,16,384]{2,1,0:T(8,128)S(1)} %all_to_all.5.received), custom_call_target="tpu_custom_call" | custom-call | bytes 196608 | tf_op jit(solution)/shard_map/add/pallas_call | solution.py:227
  47.0 3.6 %collective-permute-start.8 = (f32[16,256]{1,0:T(8,128)S(1)}, f32[16,256]{1,0:T(8,128)S(1)}, u32[]{:S(2)}, u32[]{:S(2)}) collective-permute-start(f32[16,256]{1,0:T(8,128)S(1)} %get-tuple-element.15), channel_id=1, source_target_pairs={{4,0},{8,4},{12,8},{0,12},{5,1},{9,5},{13,9},{1,13},{6,2},{10,6},{... | collective-permute-start | bytes 49160 | tf_op jit(solution)/shard_map/ppermute | solution.py:316
  50.6 0.0 collective-permute-start.9
  50.6 1.4 %collective-permute-done.8 = f32[16,256]{1,0:T(8,128)S(1)} collective-permute-done((f32[16,256]{1,0:T(8,128)S(1)}, f32[16,256]{1,0:T(8,128)S(1)}, u32[]{:S(2)}, u32[]{:S(2)}) %collective-permute-start.8) | collective-permute-done | bytes 16416 | tf_op jit(solution)/shard_map/ppermute | solution.py:316
  52.0 3.2 %collective-permute-done.9 = f32[16,256]{1,0:T(8,128)S(1)} collective-permute-done((f32[16,256]{1,0:T(8,128)S(1)}, f32[16,256]{1,0:T(8,128)S(1)}, u32[]{:S(2)}, u32[]{:S(2)}) %collective-permute-start.9) | collective-permute-done | bytes 16416 | tf_op jit(solution)/shard_map/ppermute | solution.py:316
  55.2 0.6 %add_multiply_fusion = f32[16,256]{1,0:T(8,128)} fusion(f32[16,256]{1,0:T(8,128)S(1)} %collective-permute-done.9, f32[16,256]{1,0:T(8,128)S(1)} %get-tuple-element.14, f32[16,256]{1,0:T(8,128)S(1)} %collective-permute-done.8), kind=kLoop, calls=%fused_computation.3 | loop fusion | flops 12288 | bytes 65536 | tf_op jit(solution)/shard_map/mul | solution.py:317
  (5 shorter events, 0.0 us)
Async XLA Ops:
  0.0 28.6 %collective-permute-start.1 = (f32[128,2048]{1,0:T(8,128)}, f32[128,2048]{1,0:T(8,128)S(1)}, u32[]{:S(2)}, u32[]{:S(2)}) collective-permute-start(f32[128,2048]{1,0:T(8,128)} %bitcast.17), channel_id=1, source_target_pairs={{2,0},{0,2},{3,1},{1,3},{6,4},{4,6},{7,5},{5,7},{10,8},{8,10},{11,... | collective-permute-start | bytes 3145736 | tf_op jit(solution)/shard_map/ppermute | solution.py:238
  3.0 1.2 %copy-start = (f32[1,1,2,64,2048]{4,3,2,1,0:T(8,128)S(1)}, f32[1,1,2,64,2048]{4,3,2,1,0:T(8,128)}, u32[]{:S(2)}) copy-start(f32[1,1,2,64,2048]{4,3,2,1,0:T(8,128)} %param.4) | copy-start | bytes 3145732
  5.4 25.4 %collective-permute-start.3 = (f32[32,32,128]{2,1,0:T(8,128)S(1)}, f32[32,32,128]{2,1,0:T(8,128)S(1)}, u32[]{:S(2)}, u32[]{:S(2)}) collective-permute-start(f32[32,32,128]{2,1,0:T(8,128)S(1)} %prepare.1), channel_id=1, source_target_pairs={{1,0},{0,1},{3,2},{2,3},{5,4},{4,5},{7,6},{6,7},{9,8},{8,9},{11,10... | collective-permute-start | bytes 1572872 | tf_op jit(solution)/shard_map/ppermute | solution.py:245
  5.5 25.4 %collective-permute-start.4 = (f32[32,32,128]{2,1,0:T(8,128)S(1)}, f32[32,32,128]{2,1,0:T(8,128)S(1)}, u32[]{:S(2)}, u32[]{:S(2)}) collective-permute-start(f32[32,32,128]{2,1,0:T(8,128)S(1)} %prepare.1), channel_id=1, source_target_pairs={{0,4},{4,8},{8,12},{12,0},{1,5},{5,9},{9,13},{13,1},{2,6},{6,10},{... | collective-permute-start | bytes 1572872 | tf_op jit(solution)/shard_map/ppermute | solution.py:243
  7.1 23.8 %collective-permute-start.6 = (f32[32,32,128]{2,1,0:T(8,128)S(1)}, f32[32,32,128]{2,1,0:T(8,128)S(1)}, u32[]{:S(2)}, u32[]{:S(2)}) collective-permute-start(f32[32,32,128]{2,1,0:T(8,128)S(1)} %prepare.1), channel_id=1, source_target_pairs={{0,8},{12,4},{1,9},{13,5},{2,10},{14,6},{3,11},{15,7},{16,24},{28,... | collective-permute-start | bytes 1572872 | tf_op jit(solution)/shard_map/ppermute | solution.py:243
  13.1 4.4 %collective-permute-start = (f32[136,128]{1,0:T(8,128)S(1)}, f32[136,128]{1,0:T(8,128)S(1)}, u32[]{:S(2)}, u32[]{:S(2)}) collective-permute-start(f32[136,128]{1,0:T(8,128)S(1)} %get-tuple-element.18), channel_id=1, source_target_pairs={{16,0},{0,16},{17,1},{1,17},{18,2},{2,18},{19,3},{3,19},{20,4},{4,... | collective-permute-start | bytes 208904 | tf_op jit(solution)/shard_map/ppermute | solution.py:253
  17.5 11.1 %collective-permute-start.2 = (f32[2,136,128]{2,1,0:T(8,128)S(1)}, f32[2,136,128]{2,1,0:T(8,128)S(1)}, u32[]{:S(2)}, u32[]{:S(2)}) collective-permute-start(f32[2,136,128]{2,1,0:T(8,128)S(1)} %pad_maximum_fusion.near), channel_id=1, source_target_pairs={{2,1},{3,0},{0,3},{1,2},{6,5},{7,4},{4,7},{5,6},{10,9},{11,8},{8,1... | collective-permute-start | bytes 417800 | tf_op jit(solution)/shard_map/ppermute | solution.py:257
  17.6 1.2 %copy-start.1 = (f32[1,1,2,64,2048]{4,3,2,1,0:T(8,128)S(1)}, f32[1,1,2,64,2048]{4,3,2,1,0:T(8,128)}, u32[]{:S(2)}) copy-start(f32[1,1,2,64,2048]{4,3,2,1,0:T(8,128)} %param.4) | copy-start | bytes 3145732
  30.9 2.2 %collective-permute-start.7 = (f32[32,32,128]{2,1,0:T(8,128)S(1)}, f32[32,32,128]{2,1,0:T(8,128)S(1)}, u32[]{:S(2)}, u32[]{:S(2)}) collective-permute-start(f32[32,32,128]{2,1,0:T(8,128)S(1)} %after.3), channel_id=1, source_target_pairs={{1,0},{0,1},{3,2},{2,3},{5,4},{4,5},{7,6},{6,7},{9,8},{8,9},{11,10... | collective-permute-start | bytes 1572872 | tf_op jit(solution)/shard_map/ppermute | solution.py:288
  31.5 2.3 %collective-permute-start.5 = (f32[32,32,128]{2,1,0:T(8,128)S(1)}, f32[32,32,128]{2,1,0:T(8,128)S(1)}, u32[]{:S(2)}, u32[]{:S(2)}) collective-permute-start(f32[32,32,128]{2,1,0:T(8,128)S(1)} %after.2.refs_3_), channel_id=1, source_target_pairs={{1,0},{0,1},{3,2},{2,3},{5,4},{4,5},{7,6},{6,7},{9,8},{8,9},{11,10... | collective-permute-start | bytes 1572872 | tf_op jit(solution)/shard_map/ppermute | solution.py:288
  47.0 5.0 %collective-permute-start.8 = (f32[16,256]{1,0:T(8,128)S(1)}, f32[16,256]{1,0:T(8,128)S(1)}, u32[]{:S(2)}, u32[]{:S(2)}) collective-permute-start(f32[16,256]{1,0:T(8,128)S(1)} %get-tuple-element.15), channel_id=1, source_target_pairs={{4,0},{8,4},{12,8},{0,12},{5,1},{9,5},{13,9},{1,13},{6,2},{10,6},{... | collective-permute-start | bytes 49160 | tf_op jit(solution)/shard_map/ppermute | solution.py:316
  50.6 4.6 %collective-permute-start.9 = (f32[16,256]{1,0:T(8,128)S(1)}, f32[16,256]{1,0:T(8,128)S(1)}, u32[]{:S(2)}, u32[]{:S(2)}) collective-permute-start(f32[16,256]{1,0:T(8,128)S(1)} %get-tuple-element.16), channel_id=1, source_target_pairs={{8,0},{12,4},{0,8},{4,12},{9,1},{13,5},{1,9},{5,13},{10,2},{14,6},... | collective-permute-start | bytes 49160 | tf_op jit(solution)/shard_map/ppermute | solution.py:316

commit v11 on v10

--- a/solution.py
+++ b/solution.py
@@ -126,7 +126,7 @@
 
 
 def second(place, near, acc, *refs, slots, width, share):
-    refs, (sides, token, rows) = refs[:-3], refs[-3:]
+    refs, (side_direct, side_back, token, rows) = refs[:-4], refs[-4:]
     tensors, fars = refs[: len(refs) // 2], refs[len(refs) // 2 :]
     token[...] = jnp.zeros_like(token)
     listed = slots * width
@@ -137,20 +137,37 @@
         term = mix(place, near, far, tensor, rows, slots, width, share)
         total = [x + y for x, y in zip(total, term)]
     for group in range(groups):
+        side = (side_direct, side_back)[group * 2 // groups]
+        height = groups * pairs
         high, low = halves(total[group])
         for odd in range(2):
-            row = (2 * group + odd) * pairs
+            row = (2 * (group % (groups // 2)) + odd) * pairs
             for at in range(share):
                 for part, array in enumerate((high, low)):
-                    sides[
-                        part * 2 * groups * pairs + row : part * 2 * groups * pairs + row + pairs,
-                        at * listed : (at + 1) * listed,
-                    ] = array[at * pairs : (at + 1) * pairs, odd * listed : (odd + 1) * listed]
-
-
-def meet(place, sides, *refs, share, nt, naux):
-    pieces, (out_ref, tensor, ordered) = refs[:-3], refs[-3:]
-    count = len(pieces) // 2
+                    side[part * height + row : part * height + row + pairs, at * listed : (at + 1) * listed] = array[
+                        at * pairs : (at + 1) * pairs, odd * listed : (odd + 1) * listed
+                    ]
+
+
+def unfold(products, i, ordered):
+    rows, block = ordered.shape[-2:]
+    product = products[2 * i * block : (2 * i + 1) * block] + products[(2 * i + 1) * block : 2 * (i + 1) * block]
+    product = (product[:, :rows] + product[:, rows:]).T
+    pairs = block // 4
+    for group in range(rows // (2 * pairs)):
+        for odd in range(2):
+            at = (2 * group + odd) * pairs
+            ordered[i, pl.ds(2 * group * pairs + odd, pairs, stride=2), :] = product[at : at + pairs]
+
+
+def at_sub(place, x, axis):
+    zero = jnp.zeros_like(x)
+    return jnp.where(place[2] == 0, jnp.concatenate([x, zero], axis=axis), jnp.concatenate([zero, x], axis=axis))
+
+
+def meet_back(place, side, *refs, share, nt):
+    count = (len(refs) - 1) // 3
+    pieces, (tensor, *backs, ordered) = refs[: 2 * count], refs[2 * count :]
     listed = pieces[0].shape[1]
     half = pieces[0].shape[0] // share
     block = 2 * half
@@ -161,48 +178,40 @@
                 high, low = halves(source[at * half : (at + 1) * half, :])
                 tensor[pl.ds(2 * i * block + start, half), at * listed : (at + 1) * listed] = high
                 tensor[pl.ds((2 * i + 1) * block + start, half), at * listed : (at + 1) * listed] = low
-    products = dot_nt(tensor[...], sides[...])
-    pairs = half // 2
+    products = dot_nt(tensor[2 * block :, :], side[...])
+    for i, back_ref in enumerate(backs):
+        unfold(products, i, ordered)
+        back = ordered[i].T
+        back_ref[...] = jnp.concatenate([back[:half], back[half:]], axis=1)
+
+
+def meet_direct(place, side, tensor, out_ref, ordered, *, nt, naux):
+    count = ordered.shape[0]
+    block = ordered.shape[2]
+    half = block // 2
+    products = dot_nt(tensor[...], side[...])
     for i in range(count):
-        product = products[2 * i * block : (2 * i + 1) * block] + products[(2 * i + 1) * block : 2 * (i + 1) * block]
-        product = (product[:, : 2 * nt * half] + product[:, 2 * nt * half :]).T
-        for group in range(2 * nt):
-            for odd in range(2):
-                at = (2 * group + odd) * pairs
-                ordered[i, pl.ds(group * half + odd, pairs, stride=2), :] = product[at : at + pairs]
-
-    def at_sub(x, axis):
-        zero = jnp.zeros_like(x)
-        return jnp.where(
-            place[2] == 0, jnp.concatenate([x, zero], axis=axis), jnp.concatenate([zero, x], axis=axis)
-        )
-
-    wide = naux * block
+        unfold(products, i, ordered)
     for tau in range(nt):
         here = [jnp.zeros((half, block), F32)] * naux
         for shift in range(count):
             here[(naux - shift) % naux] = ordered[shift, tau * half : (tau + 1) * half, :]
-        here = pltpu.roll(jnp.concatenate(here, axis=1), place[3] * block, 1)
-        out_ref[tau, :, :wide] = at_sub(here, 0)
-        rest = [
-            at_sub(ordered[shift, (nt + tau) * half : (nt + tau + 1) * half, :].T, 1) for shift in range(1, count)
-        ]
-        padding = out_ref.shape[2] - wide - block * len(rest)
-        if padding:
-            rest.append(jnp.zeros((block, padding), F32))
-        out_ref[tau, :, wide:] = jnp.concatenate(rest, axis=1)
-
-
-def add(place, received, *outs, block):
-    total = received[0]
-    for i in range(1, received.shape[0]):
-        total = total + received[i]
-    rows, wide = outs[0].shape
-    outs[0][...] = total[:, :wide]
-    for shift, out in enumerate(outs[1:]):
-        back = total[:, wide + shift * block : wide + (shift + 1) * block]
-        back = jnp.concatenate([back, jnp.zeros((rows, wide - block), F32)], axis=1)
-        out[...] = pltpu.roll(back, place[3] * block, 1)
+        out_ref[tau] = at_sub(place, jnp.concatenate(here, axis=1), 0)
+
+
+def complete(place, early, *refs):
+    backs, out_ref = refs[:-1], refs[-1]
+    nt, block, wide = early.shape
+    naux = wide // block
+    half = block // 2
+    for tau in range(nt):
+        parts = [jnp.zeros((block, block), F32)] * naux
+        for shift, ref in enumerate(backs, 1):
+            upper = ref[:, tau * half : (tau + 1) * half]
+            lower = ref[:, (nt + tau) * half : (nt + tau + 1) * half]
+            parts[shift] = at_sub(place, jnp.concatenate([upper, lower], axis=0), 1)
+        total = early[tau] + jnp.concatenate(parts, axis=1)
+        out_ref[tau] = pltpu.roll(total, place[3] * block, 1)
 
 
 def local(three_center, occupied_green, virtual_green, block_list, sizes):
@@ -270,9 +279,9 @@
         tensor,
         **options,
     )
-    sides, token_late = call(
+    side_direct, side_back, token_late = call(
         second,
-        [((2 * rows, depth), BF16), ((8, 128), F32)],
+        [((rows, depth), BF16)] * 2 + [((8, 128), F32)],
         [((groups * rows_aux // 2 * share, 2 * width), F32)],
         work * (nob - 1),
         near,
@@ -288,33 +297,40 @@
     others = [lax.ppermute(block, "sub", swap) for block in pieces]
     flat = lambda block: block.reshape(-1, listed)
     count = 1 + len(plan)
-    work = 16 * rows * block_aux * depth * count
     blocks = [flat(x) for pair in zip([mine] + pieces, [mine_other] + others) for x in pair]
-    wide = nauxf + -(-len(plan) * block_aux // 128) * 128
-    (partial_chi,) = call(
-        meet,
-        [((nt, block_aux, wide), F32)],
-        [((2 * count * block_aux, depth), BF16), ((count, rows, block_aux), F32)],
+    work = 8 * rows * block_aux * depth * count
+    tensor, *backs = call(
+        meet_back,
+        [((2 * count * block_aux, depth), BF16)] + [((rows_aux, 2 * nt * rows_aux), F32)] * (count - 1),
+        [((count - 1, nt * rows_aux, block_aux), F32)],
         work,
-        sides,
+        side_back,
         *blocks,
         share=share,
         nt=nt,
+    )
+    returned = [lax.ppermute(back, "aux", ring(naux, i)) for i, back in enumerate(backs, 1)]
+    shape = ((nt, block_aux, nauxf), F32)
+    (early,) = call(
+        meet_direct,
+        [shape],
+        [((count, nt * rows_aux, block_aux), F32)],
+        work,
+        side_direct,
+        tensor,
+        nt=nt,
         naux=naux,
     )
+    (partial_chi,) = call(complete, [shape], [], 0, early, *returned)
     owners = nt * nob * nsub
-    own_rows = nt * block_aux // owners
     received = lax.all_to_all(
-        partial_chi.reshape(owners, own_rows, wide),
+        partial_chi.reshape(owners, nt * block_aux // owners, nauxf),
         ("tau", "orb", "sub"),
         split_axis=0,
         concat_axis=0,
         tiled=True,
     )
-    chi, *backs = call(add, [((own_rows, nauxf), F32)] * count, [], 0, received, block=block_aux)
-    for shift, back in enumerate(backs, 1):
-        chi = chi + lax.ppermute(back, "aux", ring(naux, shift))
-    return chi * (-2.0 / math.sqrt(norb * slots * width))
+    return received.sum(axis=0) * (-2.0 / math.sqrt(norb * slots * width))
 
 
 def solution(mesh):

time: 56.1 us -> 55.3 us (0.986)
  waiting for transfers between devices: 16.9 us -> 15.2 us
  Pallas kernels: 9.13 us -> 10.6 us
  blocking collectives: 10 us -> 9.05 us
    ppermute x2, waiting for transfers between devices: 4.63 us -> 2.92 us  [local(): lax.ppermute(back, 'aux', ring(naux, i))]
    pallas_call x5 -> x6, Pallas kernels: 9.12 us -> 10.6 us  [call(): pl.pallas_call(functools.partial(kernel, **options), out_shape=shapes, in...]
    all_to_all x1, blocking collectives: 10 us -> 9.05 us  [local(): lax.all_to_all(partial_chi.reshape(owners, nt * block_aux // owners, naux...]
  transfers between devices with their start and end apart: 10 -> 10, of which waited for: 6 -> 5; matrix products, arithmetic and copies ran while one was open for 3% -> 3% of each run, Pallas kernels for 11% -> 14%
where the time goes in v11:
time: 55.3 us; the launch traced here: 55 us
  starting transfers between devices  15.4 us (28%)
  waiting for transfers between devices  15.2 us (27%)
  Pallas kernels  10.6 us (19%)
  blocking collectives  9.05 us (16%)
  local copies, waits for them, and re-layouts  2.45 us (4%)
  other arithmetic  2.15 us (4%)
    pallas_call x6, Pallas kernels, call(): pl.pallas_call(functools.partial(kernel, **options), out_shape=shapes, in...  10.6 us
    all_to_all x1, blocking collectives, local(): lax.all_to_all(partial_chi.reshape(owners, nt * block_aux // owners, naux...  9.05 us
    ppermute x1, waiting for transfers between devices, local(): fars.append(lax.ppermute(near, ('orb', 'sub'), pairs))  7.31 us
    ppermute x2, starting transfers between devices, local(): pieces = [lax.ppermute(mine, 'aux', pairs) for pairs in plan]  6.14 us
    ppermute x2, starting transfers between devices, local(): lax.ppermute(back, 'aux', ring(naux, i))  3.93 us
    ppermute x1, starting transfers between devices, local(): lax.ppermute(tensor, 'orb', ring(nob, shift))  2.94 us
    ppermute x2, waiting for transfers between devices, local(): lax.ppermute(back, 'aux', ring(naux, i))  2.92 us
    ppermute x1, waiting for transfers between devices, local(): lax.ppermute(small, 'tau', ring(nt, shift))  2.79 us
  transfers between devices with their start and end apart: 10, of which 5 were waited for; matrix products, arithmetic and copies ran while one was open for 3% of the time, Pallas kernels for 14%

profile of v11, /device:TPU:0, one launch (start us, length us, event | category | flops | bytes accessed | tf_op | source)
XLA Modules:
  0.0 55.0 jit_solution(31326920981732386)
XLA Ops:
  0.0 2.9 %collective-permute-start.1 = (f32[128,2048]{1,0:T(8,128)}, f32[128,2048]{1,0:T(8,128)S(1)}, u32[]{:S(2)}, u32[]{:S(2)}) collective-permute-start(f32[128,2048]{1,0:T(8,128)} %bitcast.19), channel_id=1, source_target_pairs={{2,0},{0,2},{3,1},{1,3},{6,4},{4,6},{7,5},{5,7},{10,8},{8,10},{11,... | collective-permute-start | bytes 3145736 | tf_op jit(solution)/shard_map/ppermute | solution.py:247
  2.9 0.1 pad_add_fusion.place
  3.0 1.2 %copy-done = f32[1,1,2,64,2048]{4,3,2,1,0:T(8,128)S(1)} copy-done((f32[1,1,2,64,2048]{4,3,2,1,0:T(8,128)S(1)}, f32[1,1,2,64,2048]{4,3,2,1,0:T(8,128)}, u32[]{:S(2)}) %copy-start) | copy-done | bytes 1048600
  4.2 1.2 %prepare.1 = f32[32,32,128]{2,1,0:T(8,128)S(1)} custom-call(s32[4]{0:T(128)S(1)} %pad_add_fusion.place, f32[128,2048]{1,0:T(8,128)S(1)} %bitcast.20), custom_call_target="tpu_custom_call" | custom-call | bytes 1048576 | tf_op jit(solution)/shard_map/prepare/pallas_call | solution.py:236
  5.4 1.6 %collective-permute-start.4 = (f32[32,32,128]{2,1,0:T(8,128)S(1)}, f32[32,32,128]{2,1,0:T(8,128)S(1)}, u32[]{:S(2)}, u32[]{:S(2)}) collective-permute-start(f32[32,32,128]{2,1,0:T(8,128)S(1)} %prepare.1), channel_id=1, source_target_pairs={{0,4},{4,8},{8,12},{12,0},{1,5},{5,9},{9,13},{13,1},{2,6},{6,10},{... | collective-permute-start | bytes 1572872 | tf_op jit(solution)/shard_map/ppermute | solution.py:252
  7.1 0.0 collective-permute-start.3
  7.1 4.5 %collective-permute-start.6 = (f32[32,32,128]{2,1,0:T(8,128)S(1)}, f32[32,32,128]{2,1,0:T(8,128)S(1)}, u32[]{:S(2)}, u32[]{:S(2)}) collective-permute-start(f32[32,32,128]{2,1,0:T(8,128)S(1)} %prepare.1), channel_id=1, source_target_pairs={{0,8},{12,4},{1,9},{13,5},{2,10},{14,6},{3,11},{15,7},{16,24},{28,... | collective-permute-start | bytes 1572872 | tf_op jit(solution)/shard_map/ppermute | solution.py:252
  11.6 0.7 %convert_element_type.5 = f32[1,2]{1,0:T(1,128)S(1)} convert(s32[1,2]{1,0:T(1,128)} %param.7) | non-fusion elementwise | flops 2 | bytes 16 | tf_op jit(solution)/shard_map/convert_element_type | solution.py:259
  12.2 0.8 %fusion = (f32[1,136,128]{2,1,0:T(8,128)S(1)}, f32[136,128]{1,0:T(8,128)S(1)}) fusion(f32[1,2]{1,0:T(1,128)S(1)} %convert_element_type.5, f32[64,128]{1,0:T(8,128)} %param.6, f32[64,128]{1,0:T(8,128)} %param.5), kind=kLoop, calls=%fused_computation.5 | loop fusion | flops 69632 | bytes 204808 | tf_op jit(solution)/shard_map/stack | solution.py:262
  13.0 1.6 %collective-permute-start = (f32[136,128]{1,0:T(8,128)S(1)}, f32[136,128]{1,0:T(8,128)S(1)}, u32[]{:S(2)}, u32[]{:S(2)}) collective-permute-start(f32[136,128]{1,0:T(8,128)S(1)} %get-tuple-element.20), channel_id=1, source_target_pairs={{16,0},{0,16},{17,1},{1,17},{18,2},{2,18},{19,3},{3,19},{20,4},{4,... | collective-permute-start | bytes 208904 | tf_op jit(solution)/shard_map/ppermute | solution.py:262
  14.6 2.8 %collective-permute-done = f32[136,128]{1,0:T(8,128)S(1)} collective-permute-done((f32[136,128]{1,0:T(8,128)S(1)}, f32[136,128]{1,0:T(8,128)S(1)}, u32[]{:S(2)}, u32[]{:S(2)}) %collective-permute-start) | collective-permute-done | bytes 69664 | tf_op jit(solution)/shard_map/ppermute | solution.py:262
  17.4 0.1 collective-permute-start.2
  17.5 0.0 copy-start.1
  17.5 1.2 %copy-done.1 = f32[1,1,2,64,2048]{4,3,2,1,0:T(8,128)S(1)} copy-done((f32[1,1,2,64,2048]{4,3,2,1,0:T(8,128)S(1)}, f32[1,1,2,64,2048]{4,3,2,1,0:T(8,128)}, u32[]{:S(2)}) %copy-start.1) | copy-done | bytes 1048600
  18.7 2.5 %first.1 = (f32[4,512,256]{2,1,0:T(8,128)S(1)}, f32[8,128]{1,0:T(8,128)}) custom-call(s32[4]{0:T(128)S(1)} %pad_add_fusion.place, f32[2,136,128]{2,1,0:T(8,128)S(1)} %pad_maximum_fusion.near, f32[128,2048]{1,0:T(8,128)S(1)} %bitcast.21), custom_call_target="tpu_custom_call" | custom-call | flops 603979776 | bytes 1187840 | tf_op jit(solution)/shard_map/first/pallas_call | solution.py:236
  21.2 7.3 %collective-permute-done.2.refs_1_ = f32[2,136,128]{2,1,0:T(8,128)S(1)} collective-permute-done((f32[2,136,128]{2,1,0:T(8,128)S(1)}, f32[2,136,128]{2,1,0:T(8,128)S(1)}, u32[]{:S(2)}, u32[]{:S(2)}) %collective-permute-start.2) | collective-permute-done | bytes 139296 | tf_op jit(solution)/shard_map/ppermute | solution.py:266
  28.6 0.0 collective-permute-done.1.refs_0_
  28.6 2.3 %second.1 = (bf16[128,4096]{1,0:T(8,128)(2,1)S(1)}, bf16[128,4096]{1,0:T(8,128)(2,1)S(1)}, f32[8,128]{1,0:T(8,128)S(1)}) custom-call(s32[4]{0:T(128)S(1)} %pad_add_fusion.place, f32[2,136,128]{2,1,0:T(8,128)S(1)} %pad_maximum_fusion.near, f32[4,512,256]{2,1,0:T(8,128)S(1)} %get-tuple-element.12.acc, f32[128,2048]{1,0:T(8,128)S(1)} %collective-permute-done.1.refs_0_, ...), custom_call_target="tpu_custom_call" | custom-call | flops 603979776 | bytes 3424256 | tf_op jit(solution)/shard_map/second/pallas_call | solution.py:236
  30.9 0.0 collective-permute-done.4.refs_0_
  30.9 0.0 collective-permute-done.6.refs_0_
  30.9 0.6 %collective-permute-start.7 = (f32[32,32,128]{2,1,0:T(8,128)S(1)}, f32[32,32,128]{2,1,0:T(8,128)S(1)}, u32[]{:S(2)}, u32[]{:S(2)}) collective-permute-start(f32[32,32,128]{2,1,0:T(8,128)S(1)} %after.3), channel_id=1, source_target_pairs={{1,0},{0,1},{3,2},{2,3},{5,4},{4,5},{7,6},{6,7},{9,8},{8,9},{11,10... | collective-permute-start | bytes 1572872 | tf_op jit(solution)/shard_map/ppermute | solution.py:297
  31.5 0.1 collective-permute-start.5
  31.6 1.5 %collective-permute-done.7 = f32[32,32,128]{2,1,0:T(8,128)S(1)} collective-permute-done((f32[32,32,128]{2,1,0:T(8,128)S(1)}, f32[32,32,128]{2,1,0:T(8,128)S(1)}, u32[]{:S(2)}, u32[]{:S(2)}) %collective-permute-start.7) | collective-permute-done | bytes 524320 | tf_op jit(solution)/shard_map/ppermute | solution.py:297
  33.1 0.7 %collective-permute-done.5 = f32[32,32,128]{2,1,0:T(8,128)S(1)} collective-permute-done((f32[32,32,128]{2,1,0:T(8,128)S(1)}, f32[32,32,128]{2,1,0:T(8,128)S(1)}, u32[]{:S(2)}, u32[]{:S(2)}) %collective-permute-start.5) | collective-permute-done | bytes 524320 | tf_op jit(solution)/shard_map/ppermute | solution.py:297
  33.8 2.1 %meet_back.1 = (bf16[384,4096]{1,0:T(8,128)(2,1)S(1)}, f32[32,128]{1,0:T(8,128)S(1)}, f32[32,128]{1,0:T(8,128)S(1)}) custom-call(s32[4]{0:T(128)S(1)} %pad_add_fusion.place, bf16[128,4096]{1,0:T(8,128)(2,1)S(1)} %get-tuple-element.14.side, f32[1024,128]{1,0:T(8,128)S(1)} %bitcast.17, f32[1024,128]{1,0:T(8,128)S(1)} %bitcast.15, f32[1024,128]{1,0:T(8,128)S(1)} %bitcast.16, ...), custom_call_target="tpu_custom_call" | custom-call | flops 805306368 | bytes 5242880 | tf_op jit(solution)/shard_map/meet_back/pallas_call | solution.py:236
  35.9 3.9 %collective-permute-start.8 = (f32[32,128]{1,0:T(8,128)S(1)}, f32[32,128]{1,0:T(8,128)S(1)}, u32[]{:S(2)}, u32[]{:S(2)}) collective-permute-start(f32[32,128]{1,0:T(8,128)S(1)} %get-tuple-element.17), channel_id=1, source_target_pairs={{4,0},{8,4},{12,8},{0,12},{5,1},{9,5},{13,9},{1,13},{6,2},{10,6},{... | collective-permute-start | bytes 49160 | tf_op jit(solution)/shard_map/ppermute | solution.py:312
  39.8 1.7 %meet_direct.1.early = f32[2,64,256]{2,1,0:T(8,128)S(1)} custom-call(s32[4]{0:T(128)S(1)} %pad_add_fusion.place, bf16[128,4096]{1,0:T(8,128)(2,1)S(1)} %get-tuple-element.13.side, bf16[384,4096]{1,0:T(8,128)(2,1)S(1)} %get-tuple-element.16.tensor), custom_call_target="tpu_custom_call" | custom-call | flops 805306368 | bytes 8388608 | tf_op jit(solution)/shard_map/meet_direct/pallas_call | solution.py:236
  41.5 0.0 collective-permute-done.8.refs_0_
  41.5 2.9 %collective-permute-done.9.refs_1_ = f32[32,128]{1,0:T(8,128)S(1)} collective-permute-done((f32[32,128]{1,0:T(8,128)S(1)}, f32[32,128]{1,0:T(8,128)S(1)}, u32[]{:S(2)}, u32[]{:S(2)}) %collective-permute-start.9) | collective-permute-done | bytes 16416 | tf_op jit(solution)/shard_map/ppermute | solution.py:312
  44.5 0.8 %complete.1 = f32[2,64,256]{2,1,0:T(8,128)S(1)} custom-call(s32[4]{0:T(128)S(1)} %pad_add_fusion.place, f32[2,64,256]{2,1,0:T(8,128)S(1)} %meet_direct.1.early, f32[32,128]{1,0:T(8,128)S(1)} %collective-permute-done.8.refs_0_, f32[32,128]{1,0:T(8,128)S(1)} %collective-permute-done.9.refs_1_), custom_call_target="tpu_custom_call" | custom-call | bytes 163840 | tf_op jit(solution)/shard_map/complete/pallas_call | solution.py:236
  45.3 9.0 %all_to_all.5 = f32[8,16,256]{2,1,0:T(8,128)S(1)} all-to-all(f32[8,16,256]{2,1,0:T(8,128)S(1)} %bitcast.24), channel_id=1, replica_groups=mesh['tau'=2,'aux'=4,'orb'=2,'sub'=2] {'tau','orb','sub'}, dimensions={0} | all-to-all | bytes 262144 | tf_op jit(solution)/shard_map/all_to_all | solution.py:326
  54.4 0.6 %broadcast_multiply_fusion = f32[16,256]{1,0:T(8,128)} fusion(f32[16,256]{1,0:T(8,128)S(1)} %reduce_sum.9), kind=kLoop, calls=%fused_computation.3 | loop fusion | flops 4096 | bytes 32768 | tf_op jit(solution)/shard_map/mul | solution.py:333
  (7 shorter events, 0.0 us)
Async XLA Ops:
  0.0 28.6 %collective-permute-start.1 = (f32[128,2048]{1,0:T(8,128)}, f32[128,2048]{1,0:T(8,128)S(1)}, u32[]{:S(2)}, u32[]{:S(2)}) collective-permute-start(f32[128,2048]{1,0:T(8,128)} %bitcast.19), channel_id=1, source_target_pairs={{2,0},{0,2},{3,1},{1,3},{6,4},{4,6},{7,5},{5,7},{10,8},{8,10},{11,... | collective-permute-start | bytes 3145736 | tf_op jit(solution)/shard_map/ppermute | solution.py:247
  3.0 1.2 %copy-start = (f32[1,1,2,64,2048]{4,3,2,1,0:T(8,128)S(1)}, f32[1,1,2,64,2048]{4,3,2,1,0:T(8,128)}, u32[]{:S(2)}) copy-start(f32[1,1,2,64,2048]{4,3,2,1,0:T(8,128)} %param.4) | copy-start | bytes 3145732
  5.4 25.4 %collective-permute-start.4 = (f32[32,32,128]{2,1,0:T(8,128)S(1)}, f32[32,32,128]{2,1,0:T(8,128)S(1)}, u32[]{:S(2)}, u32[]{:S(2)}) collective-permute-start(f32[32,32,128]{2,1,0:T(8,128)S(1)} %prepare.1), channel_id=1, source_target_pairs={{0,4},{4,8},{8,12},{12,0},{1,5},{5,9},{9,13},{13,1},{2,6},{6,10},{... | collective-permute-start | bytes 1572872 | tf_op jit(solution)/shard_map/ppermute | solution.py:252
  7.1 23.8 %collective-permute-start.3 = (f32[32,32,128]{2,1,0:T(8,128)S(1)}, f32[32,32,128]{2,1,0:T(8,128)S(1)}, u32[]{:S(2)}, u32[]{:S(2)}) collective-permute-start(f32[32,32,128]{2,1,0:T(8,128)S(1)} %prepare.1), channel_id=1, source_target_pairs={{1,0},{0,1},{3,2},{2,3},{5,4},{4,5},{7,6},{6,7},{9,8},{8,9},{11,10... | collective-permute-start | bytes 1572872 | tf_op jit(solution)/shard_map/ppermute | solution.py:254
  7.1 23.8 %collective-permute-start.6 = (f32[32,32,128]{2,1,0:T(8,128)S(1)}, f32[32,32,128]{2,1,0:T(8,128)S(1)}, u32[]{:S(2)}, u32[]{:S(2)}) collective-permute-start(f32[32,32,128]{2,1,0:T(8,128)S(1)} %prepare.1), channel_id=1, source_target_pairs={{0,8},{12,4},{1,9},{13,5},{2,10},{14,6},{3,11},{15,7},{16,24},{28,... | collective-permute-start | bytes 1572872 | tf_op jit(solution)/shard_map/ppermute | solution.py:252
  13.0 4.4 %collective-permute-start = (f32[136,128]{1,0:T(8,128)S(1)}, f32[136,128]{1,0:T(8,128)S(1)}, u32[]{:S(2)}, u32[]{:S(2)}) collective-permute-start(f32[136,128]{1,0:T(8,128)S(1)} %get-tuple-element.20), channel_id=1, source_target_pairs={{16,0},{0,16},{17,1},{1,17},{18,2},{2,18},{19,3},{3,19},{20,4},{4,... | collective-permute-start | bytes 208904 | tf_op jit(solution)/shard_map/ppermute | solution.py:262
  17.4 11.1 %collective-permute-start.2 = (f32[2,136,128]{2,1,0:T(8,128)S(1)}, f32[2,136,128]{2,1,0:T(8,128)S(1)}, u32[]{:S(2)}, u32[]{:S(2)}) collective-permute-start(f32[2,136,128]{2,1,0:T(8,128)S(1)} %pad_maximum_fusion.near), channel_id=1, source_target_pairs={{2,1},{3,0},{0,3},{1,2},{6,5},{7,4},{4,7},{5,6},{10,9},{11,8},{8,1... | collective-permute-start | bytes 417800 | tf_op jit(solution)/shard_map/ppermute | solution.py:266
  17.5 1.2 %copy-start.1 = (f32[1,1,2,64,2048]{4,3,2,1,0:T(8,128)S(1)}, f32[1,1,2,64,2048]{4,3,2,1,0:T(8,128)}, u32[]{:S(2)}) copy-start(f32[1,1,2,64,2048]{4,3,2,1,0:T(8,128)} %param.4) | copy-start | bytes 3145732
  30.9 2.2 %collective-permute-start.7 = (f32[32,32,128]{2,1,0:T(8,128)S(1)}, f32[32,32,128]{2,1,0:T(8,128)S(1)}, u32[]{:S(2)}, u32[]{:S(2)}) collective-permute-start(f32[32,32,128]{2,1,0:T(8,128)S(1)} %after.3), channel_id=1, source_target_pairs={{1,0},{0,1},{3,2},{2,3},{5,4},{4,5},{7,6},{6,7},{9,8},{8,9},{11,10... | collective-permute-start | bytes 1572872 | tf_op jit(solution)/shard_map/ppermute | solution.py:297
  31.5 2.3 %collective-permute-start.5 = (f32[32,32,128]{2,1,0:T(8,128)S(1)}, f32[32,32,128]{2,1,0:T(8,128)S(1)}, u32[]{:S(2)}, u32[]{:S(2)}) collective-permute-start(f32[32,32,128]{2,1,0:T(8,128)S(1)} %after.2.refs_3_), channel_id=1, source_target_pairs={{1,0},{0,1},{3,2},{2,3},{5,4},{4,5},{7,6},{6,7},{9,8},{8,9},{11,10... | collective-permute-start | bytes 1572872 | tf_op jit(solution)/shard_map/ppermute | solution.py:297
  35.9 5.6 %collective-permute-start.8 = (f32[32,128]{1,0:T(8,128)S(1)}, f32[32,128]{1,0:T(8,128)S(1)}, u32[]{:S(2)}, u32[]{:S(2)}) collective-permute-start(f32[32,128]{1,0:T(8,128)S(1)} %get-tuple-element.17), channel_id=1, source_target_pairs={{4,0},{8,4},{12,8},{0,12},{5,1},{9,5},{13,9},{1,13},{6,2},{10,6},{... | collective-permute-start | bytes 49160 | tf_op jit(solution)/shard_map/ppermute | solution.py:312
  39.8 4.6 %collective-permute-start.9 = (f32[32,128]{1,0:T(8,128)S(1)}, f32[32,128]{1,0:T(8,128)S(1)}, u32[]{:S(2)}, u32[]{:S(2)}) collective-permute-start(f32[32,128]{1,0:T(8,128)S(1)} %get-tuple-element.18), channel_id=1, source_target_pairs={{8,0},{12,4},{0,8},{4,12},{9,1},{13,5},{1,9},{5,13},{10,2},{14,6},... | collective-permute-start | bytes 49160 | tf_op jit(solution)/shard_map/ppermute | solution.py:312

commit v12 on v11

--- a/solution.py
+++ b/solution.py
@@ -11,7 +11,6 @@
 VMEM = pl.BlockSpec(memory_space=pltpu.VMEM)
 ANY = pl.BlockSpec(memory_space=pl.ANY)
 HBM = pl.BlockSpec(memory_space=pltpu.HBM)
-SMEM = pl.BlockSpec(memory_space=pltpu.SMEM)
 F32 = jnp.float32
 BF16 = jnp.bfloat16
 LIST_ROWS = 8
@@ -126,7 +125,7 @@
 
 
 def second(place, near, acc, *refs, slots, width, share):
-    refs, (side_direct, side_back, token, rows) = refs[:-4], refs[-4:]
+    refs, (sides, token, rows) = refs[:-3], refs[-3:]
     tensors, fars = refs[: len(refs) // 2], refs[len(refs) // 2 :]
     token[...] = jnp.zeros_like(token)
     listed = slots * width
@@ -137,61 +136,87 @@
         term = mix(place, near, far, tensor, rows, slots, width, share)
         total = [x + y for x, y in zip(total, term)]
     for group in range(groups):
-        side = (side_direct, side_back)[group * 2 // groups]
         height = groups * pairs
         high, low = halves(total[group])
         for odd in range(2):
-            row = (2 * (group % (groups // 2)) + odd) * pairs
+            row = (2 * (group % (groups // 2)) + odd) * pairs + 2 * height * (group * 2 // groups)
             for at in range(share):
                 for part, array in enumerate((high, low)):
-                    side[part * height + row : part * height + row + pairs, at * listed : (at + 1) * listed] = array[
-                        at * pairs : (at + 1) * pairs, odd * listed : (odd + 1) * listed
-                    ]
-
-
-def unfold(products, i, ordered):
-    rows, block = ordered.shape[-2:]
-    product = products[2 * i * block : (2 * i + 1) * block] + products[(2 * i + 1) * block : 2 * (i + 1) * block]
-    product = (product[:, :rows] + product[:, rows:]).T
-    pairs = block // 4
-    for group in range(rows // (2 * pairs)):
+                    sides[
+                        part * height + row : part * height + row + pairs, at * listed : (at + 1) * listed
+                    ] = array[at * pairs : (at + 1) * pairs, odd * listed : (odd + 1) * listed]
+
+
+def relay(pieces, tensor):
+    share, half, listed = pieces[0].shape
+    for i, source in enumerate(pieces):
+        for at in range(share):
+            high, low = halves(source[at])
+            tensor[2 * i * half : (2 * i + 1) * half, at * listed : (at + 1) * listed] = high
+            tensor[(2 * i + 1) * half : 2 * (i + 1) * half, at * listed : (at + 1) * listed] = low
+
+
+def products(tensor, side, half):
+    all_parts = dot_nt(tensor, side)
+    width = side.shape[0] // 2
+    rows = []
+    for i in range(tensor.shape[0] // (2 * half)):
+        block = all_parts[2 * i * half : (2 * i + 1) * half] + all_parts[(2 * i + 1) * half : 2 * (i + 1) * half]
+        rows.append(block[:, :width] + block[:, width:])
+    return jnp.concatenate(rows, axis=0)
+
+
+def unfold(block, ordered, i):
+    turned = block.T
+    pairs = block.shape[0] // 4
+    for group in range(turned.shape[0] // (2 * pairs)):
         for odd in range(2):
             at = (2 * group + odd) * pairs
-            ordered[i, pl.ds(2 * group * pairs + odd, pairs, stride=2), :] = product[at : at + pairs]
+            ordered[i, pl.ds(2 * group * pairs + odd, pairs, stride=2), :] = turned[at : at + pairs]
 
 
 def at_sub(place, x, axis):
     zero = jnp.zeros_like(x)
-    return jnp.where(place[2] == 0, jnp.concatenate([x, zero], axis=axis), jnp.concatenate([zero, x], axis=axis))
-
-
-def meet_back(place, side, *refs, share, nt):
-    count = (len(refs) - 1) // 3
-    pieces, (tensor, *backs, ordered) = refs[: 2 * count], refs[2 * count :]
-    listed = pieces[0].shape[1]
-    half = pieces[0].shape[0] // share
-    block = 2 * half
-    for i in range(count):
-        for which, source in enumerate(pieces[2 * i : 2 * i + 2]):
-            start = pl.multiple_of(jnp.where(place[2] == which, 0, half), half)
-            for at in range(share):
-                high, low = halves(source[at * half : (at + 1) * half, :])
-                tensor[pl.ds(2 * i * block + start, half), at * listed : (at + 1) * listed] = high
-                tensor[pl.ds((2 * i + 1) * block + start, half), at * listed : (at + 1) * listed] = low
-    products = dot_nt(tensor[2 * block :, :], side[...])
+    return by_sub(place, x, zero, axis)
+
+
+def by_sub(place, own, other, axis):
+    return jnp.where(
+        place[2] == 0, jnp.concatenate([own, other], axis=axis), jnp.concatenate([other, own], axis=axis)
+    )
+
+
+def meet_own(place, sides, *refs):
+    pieces, (direct, back, tensor) = refs[:-3], refs[-3:]
+    half = pieces[0].shape[1]
+    rows = sides.shape[0] // 2
+    relay(pieces, tensor)
+    direct[...] = products(tensor[...], sides[:rows, :], half)
+    back[...] = products(tensor[4 * half :, :], sides[rows:, :], half)
+
+
+def meet_back(place, sides, own, *refs):
+    count = own.shape[0] // refs[0].shape[1]
+    pieces, (tensor, *backs, ordered) = refs[:count], refs[count:]
+    half = pieces[0].shape[1]
+    relay(pieces, tensor)
+    other = products(tensor[...], sides[sides.shape[0] // 2 :, :], half)
     for i, back_ref in enumerate(backs):
-        unfold(products, i, ordered)
+        rows = slice(i * half, (i + 1) * half)
+        unfold(by_sub(place, own[rows, :], other[rows], 0), ordered, i)
         back = ordered[i].T
         back_ref[...] = jnp.concatenate([back[:half], back[half:]], axis=1)
 
 
-def meet_direct(place, side, tensor, out_ref, ordered, *, nt, naux):
+def meet_direct(place, sides, own, tensor, out_ref, ordered, *, nt, naux):
     count = ordered.shape[0]
     block = ordered.shape[2]
     half = block // 2
-    products = dot_nt(tensor[...], side[...])
-    for i in range(count):
-        unfold(products, i, ordered)
+    other = products(tensor[...], sides[: sides.shape[0] // 2, :], half)
+    unfold(by_sub(place, own[:half, :], own[half:block, :], 0), ordered, 0)
+    for i in range(1, count):
+        rows = slice((i - 1) * half, i * half)
+        unfold(by_sub(place, own[block + rows.start : block + rows.stop, :], other[rows], 0), ordered, i)
     for tau in range(nt):
         here = [jnp.zeros((half, block), F32)] * naux
         for shift in range(count):
@@ -225,24 +250,26 @@
     listed = slots * width
     share = width // nt
     nauxf = naux * block_aux
-    me_orb, me_tau, me_sub, me_aux = (lax.axis_index(axis) for axis in ("orb", "tau", "sub", "aux"))
-    place = jnp.stack([me_orb, me_tau, me_sub, me_aux]).astype(jnp.int32)
     tensor = three_center.reshape(listed, columns)
     limit = 24 + 3 * max(nob - 2, 0)
 
     def call(kernel, outs, scratch, flops, *arguments, **options):
         shapes = [jax.ShapeDtypeStruct(shape, kind) for shape, kind in outs]
         size = sum(4 * math.prod(x.shape) for x in arguments)
+
+        def here(*refs):
+            kernel([lax.axis_index(axis) for axis in ("orb", "tau", "sub", "aux")], *refs, **options)
+
         return pl.pallas_call(
-            functools.partial(kernel, **options),
+            here,
             out_shape=shapes,
-            in_specs=[SMEM] + [VMEM] * len(arguments),
+            in_specs=[VMEM] * len(arguments),
             out_specs=[VMEM] * len(shapes),
             scratch_shapes=[pltpu.VMEM(shape, kind) for shape, kind in scratch],
             compiler_params=pltpu.CompilerParams(vmem_limit_bytes=limit * MIB),
             cost_estimate=pl.CostEstimate(flops=flops, bytes_accessed=size, transcendentals=0),
             name=kernel.__name__,
-        )(place, *arguments)
+        )(*arguments)
 
     tensors = [lax.ppermute(tensor, "orb", ring(nob, shift)) for shift in range(1, nob)]
     (mine,) = call(
@@ -279,9 +306,9 @@
         tensor,
         **options,
     )
-    side_direct, side_back, token_late = call(
+    sides, token_late = call(
         second,
-        [((rows, depth), BF16)] * 2 + [((8, 128), F32)],
+        [((2 * rows, depth), BF16), ((8, 128), F32)],
         [((groups * rows_aux // 2 * share, 2 * width), F32)],
         work * (nob - 1),
         near,
@@ -295,33 +322,35 @@
         held.append(after(block, token_late, mine_other, *held[-1:]))
     pieces = held
     others = [lax.ppermute(block, "sub", swap) for block in pieces]
-    flat = lambda block: block.reshape(-1, listed)
     count = 1 + len(plan)
-    blocks = [flat(x) for pair in zip([mine] + pieces, [mine_other] + others) for x in pair]
-    work = 8 * rows * block_aux * depth * count
-    tensor, *backs = call(
+    height = (count + 1) * rows_aux
+    work = 8 * rows * depth * rows_aux
+    wide = nt * rows_aux
+    direct, back = call(
+        meet_own,
+        [((height, wide), F32), ((height - block_aux, wide), F32)],
+        [((2 * height, depth), BF16)],
+        work * count * 2,
+        sides,
+        mine,
+        mine_other,
+        *pieces,
+    )
+    others, *backs = call(
         meet_back,
-        [((2 * count * block_aux, depth), BF16)] + [((rows_aux, 2 * nt * rows_aux), F32)] * (count - 1),
-        [((count - 1, nt * rows_aux, block_aux), F32)],
-        work,
-        side_back,
-        *blocks,
-        share=share,
-        nt=nt,
+        [((2 * len(plan) * rows_aux, depth), BF16)] + [((rows_aux, 2 * wide), F32)] * len(plan),
+        [((len(plan), wide, block_aux), F32)],
+        work * len(plan),
+        sides,
+        back,
+        *others,
     )
     returned = [lax.ppermute(back, "aux", ring(naux, i)) for i, back in enumerate(backs, 1)]
     shape = ((nt, block_aux, nauxf), F32)
-    (early,) = call(
-        meet_direct,
-        [shape],
-        [((count, nt * rows_aux, block_aux), F32)],
-        work,
-        side_direct,
-        tensor,
-        nt=nt,
-        naux=naux,
-    )
-    (partial_chi,) = call(complete, [shape], [], 0, early, *returned)
+    (direct,) = call(
+        meet_direct, [shape], [((count, wide, block_aux), F32)], work * len(plan), sides, direct, others, nt=nt, naux=naux
+    )
+    (partial_chi,) = call(complete, [shape], [], 0, direct, *returned)
     owners = nt * nob * nsub
     received = lax.all_to_all(
         partial_chi.reshape(owners, nt * block_aux // owners, nauxf),

time: 55.3 us -> 52.9 us (0.957)
  Pallas kernels: 10.6 us -> 7.11 us
  waiting for transfers between devices: 15.2 us -> 16.3 us
    pallas_call x6 -> x7, Pallas kernels: 10.6 us -> 7.11 us  [call(): pl.pallas_call(here, out_shape=shapes, in_specs=[VMEM] * len(arguments),...]
    ppermute x1, waiting for transfers between devices: 7.31 us -> 8.4 us  [local(): fars.append(lax.ppermute(near, ('orb', 'sub'), pairs))]
    ppermute x2, waiting for transfers between devices: 2.21 us -> 1.11 us  [local(): others = [lax.ppermute(block, 'sub', swap) for block in pieces]]
    ppermute x2, waiting for transfers between devices: 2.92 us -> 3.94 us  [local(): lax.ppermute(back, 'aux', ring(naux, i))]
  transfers between devices with their start and end apart: 10 -> 10, of which waited for: 5 -> 6; matrix products, arithmetic and copies ran while one was open for 3% -> 3% of each run, Pallas kernels for 14% -> 12%
where the time goes in v12:
time: 52.9 us; the launch traced here: 52.6 us
  waiting for transfers between devices  16.3 us (31%)
  starting transfers between devices  15.4 us (29%)
  blocking collectives  9.05 us (17%)
  Pallas kernels  7.11 us (13%)
  local copies, waits for them, and re-layouts  2.48 us (5%)
  other arithmetic  2.08 us (4%)
    all_to_all x1, blocking collectives, local(): lax.all_to_all(partial_chi.reshape(owners, nt * block_aux // owners, naux...  9.05 us
    ppermute x1, waiting for transfers between devices, local(): fars.append(lax.ppermute(near, ('orb', 'sub'), pairs))  8.4 us
    pallas_call x7, Pallas kernels, call(): pl.pallas_call(here, out_shape=shapes, in_specs=[VMEM] * len(arguments),...  7.11 us
    ppermute x2, starting transfers between devices, local(): pieces = [lax.ppermute(mine, 'aux', pairs) for pairs in plan]  6.14 us
    ppermute x2, waiting for transfers between devices, local(): lax.ppermute(back, 'aux', ring(naux, i))  3.94 us
    ppermute x2, starting transfers between devices, local(): lax.ppermute(back, 'aux', ring(naux, i))  3.92 us
    ppermute x1, starting transfers between devices, local(): lax.ppermute(tensor, 'orb', ring(nob, shift))  2.94 us
    ppermute x1, waiting for transfers between devices, local(): lax.ppermute(small, 'tau', ring(nt, shift))  2.79 us
  transfers between devices with their start and end apart: 10, of which 6 were waited for; matrix products, arithmetic and copies ran while one was open for 3% of the time, Pallas kernels for 12%

profile of v12, /device:TPU:0, one launch (start us, length us, event | category | flops | bytes accessed | tf_op | source)
XLA Modules:
  0.0 52.6 jit_solution(2574550702296018404)
XLA Ops:
  0.0 2.9 %collective-permute-start.1 = (f32[128,2048]{1,0:T(8,128)}, f32[128,2048]{1,0:T(8,128)S(1)}, u32[]{:S(2)}, u32[]{:S(2)}) collective-permute-start(f32[128,2048]{1,0:T(8,128)} %bitcast.5), channel_id=1, source_target_pairs={{2,0},{0,2},{3,1},{1,3},{6,4},{4,6},{7,5},{5,7},{10,8},{8,10},{11,... | collective-permute-start | bytes 3145736 | tf_op jit(solution)/shard_map/ppermute | solution.py:274
  2.9 1.3 %copy-done = f32[1,1,2,64,2048]{4,3,2,1,0:T(8,128)S(1)} copy-done((f32[1,1,2,64,2048]{4,3,2,1,0:T(8,128)S(1)}, f32[1,1,2,64,2048]{4,3,2,1,0:T(8,128)}, u32[]{:S(2)}) %copy-start) | copy-done | bytes 1048600
  4.2 0.6 %prepare.1.refs_1_ = f32[32,32,128]{2,1,0:T(8,128)S(1)} custom-call(f32[128,2048]{1,0:T(8,128)S(1)} %bitcast.6), custom_call_target="tpu_custom_call" | custom-call | bytes 1048576 | tf_op jit(solution)/shard_map/prepare/pallas_call | solution.py:263
  4.8 0.1 collective-permute-start.3
  4.9 1.6 %collective-permute-start.4 = (f32[32,32,128]{2,1,0:T(8,128)S(1)}, f32[32,32,128]{2,1,0:T(8,128)S(1)}, u32[]{:S(2)}, u32[]{:S(2)}) collective-permute-start(f32[32,32,128]{2,1,0:T(8,128)S(1)} %prepare.1.refs_1_), channel_id=1, source_target_pairs={{0,4},{4,8},{8,12},{12,0},{1,5},{5,9},{9,13},{13,1},{2,6},{6,10},{... | collective-permute-start | bytes 1572872 | tf_op jit(solution)/shard_map/ppermute | solution.py:279
  6.5 4.5 %collective-permute-start.5 = (f32[32,32,128]{2,1,0:T(8,128)S(1)}, f32[32,32,128]{2,1,0:T(8,128)S(1)}, u32[]{:S(2)}, u32[]{:S(2)}) collective-permute-start(f32[32,32,128]{2,1,0:T(8,128)S(1)} %prepare.1.refs_1_), channel_id=1, source_target_pairs={{0,8},{12,4},{1,9},{13,5},{2,10},{14,6},{3,11},{15,7},{16,24},{28,... | collective-permute-start | bytes 1572872 | tf_op jit(solution)/shard_map/ppermute | solution.py:279
  11.0 0.7 %convert_element_type.5 = f32[1,2]{1,0:T(1,128)S(1)} convert(s32[1,2]{1,0:T(1,128)} %param.7) | non-fusion elementwise | flops 2 | bytes 16 | tf_op jit(solution)/shard_map/convert_element_type | solution.py:286
  11.7 0.8 %fusion = (f32[1,136,128]{2,1,0:T(8,128)S(1)}, f32[136,128]{1,0:T(8,128)S(1)}) fusion(f32[1,2]{1,0:T(1,128)S(1)} %convert_element_type.5, f32[64,128]{1,0:T(8,128)} %param.6, f32[64,128]{1,0:T(8,128)} %param.5), kind=kLoop, calls=%fused_computation.4 | loop fusion | flops 69632 | bytes 204808 | tf_op jit(solution)/shard_map/stack | solution.py:289
  12.5 1.6 %collective-permute-start = (f32[136,128]{1,0:T(8,128)S(1)}, f32[136,128]{1,0:T(8,128)S(1)}, u32[]{:S(2)}, u32[]{:S(2)}) collective-permute-start(f32[136,128]{1,0:T(8,128)S(1)} %get-tuple-element.22), channel_id=1, source_target_pairs={{16,0},{0,16},{17,1},{1,17},{18,2},{2,18},{19,3},{3,19},{20,4},{4,... | collective-permute-start | bytes 208904 | tf_op jit(solution)/shard_map/ppermute | solution.py:289
  14.1 2.8 %collective-permute-done = f32[136,128]{1,0:T(8,128)S(1)} collective-permute-done((f32[136,128]{1,0:T(8,128)S(1)}, f32[136,128]{1,0:T(8,128)S(1)}, u32[]{:S(2)}, u32[]{:S(2)}) %collective-permute-start) | collective-permute-done | bytes 69664 | tf_op jit(solution)/shard_map/ppermute | solution.py:289
  16.9 0.1 collective-permute-start.2
  16.9 0.0 copy-start.1
  16.9 1.2 %copy-done.1 = f32[1,1,2,64,2048]{4,3,2,1,0:T(8,128)S(1)} copy-done((f32[1,1,2,64,2048]{4,3,2,1,0:T(8,128)S(1)}, f32[1,1,2,64,2048]{4,3,2,1,0:T(8,128)}, u32[]{:S(2)}) %copy-start.1) | copy-done | bytes 1048600
  18.2 2.0 %first.1 = (f32[4,512,256]{2,1,0:T(8,128)S(1)}, f32[8,128]{1,0:T(8,128)}) custom-call(f32[2,136,128]{2,1,0:T(8,128)S(1)} %pad_maximum_fusion.refs_0_, f32[128,2048]{1,0:T(8,128)S(1)} %bitcast.7), custom_call_target="tpu_custom_call" | custom-call | flops 603979776 | bytes 1187840 | tf_op jit(solution)/shard_map/first/pallas_call | solution.py:263
  20.1 8.4 %collective-permute-done.2.refs_3_ = f32[2,136,128]{2,1,0:T(8,128)S(1)} collective-permute-done((f32[2,136,128]{2,1,0:T(8,128)S(1)}, f32[2,136,128]{2,1,0:T(8,128)S(1)}, u32[]{:S(2)}, u32[]{:S(2)}) %collective-permute-start.2) | collective-permute-done | bytes 139296 | tf_op jit(solution)/shard_map/ppermute | solution.py:293
  28.6 0.0 collective-permute-done.1.refs_2_
  28.6 1.7 %second.1 = (bf16[256,4096]{1,0:T(8,128)(2,1)S(1)}, f32[8,128]{1,0:T(8,128)S(1)}) custom-call(f32[2,136,128]{2,1,0:T(8,128)S(1)} %pad_maximum_fusion.refs_0_, f32[4,512,256]{2,1,0:T(8,128)S(1)} %get-tuple-element.13.refs_1_, f32[128,2048]{1,0:T(8,128)S(1)} %collective-permute-done.1.refs_2_, f32[2,136,128]{2,1,0:T(8,128)S(1)} %collective-permute-done.2.refs_3_), custom_call_target="tpu_custom_call" | custom-call | flops 603979776 | bytes 3424256 | tf_op jit(solution)/shard_map/second/pallas_call | solution.py:263
  30.3 0.0 collective-permute-done.5.refs_0_
  30.4 0.6 %collective-permute-start.7 = (f32[32,32,128]{2,1,0:T(8,128)S(1)}, f32[32,32,128]{2,1,0:T(8,128)S(1)}, u32[]{:S(2)}, u32[]{:S(2)}) collective-permute-start(f32[32,32,128]{2,1,0:T(8,128)S(1)} %after.3.refs_4_), channel_id=1, source_target_pairs={{1,0},{0,1},{3,2},{2,3},{5,4},{4,5},{7,6},{6,7},{9,8},{8,9},{11,10... | collective-permute-start | bytes 1572872 | tf_op jit(solution)/shard_map/ppermute | solution.py:324
  31.0 0.1 collective-permute-start.6
  31.1 1.1 %meet_own.1 = (f32[128,64]{1,0:T(8,128)S(1)}, f32[64,64]{1,0:T(8,128)S(1)}) custom-call(bf16[256,4096]{1,0:T(8,128)(2,1)S(1)} %get-tuple-element.14.refs_0_, f32[32,32,128]{2,1,0:T(8,128)S(1)} %prepare.1.refs_1_, f32[32,32,128]{2,1,0:T(8,128)S(1)} %collective-permute-done.3.refs_2_, f32[32,32,128]{2,1,0:T(8,128)S(1)} %after.2.refs_3_, ...), custom_call_target="tpu_custom_call" | custom-call | flops 805306368 | bytes 6291456 | tf_op jit(solution)/shard_map/meet_own/pallas_call | solution.py:263
  32.2 0.4 collective-permute-done.7.refs_3_
  32.5 0.7 %collective-permute-done.6.refs_2_ = f32[32,32,128]{2,1,0:T(8,128)S(1)} collective-permute-done((f32[32,32,128]{2,1,0:T(8,128)S(1)}, f32[32,32,128]{2,1,0:T(8,128)S(1)}, u32[]{:S(2)}, u32[]{:S(2)}) %collective-permute-start.6) | collective-permute-done | bytes 524320 | tf_op jit(solution)/shard_map/ppermute | solution.py:324
  33.3 0.7 %meet_back.1 = (bf16[128,4096]{1,0:T(8,128)(2,1)S(1)}, f32[32,128]{1,0:T(8,128)S(1)}, f32[32,128]{1,0:T(8,128)S(1)}) custom-call(bf16[256,4096]{1,0:T(8,128)(2,1)S(1)} %get-tuple-element.14.refs_0_, f32[64,64]{1,0:T(8,128)S(1)} %get-tuple-element.17.refs_1_, f32[32,32,128]{2,1,0:T(8,128)S(1)} %collective-permute-done.6.refs_2_, ...), custom_call_target="tpu_custom_call" | custom-call | flops 268435456 | bytes 5259264 | tf_op jit(solution)/shard_map/meet_back/pallas_call | solution.py:263
  34.0 3.9 %collective-permute-start.8 = (f32[32,128]{1,0:T(8,128)S(1)}, f32[32,128]{1,0:T(8,128)S(1)}, u32[]{:S(2)}, u32[]{:S(2)}) collective-permute-start(f32[32,128]{1,0:T(8,128)S(1)} %get-tuple-element.19), channel_id=1, source_target_pairs={{4,0},{8,4},{12,8},{0,12},{5,1},{9,5},{13,9},{1,13},{6,2},{10,6},{... | collective-permute-start | bytes 49160 | tf_op jit(solution)/shard_map/ppermute | solution.py:348
  38.0 0.0 collective-permute-start.9
  38.0 0.7 %meet_direct.1.refs_0_ = f32[2,64,256]{2,1,0:T(8,128)S(1)} custom-call(bf16[256,4096]{1,0:T(8,128)(2,1)S(1)} %get-tuple-element.14.refs_0_, f32[128,64]{1,0:T(8,128)S(1)} %get-tuple-element.16.refs_1_, bf16[128,4096]{1,0:T(8,128)(2,1)S(1)} %get-tuple-element.18.refs_2_), custom_call_target="tpu_custom_call" | custom-call | flops 268435456 | bytes 6324224 | tf_op jit(solution)/shard_map/meet_direct/pallas_call | solution.py:263
  38.7 0.7 %collective-permute-done.8.refs_1_ = f32[32,128]{1,0:T(8,128)S(1)} collective-permute-done((f32[32,128]{1,0:T(8,128)S(1)}, f32[32,128]{1,0:T(8,128)S(1)}, u32[]{:S(2)}, u32[]{:S(2)}) %collective-permute-start.8) | collective-permute-done | bytes 16416 | tf_op jit(solution)/shard_map/ppermute | solution.py:348
  39.4 3.2 %collective-permute-done.9.refs_2_ = f32[32,128]{1,0:T(8,128)S(1)} collective-permute-done((f32[32,128]{1,0:T(8,128)S(1)}, f32[32,128]{1,0:T(8,128)S(1)}, u32[]{:S(2)}, u32[]{:S(2)}) %collective-permute-start.9) | collective-permute-done | bytes 16416 | tf_op jit(solution)/shard_map/ppermute | solution.py:348
  42.6 0.3 complete.1
  42.9 9.1 %all_to_all.5 = f32[8,16,256]{2,1,0:T(8,128)S(1)} all-to-all(f32[8,16,256]{2,1,0:T(8,128)S(1)} %bitcast.8), channel_id=1, replica_groups=mesh['tau'=2,'aux'=4,'orb'=2,'sub'=2] {'tau','orb','sub'}, dimensions={0} | all-to-all | bytes 262144 | tf_op jit(solution)/shard_map/all_to_all | solution.py:355
  52.0 0.6 %broadcast_multiply_fusion = f32[16,256]{1,0:T(8,128)} fusion(f32[16,256]{1,0:T(8,128)S(1)} %reduce_sum.9), kind=kLoop, calls=%fused_computation.3 | loop fusion | flops 4096 | bytes 32768 | tf_op jit(solution)/shard_map/mul | solution.py:362
  (7 shorter events, 0.0 us)
Async XLA Ops:
  0.0 28.6 %collective-permute-start.1 = (f32[128,2048]{1,0:T(8,128)}, f32[128,2048]{1,0:T(8,128)S(1)}, u32[]{:S(2)}, u32[]{:S(2)}) collective-permute-start(f32[128,2048]{1,0:T(8,128)} %bitcast.5), channel_id=1, source_target_pairs={{2,0},{0,2},{3,1},{1,3},{6,4},{4,6},{7,5},{5,7},{10,8},{8,10},{11,... | collective-permute-start | bytes 3145736 | tf_op jit(solution)/shard_map/ppermute | solution.py:274
  2.9 1.3 %copy-start = (f32[1,1,2,64,2048]{4,3,2,1,0:T(8,128)S(1)}, f32[1,1,2,64,2048]{4,3,2,1,0:T(8,128)}, u32[]{:S(2)}) copy-start(f32[1,1,2,64,2048]{4,3,2,1,0:T(8,128)} %param.4) | copy-start | bytes 3145732
  4.8 25.5 %collective-permute-start.3 = (f32[32,32,128]{2,1,0:T(8,128)S(1)}, f32[32,32,128]{2,1,0:T(8,128)S(1)}, u32[]{:S(2)}, u32[]{:S(2)}) collective-permute-start(f32[32,32,128]{2,1,0:T(8,128)S(1)} %prepare.1.refs_1_), channel_id=1, source_target_pairs={{1,0},{0,1},{3,2},{2,3},{5,4},{4,5},{7,6},{6,7},{9,8},{8,9},{11,10... | collective-permute-start | bytes 1572872 | tf_op jit(solution)/shard_map/ppermute | solution.py:281
  4.9 25.5 %collective-permute-start.4 = (f32[32,32,128]{2,1,0:T(8,128)S(1)}, f32[32,32,128]{2,1,0:T(8,128)S(1)}, u32[]{:S(2)}, u32[]{:S(2)}) collective-permute-start(f32[32,32,128]{2,1,0:T(8,128)S(1)} %prepare.1.refs_1_), channel_id=1, source_target_pairs={{0,4},{4,8},{8,12},{12,0},{1,5},{5,9},{9,13},{13,1},{2,6},{6,10},{... | collective-permute-start | bytes 1572872 | tf_op jit(solution)/shard_map/ppermute | solution.py:279
  6.5 23.8 %collective-permute-start.5 = (f32[32,32,128]{2,1,0:T(8,128)S(1)}, f32[32,32,128]{2,1,0:T(8,128)S(1)}, u32[]{:S(2)}, u32[]{:S(2)}) collective-permute-start(f32[32,32,128]{2,1,0:T(8,128)S(1)} %prepare.1.refs_1_), channel_id=1, source_target_pairs={{0,8},{12,4},{1,9},{13,5},{2,10},{14,6},{3,11},{15,7},{16,24},{28,... | collective-permute-start | bytes 1572872 | tf_op jit(solution)/shard_map/ppermute | solution.py:279
  12.5 4.4 %collective-permute-start = (f32[136,128]{1,0:T(8,128)S(1)}, f32[136,128]{1,0:T(8,128)S(1)}, u32[]{:S(2)}, u32[]{:S(2)}) collective-permute-start(f32[136,128]{1,0:T(8,128)S(1)} %get-tuple-element.22), channel_id=1, source_target_pairs={{16,0},{0,16},{17,1},{1,17},{18,2},{2,18},{19,3},{3,19},{20,4},{4,... | collective-permute-start | bytes 208904 | tf_op jit(solution)/shard_map/ppermute | solution.py:289
  16.9 11.7 %collective-permute-start.2 = (f32[2,136,128]{2,1,0:T(8,128)S(1)}, f32[2,136,128]{2,1,0:T(8,128)S(1)}, u32[]{:S(2)}, u32[]{:S(2)}) collective-permute-start(f32[2,136,128]{2,1,0:T(8,128)S(1)} %pad_maximum_fusion.refs_0_), channel_id=1, source_target_pairs={{2,1},{3,0},{0,3},{1,2},{6,5},{7,4},{4,7},{5,6},{10,9},{11,8},{8,1... | collective-permute-start | bytes 417800 | tf_op jit(solution)/shard_map/ppermute | solution.py:293
  16.9 1.2 %copy-start.1 = (f32[1,1,2,64,2048]{4,3,2,1,0:T(8,128)S(1)}, f32[1,1,2,64,2048]{4,3,2,1,0:T(8,128)}, u32[]{:S(2)}) copy-start(f32[1,1,2,64,2048]{4,3,2,1,0:T(8,128)} %param.4) | copy-start | bytes 3145732
  30.4 2.2 %collective-permute-start.7 = (f32[32,32,128]{2,1,0:T(8,128)S(1)}, f32[32,32,128]{2,1,0:T(8,128)S(1)}, u32[]{:S(2)}, u32[]{:S(2)}) collective-permute-start(f32[32,32,128]{2,1,0:T(8,128)S(1)} %after.3.refs_4_), channel_id=1, source_target_pairs={{1,0},{0,1},{3,2},{2,3},{5,4},{4,5},{7,6},{6,7},{9,8},{8,9},{11,10... | collective-permute-start | bytes 1572872 | tf_op jit(solution)/shard_map/ppermute | solution.py:324
  31.0 2.3 %collective-permute-start.6 = (f32[32,32,128]{2,1,0:T(8,128)S(1)}, f32[32,32,128]{2,1,0:T(8,128)S(1)}, u32[]{:S(2)}, u32[]{:S(2)}) collective-permute-start(f32[32,32,128]{2,1,0:T(8,128)S(1)} %after.2.refs_3_), channel_id=1, source_target_pairs={{1,0},{0,1},{3,2},{2,3},{5,4},{4,5},{7,6},{6,7},{9,8},{8,9},{11,10... | collective-permute-start | bytes 1572872 | tf_op jit(solution)/shard_map/ppermute | solution.py:324
  34.0 5.4 %collective-permute-start.8 = (f32[32,128]{1,0:T(8,128)S(1)}, f32[32,128]{1,0:T(8,128)S(1)}, u32[]{:S(2)}, u32[]{:S(2)}) collective-permute-start(f32[32,128]{1,0:T(8,128)S(1)} %get-tuple-element.19), channel_id=1, source_target_pairs={{4,0},{8,4},{12,8},{0,12},{5,1},{9,5},{13,9},{1,13},{6,2},{10,6},{... | collective-permute-start | bytes 49160 | tf_op jit(solution)/shard_map/ppermute | solution.py:348
  38.0 4.6 %collective-permute-start.9 = (f32[32,128]{1,0:T(8,128)S(1)}, f32[32,128]{1,0:T(8,128)S(1)}, u32[]{:S(2)}, u32[]{:S(2)}) collective-permute-start(f32[32,128]{1,0:T(8,128)S(1)} %get-tuple-element.20), channel_id=1, source_target_pairs={{8,0},{12,4},{0,8},{4,12},{9,1},{13,5},{1,9},{5,13},{10,2},{14,6},... | collective-permute-start | bytes 49160 | tf_op jit(solution)/shard_map/ppermute | solution.py:348

commit v13 on v12

--- a/solution.py
+++ b/solution.py
@@ -34,12 +34,14 @@
     return [((target + shift) % count, target) for target in range(count)]
 
 
-def prepare(place, tensor, mine, turned, *, share):
+def prepare(place, tensor, mine, again, turned, *, share):
     some = mine.shape[1]
     turned[...] = tensor[...].T
     start = place[1] * share
     for at in range(share):
-        mine[at] = turned[pl.ds(start + at, some, stride=turned.shape[0] // some), :]
+        rows = turned[pl.ds(start + at, some, stride=turned.shape[0] // some), :]
+        mine[at] = rows
+        again[at] = rows
 
 
 def after(block, *tokens):
@@ -124,8 +126,8 @@
         acc[group] = result
 
 
-def second(place, near, acc, *refs, slots, width, share):
-    refs, (sides, token, rows) = refs[:-3], refs[-3:]
+def second(place, near, acc, *refs, slots, width, share, others):
+    refs, (sides, token, rows) = refs[: 2 * others], refs[-3:]
     tensors, fars = refs[: len(refs) // 2], refs[len(refs) // 2 :]
     token[...] = jnp.zeros_like(token)
     listed = slots * width
@@ -186,26 +188,33 @@
     )
 
 
+def fold(place, own, other, ordered):
+    unfold(by_sub(place, own, other, 0), ordered, 0)
+    back = ordered[0].T
+    half = own.shape[0]
+    return jnp.concatenate([back[:half], back[half:]], axis=1)
+
+
 def meet_own(place, sides, *refs):
-    pieces, (direct, back, tensor) = refs[:-3], refs[-3:]
+    count = (len(refs) - 4) // 3
+    pieces, (direct, back, *backs, tensor, ordered) = refs[: 2 * count + 1], refs[2 * count + 1 :]
     half = pieces[0].shape[1]
     rows = sides.shape[0] // 2
     relay(pieces, tensor)
     direct[...] = products(tensor[...], sides[:rows, :], half)
-    back[...] = products(tensor[4 * half :, :], sides[rows:, :], half)
-
-
-def meet_back(place, sides, own, *refs):
-    count = own.shape[0] // refs[0].shape[1]
-    pieces, (tensor, *backs, ordered) = refs[:count], refs[count:]
-    half = pieces[0].shape[1]
-    relay(pieces, tensor)
+    rest = products(tensor[4 * half :, :], sides[rows:, :], half)
+    for i, back_ref in enumerate(backs):
+        back_ref[...] = fold(
+            place, rest[2 * i * half : (2 * i + 1) * half], rest[(2 * i + 1) * half : 2 * (i + 1) * half], ordered
+        )
+    back[...] = rest[-half:]
+
+
+def meet_back(place, sides, own, piece, tensor, back_ref, ordered):
+    half = piece.shape[1]
+    relay([piece], tensor)
     other = products(tensor[...], sides[sides.shape[0] // 2 :, :], half)
-    for i, back_ref in enumerate(backs):
-        rows = slice(i * half, (i + 1) * half)
-        unfold(by_sub(place, own[rows, :], other[rows], 0), ordered, i)
-        back = ordered[i].T
-        back_ref[...] = jnp.concatenate([back[:half], back[half:]], axis=1)
+    back_ref[...] = fold(place, own[...], other, ordered)
 
 
 def meet_direct(place, sides, own, tensor, out_ref, ordered, *, nt, naux):
@@ -213,10 +222,10 @@
     block = ordered.shape[2]
     half = block // 2
     other = products(tensor[...], sides[: sides.shape[0] // 2, :], half)
-    unfold(by_sub(place, own[:half, :], own[half:block, :], 0), ordered, 0)
-    for i in range(1, count):
-        rows = slice((i - 1) * half, i * half)
-        unfold(by_sub(place, own[block + rows.start : block + rows.stop, :], other[rows], 0), ordered, i)
+    for i in range(count):
+        first_half = own[i * block : i * block + half, :]
+        second_half = own[i * block + half : (i + 1) * block, :] if i < count - 1 else other
+        unfold(by_sub(place, first_half, second_half, 0), ordered, i)
     for tau in range(nt):
         here = [jnp.zeros((half, block), F32)] * naux
         for shift in range(count):
@@ -272,11 +281,10 @@
         )(*arguments)
 
     tensors = [lax.ppermute(tensor, "orb", ring(nob, shift)) for shift in range(1, nob)]
-    (mine,) = call(
-        prepare, [((share, rows_aux, listed), F32)], [((columns, listed), F32)], 0, tensor, share=share
+    mine, again = call(
+        prepare, [((share, rows_aux, listed), F32)] * 2, [((columns, listed), F32)], 0, tensor, share=share
     )
     plan = shifts_of(naux)
-    pieces = [lax.ppermute(mine, "aux", pairs) for pairs in plan]
     swap = ring(nsub, 1)
     mine_other = lax.ppermute(mine, "sub", swap)
     small = jnp.concatenate(
@@ -306,6 +314,12 @@
         tensor,
         **options,
     )
+    again = after(again, mine_other)
+    pieces = [after(lax.ppermute(mine, "aux", pairs), token, *fars[-1:]) for pairs in plan[:-1]]
+    pieces.append(lax.ppermute(again, "aux", plan[-1]))
+    early = [mine_other, again]
+    for block in pieces[:-1]:
+        early += [block, lax.ppermute(block, "sub", swap)]
     sides, token_late = call(
         second,
         [((2 * rows, depth), BF16), ((8, 128), F32)],
@@ -315,40 +329,42 @@
         acc,
         *tensors,
         *fars,
+        *early[::2],
+        others=nob - 1,
         **options,
     )
-    held = []
-    for block in pieces:
-        held.append(after(block, token_late, mine_other, *held[-1:]))
-    pieces = held
-    others = [lax.ppermute(block, "sub", swap) for block in pieces]
+    last = after(pieces[-1], token_late)
+    last_other = lax.ppermute(last, "sub", swap)
     count = 1 + len(plan)
-    height = (count + 1) * rows_aux
     work = 8 * rows * depth * rows_aux
     wide = nt * rows_aux
-    direct, back = call(
+    shape = ((rows_aux, 2 * wide), F32)
+    scratch = lambda count: ((count, wide, block_aux), F32)
+    direct, back, *backs = call(
         meet_own,
-        [((height, wide), F32), ((height - block_aux, wide), F32)],
-        [((2 * height, depth), BF16)],
-        work * count * 2,
+        [(((2 * count - 1) * rows_aux, wide), F32), ((rows_aux, wide), F32)] + [shape] * (len(plan) - 1),
+        [((2 * (2 * count - 1) * rows_aux, depth), BF16), scratch(1)],
+        work * (2 * count - 1) * 2,
         sides,
         mine,
-        mine_other,
-        *pieces,
-    )
-    others, *backs = call(
+        *early[:1],
+        *early[2:],
+        last,
+    )
+    tensor, *last_back = call(
         meet_back,
-        [((2 * len(plan) * rows_aux, depth), BF16)] + [((rows_aux, 2 * wide), F32)] * len(plan),
-        [((len(plan), wide, block_aux), F32)],
-        work * len(plan),
+        [((2 * rows_aux, depth), BF16), shape],
+        [scratch(1)],
+        work,
         sides,
         back,
-        *others,
-    )
+        last_other,
+    )
+    backs += last_back
     returned = [lax.ppermute(back, "aux", ring(naux, i)) for i, back in enumerate(backs, 1)]
     shape = ((nt, block_aux, nauxf), F32)
     (direct,) = call(
-        meet_direct, [shape], [((count, wide, block_aux), F32)], work * len(plan), sides, direct, others, nt=nt, naux=naux
+        meet_direct, [shape], [scratch(count)], work, sides, direct, tensor, nt=nt, naux=naux
     )
     (partial_chi,) = call(complete, [shape], [], 0, direct, *returned)
     owners = nt * nob * nsub

time: 52.9 us -> 52 us (0.983)
  local copies, waits for them, and re-layouts: 2.48 us -> 1.27 us
  other arithmetic: 2.08 us -> 1.3 us
  starting transfers between devices: 15.4 us -> 16 us
  waiting for transfers between devices: 16.3 us -> 16.9 us
    ppermute x1, waiting for transfers between devices: 8.4 us -> 10.8 us  [local(): fars.append(lax.ppermute(near, ('orb', 'sub'), pairs))]
    unnamed x4 -> x8, local copies, waits for them, and re-layouts: 2.48 us -> 1.27 us
    ppermute x4, waiting for transfers between devices: 1.12 us -> 0.01 us  [the longest x1 0.01 us: local(): lax.ppermute(mine, 'aux', pairs)]
    another operation x2, other arithmetic: 0.79 us -> 0.02 us  [local(): jnp.stack([small] + [lax.ppermute(small, 'tau', ring(nt, shift)) for shif...]
    ppermute x2, waiting for transfers between devices: 3.94 us -> 3.29 us  [local(): lax.ppermute(back, 'aux', ring(naux, i))]
    ppermute x2, starting transfers between devices: 3.92 us -> 4.54 us  [local(): lax.ppermute(back, 'aux', ring(naux, i))]
  transfers between devices with their start and end apart: 10 -> 10, of which waited for: 6 -> 3; matrix products, arithmetic and copies ran while one was open for 3% -> 1% of each run, Pallas kernels for 12% -> 13%
where the time goes in v13:
time: 52 us; the launch traced here: 51.8 us
  waiting for transfers between devices  16.9 us (32%)
  starting transfers between devices  16 us (31%)
  blocking collectives  9.05 us (17%)
  Pallas kernels  7.13 us (14%)
  other arithmetic  1.3 us (2%)
  local copies, waits for them, and re-layouts  1.27 us (2%)
    ppermute x1, waiting for transfers between devices, local(): fars.append(lax.ppermute(near, ('orb', 'sub'), pairs))  10.8 us
    all_to_all x1, blocking collectives, local(): lax.all_to_all(partial_chi.reshape(owners, nt * block_aux // owners, naux...  9.05 us
    pallas_call x7, Pallas kernels, call(): pl.pallas_call(here, out_shape=shapes, in_specs=[VMEM] * len(arguments),...  7.12 us
    ppermute x2, starting transfers between devices, local(): lax.ppermute(back, 'aux', ring(naux, i))  4.54 us
    ppermute x1, starting transfers between devices, local(): pieces.append(lax.ppermute(again, 'aux', plan[-1]))  4.51 us
    ppermute x2, waiting for transfers between devices, local(): lax.ppermute(back, 'aux', ring(naux, i))  3.29 us
    ppermute x1, starting transfers between devices, local(): lax.ppermute(tensor, 'orb', ring(nob, shift))  2.94 us
    ppermute x1, waiting for transfers between devices, local(): lax.ppermute(small, 'tau', ring(nt, shift))  2.79 us
  transfers between devices with their start and end apart: 10, of which 3 were waited for; matrix products, arithmetic and copies ran while one was open for 1% of the time, Pallas kernels for 13%

profile of v13, /device:TPU:0, one launch (start us, length us, event | category | flops | bytes accessed | tf_op | source)
XLA Modules:
  0.0 51.8 jit_solution(6133177112430806711)
XLA Ops:
  0.0 2.9 %collective-permute-start.1 = (f32[128,2048]{1,0:T(8,128)}, f32[128,2048]{1,0:T(8,128)S(1)}, u32[]{:S(2)}, u32[]{:S(2)}) collective-permute-start(f32[128,2048]{1,0:T(8,128)} %bitcast.5), channel_id=1, source_target_pairs={{2,0},{0,2},{3,1},{1,3},{6,4},{4,6},{7,5},{5,7},{10,8},{8,10},{11,... | collective-permute-start | bytes 3145736 | tf_op jit(solution)/shard_map/ppermute | solution.py:283
  2.9 1.3 %copy-done = f32[1,1,2,64,2048]{4,3,2,1,0:T(8,128)S(1)} copy-done((f32[1,1,2,64,2048]{4,3,2,1,0:T(8,128)S(1)}, f32[1,1,2,64,2048]{4,3,2,1,0:T(8,128)}, u32[]{:S(2)}) %copy-start) | copy-done | bytes 1048600
  4.2 0.6 %prepare.1 = (f32[32,32,128]{2,1,0:T(8,128)S(1)}, f32[32,32,128]{2,1,0:T(8,128)S(1)}) custom-call(f32[128,2048]{1,0:T(8,128)S(1)} %bitcast.6), custom_call_target="tpu_custom_call" | custom-call | bytes 1048576 | tf_op jit(solution)/shard_map/prepare/pallas_call | solution.py:272
  4.8 0.1 collective-permute-start.3
  4.9 1.6 %collective-permute-start.4 = (f32[32,32,128]{2,1,0:T(8,128)S(1)}, f32[32,32,128]{2,1,0:T(8,128)S(1)}, u32[]{:S(2)}, u32[]{:S(2)}) collective-permute-start(f32[32,32,128]{2,1,0:T(8,128)S(1)} %get-tuple-element.17.refs_1_), channel_id=1, source_target_pairs={{0,4},{4,8},{8,12},{12,0},{1,5},{5,9},{9,13},{13,1},{2,6},{6,10},{... | collective-permute-start | bytes 1572872 | tf_op jit(solution)/shard_map/ppermute | solution.py:318
  6.5 0.7 %convert_element_type.5 = f32[1,2]{1,0:T(1,128)S(1)} convert(s32[1,2]{1,0:T(1,128)} %param.7) | non-fusion elementwise | flops 2 | bytes 16 | tf_op jit(solution)/shard_map/convert_element_type | solution.py:294
  7.2 0.0 collective-permute-done.3.refs_4_.refs_1_.refs_2_
  7.2 4.5 %collective-permute-start.6 = (f32[32,32,128]{2,1,0:T(8,128)S(1)}, f32[32,32,128]{2,1,0:T(8,128)S(1)}, u32[]{:S(2)}, u32[]{:S(2)}) collective-permute-start(f32[32,32,128]{2,1,0:T(8,128)S(1)} %after.4), channel_id=1, source_target_pairs={{0,8},{12,4},{1,9},{13,5},{2,10},{14,6},{3,11},{15,7},{16,24},{28,... | collective-permute-start | bytes 1572872 | tf_op jit(solution)/shard_map/ppermute | solution.py:319
  11.7 0.0 copy-done.2
  11.7 1.6 %collective-permute-start = (f32[136,128]{1,0:T(8,128)S(1)}, f32[136,128]{1,0:T(8,128)S(1)}, u32[]{:S(2)}, u32[]{:S(2)}) collective-permute-start(f32[136,128]{1,0:T(8,128)S(1)} %get-tuple-element.28), channel_id=1, source_target_pairs={{16,0},{0,16},{17,1},{1,17},{18,2},{2,18},{19,3},{3,19},{20,4},{4,... | collective-permute-start | bytes 208904 | tf_op jit(solution)/shard_map/ppermute | solution.py:297
  13.3 2.8 %collective-permute-done = f32[136,128]{1,0:T(8,128)S(1)} collective-permute-done((f32[136,128]{1,0:T(8,128)S(1)}, f32[136,128]{1,0:T(8,128)S(1)}, u32[]{:S(2)}, u32[]{:S(2)}) %collective-permute-start) | collective-permute-done | bytes 69664 | tf_op jit(solution)/shard_map/ppermute | solution.py:297
  16.1 0.1 collective-permute-start.2
  16.2 1.5 %first.1 = (f32[4,512,256]{2,1,0:T(8,128)S(1)}, f32[8,128]{1,0:T(8,128)S(1)}) custom-call(f32[2,136,128]{2,1,0:T(8,128)S(1)} %pad_maximum_fusion.refs_0_, f32[128,2048]{1,0:T(8,128)S(1)} %bitcast.7), custom_call_target="tpu_custom_call" | custom-call | flops 603979776 | bytes 1187840 | tf_op jit(solution)/shard_map/first/pallas_call | solution.py:272
  17.7 10.8 %collective-permute-done.2.refs_2_.refs_3_ = f32[2,136,128]{2,1,0:T(8,128)S(1)} collective-permute-done((f32[2,136,128]{2,1,0:T(8,128)S(1)}, f32[2,136,128]{2,1,0:T(8,128)S(1)}, u32[]{:S(2)}, u32[]{:S(2)}) %collective-permute-start.2) | collective-permute-done | bytes 139296 | tf_op jit(solution)/shard_map/ppermute | solution.py:301
  28.6 0.0 collective-permute-done.4.refs_0_
  28.6 0.6 %collective-permute-start.5 = (f32[32,32,128]{2,1,0:T(8,128)S(1)}, f32[32,32,128]{2,1,0:T(8,128)S(1)}, u32[]{:S(2)}, u32[]{:S(2)}) collective-permute-start(f32[32,32,128]{2,1,0:T(8,128)S(1)} %after.3.refs_5_.refs_3_), channel_id=1, source_target_pairs={{1,0},{0,1},{3,2},{2,3},{5,4},{4,5},{7,6},{6,7},{9,8},{8,9},{11,10... | collective-permute-start | bytes 1572872 | tf_op jit(solution)/shard_map/ppermute | solution.py:322
  29.1 0.0 collective-permute-done.1.refs_2_
  29.1 1.7 %second.1 = (bf16[256,4096]{1,0:T(8,128)(2,1)S(1)}, f32[8,128]{1,0:T(8,128)S(1)}) custom-call(f32[2,136,128]{2,1,0:T(8,128)S(1)} %pad_maximum_fusion.refs_0_, f32[4,512,256]{2,1,0:T(8,128)S(1)} %get-tuple-element.16.refs_1_, f32[128,2048]{1,0:T(8,128)S(1)} %collective-permute-done.1.refs_2_, f32[2,136,128]{2,1,0:T(8,128)S(1)} %collective-permute-done.2.refs_2_.refs_3_, ...), custom_call_target="tpu_custom_call" | custom-call | flops 603979776 | bytes 4472832 | tf_op jit(solution)/shard_map/second/pallas_call | solution.py:272
  30.9 0.0 collective-permute-done.6.refs_0_
  30.9 0.1 collective-permute-start.7
  31.0 0.0 collective-permute-done.5.refs_4_
  31.0 1.5 %meet_own.1 = (f32[160,64]{1,0:T(8,128)S(1)}, f32[32,64]{1,0:T(8,128)S(1)}, f32[32,128]{1,0:T(8,128)S(1)}) custom-call(bf16[256,4096]{1,0:T(8,128)(2,1)S(1)} %get-tuple-element.19.refs_0_, f32[32,32,128]{2,1,0:T(8,128)S(1)} %get-tuple-element.17.refs_1_, f32[32,32,128]{2,1,0:T(8,128)S(1)} %collective-permute-done.3.refs_4_.refs_1_.refs_2_, ...), custom_call_target="tpu_custom_call" | custom-call | flops 1342177280 | bytes 6815744 | tf_op jit(solution)/shard_map/meet_own/pallas_call | solution.py:272
  32.5 3.9 %collective-permute-start.8 = (f32[32,128]{1,0:T(8,128)S(1)}, f32[32,128]{1,0:T(8,128)S(1)}, u32[]{:S(2)}, u32[]{:S(2)}) collective-permute-start(f32[32,128]{1,0:T(8,128)S(1)} %get-tuple-element.25), channel_id=1, source_target_pairs={{4,0},{8,4},{12,8},{0,12},{5,1},{9,5},{13,9},{1,13},{6,2},{10,6},{... | collective-permute-start | bytes 49160 | tf_op jit(solution)/shard_map/ppermute | solution.py:364
  36.4 0.0 collective-permute-done.7.refs_2_
  36.4 0.7 %meet_back.1 = (bf16[64,4096]{1,0:T(8,128)(2,1)S(1)}, f32[32,128]{1,0:T(8,128)S(1)}) custom-call(bf16[256,4096]{1,0:T(8,128)(2,1)S(1)} %get-tuple-element.19.refs_0_, f32[32,64]{1,0:T(8,128)S(1)} %get-tuple-element.23.refs_1_, f32[32,32,128]{2,1,0:T(8,128)S(1)} %collective-permute-done.7.refs_2_), custom_call_target="tpu_custom_call" | custom-call | flops 134217728 | bytes 4726784 | tf_op jit(solution)/shard_map/meet_back/pallas_call | solution.py:272
  37.1 0.7 %collective-permute-start.9 = (f32[32,128]{1,0:T(8,128)S(1)}, f32[32,128]{1,0:T(8,128)S(1)}, u32[]{:S(2)}, u32[]{:S(2)}) collective-permute-start(f32[32,128]{1,0:T(8,128)S(1)} %get-tuple-element.26), channel_id=1, source_target_pairs={{8,0},{12,4},{0,8},{4,12},{9,1},{13,5},{1,9},{5,13},{10,2},{14,6},... | collective-permute-start | bytes 49160 | tf_op jit(solution)/shard_map/ppermute | solution.py:364
  37.8 0.7 %meet_direct.1.refs_0_ = f32[2,64,256]{2,1,0:T(8,128)S(1)} custom-call(bf16[256,4096]{1,0:T(8,128)(2,1)S(1)} %get-tuple-element.19.refs_0_, f32[160,64]{1,0:T(8,128)S(1)} %get-tuple-element.22.refs_1_, bf16[64,4096]{1,0:T(8,128)(2,1)S(1)} %get-tuple-element.24.refs_2_), custom_call_target="tpu_custom_call" | custom-call | flops 134217728 | bytes 5283840 | tf_op jit(solution)/shard_map/meet_direct/pallas_call | solution.py:272
  38.5 0.0 collective-permute-done.8.refs_1_
  38.5 3.3 %collective-permute-done.9.refs_2_ = f32[32,128]{1,0:T(8,128)S(1)} collective-permute-done((f32[32,128]{1,0:T(8,128)S(1)}, f32[32,128]{1,0:T(8,128)S(1)}, u32[]{:S(2)}, u32[]{:S(2)}) %collective-permute-start.9) | collective-permute-done | bytes 16416 | tf_op jit(solution)/shard_map/ppermute | solution.py:364
  41.8 0.3 complete.1
  42.2 9.1 %all_to_all.5 = f32[8,16,256]{2,1,0:T(8,128)S(1)} all-to-all(f32[8,16,256]{2,1,0:T(8,128)S(1)} %bitcast.8), channel_id=1, replica_groups=mesh['tau'=2,'aux'=4,'orb'=2,'sub'=2] {'tau','orb','sub'}, dimensions={0} | all-to-all | bytes 262144 | tf_op jit(solution)/shard_map/all_to_all | solution.py:371
  51.2 0.6 %broadcast_multiply_fusion = f32[16,256]{1,0:T(8,128)} fusion(f32[16,256]{1,0:T(8,128)S(1)} %reduce_sum.9), kind=kLoop, calls=%fused_computation.3 | loop fusion | flops 4096 | bytes 32768 | tf_op jit(solution)/shard_map/mul | solution.py:378
  (12 shorter events, 0.0 us)
Async XLA Ops:
  0.0 29.1 %collective-permute-start.1 = (f32[128,2048]{1,0:T(8,128)}, f32[128,2048]{1,0:T(8,128)S(1)}, u32[]{:S(2)}, u32[]{:S(2)}) collective-permute-start(f32[128,2048]{1,0:T(8,128)} %bitcast.5), channel_id=1, source_target_pairs={{2,0},{0,2},{3,1},{1,3},{6,4},{4,6},{7,5},{5,7},{10,8},{8,10},{11,... | collective-permute-start | bytes 3145736 | tf_op jit(solution)/shard_map/ppermute | solution.py:283
  2.9 1.3 %copy-start = (f32[1,1,2,64,2048]{4,3,2,1,0:T(8,128)S(1)}, f32[1,1,2,64,2048]{4,3,2,1,0:T(8,128)}, u32[]{:S(2)}) copy-start(f32[1,1,2,64,2048]{4,3,2,1,0:T(8,128)} %param.4) | copy-start | bytes 3145732
  4.2 7.5 %copy-start.2 = (f32[64,128]{1,0:T(8,128)S(1)}, f32[64,128]{1,0:T(8,128)}, u32[]{:S(2)}) copy-start(f32[64,128]{1,0:T(8,128)} %param.6) | copy-start | bytes 98308
  4.2 7.5 %copy-start.3 = (f32[64,128]{1,0:T(8,128)S(1)}, f32[64,128]{1,0:T(8,128)}, u32[]{:S(2)}) copy-start(f32[64,128]{1,0:T(8,128)} %param.5) | copy-start | bytes 98308
  4.2 12.0 %copy-start.1 = (f32[1,1,2,64,2048]{4,3,2,1,0:T(8,128)S(1)}, f32[1,1,2,64,2048]{4,3,2,1,0:T(8,128)}, u32[]{:S(2)}) copy-start(f32[1,1,2,64,2048]{4,3,2,1,0:T(8,128)} %param.4) | copy-start | bytes 3145732
  4.8 2.4 %collective-permute-start.3 = (f32[32,32,128]{2,1,0:T(8,128)S(1)}, f32[32,32,128]{2,1,0:T(8,128)S(1)}, u32[]{:S(2)}, u32[]{:S(2)}) collective-permute-start(f32[32,32,128]{2,1,0:T(8,128)S(1)} %get-tuple-element.17.refs_1_), channel_id=1, source_target_pairs={{1,0},{0,1},{3,2},{2,3},{5,4},{4,5},{7,6},{6,7},{9,8},{8,9},{11,10... | collective-permute-start | bytes 1572872 | tf_op jit(solution)/shard_map/ppermute | solution.py:289
  4.9 23.7 %collective-permute-start.4 = (f32[32,32,128]{2,1,0:T(8,128)S(1)}, f32[32,32,128]{2,1,0:T(8,128)S(1)}, u32[]{:S(2)}, u32[]{:S(2)}) collective-permute-start(f32[32,32,128]{2,1,0:T(8,128)S(1)} %get-tuple-element.17.refs_1_), channel_id=1, source_target_pairs={{0,4},{4,8},{8,12},{12,0},{1,5},{5,9},{9,13},{13,1},{2,6},{6,10},{... | collective-permute-start | bytes 1572872 | tf_op jit(solution)/shard_map/ppermute | solution.py:318
  7.2 23.7 %collective-permute-start.6 = (f32[32,32,128]{2,1,0:T(8,128)S(1)}, f32[32,32,128]{2,1,0:T(8,128)S(1)}, u32[]{:S(2)}, u32[]{:S(2)}) collective-permute-start(f32[32,32,128]{2,1,0:T(8,128)S(1)} %after.4), channel_id=1, source_target_pairs={{0,8},{12,4},{1,9},{13,5},{2,10},{14,6},{3,11},{15,7},{16,24},{28,... | collective-permute-start | bytes 1572872 | tf_op jit(solution)/shard_map/ppermute | solution.py:319
  11.7 4.4 %collective-permute-start = (f32[136,128]{1,0:T(8,128)S(1)}, f32[136,128]{1,0:T(8,128)S(1)}, u32[]{:S(2)}, u32[]{:S(2)}) collective-permute-start(f32[136,128]{1,0:T(8,128)S(1)} %get-tuple-element.28), channel_id=1, source_target_pairs={{16,0},{0,16},{17,1},{1,17},{18,2},{2,18},{19,3},{3,19},{20,4},{4,... | collective-permute-start | bytes 208904 | tf_op jit(solution)/shard_map/ppermute | solution.py:297
  16.1 12.4 %collective-permute-start.2 = (f32[2,136,128]{2,1,0:T(8,128)S(1)}, f32[2,136,128]{2,1,0:T(8,128)S(1)}, u32[]{:S(2)}, u32[]{:S(2)}) collective-permute-start(f32[2,136,128]{2,1,0:T(8,128)S(1)} %pad_maximum_fusion.refs_0_), channel_id=1, source_target_pairs={{2,1},{3,0},{0,3},{1,2},{6,5},{7,4},{4,7},{5,6},{10,9},{11,8},{8,1... | collective-permute-start | bytes 417800 | tf_op jit(solution)/shard_map/ppermute | solution.py:301
  28.6 2.4 %collective-permute-start.5 = (f32[32,32,128]{2,1,0:T(8,128)S(1)}, f32[32,32,128]{2,1,0:T(8,128)S(1)}, u32[]{:S(2)}, u32[]{:S(2)}) collective-permute-start(f32[32,32,128]{2,1,0:T(8,128)S(1)} %after.3.refs_5_.refs_3_), channel_id=1, source_target_pairs={{1,0},{0,1},{3,2},{2,3},{5,4},{4,5},{7,6},{6,7},{9,8},{8,9},{11,10... | collective-permute-start | bytes 1572872 | tf_op jit(solution)/shard_map/ppermute | solution.py:322
  30.9 5.5 %collective-permute-start.7 = (f32[32,32,128]{2,1,0:T(8,128)S(1)}, f32[32,32,128]{2,1,0:T(8,128)S(1)}, u32[]{:S(2)}, u32[]{:S(2)}) collective-permute-start(f32[32,32,128]{2,1,0:T(8,128)S(1)} %after.5.refs_5_), channel_id=1, source_target_pairs={{1,0},{0,1},{3,2},{2,3},{5,4},{4,5},{7,6},{6,7},{9,8},{8,9},{11,10... | collective-permute-start | bytes 1572872 | tf_op jit(solution)/shard_map/ppermute | solution.py:337
  32.5 6.0 %collective-permute-start.8 = (f32[32,128]{1,0:T(8,128)S(1)}, f32[32,128]{1,0:T(8,128)S(1)}, u32[]{:S(2)}, u32[]{:S(2)}) collective-permute-start(f32[32,128]{1,0:T(8,128)S(1)} %get-tuple-element.25), channel_id=1, source_target_pairs={{4,0},{8,4},{12,8},{0,12},{5,1},{9,5},{13,9},{1,13},{6,2},{10,6},{... | collective-permute-start | bytes 49160 | tf_op jit(solution)/shard_map/ppermute | solution.py:364
  37.1 4.7 %collective-permute-start.9 = (f32[32,128]{1,0:T(8,128)S(1)}, f32[32,128]{1,0:T(8,128)S(1)}, u32[]{:S(2)}, u32[]{:S(2)}) collective-permute-start(f32[32,128]{1,0:T(8,128)S(1)} %get-tuple-element.26), channel_id=1, source_target_pairs={{8,0},{12,4},{0,8},{4,12},{9,1},{13,5},{1,9},{5,13},{10,2},{14,6},... | collective-permute-start | bytes 49160 | tf_op jit(solution)/shard_map/ppermute | solution.py:364

commit v14 on v13

--- a/solution.py
+++ b/solution.py
@@ -42,6 +42,12 @@
         rows = turned[pl.ds(start + at, some, stride=turned.shape[0] // some), :]
         mine[at] = rows
         again[at] = rows
+
+
+def halve(place, block, token, *outs):
+    some = outs[0].shape[0]
+    for i, out in enumerate(outs):
+        out[...] = block[i * some : (i + 1) * some]
 
 
 def after(block, *tokens):
@@ -150,12 +156,15 @@
 
 
 def relay(pieces, tensor):
-    share, half, listed = pieces[0].shape
-    for i, source in enumerate(pieces):
-        for at in range(share):
-            high, low = halves(source[at])
-            tensor[2 * i * half : (2 * i + 1) * half, at * listed : (at + 1) * listed] = high
-            tensor[(2 * i + 1) * half : 2 * (i + 1) * half, at * listed : (at + 1) * listed] = low
+    for i, parts in enumerate(pieces):
+        at = 0
+        for part in parts:
+            per, half, listed = part.shape
+            for inner in range(per):
+                high, low = halves(part[inner])
+                tensor[2 * i * half : (2 * i + 1) * half, at * listed : (at + 1) * listed] = high
+                tensor[(2 * i + 1) * half : 2 * (i + 1) * half, at * listed : (at + 1) * listed] = low
+                at += 1
 
 
 def products(tensor, side, half):
@@ -195,10 +204,10 @@
     return jnp.concatenate([back[:half], back[half:]], axis=1)
 
 
-def meet_own(place, sides, *refs):
-    count = (len(refs) - 4) // 3
-    pieces, (direct, back, *backs, tensor, ordered) = refs[: 2 * count + 1], refs[2 * count + 1 :]
-    half = pieces[0].shape[1]
+def meet_own(place, sides, *refs, count):
+    refs, (direct, back, *backs, tensor, ordered) = refs[: 4 * count - 1], refs[4 * count - 1 :]
+    pieces = [refs[:1], refs[1:2]] + [refs[i : i + 2] for i in range(2, 4 * count - 2, 2)] + [refs[-1:]]
+    half = refs[0].shape[1]
     rows = sides.shape[0] // 2
     relay(pieces, tensor)
     direct[...] = products(tensor[...], sides[:rows, :], half)
@@ -212,7 +221,7 @@
 
 def meet_back(place, sides, own, piece, tensor, back_ref, ordered):
     half = piece.shape[1]
-    relay([piece], tensor)
+    relay([[piece]], tensor)
     other = products(tensor[...], sides[sides.shape[0] // 2 :, :], half)
     back_ref[...] = fold(place, own[...], other, ordered)
 
@@ -295,11 +304,6 @@
         ]
     )
     near = jnp.stack([small] + [lax.ppermute(small, "tau", ring(nt, shift)) for shift in range(1, nt)])
-    fars = []
-    for shift in range(1, nob):
-        pairs = [(a * nsub + c, b * nsub + (c + 1) % nsub) for a, b in ring(nob, shift) for c in range(nsub)]
-        fars.append(lax.ppermute(near, ("orb", "sub"), pairs))
-
     groups = 2 * nt
     work = 6 * groups * share * columns * listed * 3
     rows = groups * rows_aux
@@ -314,12 +318,19 @@
         tensor,
         **options,
     )
-    again = after(again, mine_other)
-    pieces = [after(lax.ppermute(mine, "aux", pairs), token, *fars[-1:]) for pairs in plan[:-1]]
-    pieces.append(lax.ppermute(again, "aux", plan[-1]))
-    early = [mine_other, again]
-    for block in pieces[:-1]:
-        early += [block, lax.ppermute(block, "sub", swap)]
+    again = after(again, token)
+    early = [mine_other]
+    for pairs in plan[:-1]:
+        parts = call(
+            halve, [((share // 2, rows_aux, listed), F32)] * 2, [], 0, lax.ppermute(mine, "aux", pairs), token
+        )
+        early += [*parts, *(lax.ppermute(part, "sub", swap) for part in parts)]
+    last = lax.ppermute(again, "aux", plan[-1])
+    fars = []
+    late_near = after(near, *early)
+    for shift in range(1, nob):
+        pairs = [(a * nsub + c, b * nsub + (c + 1) % nsub) for a, b in ring(nob, shift) for c in range(nsub)]
+        fars.append(lax.ppermute(late_near, ("orb", "sub"), pairs))
     sides, token_late = call(
         second,
         [((2 * rows, depth), BF16), ((8, 128), F32)],
@@ -329,11 +340,11 @@
         acc,
         *tensors,
         *fars,
-        *early[::2],
+        *early,
         others=nob - 1,
         **options,
     )
-    last = after(pieces[-1], token_late)
+    last = after(last, token_late)
     last_other = lax.ppermute(last, "sub", swap)
     count = 1 + len(plan)
     work = 8 * rows * depth * rows_aux
@@ -347,9 +358,9 @@
         work * (2 * count - 1) * 2,
         sides,
         mine,
-        *early[:1],
-        *early[2:],
+        *early,
         last,
+        count=len(plan),
     )
     tensor, *last_back = call(
         meet_back,

time: 52 us -> 55.3 us (1.063)
  starting transfers between devices: 16 us -> 22.3 us
  waiting for transfers between devices: 16.9 us -> 14 us
  blocking collectives: 9.05 us -> 8.14 us
  other arithmetic: 1.3 us -> 2.07 us
    ppermute x2, starting transfers between devices: 4.54 us -> 10.9 us  [local(): lax.ppermute(back, 'aux', ring(naux, i))]
    ppermute x3 -> x4, waiting for transfers between devices: 10.8 us -> 7.01 us  [the longest x1 5.63 us: local(): fars.append(lax.ppermute(late_near, ('orb', 'sub'), pairs))]
    ppermute x1, waiting for transfers between devices: 0.01 us -> 3.2 us  [local(): lax.ppermute(mine, 'aux', pairs)]
    ppermute x2, waiting for transfers between devices: 3.29 us -> 0.97 us  [local(): lax.ppermute(back, 'aux', ring(naux, i))]
    all_to_all x1, blocking collectives: 9.05 us -> 8.14 us  [local(): lax.all_to_all(partial_chi.reshape(owners, nt * block_aux // owners, naux...]
    another operation x2, other arithmetic: 0.02 us -> 0.79 us  [local(): jnp.stack([small] + [lax.ppermute(small, 'tau', ring(nt, shift)) for shif...]
    ppermute x3 -> x4, starting transfers between devices: 5.15 us -> 5.12 us  [the longest x1 4.53 us: local(): last = lax.ppermute(again, 'aux', plan[-1])]
    pallas_call x7 -> x8, Pallas kernels: 7.12 us -> 7.14 us  [call(): pl.pallas_call(here, out_shape=shapes, in_specs=[VMEM] * len(arguments),...]
  transfers between devices with their start and end apart: 10 -> 11, of which waited for: 3 -> 6; matrix products, arithmetic and copies ran while one was open for 1% -> 3% of each run, Pallas kernels for 13% -> 12%
where the time goes in v14:
time: 55.3 us; the launch traced here: 55.1 us
  starting transfers between devices  22.3 us (40%)
  waiting for transfers between devices  14 us (25%)
  blocking collectives  8.14 us (15%)
  Pallas kernels  7.15 us (13%)
  other arithmetic  2.07 us (4%)
  local copies, waits for them, and re-layouts  1.27 us (2%)
    ppermute x2, starting transfers between devices, local(): lax.ppermute(back, 'aux', ring(naux, i))  10.9 us
    all_to_all x1, blocking collectives, local(): lax.all_to_all(partial_chi.reshape(owners, nt * block_aux // owners, naux...  8.14 us
    pallas_call x8, Pallas kernels, call(): pl.pallas_call(here, out_shape=shapes, in_specs=[VMEM] * len(arguments),...  7.14 us
    ppermute x1, waiting for transfers between devices, local(): fars.append(lax.ppermute(late_near, ('orb', 'sub'), pairs))  5.63 us
    ppermute x1, starting transfers between devices, local(): last = lax.ppermute(again, 'aux', plan[-1])  4.53 us
    ppermute x1, waiting for transfers between devices, local(): lax.ppermute(mine, 'aux', pairs)  3.2 us
    ppermute x1, starting transfers between devices, local(): lax.ppermute(tensor, 'orb', ring(nob, shift))  2.94 us
    ppermute x1, waiting for transfers between devices, local(): lax.ppermute(small, 'tau', ring(nt, shift))  2.79 us
  transfers between devices with their start and end apart: 11, of which 6 were waited for; matrix products, arithmetic and copies ran while one was open for 3% of the time, Pallas kernels for 12%

profile of v14, /device:TPU:0, one launch (start us, length us, event | category | flops | bytes accessed | tf_op | source)
XLA Modules:
  0.0 55.1 jit_solution(1840441700103887977)
XLA Ops:
  0.0 2.9 %collective-permute-start.1 = (f32[128,2048]{1,0:T(8,128)}, f32[128,2048]{1,0:T(8,128)S(1)}, u32[]{:S(2)}, u32[]{:S(2)}) collective-permute-start(f32[128,2048]{1,0:T(8,128)} %bitcast.5), channel_id=1, source_target_pairs={{2,0},{0,2},{3,1},{1,3},{6,4},{4,6},{7,5},{5,7},{10,8},{8,10},{11,... | collective-permute-start | bytes 3145736 | tf_op jit(solution)/shard_map/ppermute | solution.py:292
  2.9 1.3 %copy-done = f32[1,1,2,64,2048]{4,3,2,1,0:T(8,128)S(1)} copy-done((f32[1,1,2,64,2048]{4,3,2,1,0:T(8,128)S(1)}, f32[1,1,2,64,2048]{4,3,2,1,0:T(8,128)}, u32[]{:S(2)}) %copy-start) | copy-done | bytes 1048600
  4.2 0.6 %prepare.1 = (f32[32,32,128]{2,1,0:T(8,128)S(1)}, f32[32,32,128]{2,1,0:T(8,128)S(1)}) custom-call(f32[128,2048]{1,0:T(8,128)S(1)} %bitcast.6), custom_call_target="tpu_custom_call" | custom-call | bytes 1048576 | tf_op jit(solution)/shard_map/prepare/pallas_call | solution.py:281
  4.8 1.6 %collective-permute-start.3 = (f32[32,32,128]{2,1,0:T(8,128)S(1)}, f32[32,32,128]{2,1,0:T(8,128)S(1)}, u32[]{:S(2)}, u32[]{:S(2)}) collective-permute-start(f32[32,32,128]{2,1,0:T(8,128)S(1)} %get-tuple-element.19.refs_1_), channel_id=1, source_target_pairs={{0,4},{4,8},{8,12},{12,0},{1,5},{5,9},{9,13},{13,1},{2,6},{6,10},{... | collective-permute-start | bytes 1572872 | tf_op jit(solution)/shard_map/ppermute | solution.py:325
  6.4 0.7 %convert_element_type.5 = f32[1,2]{1,0:T(1,128)S(1)} convert(s32[1,2]{1,0:T(1,128)} %param.7) | non-fusion elementwise | flops 2 | bytes 16 | tf_op jit(solution)/shard_map/convert_element_type | solution.py:303
  7.1 0.8 %fusion = (f32[1,136,128]{2,1,0:T(8,128)S(1)}, f32[136,128]{1,0:T(8,128)S(1)}) fusion(f32[1,2]{1,0:T(1,128)S(1)} %convert_element_type.5, f32[64,128]{1,0:T(8,128)} %param.6, f32[64,128]{1,0:T(8,128)} %param.5), kind=kLoop, calls=%fused_computation.4 | loop fusion | flops 69632 | bytes 204808 | tf_op jit(solution)/shard_map/stack | solution.py:306
  7.9 1.6 %collective-permute-start = (f32[136,128]{1,0:T(8,128)S(1)}, f32[136,128]{1,0:T(8,128)S(1)}, u32[]{:S(2)}, u32[]{:S(2)}) collective-permute-start(f32[136,128]{1,0:T(8,128)S(1)} %get-tuple-element.32), channel_id=1, source_target_pairs={{16,0},{0,16},{17,1},{1,17},{18,2},{2,18},{19,3},{3,19},{20,4},{4,... | collective-permute-start | bytes 208904 | tf_op jit(solution)/shard_map/ppermute | solution.py:306
  9.5 0.0 collective-permute-start.2
  9.5 2.8 %collective-permute-done = f32[136,128]{1,0:T(8,128)S(1)} collective-permute-done((f32[136,128]{1,0:T(8,128)S(1)}, f32[136,128]{1,0:T(8,128)S(1)}, u32[]{:S(2)}, u32[]{:S(2)}) %collective-permute-start) | collective-permute-done | bytes 69664 | tf_op jit(solution)/shard_map/ppermute | solution.py:306
  12.3 1.5 %first.1 = (f32[4,512,256]{2,1,0:T(8,128)S(1)}, f32[8,128]{1,0:T(8,128)S(1)}) custom-call(f32[2,136,128]{2,1,0:T(8,128)S(1)} %pad_maximum_fusion.refs_0_, f32[128,2048]{1,0:T(8,128)S(1)} %bitcast.7), custom_call_target="tpu_custom_call" | custom-call | flops 603979776 | bytes 1187840 | tf_op jit(solution)/shard_map/first/pallas_call | solution.py:281
  13.8 4.5 %collective-permute-start.7 = (f32[32,32,128]{2,1,0:T(8,128)S(1)}, f32[32,32,128]{2,1,0:T(8,128)S(1)}, u32[]{:S(2)}, u32[]{:S(2)}) collective-permute-start(f32[32,32,128]{2,1,0:T(8,128)S(1)} %after.4), channel_id=1, source_target_pairs={{0,8},{12,4},{1,9},{13,5},{2,10},{14,6},{3,11},{15,7},{16,24},{28,... | collective-permute-start | bytes 1572872 | tf_op jit(solution)/shard_map/ppermute | solution.py:328
  18.3 3.2 %collective-permute-done.3.refs_0_ = f32[32,32,128]{2,1,0:T(8,128)S(1)} collective-permute-done((f32[32,32,128]{2,1,0:T(8,128)S(1)}, f32[32,32,128]{2,1,0:T(8,128)S(1)}, u32[]{:S(2)}, u32[]{:S(2)}) %collective-permute-start.3) | collective-permute-done | bytes 524320 | tf_op jit(solution)/shard_map/ppermute | solution.py:325
  21.5 0.1 collective-permute-start.4
  21.6 0.5 collective-permute-start.5
  22.1 0.0 collective-permute-done.2.refs_1_.refs_4_.refs_2_
  22.1 1.0 %collective-permute-done.4.refs_4_.refs_7_.refs_5_ = f32[16,32,128]{2,1,0:T(8,128)S(1)} collective-permute-done((f32[16,32,128]{2,1,0:T(8,128)S(1)}, f32[16,32,128]{2,1,0:T(8,128)S(1)}, u32[]{:S(2)}, u32[]{:S(2)}) %collective-permute-start.4) | collective-permute-done | bytes 262176 | tf_op jit(solution)/shard_map/ppermute | solution.py:327
  23.1 0.4 collective-permute-done.5.refs_5_.refs_8_.refs_6_
  23.5 0.0 collective-permute-start.6
  23.5 5.6 %collective-permute-done.6.refs_3_ = f32[2,136,128]{2,1,0:T(8,128)S(1)} collective-permute-done((f32[2,136,128]{2,1,0:T(8,128)S(1)}, f32[2,136,128]{2,1,0:T(8,128)S(1)}, u32[]{:S(2)}, u32[]{:S(2)}) %collective-permute-start.6) | collective-permute-done | bytes 139296 | tf_op jit(solution)/shard_map/ppermute | solution.py:333
  29.2 0.0 collective-permute-done.1.refs_2_
  29.2 1.7 %second.1 = (bf16[256,4096]{1,0:T(8,128)(2,1)S(1)}, f32[8,128]{1,0:T(8,128)S(1)}) custom-call(f32[2,136,128]{2,1,0:T(8,128)S(1)} %pad_maximum_fusion.refs_0_, f32[4,512,256]{2,1,0:T(8,128)S(1)} %get-tuple-element.18.refs_1_, f32[128,2048]{1,0:T(8,128)S(1)} %collective-permute-done.1.refs_2_, f32[2,136,128]{2,1,0:T(8,128)S(1)} %collective-permute-done.6.refs_3_, ...), custom_call_target="tpu_custom_call" | custom-call | flops 603979776 | bytes 4997120 | tf_op jit(solution)/shard_map/second/pallas_call | solution.py:281
  30.9 0.2 collective-permute-start.8
  31.2 1.5 %meet_own.1 = (f32[160,64]{1,0:T(8,128)S(1)}, f32[32,64]{1,0:T(8,128)S(1)}, f32[32,128]{1,0:T(8,128)S(1)}) custom-call(bf16[256,4096]{1,0:T(8,128)(2,1)S(1)} %get-tuple-element.23.refs_0_, f32[32,32,128]{2,1,0:T(8,128)S(1)} %get-tuple-element.19.refs_1_, f32[32,32,128]{2,1,0:T(8,128)S(1)} %collective-permute-done.2.refs_1_.refs_4_.refs_2_, ...), custom_call_target="tpu_custom_call" | custom-call | flops 1342177280 | bytes 6815744 | tf_op jit(solution)/shard_map/meet_own/pallas_call | solution.py:281
  32.7 3.7 %collective-permute-start.9 = (f32[32,128]{1,0:T(8,128)S(1)}, f32[32,128]{1,0:T(8,128)S(1)}, u32[]{:S(2)}, u32[]{:S(2)}) collective-permute-start(f32[32,128]{1,0:T(8,128)S(1)} %get-tuple-element.29), channel_id=1, source_target_pairs={{4,0},{8,4},{12,8},{0,12},{5,1},{9,5},{13,9},{1,13},{6,2},{10,6},{... | collective-permute-start | bytes 49160 | tf_op jit(solution)/shard_map/ppermute | solution.py:375
  36.4 0.7 %meet_back.1 = (bf16[64,4096]{1,0:T(8,128)(2,1)S(1)}, f32[32,128]{1,0:T(8,128)S(1)}) custom-call(bf16[256,4096]{1,0:T(8,128)(2,1)S(1)} %get-tuple-element.23.refs_0_, f32[32,64]{1,0:T(8,128)S(1)} %get-tuple-element.27.refs_1_, f32[32,32,128]{2,1,0:T(8,128)S(1)} %collective-permute-done.8.refs_2_), custom_call_target="tpu_custom_call" | custom-call | flops 134217728 | bytes 4726784 | tf_op jit(solution)/shard_map/meet_back/pallas_call | solution.py:281
  37.1 7.2 %collective-permute-start.10 = (f32[32,128]{1,0:T(8,128)S(1)}, f32[32,128]{1,0:T(8,128)S(1)}, u32[]{:S(2)}, u32[]{:S(2)}) collective-permute-start(f32[32,128]{1,0:T(8,128)S(1)} %get-tuple-element.30), channel_id=1, source_target_pairs={{8,0},{12,4},{0,8},{4,12},{9,1},{13,5},{1,9},{5,13},{10,2},{14,6},... | collective-permute-start | bytes 49160 | tf_op jit(solution)/shard_map/ppermute | solution.py:375
  44.3 0.7 %meet_direct.1.refs_0_ = f32[2,64,256]{2,1,0:T(8,128)S(1)} custom-call(bf16[256,4096]{1,0:T(8,128)(2,1)S(1)} %get-tuple-element.23.refs_0_, f32[160,64]{1,0:T(8,128)S(1)} %get-tuple-element.26.refs_1_, bf16[64,4096]{1,0:T(8,128)(2,1)S(1)} %get-tuple-element.28.refs_2_), custom_call_target="tpu_custom_call" | custom-call | flops 134217728 | bytes 5283840 | tf_op jit(solution)/shard_map/meet_direct/pallas_call | solution.py:281
  45.0 0.0 collective-permute-done.9.refs_1_
  45.0 1.0 %collective-permute-done.10.refs_2_ = f32[32,128]{1,0:T(8,128)S(1)} collective-permute-done((f32[32,128]{1,0:T(8,128)S(1)}, f32[32,128]{1,0:T(8,128)S(1)}, u32[]{:S(2)}, u32[]{:S(2)}) %collective-permute-start.10) | collective-permute-done | bytes 16416 | tf_op jit(solution)/shard_map/ppermute | solution.py:375
  46.0 0.3 complete.1
  46.3 8.1 %all_to_all.5 = f32[8,16,256]{2,1,0:T(8,128)S(1)} all-to-all(f32[8,16,256]{2,1,0:T(8,128)S(1)} %bitcast.8), channel_id=1, replica_groups=mesh['tau'=2,'aux'=4,'orb'=2,'sub'=2] {'tau','orb','sub'}, dimensions={0} | all-to-all | bytes 262144 | tf_op jit(solution)/shard_map/all_to_all | solution.py:382
  54.5 0.6 %broadcast_multiply_fusion = f32[16,256]{1,0:T(8,128)} fusion(f32[16,256]{1,0:T(8,128)S(1)} %reduce_sum.9), kind=kLoop, calls=%fused_computation.3 | loop fusion | flops 4096 | bytes 32768 | tf_op jit(solution)/shard_map/mul | solution.py:389
  (10 shorter events, 0.1 us)
Async XLA Ops:
  0.0 29.2 %collective-permute-start.1 = (f32[128,2048]{1,0:T(8,128)}, f32[128,2048]{1,0:T(8,128)S(1)}, u32[]{:S(2)}, u32[]{:S(2)}) collective-permute-start(f32[128,2048]{1,0:T(8,128)} %bitcast.5), channel_id=1, source_target_pairs={{2,0},{0,2},{3,1},{1,3},{6,4},{4,6},{7,5},{5,7},{10,8},{8,10},{11,... | collective-permute-start | bytes 3145736 | tf_op jit(solution)/shard_map/ppermute | solution.py:292
  2.9 1.3 %copy-start = (f32[1,1,2,64,2048]{4,3,2,1,0:T(8,128)S(1)}, f32[1,1,2,64,2048]{4,3,2,1,0:T(8,128)}, u32[]{:S(2)}) copy-start(f32[1,1,2,64,2048]{4,3,2,1,0:T(8,128)} %param.4) | copy-start | bytes 3145732
  4.8 16.7 %collective-permute-start.3 = (f32[32,32,128]{2,1,0:T(8,128)S(1)}, f32[32,32,128]{2,1,0:T(8,128)S(1)}, u32[]{:S(2)}, u32[]{:S(2)}) collective-permute-start(f32[32,32,128]{2,1,0:T(8,128)S(1)} %get-tuple-element.19.refs_1_), channel_id=1, source_target_pairs={{0,4},{4,8},{8,12},{12,0},{1,5},{5,9},{9,13},{13,1},{2,6},{6,10},{... | collective-permute-start | bytes 1572872 | tf_op jit(solution)/shard_map/ppermute | solution.py:325
  7.9 4.4 %collective-permute-start = (f32[136,128]{1,0:T(8,128)S(1)}, f32[136,128]{1,0:T(8,128)S(1)}, u32[]{:S(2)}, u32[]{:S(2)}) collective-permute-start(f32[136,128]{1,0:T(8,128)S(1)} %get-tuple-element.32), channel_id=1, source_target_pairs={{16,0},{0,16},{17,1},{1,17},{18,2},{2,18},{19,3},{3,19},{20,4},{4,... | collective-permute-start | bytes 208904 | tf_op jit(solution)/shard_map/ppermute | solution.py:306
  9.5 12.7 %collective-permute-start.2 = (f32[32,32,128]{2,1,0:T(8,128)S(1)}, f32[32,32,128]{2,1,0:T(8,128)S(1)}, u32[]{:S(2)}, u32[]{:S(2)}) collective-permute-start(f32[32,32,128]{2,1,0:T(8,128)S(1)} %get-tuple-element.19.refs_1_), channel_id=1, source_target_pairs={{1,0},{0,1},{3,2},{2,3},{5,4},{4,5},{7,6},{6,7},{9,8},{8,9},{11,10... | collective-permute-start | bytes 1572872 | tf_op jit(solution)/shard_map/ppermute | solution.py:298
  13.8 17.2 %collective-permute-start.7 = (f32[32,32,128]{2,1,0:T(8,128)S(1)}, f32[32,32,128]{2,1,0:T(8,128)S(1)}, u32[]{:S(2)}, u32[]{:S(2)}) collective-permute-start(f32[32,32,128]{2,1,0:T(8,128)S(1)} %after.4), channel_id=1, source_target_pairs={{0,8},{12,4},{1,9},{13,5},{2,10},{14,6},{3,11},{15,7},{16,24},{28,... | collective-permute-start | bytes 1572872 | tf_op jit(solution)/shard_map/ppermute | solution.py:328
  21.5 1.6 %collective-permute-start.4 = (f32[16,32,128]{2,1,0:T(8,128)S(1)}, f32[16,32,128]{2,1,0:T(8,128)S(1)}, u32[]{:S(2)}, u32[]{:S(2)}) collective-permute-start(f32[16,32,128]{2,1,0:T(8,128)S(1)} %get-tuple-element.21.refs_2_.refs_5_.refs_3_), channel_id=1, source_target_pairs={{1,0},{0,1},{3,2},{2,3},{5,4},{4,5},{7,6},{6,7},{9,8},{8,9},{11,10... | collective-permute-start | bytes 786440 | tf_op jit(solution)/shard_map/ppermute | solution.py:327
  21.6 1.9 %collective-permute-start.5 = (f32[16,32,128]{2,1,0:T(8,128)S(1)}, f32[16,32,128]{2,1,0:T(8,128)S(1)}, u32[]{:S(2)}, u32[]{:S(2)}) collective-permute-start(f32[16,32,128]{2,1,0:T(8,128)S(1)} %get-tuple-element.22.refs_3_.refs_6_.refs_4_), channel_id=1, source_target_pairs={{1,0},{0,1},{3,2},{2,3},{5,4},{4,5},{7,6},{6,7},{9,8},{8,9},{11,10... | collective-permute-start | bytes 786440 | tf_op jit(solution)/shard_map/ppermute | solution.py:327
  23.5 5.7 %collective-permute-start.6 = (f32[2,136,128]{2,1,0:T(8,128)S(1)}, f32[2,136,128]{2,1,0:T(8,128)S(1)}, u32[]{:S(2)}, u32[]{:S(2)}) collective-permute-start(f32[2,136,128]{2,1,0:T(8,128)S(1)} %after.3), channel_id=1, source_target_pairs={{2,1},{3,0},{0,3},{1,2},{6,5},{7,4},{4,7},{5,6},{10,9},{11,8},{8,1... | collective-permute-start | bytes 417800 | tf_op jit(solution)/shard_map/ppermute | solution.py:333
  30.9 5.4 %collective-permute-start.8 = (f32[32,32,128]{2,1,0:T(8,128)S(1)}, f32[32,32,128]{2,1,0:T(8,128)S(1)}, u32[]{:S(2)}, u32[]{:S(2)}) collective-permute-start(f32[32,32,128]{2,1,0:T(8,128)S(1)} %after.5.refs_7_), channel_id=1, source_target_pairs={{1,0},{0,1},{3,2},{2,3},{5,4},{4,5},{7,6},{6,7},{9,8},{8,9},{11,10... | collective-permute-start | bytes 1572872 | tf_op jit(solution)/shard_map/ppermute | solution.py:348
  32.7 12.3 %collective-permute-start.9 = (f32[32,128]{1,0:T(8,128)S(1)}, f32[32,128]{1,0:T(8,128)S(1)}, u32[]{:S(2)}, u32[]{:S(2)}) collective-permute-start(f32[32,128]{1,0:T(8,128)S(1)} %get-tuple-element.29), channel_id=1, source_target_pairs={{4,0},{8,4},{12,8},{0,12},{5,1},{9,5},{13,9},{1,13},{6,2},{10,6},{... | collective-permute-start | bytes 49160 | tf_op jit(solution)/shard_map/ppermute | solution.py:375
  37.1 8.9 %collective-permute-start.10 = (f32[32,128]{1,0:T(8,128)S(1)}, f32[32,128]{1,0:T(8,128)S(1)}, u32[]{:S(2)}, u32[]{:S(2)}) collective-permute-start(f32[32,128]{1,0:T(8,128)S(1)} %get-tuple-element.30), channel_id=1, source_target_pairs={{8,0},{12,4},{0,8},{4,12},{9,1},{13,5},{1,9},{5,13},{10,2},{14,6},... | collective-permute-start | bytes 49160 | tf_op jit(solution)/shard_map/ppermute | solution.py:375

commit v15 on v14

--- a/solution.py
+++ b/solution.py
@@ -318,14 +318,13 @@
         tensor,
         **options,
     )
-    again = after(again, token)
     early = [mine_other]
     for pairs in plan[:-1]:
         parts = call(
             halve, [((share // 2, rows_aux, listed), F32)] * 2, [], 0, lax.ppermute(mine, "aux", pairs), token
         )
         early += [*parts, *(lax.ppermute(part, "sub", swap) for part in parts)]
-    last = lax.ppermute(again, "aux", plan[-1])
+    last = lax.ppermute(after(again, *early[1:2]), "aux", plan[-1])
     fars = []
     late_near = after(near, *early)
     for shift in range(1, nob):
@@ -335,7 +334,7 @@
         second,
         [((2 * rows, depth), BF16), ((8, 128), F32)],
         [((groups * rows_aux // 2 * share, 2 * width), F32)],
-        work * (nob - 1),
+        work * 2,
         near,
         acc,
         *tensors,

time: 55.3 us -> 52.1 us (0.942)
  starting transfers between devices: 22.3 us -> 13.6 us
  waiting for transfers between devices: 14 us -> 18.6 us
  blocking collectives: 8.14 us -> 9.04 us
    ppermute x2, starting transfers between devices: 10.9 us -> 3.93 us  [local(): lax.ppermute(back, 'aux', ring(naux, i))]
    ppermute x1, waiting for transfers between devices: 3.2 us -> 6.06 us  [local(): lax.ppermute(mine, 'aux', pairs)]
    ppermute x1, starting transfers between devices: 4.53 us -> 2.66 us  [local(): last = lax.ppermute(after(again, *early[1:2]), 'aux', plan[-1])]
    ppermute x2, waiting for transfers between devices: 0.97 us -> 2.12 us  [local(): lax.ppermute(back, 'aux', ring(naux, i))]
    all_to_all x1, blocking collectives: 8.14 us -> 9.04 us  [local(): lax.all_to_all(partial_chi.reshape(owners, nt * block_aux // owners, naux...]
  transfers between devices with their start and end apart: 11 -> 11, of which waited for: 6 -> 7; matrix products, arithmetic and copies ran while one was open for 3% -> 3% of each run, Pallas kernels for 12% -> 13%
where the time goes in v15:
time: 52.1 us; the launch traced here: 51.8 us
  waiting for transfers between devices  18.6 us (36%)
  starting transfers between devices  13.6 us (26%)
  blocking collectives  9.04 us (17%)
  Pallas kernels  7.14 us (14%)
  other arithmetic  2.07 us (4%)
  local copies, waits for them, and re-layouts  1.27 us (2%)
    all_to_all x1, blocking collectives, local(): lax.all_to_all(partial_chi.reshape(owners, nt * block_aux // owners, naux...  9.04 us
    pallas_call x8, Pallas kernels, call(): pl.pallas_call(here, out_shape=shapes, in_specs=[VMEM] * len(arguments),...  7.14 us
    ppermute x1, waiting for transfers between devices, local(): lax.ppermute(mine, 'aux', pairs)  6.06 us
    ppermute x1, waiting for transfers between devices, local(): fars.append(lax.ppermute(late_near, ('orb', 'sub'), pairs))  5.38 us
    ppermute x2, starting transfers between devices, local(): lax.ppermute(back, 'aux', ring(naux, i))  3.93 us
    ppermute x1, waiting for transfers between devices, local(): lax.ppermute(small, 'tau', ring(nt, shift))  3.07 us
    ppermute x1, starting transfers between devices, local(): lax.ppermute(tensor, 'orb', ring(nob, shift))  2.94 us
    ppermute x1, starting transfers between devices, local(): last = lax.ppermute(after(again, *early[1:2]), 'aux', plan[-1])  2.66 us
  transfers between devices with their start and end apart: 11, of which 7 were waited for; matrix products, arithmetic and copies ran while one was open for 3% of the time, Pallas kernels for 13%

profile of v15, /device:TPU:0, one launch (start us, length us, event | category | flops | bytes accessed | tf_op | source)
XLA Modules:
  0.0 51.8 jit_solution(3650291597601257142)
XLA Ops:
  0.0 2.9 %collective-permute-start.1 = (f32[128,2048]{1,0:T(8,128)}, f32[128,2048]{1,0:T(8,128)S(1)}, u32[]{:S(2)}, u32[]{:S(2)}) collective-permute-start(f32[128,2048]{1,0:T(8,128)} %bitcast.5), channel_id=1, source_target_pairs={{2,0},{0,2},{3,1},{1,3},{6,4},{4,6},{7,5},{5,7},{10,8},{8,10},{11,... | collective-permute-start | bytes 3145736 | tf_op jit(solution)/shard_map/ppermute | solution.py:292
  2.9 1.3 %copy-done = f32[1,1,2,64,2048]{4,3,2,1,0:T(8,128)S(1)} copy-done((f32[1,1,2,64,2048]{4,3,2,1,0:T(8,128)S(1)}, f32[1,1,2,64,2048]{4,3,2,1,0:T(8,128)}, u32[]{:S(2)}) %copy-start) | copy-done | bytes 1048600
  4.2 0.6 %prepare.1 = (f32[32,32,128]{2,1,0:T(8,128)S(1)}, f32[32,32,128]{2,1,0:T(8,128)S(1)}) custom-call(f32[128,2048]{1,0:T(8,128)S(1)} %bitcast.6), custom_call_target="tpu_custom_call" | custom-call | bytes 1048576 | tf_op jit(solution)/shard_map/prepare/pallas_call | solution.py:281
  4.8 1.6 %collective-permute-start.3 = (f32[32,32,128]{2,1,0:T(8,128)S(1)}, f32[32,32,128]{2,1,0:T(8,128)S(1)}, u32[]{:S(2)}, u32[]{:S(2)}) collective-permute-start(f32[32,32,128]{2,1,0:T(8,128)S(1)} %get-tuple-element.19.refs_1_), channel_id=1, source_target_pairs={{0,4},{4,8},{8,12},{12,0},{1,5},{5,9},{9,13},{13,1},{2,6},{6,10},{... | collective-permute-start | bytes 1572872 | tf_op jit(solution)/shard_map/ppermute | solution.py:324
  6.4 0.0 collective-permute-start.2
  6.4 0.7 %convert_element_type.5 = f32[1,2]{1,0:T(1,128)S(1)} convert(s32[1,2]{1,0:T(1,128)} %param.7) | non-fusion elementwise | flops 2 | bytes 16 | tf_op jit(solution)/shard_map/convert_element_type | solution.py:303
  7.1 0.8 %fusion = (f32[1,136,128]{2,1,0:T(8,128)S(1)}, f32[136,128]{1,0:T(8,128)S(1)}) fusion(f32[1,2]{1,0:T(1,128)S(1)} %convert_element_type.5, f32[64,128]{1,0:T(8,128)} %param.6, f32[64,128]{1,0:T(8,128)} %param.5), kind=kLoop, calls=%fused_computation.4 | loop fusion | flops 69632 | bytes 204808 | tf_op jit(solution)/shard_map/stack | solution.py:306
  7.9 1.6 %collective-permute-start = (f32[136,128]{1,0:T(8,128)S(1)}, f32[136,128]{1,0:T(8,128)S(1)}, u32[]{:S(2)}, u32[]{:S(2)}) collective-permute-start(f32[136,128]{1,0:T(8,128)S(1)} %get-tuple-element.32), channel_id=1, source_target_pairs={{16,0},{0,16},{17,1},{1,17},{18,2},{2,18},{19,3},{3,19},{20,4},{4,... | collective-permute-start | bytes 208904 | tf_op jit(solution)/shard_map/ppermute | solution.py:306
  9.5 3.1 %collective-permute-done = f32[136,128]{1,0:T(8,128)S(1)} collective-permute-done((f32[136,128]{1,0:T(8,128)S(1)}, f32[136,128]{1,0:T(8,128)S(1)}, u32[]{:S(2)}, u32[]{:S(2)}) %collective-permute-start) | collective-permute-done | bytes 69664 | tf_op jit(solution)/shard_map/ppermute | solution.py:306
  12.5 1.5 %first.1 = (f32[4,512,256]{2,1,0:T(8,128)S(1)}, f32[8,128]{1,0:T(8,128)S(1)}) custom-call(f32[2,136,128]{2,1,0:T(8,128)S(1)} %pad_maximum_fusion.refs_0_, f32[128,2048]{1,0:T(8,128)S(1)} %bitcast.7), custom_call_target="tpu_custom_call" | custom-call | flops 603979776 | bytes 1187840 | tf_op jit(solution)/shard_map/first/pallas_call | solution.py:281
  14.0 6.1 %collective-permute-done.3.refs_0_ = f32[32,32,128]{2,1,0:T(8,128)S(1)} collective-permute-done((f32[32,32,128]{2,1,0:T(8,128)S(1)}, f32[32,32,128]{2,1,0:T(8,128)S(1)}, u32[]{:S(2)}, u32[]{:S(2)}) %collective-permute-start.3) | collective-permute-done | bytes 524320 | tf_op jit(solution)/shard_map/ppermute | solution.py:324
  20.1 2.7 %collective-permute-start.7 = (f32[32,32,128]{2,1,0:T(8,128)S(1)}, f32[32,32,128]{2,1,0:T(8,128)S(1)}, u32[]{:S(2)}, u32[]{:S(2)}) collective-permute-start(f32[32,32,128]{2,1,0:T(8,128)S(1)} %after.4), channel_id=1, source_target_pairs={{0,8},{12,4},{1,9},{13,5},{2,10},{14,6},{3,11},{15,7},{16,24},{28,... | collective-permute-start | bytes 1572872 | tf_op jit(solution)/shard_map/ppermute | solution.py:327
  22.8 0.1 collective-permute-start.5
  22.9 0.5 collective-permute-start.4
  23.4 0.0 collective-permute-done.2.refs_1_.refs_4_.refs_2_
  23.4 1.0 %collective-permute-done.5.refs_5_.refs_8_.refs_6_ = f32[16,32,128]{2,1,0:T(8,128)S(1)} collective-permute-done((f32[16,32,128]{2,1,0:T(8,128)S(1)}, f32[16,32,128]{2,1,0:T(8,128)S(1)}, u32[]{:S(2)}, u32[]{:S(2)}) %collective-permute-start.5) | collective-permute-done | bytes 262176 | tf_op jit(solution)/shard_map/ppermute | solution.py:326
  24.4 0.4 collective-permute-done.4.refs_4_.refs_7_.refs_5_
  24.8 0.3 collective-permute-start.6
  25.1 5.4 %collective-permute-done.6.refs_3_ = f32[2,136,128]{2,1,0:T(8,128)S(1)} collective-permute-done((f32[2,136,128]{2,1,0:T(8,128)S(1)}, f32[2,136,128]{2,1,0:T(8,128)S(1)}, u32[]{:S(2)}, u32[]{:S(2)}) %collective-permute-start.6) | collective-permute-done | bytes 139296 | tf_op jit(solution)/shard_map/ppermute | solution.py:332
  30.5 0.0 collective-permute-done.1.refs_2_
  30.5 1.8 %second.1 = (bf16[256,4096]{1,0:T(8,128)(2,1)S(1)}, f32[8,128]{1,0:T(8,128)S(1)}) custom-call(f32[2,136,128]{2,1,0:T(8,128)S(1)} %pad_maximum_fusion.refs_0_, f32[4,512,256]{2,1,0:T(8,128)S(1)} %get-tuple-element.18.refs_1_, f32[128,2048]{1,0:T(8,128)S(1)} %collective-permute-done.1.refs_2_, f32[2,136,128]{2,1,0:T(8,128)S(1)} %collective-permute-done.6.refs_3_, ...), custom_call_target="tpu_custom_call" | custom-call | flops 1207959552 | bytes 4997120 | tf_op jit(solution)/shard_map/second/pallas_call | solution.py:281
  32.2 0.5 %collective-permute-done.7.refs_0_ = f32[32,32,128]{2,1,0:T(8,128)S(1)} collective-permute-done((f32[32,32,128]{2,1,0:T(8,128)S(1)}, f32[32,32,128]{2,1,0:T(8,128)S(1)}, u32[]{:S(2)}, u32[]{:S(2)}) %collective-permute-start.7) | collective-permute-done | bytes 524320 | tf_op jit(solution)/shard_map/ppermute | solution.py:327
  32.8 1.5 %meet_own.1 = (f32[160,64]{1,0:T(8,128)S(1)}, f32[32,64]{1,0:T(8,128)S(1)}, f32[32,128]{1,0:T(8,128)S(1)}) custom-call(bf16[256,4096]{1,0:T(8,128)(2,1)S(1)} %get-tuple-element.23.refs_0_, f32[32,32,128]{2,1,0:T(8,128)S(1)} %get-tuple-element.19.refs_1_, f32[32,32,128]{2,1,0:T(8,128)S(1)} %collective-permute-done.2.refs_1_.refs_4_.refs_2_, ...), custom_call_target="tpu_custom_call" | custom-call | flops 1342177280 | bytes 6815744 | tf_op jit(solution)/shard_map/meet_own/pallas_call | solution.py:281
  34.3 2.1 %collective-permute-start.9 = (f32[32,128]{1,0:T(8,128)S(1)}, f32[32,128]{1,0:T(8,128)S(1)}, u32[]{:S(2)}, u32[]{:S(2)}) collective-permute-start(f32[32,128]{1,0:T(8,128)S(1)} %get-tuple-element.29), channel_id=1, source_target_pairs={{4,0},{8,4},{12,8},{0,12},{5,1},{9,5},{13,9},{1,13},{6,2},{10,6},{... | collective-permute-start | bytes 49160 | tf_op jit(solution)/shard_map/ppermute | solution.py:374
  36.4 0.7 %meet_back.1 = (bf16[64,4096]{1,0:T(8,128)(2,1)S(1)}, f32[32,128]{1,0:T(8,128)S(1)}) custom-call(bf16[256,4096]{1,0:T(8,128)(2,1)S(1)} %get-tuple-element.23.refs_0_, f32[32,64]{1,0:T(8,128)S(1)} %get-tuple-element.27.refs_1_, f32[32,32,128]{2,1,0:T(8,128)S(1)} %collective-permute-done.8.refs_2_), custom_call_target="tpu_custom_call" | custom-call | flops 134217728 | bytes 4726784 | tf_op jit(solution)/shard_map/meet_back/pallas_call | solution.py:281
  37.1 1.8 %collective-permute-start.10 = (f32[32,128]{1,0:T(8,128)S(1)}, f32[32,128]{1,0:T(8,128)S(1)}, u32[]{:S(2)}, u32[]{:S(2)}) collective-permute-start(f32[32,128]{1,0:T(8,128)S(1)} %get-tuple-element.30), channel_id=1, source_target_pairs={{8,0},{12,4},{0,8},{4,12},{9,1},{13,5},{1,9},{5,13},{10,2},{14,6},... | collective-permute-start | bytes 49160 | tf_op jit(solution)/shard_map/ppermute | solution.py:374
  38.9 0.7 %meet_direct.1.refs_0_ = f32[2,64,256]{2,1,0:T(8,128)S(1)} custom-call(bf16[256,4096]{1,0:T(8,128)(2,1)S(1)} %get-tuple-element.23.refs_0_, f32[160,64]{1,0:T(8,128)S(1)} %get-tuple-element.26.refs_1_, bf16[64,4096]{1,0:T(8,128)(2,1)S(1)} %get-tuple-element.28.refs_2_), custom_call_target="tpu_custom_call" | custom-call | flops 134217728 | bytes 5283840 | tf_op jit(solution)/shard_map/meet_direct/pallas_call | solution.py:281
  39.7 0.0 collective-permute-done.9.refs_1_
  39.7 2.1 %collective-permute-done.10.refs_2_ = f32[32,128]{1,0:T(8,128)S(1)} collective-permute-done((f32[32,128]{1,0:T(8,128)S(1)}, f32[32,128]{1,0:T(8,128)S(1)}, u32[]{:S(2)}, u32[]{:S(2)}) %collective-permute-start.10) | collective-permute-done | bytes 16416 | tf_op jit(solution)/shard_map/ppermute | solution.py:374
  41.8 0.3 complete.1
  42.1 9.0 %all_to_all.5 = f32[8,16,256]{2,1,0:T(8,128)S(1)} all-to-all(f32[8,16,256]{2,1,0:T(8,128)S(1)} %bitcast.8), channel_id=1, replica_groups=mesh['tau'=2,'aux'=4,'orb'=2,'sub'=2] {'tau','orb','sub'}, dimensions={0} | all-to-all | bytes 262144 | tf_op jit(solution)/shard_map/all_to_all | solution.py:381
  51.2 0.6 %broadcast_multiply_fusion = f32[16,256]{1,0:T(8,128)} fusion(f32[16,256]{1,0:T(8,128)S(1)} %reduce_sum.9), kind=kLoop, calls=%fused_computation.3 | loop fusion | flops 4096 | bytes 32768 | tf_op jit(solution)/shard_map/mul | solution.py:388
  (10 shorter events, 0.1 us)
Async XLA Ops:
  0.0 30.5 %collective-permute-start.1 = (f32[128,2048]{1,0:T(8,128)}, f32[128,2048]{1,0:T(8,128)S(1)}, u32[]{:S(2)}, u32[]{:S(2)}) collective-permute-start(f32[128,2048]{1,0:T(8,128)} %bitcast.5), channel_id=1, source_target_pairs={{2,0},{0,2},{3,1},{1,3},{6,4},{4,6},{7,5},{5,7},{10,8},{8,10},{11,... | collective-permute-start | bytes 3145736 | tf_op jit(solution)/shard_map/ppermute | solution.py:292
  2.9 1.3 %copy-start = (f32[1,1,2,64,2048]{4,3,2,1,0:T(8,128)S(1)}, f32[1,1,2,64,2048]{4,3,2,1,0:T(8,128)}, u32[]{:S(2)}) copy-start(f32[1,1,2,64,2048]{4,3,2,1,0:T(8,128)} %param.4) | copy-start | bytes 3145732
  4.8 15.3 %collective-permute-start.3 = (f32[32,32,128]{2,1,0:T(8,128)S(1)}, f32[32,32,128]{2,1,0:T(8,128)S(1)}, u32[]{:S(2)}, u32[]{:S(2)}) collective-permute-start(f32[32,32,128]{2,1,0:T(8,128)S(1)} %get-tuple-element.19.refs_1_), channel_id=1, source_target_pairs={{0,4},{4,8},{8,12},{12,0},{1,5},{5,9},{9,13},{13,1},{2,6},{6,10},{... | collective-permute-start | bytes 1572872 | tf_op jit(solution)/shard_map/ppermute | solution.py:324
  6.4 17.0 %collective-permute-start.2 = (f32[32,32,128]{2,1,0:T(8,128)S(1)}, f32[32,32,128]{2,1,0:T(8,128)S(1)}, u32[]{:S(2)}, u32[]{:S(2)}) collective-permute-start(f32[32,32,128]{2,1,0:T(8,128)S(1)} %get-tuple-element.19.refs_1_), channel_id=1, source_target_pairs={{1,0},{0,1},{3,2},{2,3},{5,4},{4,5},{7,6},{6,7},{9,8},{8,9},{11,10... | collective-permute-start | bytes 1572872 | tf_op jit(solution)/shard_map/ppermute | solution.py:298
  7.9 4.7 %collective-permute-start = (f32[136,128]{1,0:T(8,128)S(1)}, f32[136,128]{1,0:T(8,128)S(1)}, u32[]{:S(2)}, u32[]{:S(2)}) collective-permute-start(f32[136,128]{1,0:T(8,128)S(1)} %get-tuple-element.32), channel_id=1, source_target_pairs={{16,0},{0,16},{17,1},{1,17},{18,2},{2,18},{19,3},{3,19},{20,4},{4,... | collective-permute-start | bytes 208904 | tf_op jit(solution)/shard_map/ppermute | solution.py:306
  20.1 12.6 %collective-permute-start.7 = (f32[32,32,128]{2,1,0:T(8,128)S(1)}, f32[32,32,128]{2,1,0:T(8,128)S(1)}, u32[]{:S(2)}, u32[]{:S(2)}) collective-permute-start(f32[32,32,128]{2,1,0:T(8,128)S(1)} %after.4), channel_id=1, source_target_pairs={{0,8},{12,4},{1,9},{13,5},{2,10},{14,6},{3,11},{15,7},{16,24},{28,... | collective-permute-start | bytes 1572872 | tf_op jit(solution)/shard_map/ppermute | solution.py:327
  22.8 1.6 %collective-permute-start.5 = (f32[16,32,128]{2,1,0:T(8,128)S(1)}, f32[16,32,128]{2,1,0:T(8,128)S(1)}, u32[]{:S(2)}, u32[]{:S(2)}) collective-permute-start(f32[16,32,128]{2,1,0:T(8,128)S(1)} %get-tuple-element.22.refs_3_.refs_6_.refs_4_), channel_id=1, source_target_pairs={{1,0},{0,1},{3,2},{2,3},{5,4},{4,5},{7,6},{6,7},{9,8},{8,9},{11,10... | collective-permute-start | bytes 786440 | tf_op jit(solution)/shard_map/ppermute | solution.py:326
  22.9 1.9 %collective-permute-start.4 = (f32[16,32,128]{2,1,0:T(8,128)S(1)}, f32[16,32,128]{2,1,0:T(8,128)S(1)}, u32[]{:S(2)}, u32[]{:S(2)}) collective-permute-start(f32[16,32,128]{2,1,0:T(8,128)S(1)} %get-tuple-element.21.refs_2_.refs_5_.refs_1_.refs_3_), channel_id=1, source_target_pairs={{1,0},{0,1},{3,2},{2,3},{5,4},{4,5},{7,6},{6,7},{9,8},{8,9},{11,10... | collective-permute-start | bytes 786440 | tf_op jit(solution)/shard_map/ppermute | solution.py:326
  24.8 5.7 %collective-permute-start.6 = (f32[2,136,128]{2,1,0:T(8,128)S(1)}, f32[2,136,128]{2,1,0:T(8,128)S(1)}, u32[]{:S(2)}, u32[]{:S(2)}) collective-permute-start(f32[2,136,128]{2,1,0:T(8,128)S(1)} %after.3), channel_id=1, source_target_pairs={{2,1},{3,0},{0,3},{1,2},{6,5},{7,4},{4,7},{5,6},{10,9},{11,8},{8,1... | collective-permute-start | bytes 417800 | tf_op jit(solution)/shard_map/ppermute | solution.py:332
  32.8 3.6 %collective-permute-start.8 = (f32[32,32,128]{2,1,0:T(8,128)S(1)}, f32[32,32,128]{2,1,0:T(8,128)S(1)}, u32[]{:S(2)}, u32[]{:S(2)}) collective-permute-start(f32[32,32,128]{2,1,0:T(8,128)S(1)} %after.5.refs_7_), channel_id=1, source_target_pairs={{1,0},{0,1},{3,2},{2,3},{5,4},{4,5},{7,6},{6,7},{9,8},{8,9},{11,10... | collective-permute-start | bytes 1572872 | tf_op jit(solution)/shard_map/ppermute | solution.py:347
  34.3 5.4 %collective-permute-start.9 = (f32[32,128]{1,0:T(8,128)S(1)}, f32[32,128]{1,0:T(8,128)S(1)}, u32[]{:S(2)}, u32[]{:S(2)}) collective-permute-start(f32[32,128]{1,0:T(8,128)S(1)} %get-tuple-element.29), channel_id=1, source_target_pairs={{4,0},{8,4},{12,8},{0,12},{5,1},{9,5},{13,9},{1,13},{6,2},{10,6},{... | collective-permute-start | bytes 49160 | tf_op jit(solution)/shard_map/ppermute | solution.py:374
  37.1 4.7 %collective-permute-start.10 = (f32[32,128]{1,0:T(8,128)S(1)}, f32[32,128]{1,0:T(8,128)S(1)}, u32[]{:S(2)}, u32[]{:S(2)}) collective-permute-start(f32[32,128]{1,0:T(8,128)S(1)} %get-tuple-element.30), channel_id=1, source_target_pairs={{8,0},{12,4},{0,8},{4,12},{9,1},{13,5},{1,9},{5,13},{10,2},{14,6},... | collective-permute-start | bytes 49160 | tf_op jit(solution)/shard_map/ppermute | solution.py:374

commit v16 on v15

--- a/solution.py
+++ b/solution.py
@@ -295,7 +295,6 @@
     )
     plan = shifts_of(naux)
     swap = ring(nsub, 1)
-    mine_other = lax.ppermute(mine, "sub", swap)
     small = jnp.concatenate(
         [
             occupied_green,
@@ -313,18 +312,19 @@
         first,
         [((groups, rows_aux // 2 * share, 2 * listed), F32), ((8, 128), F32)],
         [((groups * rows_aux // 2 * share, 2 * width), F32)],
-        work,
+        0,
         near,
         tensor,
         **options,
     )
+    mine_other = lax.ppermute(mine, "sub", swap)
     early = [mine_other]
     for pairs in plan[:-1]:
         parts = call(
             halve, [((share // 2, rows_aux, listed), F32)] * 2, [], 0, lax.ppermute(mine, "aux", pairs), token
         )
         early += [*parts, *(lax.ppermute(part, "sub", swap) for part in parts)]
-    last = lax.ppermute(after(again, *early[1:2]), "aux", plan[-1])
+    last = lax.ppermute(after(again, lax.ppermute(token, "sub", swap)), "aux", plan[-1])
     fars = []
     late_near = after(near, *early)
     for shift in range(1, nob):
@@ -334,7 +334,7 @@
         second,
         [((2 * rows, depth), BF16), ((8, 128), F32)],
         [((groups * rows_aux // 2 * share, 2 * width), F32)],
-        work * 2,
+        work,
         near,
         acc,
         *tensors,

time: 52.1 us -> 52.1 us (level)
  waiting for transfers between devices: 18.6 us -> 16.6 us
  starting transfers between devices: 13.6 us -> 15.5 us
    ppermute x1, waiting for transfers between devices: 6.06 us -> 0.3 us  [local(): lax.ppermute(mine, 'aux', pairs)]
    ppermute x1 -> x2, starting transfers between devices: 2.66 us -> 4.59 us  [the longest x1 4.51 us: local(): lax.ppermute(after(again, lax.ppermute(token, 'sub', swap)), 'aux', plan[...]
    ppermute x1 -> x2, waiting for transfers between devices: 0.55 us -> 2.1 us  [the longest x1 1.15 us: local(): lax.ppermute(token, 'sub', swap)]
    ppermute x2, waiting for transfers between devices: 2.12 us -> 3.6 us  [local(): lax.ppermute(back, 'aux', ring(naux, i))]
    ppermute x1, waiting for transfers between devices: 5.38 us -> 6.16 us  [local(): fars.append(lax.ppermute(late_near, ('orb', 'sub'), pairs))]
    unnamed x3 -> x5, local copies, waits for them, and re-layouts: 1.27 us -> 1.27 us
  transfers between devices with their start and end apart: 11 -> 12, of which waited for: 7 -> 8; matrix products, arithmetic and copies ran while one was open for 3% -> 3% of each run, Pallas kernels for 13% -> 13%
where the time goes in v16:
time: 52.1 us; the launch traced here: 51.8 us
  waiting for transfers between devices  16.6 us (32%)
  starting transfers between devices  15.5 us (30%)
  blocking collectives  9.05 us (17%)
  Pallas kernels  7.15 us (14%)
  other arithmetic  2.07 us (4%)
  local copies, waits for them, and re-layouts  1.27 us (2%)
    all_to_all x1, blocking collectives, local(): lax.all_to_all(partial_chi.reshape(owners, nt * block_aux // owners, naux...  9.05 us
    pallas_call x8, Pallas kernels, call(): pl.pallas_call(here, out_shape=shapes, in_specs=[VMEM] * len(arguments),...  7.15 us
    ppermute x1, waiting for transfers between devices, local(): fars.append(lax.ppermute(late_near, ('orb', 'sub'), pairs))  6.16 us
    ppermute x1, starting transfers between devices, local(): lax.ppermute(after(again, lax.ppermute(token, 'sub', swap)), 'aux', plan[...  4.51 us
    ppermute x2, starting transfers between devices, local(): lax.ppermute(back, 'aux', ring(naux, i))  3.93 us
    ppermute x2, waiting for transfers between devices, local(): lax.ppermute(back, 'aux', ring(naux, i))  3.6 us
    ppermute x1, waiting for transfers between devices, local(): lax.ppermute(small, 'tau', ring(nt, shift))  3.07 us
    ppermute x1, starting transfers between devices, local(): lax.ppermute(tensor, 'orb', ring(nob, shift))  2.94 us
  transfers between devices with their start and end apart: 12, of which 8 were waited for; matrix products, arithmetic and copies ran while one was open for 3% of the time, Pallas kernels for 13%

profile of v16, /device:TPU:0, one launch (start us, length us, event | category | flops | bytes accessed | tf_op | source)
XLA Modules:
  0.0 51.8 jit_solution(13445493957055741383)
XLA Ops:
  0.0 2.9 %collective-permute-start.1 = (f32[128,2048]{1,0:T(8,128)}, f32[128,2048]{1,0:T(8,128)S(1)}, u32[]{:S(2)}, u32[]{:S(2)}) collective-permute-start(f32[128,2048]{1,0:T(8,128)} %bitcast.5), channel_id=1, source_target_pairs={{2,0},{0,2},{3,1},{1,3},{6,4},{4,6},{7,5},{5,7},{10,8},{8,10},{11,... | collective-permute-start | bytes 3145736 | tf_op jit(solution)/shard_map/ppermute | solution.py:292
  2.9 1.3 %copy-done = f32[1,1,2,64,2048]{4,3,2,1,0:T(8,128)S(1)} copy-done((f32[1,1,2,64,2048]{4,3,2,1,0:T(8,128)S(1)}, f32[1,1,2,64,2048]{4,3,2,1,0:T(8,128)}, u32[]{:S(2)}) %copy-start) | copy-done | bytes 1048600
  4.2 0.6 %prepare.1 = (f32[32,32,128]{2,1,0:T(8,128)S(1)}, f32[32,32,128]{2,1,0:T(8,128)S(1)}) custom-call(f32[128,2048]{1,0:T(8,128)S(1)} %bitcast.6), custom_call_target="tpu_custom_call" | custom-call | bytes 1048576 | tf_op jit(solution)/shard_map/prepare/pallas_call | solution.py:281
  4.8 1.6 %collective-permute-start.3 = (f32[32,32,128]{2,1,0:T(8,128)S(1)}, f32[32,32,128]{2,1,0:T(8,128)S(1)}, u32[]{:S(2)}, u32[]{:S(2)}) collective-permute-start(f32[32,32,128]{2,1,0:T(8,128)S(1)} %get-tuple-element.19.refs_1_), channel_id=1, source_target_pairs={{0,4},{4,8},{8,12},{12,0},{1,5},{5,9},{9,13},{13,1},{2,6},{6,10},{... | collective-permute-start | bytes 1572872 | tf_op jit(solution)/shard_map/ppermute | solution.py:324
  6.4 0.7 %convert_element_type.5 = f32[1,2]{1,0:T(1,128)S(1)} convert(s32[1,2]{1,0:T(1,128)} %param.7) | non-fusion elementwise | flops 2 | bytes 16 | tf_op jit(solution)/shard_map/convert_element_type | solution.py:302
  7.1 0.8 %fusion = (f32[1,136,128]{2,1,0:T(8,128)S(1)}, f32[136,128]{1,0:T(8,128)S(1)}) fusion(f32[1,2]{1,0:T(1,128)S(1)} %convert_element_type.5, f32[64,128]{1,0:T(8,128)} %param.6, f32[64,128]{1,0:T(8,128)} %param.5), kind=kLoop, calls=%fused_computation.4 | loop fusion | flops 69632 | bytes 204808 | tf_op jit(solution)/shard_map/stack | solution.py:305
  7.9 1.6 %collective-permute-start = (f32[136,128]{1,0:T(8,128)S(1)}, f32[136,128]{1,0:T(8,128)S(1)}, u32[]{:S(2)}, u32[]{:S(2)}) collective-permute-start(f32[136,128]{1,0:T(8,128)S(1)} %get-tuple-element.32), channel_id=1, source_target_pairs={{16,0},{0,16},{17,1},{1,17},{18,2},{2,18},{19,3},{3,19},{20,4},{4,... | collective-permute-start | bytes 208904 | tf_op jit(solution)/shard_map/ppermute | solution.py:305
  9.5 3.1 %collective-permute-done = f32[136,128]{1,0:T(8,128)S(1)} collective-permute-done((f32[136,128]{1,0:T(8,128)S(1)}, f32[136,128]{1,0:T(8,128)S(1)}, u32[]{:S(2)}, u32[]{:S(2)}) %collective-permute-start) | collective-permute-done | bytes 69664 | tf_op jit(solution)/shard_map/ppermute | solution.py:305
  12.6 1.5 %first.1 = (f32[4,512,256]{2,1,0:T(8,128)S(1)}, f32[8,128]{1,0:T(8,128)S(1)}) custom-call(f32[2,136,128]{2,1,0:T(8,128)S(1)} %pad_maximum_fusion.refs_0_, f32[128,2048]{1,0:T(8,128)S(1)} %bitcast.7), custom_call_target="tpu_custom_call" | custom-call | bytes 1187840 | tf_op jit(solution)/shard_map/first/pallas_call | solution.py:281
  14.0 0.1 collective-permute-start.7
  14.1 1.2 %collective-permute-done.7.refs_1_ = f32[8,128]{1,0:T(8,128)S(1)} collective-permute-done((f32[8,128]{1,0:T(8,128)S(1)}, f32[8,128]{1,0:T(8,128)S(1)}, u32[]{:S(2)}, u32[]{:S(2)}) %collective-permute-start.7) | collective-permute-done | bytes 4128 | tf_op jit(solution)/shard_map/ppermute | solution.py:327
  15.3 4.5 %collective-permute-start.8 = (f32[32,32,128]{2,1,0:T(8,128)S(1)}, f32[32,32,128]{2,1,0:T(8,128)S(1)}, u32[]{:S(2)}, u32[]{:S(2)}) collective-permute-start(f32[32,32,128]{2,1,0:T(8,128)S(1)} %after.4), channel_id=1, source_target_pairs={{0,8},{12,4},{1,9},{13,5},{2,10},{14,6},{3,11},{15,7},{16,24},{28,... | collective-permute-start | bytes 1572872 | tf_op jit(solution)/shard_map/ppermute | solution.py:327
  19.8 0.3 collective-permute-done.3.refs_0_
  20.1 0.1 collective-permute-start.4
  20.2 0.5 collective-permute-start.5
  20.7 0.0 collective-permute-done.2.refs_1_.refs_4_.refs_2_
  20.7 1.0 %collective-permute-done.4.refs_4_.refs_7_.refs_5_ = f32[16,32,128]{2,1,0:T(8,128)S(1)} collective-permute-done((f32[16,32,128]{2,1,0:T(8,128)S(1)}, f32[16,32,128]{2,1,0:T(8,128)S(1)}, u32[]{:S(2)}, u32[]{:S(2)}) %collective-permute-start.4) | collective-permute-done | bytes 262176 | tf_op jit(solution)/shard_map/ppermute | solution.py:326
  21.7 0.4 collective-permute-done.5.refs_5_.refs_8_.refs_6_
  22.1 0.3 collective-permute-start.6
  22.4 6.2 %collective-permute-done.6.refs_3_ = f32[2,136,128]{2,1,0:T(8,128)S(1)} collective-permute-done((f32[2,136,128]{2,1,0:T(8,128)S(1)}, f32[2,136,128]{2,1,0:T(8,128)S(1)}, u32[]{:S(2)}, u32[]{:S(2)}) %collective-permute-start.6) | collective-permute-done | bytes 139296 | tf_op jit(solution)/shard_map/ppermute | solution.py:332
  28.6 0.0 collective-permute-done.1.refs_2_
  28.6 1.8 %second.1 = (bf16[256,4096]{1,0:T(8,128)(2,1)S(1)}, f32[8,128]{1,0:T(8,128)S(1)}) custom-call(f32[2,136,128]{2,1,0:T(8,128)S(1)} %pad_maximum_fusion.refs_0_, f32[4,512,256]{2,1,0:T(8,128)S(1)} %get-tuple-element.18.refs_1_, f32[128,2048]{1,0:T(8,128)S(1)} %collective-permute-done.1.refs_2_, f32[2,136,128]{2,1,0:T(8,128)S(1)} %collective-permute-done.6.refs_3_, ...), custom_call_target="tpu_custom_call" | custom-call | flops 603979776 | bytes 4997120 | tf_op jit(solution)/shard_map/second/pallas_call | solution.py:281
  30.3 0.9 %collective-permute-done.8.refs_0_ = f32[32,32,128]{2,1,0:T(8,128)S(1)} collective-permute-done((f32[32,32,128]{2,1,0:T(8,128)S(1)}, f32[32,32,128]{2,1,0:T(8,128)S(1)}, u32[]{:S(2)}, u32[]{:S(2)}) %collective-permute-start.8) | collective-permute-done | bytes 524320 | tf_op jit(solution)/shard_map/ppermute | solution.py:327
  31.3 1.5 %meet_own.1 = (f32[160,64]{1,0:T(8,128)S(1)}, f32[32,64]{1,0:T(8,128)S(1)}, f32[32,128]{1,0:T(8,128)S(1)}) custom-call(bf16[256,4096]{1,0:T(8,128)(2,1)S(1)} %get-tuple-element.23.refs_0_, f32[32,32,128]{2,1,0:T(8,128)S(1)} %get-tuple-element.19.refs_1_, f32[32,32,128]{2,1,0:T(8,128)S(1)} %collective-permute-done.2.refs_1_.refs_4_.refs_2_, ...), custom_call_target="tpu_custom_call" | custom-call | flops 1342177280 | bytes 6815744 | tf_op jit(solution)/shard_map/meet_own/pallas_call | solution.py:281
  32.8 3.6 %collective-permute-start.10 = (f32[32,128]{1,0:T(8,128)S(1)}, f32[32,128]{1,0:T(8,128)S(1)}, u32[]{:S(2)}, u32[]{:S(2)}) collective-permute-start(f32[32,128]{1,0:T(8,128)S(1)} %get-tuple-element.29), channel_id=1, source_target_pairs={{4,0},{8,4},{12,8},{0,12},{5,1},{9,5},{13,9},{1,13},{6,2},{10,6},{... | collective-permute-start | bytes 49160 | tf_op jit(solution)/shard_map/ppermute | solution.py:374
  36.4 0.7 %meet_back.1 = (bf16[64,4096]{1,0:T(8,128)(2,1)S(1)}, f32[32,128]{1,0:T(8,128)S(1)}) custom-call(bf16[256,4096]{1,0:T(8,128)(2,1)S(1)} %get-tuple-element.23.refs_0_, f32[32,64]{1,0:T(8,128)S(1)} %get-tuple-element.27.refs_1_, f32[32,32,128]{2,1,0:T(8,128)S(1)} %collective-permute-done.9.refs_2_), custom_call_target="tpu_custom_call" | custom-call | flops 134217728 | bytes 4726784 | tf_op jit(solution)/shard_map/meet_back/pallas_call | solution.py:281
  37.1 0.4 collective-permute-start.11
  37.5 0.7 %meet_direct.1.refs_0_ = f32[2,64,256]{2,1,0:T(8,128)S(1)} custom-call(bf16[256,4096]{1,0:T(8,128)(2,1)S(1)} %get-tuple-element.23.refs_0_, f32[160,64]{1,0:T(8,128)S(1)} %get-tuple-element.26.refs_1_, bf16[64,4096]{1,0:T(8,128)(2,1)S(1)} %get-tuple-element.28.refs_2_), custom_call_target="tpu_custom_call" | custom-call | flops 134217728 | bytes 5283840 | tf_op jit(solution)/shard_map/meet_direct/pallas_call | solution.py:281
  38.2 3.6 %collective-permute-done.11.refs_2_ = f32[32,128]{1,0:T(8,128)S(1)} collective-permute-done((f32[32,128]{1,0:T(8,128)S(1)}, f32[32,128]{1,0:T(8,128)S(1)}, u32[]{:S(2)}, u32[]{:S(2)}) %collective-permute-start.11) | collective-permute-done | bytes 16416 | tf_op jit(solution)/shard_map/ppermute | solution.py:374
  41.8 0.3 complete.1
  42.1 9.0 %all_to_all.5 = f32[8,16,256]{2,1,0:T(8,128)S(1)} all-to-all(f32[8,16,256]{2,1,0:T(8,128)S(1)} %bitcast.8), channel_id=1, replica_groups=mesh['tau'=2,'aux'=4,'orb'=2,'sub'=2] {'tau','orb','sub'}, dimensions={0} | all-to-all | bytes 262144 | tf_op jit(solution)/shard_map/all_to_all | solution.py:381
  51.2 0.6 %broadcast_multiply_fusion = f32[16,256]{1,0:T(8,128)} fusion(f32[16,256]{1,0:T(8,128)S(1)} %reduce_sum.9), kind=kLoop, calls=%fused_computation.3 | loop fusion | flops 4096 | bytes 32768 | tf_op jit(solution)/shard_map/mul | solution.py:388
  (14 shorter events, 0.1 us)
Async XLA Ops:
  0.0 28.6 %collective-permute-start.1 = (f32[128,2048]{1,0:T(8,128)}, f32[128,2048]{1,0:T(8,128)S(1)}, u32[]{:S(2)}, u32[]{:S(2)}) collective-permute-start(f32[128,2048]{1,0:T(8,128)} %bitcast.5), channel_id=1, source_target_pairs={{2,0},{0,2},{3,1},{1,3},{6,4},{4,6},{7,5},{5,7},{10,8},{8,10},{11,... | collective-permute-start | bytes 3145736 | tf_op jit(solution)/shard_map/ppermute | solution.py:292
  2.9 1.3 %copy-start = (f32[1,1,2,64,2048]{4,3,2,1,0:T(8,128)S(1)}, f32[1,1,2,64,2048]{4,3,2,1,0:T(8,128)}, u32[]{:S(2)}) copy-start(f32[1,1,2,64,2048]{4,3,2,1,0:T(8,128)} %param.4) | copy-start | bytes 3145732
  4.2 8.4 %copy-start.1 = (f32[1,1,2,64,2048]{4,3,2,1,0:T(8,128)S(1)}, f32[1,1,2,64,2048]{4,3,2,1,0:T(8,128)}, u32[]{:S(2)}) copy-start(f32[1,1,2,64,2048]{4,3,2,1,0:T(8,128)} %param.4) | copy-start | bytes 3145732
  4.8 15.3 %collective-permute-start.3 = (f32[32,32,128]{2,1,0:T(8,128)S(1)}, f32[32,32,128]{2,1,0:T(8,128)S(1)}, u32[]{:S(2)}, u32[]{:S(2)}) collective-permute-start(f32[32,32,128]{2,1,0:T(8,128)S(1)} %get-tuple-element.19.refs_1_), channel_id=1, source_target_pairs={{0,4},{4,8},{8,12},{12,0},{1,5},{5,9},{9,13},{13,1},{2,6},{6,10},{... | collective-permute-start | bytes 1572872 | tf_op jit(solution)/shard_map/ppermute | solution.py:324
  6.4 14.3 %collective-permute-start.2 = (f32[32,32,128]{2,1,0:T(8,128)S(1)}, f32[32,32,128]{2,1,0:T(8,128)S(1)}, u32[]{:S(2)}, u32[]{:S(2)}) collective-permute-start(f32[32,32,128]{2,1,0:T(8,128)S(1)} %get-tuple-element.19.refs_1_), channel_id=1, source_target_pairs={{1,0},{0,1},{3,2},{2,3},{5,4},{4,5},{7,6},{6,7},{9,8},{8,9},{11,10... | collective-permute-start | bytes 1572872 | tf_op jit(solution)/shard_map/ppermute | solution.py:320
  7.9 4.7 %collective-permute-start = (f32[136,128]{1,0:T(8,128)S(1)}, f32[136,128]{1,0:T(8,128)S(1)}, u32[]{:S(2)}, u32[]{:S(2)}) collective-permute-start(f32[136,128]{1,0:T(8,128)S(1)} %get-tuple-element.32), channel_id=1, source_target_pairs={{16,0},{0,16},{17,1},{1,17},{18,2},{2,18},{19,3},{3,19},{20,4},{4,... | collective-permute-start | bytes 208904 | tf_op jit(solution)/shard_map/ppermute | solution.py:305
  14.0 1.2 %collective-permute-start.7 = (f32[8,128]{1,0:T(8,128)S(1)}, f32[8,128]{1,0:T(8,128)S(1)}, u32[]{:S(2)}, u32[]{:S(2)}) collective-permute-start(f32[8,128]{1,0:T(8,128)S(1)} %get-tuple-element.20.refs_1_), channel_id=1, source_target_pairs={{1,0},{0,1},{3,2},{2,3},{5,4},{4,5},{7,6},{6,7},{9,8},{8,9},{11,10... | collective-permute-start | bytes 12296 | tf_op jit(solution)/shard_map/ppermute | solution.py:327
  15.3 16.0 %collective-permute-start.8 = (f32[32,32,128]{2,1,0:T(8,128)S(1)}, f32[32,32,128]{2,1,0:T(8,128)S(1)}, u32[]{:S(2)}, u32[]{:S(2)}) collective-permute-start(f32[32,32,128]{2,1,0:T(8,128)S(1)} %after.4), channel_id=1, source_target_pairs={{0,8},{12,4},{1,9},{13,5},{2,10},{14,6},{3,11},{15,7},{16,24},{28,... | collective-permute-start | bytes 1572872 | tf_op jit(solution)/shard_map/ppermute | solution.py:327
  20.1 1.6 %collective-permute-start.4 = (f32[16,32,128]{2,1,0:T(8,128)S(1)}, f32[16,32,128]{2,1,0:T(8,128)S(1)}, u32[]{:S(2)}, u32[]{:S(2)}) collective-permute-start(f32[16,32,128]{2,1,0:T(8,128)S(1)} %get-tuple-element.21.refs_2_.refs_5_.refs_3_), channel_id=1, source_target_pairs={{1,0},{0,1},{3,2},{2,3},{5,4},{4,5},{7,6},{6,7},{9,8},{8,9},{11,10... | collective-permute-start | bytes 786440 | tf_op jit(solution)/shard_map/ppermute | solution.py:326
  20.2 1.9 %collective-permute-start.5 = (f32[16,32,128]{2,1,0:T(8,128)S(1)}, f32[16,32,128]{2,1,0:T(8,128)S(1)}, u32[]{:S(2)}, u32[]{:S(2)}) collective-permute-start(f32[16,32,128]{2,1,0:T(8,128)S(1)} %get-tuple-element.22.refs_3_.refs_6_.refs_4_), channel_id=1, source_target_pairs={{1,0},{0,1},{3,2},{2,3},{5,4},{4,5},{7,6},{6,7},{9,8},{8,9},{11,10... | collective-permute-start | bytes 786440 | tf_op jit(solution)/shard_map/ppermute | solution.py:326
  22.1 6.4 %collective-permute-start.6 = (f32[2,136,128]{2,1,0:T(8,128)S(1)}, f32[2,136,128]{2,1,0:T(8,128)S(1)}, u32[]{:S(2)}, u32[]{:S(2)}) collective-permute-start(f32[2,136,128]{2,1,0:T(8,128)S(1)} %after.3), channel_id=1, source_target_pairs={{2,1},{3,0},{0,3},{1,2},{6,5},{7,4},{4,7},{5,6},{10,9},{11,8},{8,1... | collective-permute-start | bytes 417800 | tf_op jit(solution)/shard_map/ppermute | solution.py:332
  31.3 5.1 %collective-permute-start.9 = (f32[32,32,128]{2,1,0:T(8,128)S(1)}, f32[32,32,128]{2,1,0:T(8,128)S(1)}, u32[]{:S(2)}, u32[]{:S(2)}) collective-permute-start(f32[32,32,128]{2,1,0:T(8,128)S(1)} %after.5.refs_7_), channel_id=1, source_target_pairs={{1,0},{0,1},{3,2},{2,3},{5,4},{4,5},{7,6},{6,7},{9,8},{8,9},{11,10... | collective-permute-start | bytes 1572872 | tf_op jit(solution)/shard_map/ppermute | solution.py:347
  32.8 5.4 %collective-permute-start.10 = (f32[32,128]{1,0:T(8,128)S(1)}, f32[32,128]{1,0:T(8,128)S(1)}, u32[]{:S(2)}, u32[]{:S(2)}) collective-permute-start(f32[32,128]{1,0:T(8,128)S(1)} %get-tuple-element.29), channel_id=1, source_target_pairs={{4,0},{8,4},{12,8},{0,12},{5,1},{9,5},{13,9},{1,13},{6,2},{10,6},{... | collective-permute-start | bytes 49160 | tf_op jit(solution)/shard_map/ppermute | solution.py:374
  37.1 4.7 %collective-permute-start.11 = (f32[32,128]{1,0:T(8,128)S(1)}, f32[32,128]{1,0:T(8,128)S(1)}, u32[]{:S(2)}, u32[]{:S(2)}) collective-permute-start(f32[32,128]{1,0:T(8,128)S(1)} %get-tuple-element.30), channel_id=1, source_target_pairs={{8,0},{12,4},{0,8},{4,12},{9,1},{13,5},{1,9},{5,13},{10,2},{14,6},... | collective-permute-start | bytes 49160 | tf_op jit(solution)/shard_map/ppermute | solution.py:374

commit v17 on v16

--- a/solution.py
+++ b/solution.py
@@ -66,10 +66,10 @@
     plan = []
     for shift in range(1, naux // 2 + 1):
         if 2 * shift < naux:
-            plan.append([(source, (source + shift) % naux) for source in range(naux)])
+            plan.append((shift, [(source, (source + shift) % naux) for source in range(naux)]))
         else:
-            plan.append([(z, z + shift) if z % 2 == 0 else (z + shift, z) for z in range(shift)])
-    return plan
+            plan.append((shift, [(z, z + shift) if z % 2 == 0 else (z + shift, z) for z in range(shift)]))
+    return plan[::-1]
 
 
 def select(block, list_rows, slots, width):
@@ -237,8 +237,8 @@
         unfold(by_sub(place, first_half, second_half, 0), ordered, i)
     for tau in range(nt):
         here = [jnp.zeros((half, block), F32)] * naux
-        for shift in range(count):
-            here[(naux - shift) % naux] = ordered[shift, tau * half : (tau + 1) * half, :]
+        for i in range(count):
+            here[(naux - count + i) % naux if i else 0] = ordered[i, tau * half : (tau + 1) * half, :]
         out_ref[tau] = at_sub(place, jnp.concatenate(here, axis=1), 0)
 
 
@@ -249,7 +249,7 @@
     half = block // 2
     for tau in range(nt):
         parts = [jnp.zeros((block, block), F32)] * naux
-        for shift, ref in enumerate(backs, 1):
+        for shift, ref in enumerate(backs[::-1], 1):
             upper = ref[:, tau * half : (tau + 1) * half]
             lower = ref[:, (nt + tau) * half : (nt + tau + 1) * half]
             parts[shift] = at_sub(place, jnp.concatenate([upper, lower], axis=0), 1)
@@ -319,12 +319,12 @@
     )
     mine_other = lax.ppermute(mine, "sub", swap)
     early = [mine_other]
-    for pairs in plan[:-1]:
+    for _, pairs in plan[:-1]:
         parts = call(
             halve, [((share // 2, rows_aux, listed), F32)] * 2, [], 0, lax.ppermute(mine, "aux", pairs), token
         )
         early += [*parts, *(lax.ppermute(part, "sub", swap) for part in parts)]
-    last = lax.ppermute(after(again, lax.ppermute(token, "sub", swap)), "aux", plan[-1])
+    last = lax.ppermute(after(again, lax.ppermute(token, "sub", swap)), "aux", plan[-1][1])
     fars = []
     late_near = after(near, *early)
     for shift in range(1, nob):
@@ -371,7 +371,10 @@
         last_other,
     )
     backs += last_back
-    returned = [lax.ppermute(back, "aux", ring(naux, i)) for i, back in enumerate(backs, 1)]
+    returned = [
+        lax.ppermute(back, "aux", [(target, source) for source, target in pairs])
+        for back, (_, pairs) in zip(backs, plan)
+    ]
     shape = ((nt, block_aux, nauxf), F32)
     (direct,) = call(
         meet_direct, [shape], [scratch(count)], work, sides, direct, tensor, nt=nt, naux=naux

time: 52.1 us -> 51.6 us (level)
  waiting for transfers between devices: 16.6 us -> 20 us
  starting transfers between devices: 15.5 us -> 12.5 us
  blocking collectives: 9.05 us -> 8.27 us
    ppermute x1, starting transfers between devices: 4.51 us -> 0.01 us  [local(): lax.ppermute(after(again, lax.ppermute(token, 'sub', swap)), 'aux', plan[...]
    ppermute x1, waiting for transfers between devices: 0.3 us -> 3.31 us  [local(): lax.ppermute(mine, 'aux', pairs)]
    ppermute x1, starting transfers between devices: 1.63 us -> 4.53 us  [local(): lax.ppermute(mine, 'aux', pairs)]
    ppermute x1, waiting for transfers between devices: 0.95 us -> 3.05 us  [local(): lax.ppermute(after(again, lax.ppermute(token, 'sub', swap)), 'aux', plan[...]
    ppermute x2, starting transfers between devices: 3.93 us -> 2.42 us  [local(): lax.ppermute(back, 'aux', [(target, source) for source, target in pairs])]
    ppermute x2, waiting for transfers between devices: 3.6 us -> 2.63 us  [local(): lax.ppermute(back, 'aux', [(target, source) for source, target in pairs])]
    all_to_all x1, blocking collectives: 9.05 us -> 8.27 us  [local(): lax.all_to_all(partial_chi.reshape(owners, nt * block_aux // owners, naux...]
    ppermute x1, waiting for transfers between devices: 6.16 us -> 5.38 us  [local(): fars.append(lax.ppermute(late_near, ('orb', 'sub'), pairs))]
where the time goes in v17:
time: 51.6 us; the launch traced here: 51.3 us
  waiting for transfers between devices  20 us (39%)
  starting transfers between devices  12.5 us (24%)
  blocking collectives  8.27 us (16%)
  Pallas kernels  7.16 us (14%)
  other arithmetic  2.08 us (4%)
  local copies, waits for them, and re-layouts  1.27 us (2%)
    all_to_all x1, blocking collectives, local(): lax.all_to_all(partial_chi.reshape(owners, nt * block_aux // owners, naux...  8.27 us
    pallas_call x8, Pallas kernels, call(): pl.pallas_call(here, out_shape=shapes, in_specs=[VMEM] * len(arguments),...  7.16 us
    ppermute x1, waiting for transfers between devices, local(): fars.append(lax.ppermute(late_near, ('orb', 'sub'), pairs))  5.38 us
    ppermute x1, starting transfers between devices, local(): lax.ppermute(mine, 'aux', pairs)  4.53 us
    ppermute x1, waiting for transfers between devices, local(): lax.ppermute(mine, 'aux', pairs)  3.31 us
    ppermute x1, waiting for transfers between devices, local(): lax.ppermute(small, 'tau', ring(nt, shift))  3.06 us
    ppermute x1, waiting for transfers between devices, local(): lax.ppermute(after(again, lax.ppermute(token, 'sub', swap)), 'aux', plan[...  3.05 us
    ppermute x1, starting transfers between devices, local(): lax.ppermute(tensor, 'orb', ring(nob, shift))  2.94 us
  transfers between devices with their start and end apart: 12, of which 8 were waited for; matrix products, arithmetic and copies ran while one was open for 3% of the time, Pallas kernels for 13%

profile of v17, /device:TPU:0, one launch (start us, length us, event | category | flops | bytes accessed | tf_op | source)
XLA Modules:
  0.0 51.3 jit_solution(8631991014107830718)
XLA Ops:
  0.0 2.9 %collective-permute-start.1 = (f32[128,2048]{1,0:T(8,128)}, f32[128,2048]{1,0:T(8,128)S(1)}, u32[]{:S(2)}, u32[]{:S(2)}) collective-permute-start(f32[128,2048]{1,0:T(8,128)} %bitcast.5), channel_id=1, source_target_pairs={{2,0},{0,2},{3,1},{1,3},{6,4},{4,6},{7,5},{5,7},{10,8},{8,10},{11,... | collective-permute-start | bytes 3145736 | tf_op jit(solution)/shard_map/ppermute | solution.py:292
  2.9 1.3 %copy-done = f32[1,1,2,64,2048]{4,3,2,1,0:T(8,128)S(1)} copy-done((f32[1,1,2,64,2048]{4,3,2,1,0:T(8,128)S(1)}, f32[1,1,2,64,2048]{4,3,2,1,0:T(8,128)}, u32[]{:S(2)}) %copy-start) | copy-done | bytes 1048600
  4.2 0.6 %prepare.1 = (f32[32,32,128]{2,1,0:T(8,128)S(1)}, f32[32,32,128]{2,1,0:T(8,128)S(1)}) custom-call(f32[128,2048]{1,0:T(8,128)S(1)} %bitcast.6), custom_call_target="tpu_custom_call" | custom-call | bytes 1048576 | tf_op jit(solution)/shard_map/prepare/pallas_call | solution.py:281
  4.8 4.5 %collective-permute-start.3 = (f32[32,32,128]{2,1,0:T(8,128)S(1)}, f32[32,32,128]{2,1,0:T(8,128)S(1)}, u32[]{:S(2)}, u32[]{:S(2)}) collective-permute-start(f32[32,32,128]{2,1,0:T(8,128)S(1)} %get-tuple-element.19.refs_1_), channel_id=1, source_target_pairs={{0,8},{12,4},{1,9},{13,5},{2,10},{14,6},{3,11},{15,7},{16,24},{28,... | collective-permute-start | bytes 1572872 | tf_op jit(solution)/shard_map/ppermute | solution.py:324
  9.3 0.1 collective-permute-start.2
  9.4 0.7 %convert_element_type.5 = f32[1,2]{1,0:T(1,128)S(1)} convert(s32[1,2]{1,0:T(1,128)} %param.7) | non-fusion elementwise | flops 2 | bytes 16 | tf_op jit(solution)/shard_map/convert_element_type | solution.py:302
  10.1 0.8 %fusion = (f32[1,136,128]{2,1,0:T(8,128)S(1)}, f32[136,128]{1,0:T(8,128)S(1)}) fusion(f32[1,2]{1,0:T(1,128)S(1)} %convert_element_type.5, f32[64,128]{1,0:T(8,128)} %param.6, f32[64,128]{1,0:T(8,128)} %param.5), kind=kLoop, calls=%fused_computation.4 | loop fusion | flops 69632 | bytes 204808 | tf_op jit(solution)/shard_map/stack | solution.py:305
  10.9 1.6 %collective-permute-start = (f32[136,128]{1,0:T(8,128)S(1)}, f32[136,128]{1,0:T(8,128)S(1)}, u32[]{:S(2)}, u32[]{:S(2)}) collective-permute-start(f32[136,128]{1,0:T(8,128)S(1)} %get-tuple-element.32), channel_id=1, source_target_pairs={{16,0},{0,16},{17,1},{1,17},{18,2},{2,18},{19,3},{3,19},{20,4},{4,... | collective-permute-start | bytes 208904 | tf_op jit(solution)/shard_map/ppermute | solution.py:305
  12.4 3.1 %collective-permute-done = f32[136,128]{1,0:T(8,128)S(1)} collective-permute-done((f32[136,128]{1,0:T(8,128)S(1)}, f32[136,128]{1,0:T(8,128)S(1)}, u32[]{:S(2)}, u32[]{:S(2)}) %collective-permute-start) | collective-permute-done | bytes 69664 | tf_op jit(solution)/shard_map/ppermute | solution.py:305
  15.5 1.5 %first.1 = (f32[4,512,256]{2,1,0:T(8,128)S(1)}, f32[8,128]{1,0:T(8,128)S(1)}) custom-call(f32[2,136,128]{2,1,0:T(8,128)S(1)} %pad_maximum_fusion.refs_0_, f32[128,2048]{1,0:T(8,128)S(1)} %bitcast.7), custom_call_target="tpu_custom_call" | custom-call | bytes 1187840 | tf_op jit(solution)/shard_map/first/pallas_call | solution.py:281
  17.0 0.1 collective-permute-start.7
  17.1 1.2 %collective-permute-done.7.refs_1_ = f32[8,128]{1,0:T(8,128)S(1)} collective-permute-done((f32[8,128]{1,0:T(8,128)S(1)}, f32[8,128]{1,0:T(8,128)S(1)}, u32[]{:S(2)}, u32[]{:S(2)}) %collective-permute-start.7) | collective-permute-done | bytes 4128 | tf_op jit(solution)/shard_map/ppermute | solution.py:327
  18.3 0.0 collective-permute-start.8
  18.3 3.3 %collective-permute-done.3.refs_0_ = f32[32,32,128]{2,1,0:T(8,128)S(1)} collective-permute-done((f32[32,32,128]{2,1,0:T(8,128)S(1)}, f32[32,32,128]{2,1,0:T(8,128)S(1)}, u32[]{:S(2)}, u32[]{:S(2)}) %collective-permute-start.3) | collective-permute-done | bytes 524320 | tf_op jit(solution)/shard_map/ppermute | solution.py:324
  21.6 0.1 collective-permute-start.4
  21.7 0.5 collective-permute-start.5
  22.2 0.0 collective-permute-done.2.refs_1_.refs_4_.refs_2_
  22.2 1.0 %collective-permute-done.4.refs_4_.refs_7_.refs_5_ = f32[16,32,128]{2,1,0:T(8,128)S(1)} collective-permute-done((f32[16,32,128]{2,1,0:T(8,128)S(1)}, f32[16,32,128]{2,1,0:T(8,128)S(1)}, u32[]{:S(2)}, u32[]{:S(2)}) %collective-permute-start.4) | collective-permute-done | bytes 262176 | tf_op jit(solution)/shard_map/ppermute | solution.py:326
  23.2 0.4 collective-permute-done.5.refs_5_.refs_8_.refs_6_
  23.6 0.3 collective-permute-start.6
  23.9 5.4 %collective-permute-done.6.refs_3_ = f32[2,136,128]{2,1,0:T(8,128)S(1)} collective-permute-done((f32[2,136,128]{2,1,0:T(8,128)S(1)}, f32[2,136,128]{2,1,0:T(8,128)S(1)}, u32[]{:S(2)}, u32[]{:S(2)}) %collective-permute-start.6) | collective-permute-done | bytes 139296 | tf_op jit(solution)/shard_map/ppermute | solution.py:332
  29.2 1.7 %second.1 = (bf16[256,4096]{1,0:T(8,128)(2,1)S(1)}, f32[8,128]{1,0:T(8,128)S(1)}) custom-call(f32[2,136,128]{2,1,0:T(8,128)S(1)} %pad_maximum_fusion.refs_0_, f32[4,512,256]{2,1,0:T(8,128)S(1)} %get-tuple-element.18.refs_1_, f32[128,2048]{1,0:T(8,128)S(1)} %collective-permute-done.1.refs_2_, f32[2,136,128]{2,1,0:T(8,128)S(1)} %collective-permute-done.6.refs_3_, ...), custom_call_target="tpu_custom_call" | custom-call | flops 603979776 | bytes 4997120 | tf_op jit(solution)/shard_map/second/pallas_call | solution.py:281
  31.0 3.0 %collective-permute-done.8.refs_0_ = f32[32,32,128]{2,1,0:T(8,128)S(1)} collective-permute-done((f32[32,32,128]{2,1,0:T(8,128)S(1)}, f32[32,32,128]{2,1,0:T(8,128)S(1)}, u32[]{:S(2)}, u32[]{:S(2)}) %collective-permute-start.8) | collective-permute-done | bytes 524320 | tf_op jit(solution)/shard_map/ppermute | solution.py:327
  34.0 1.5 %meet_own.1 = (f32[160,64]{1,0:T(8,128)S(1)}, f32[32,64]{1,0:T(8,128)S(1)}, f32[32,128]{1,0:T(8,128)S(1)}) custom-call(bf16[256,4096]{1,0:T(8,128)(2,1)S(1)} %get-tuple-element.23.refs_0_, f32[32,32,128]{2,1,0:T(8,128)S(1)} %get-tuple-element.19.refs_1_, f32[32,32,128]{2,1,0:T(8,128)S(1)} %collective-permute-done.2.refs_1_.refs_4_.refs_2_, ...), custom_call_target="tpu_custom_call" | custom-call | flops 1342177280 | bytes 6815744 | tf_op jit(solution)/shard_map/meet_own/pallas_call | solution.py:281
  35.6 1.3 %collective-permute-start.10 = (f32[32,128]{1,0:T(8,128)S(1)}, f32[32,128]{1,0:T(8,128)S(1)}, u32[]{:S(2)}, u32[]{:S(2)}) collective-permute-start(f32[32,128]{1,0:T(8,128)S(1)} %get-tuple-element.29), channel_id=1, source_target_pairs={{8,0},{4,12},{9,1},{5,13},{10,2},{6,14},{11,3},{7,15},{24,16},{20,... | collective-permute-start | bytes 49160 | tf_op jit(solution)/shard_map/ppermute | solution.py:375
  36.9 0.7 %meet_back.1 = (bf16[64,4096]{1,0:T(8,128)(2,1)S(1)}, f32[32,128]{1,0:T(8,128)S(1)}) custom-call(bf16[256,4096]{1,0:T(8,128)(2,1)S(1)} %get-tuple-element.23.refs_0_, f32[32,64]{1,0:T(8,128)S(1)} %get-tuple-element.27.refs_1_, f32[32,32,128]{2,1,0:T(8,128)S(1)} %collective-permute-done.9.refs_2_), custom_call_target="tpu_custom_call" | custom-call | flops 134217728 | bytes 4726784 | tf_op jit(solution)/shard_map/meet_back/pallas_call | solution.py:281
  37.6 1.1 %collective-permute-start.11 = (f32[32,128]{1,0:T(8,128)S(1)}, f32[32,128]{1,0:T(8,128)S(1)}, u32[]{:S(2)}, u32[]{:S(2)}) collective-permute-start(f32[32,128]{1,0:T(8,128)S(1)} %get-tuple-element.30), channel_id=1, source_target_pairs={{4,0},{8,4},{12,8},{0,12},{5,1},{9,5},{13,9},{1,13},{6,2},{10,6},{... | collective-permute-start | bytes 49160 | tf_op jit(solution)/shard_map/ppermute | solution.py:375
  38.7 0.7 %meet_direct.1.refs_0_ = f32[2,64,256]{2,1,0:T(8,128)S(1)} custom-call(bf16[256,4096]{1,0:T(8,128)(2,1)S(1)} %get-tuple-element.23.refs_0_, f32[160,64]{1,0:T(8,128)S(1)} %get-tuple-element.26.refs_1_, bf16[64,4096]{1,0:T(8,128)(2,1)S(1)} %get-tuple-element.28.refs_2_), custom_call_target="tpu_custom_call" | custom-call | flops 134217728 | bytes 5283840 | tf_op jit(solution)/shard_map/meet_direct/pallas_call | solution.py:281
  39.5 2.6 %collective-permute-done.10.refs_1_ = f32[32,128]{1,0:T(8,128)S(1)} collective-permute-done((f32[32,128]{1,0:T(8,128)S(1)}, f32[32,128]{1,0:T(8,128)S(1)}, u32[]{:S(2)}, u32[]{:S(2)}) %collective-permute-start.10) | collective-permute-done | bytes 16416 | tf_op jit(solution)/shard_map/ppermute | solution.py:375
  42.1 0.3 complete.1
  42.4 8.3 %all_to_all.5 = f32[8,16,256]{2,1,0:T(8,128)S(1)} all-to-all(f32[8,16,256]{2,1,0:T(8,128)S(1)} %bitcast.8), channel_id=1, replica_groups=mesh['tau'=2,'aux'=4,'orb'=2,'sub'=2] {'tau','orb','sub'}, dimensions={0} | all-to-all | bytes 262144 | tf_op jit(solution)/shard_map/all_to_all | solution.py:384
  50.7 0.6 %broadcast_multiply_fusion = f32[16,256]{1,0:T(8,128)} fusion(f32[16,256]{1,0:T(8,128)S(1)} %reduce_sum.9), kind=kLoop, calls=%fused_computation.3 | loop fusion | flops 4096 | bytes 32768 | tf_op jit(solution)/shard_map/mul | solution.py:391
  (14 shorter events, 0.1 us)
Async XLA Ops:
  0.0 29.2 %collective-permute-start.1 = (f32[128,2048]{1,0:T(8,128)}, f32[128,2048]{1,0:T(8,128)S(1)}, u32[]{:S(2)}, u32[]{:S(2)}) collective-permute-start(f32[128,2048]{1,0:T(8,128)} %bitcast.5), channel_id=1, source_target_pairs={{2,0},{0,2},{3,1},{1,3},{6,4},{4,6},{7,5},{5,7},{10,8},{8,10},{11,... | collective-permute-start | bytes 3145736 | tf_op jit(solution)/shard_map/ppermute | solution.py:292
  2.9 1.3 %copy-start = (f32[1,1,2,64,2048]{4,3,2,1,0:T(8,128)S(1)}, f32[1,1,2,64,2048]{4,3,2,1,0:T(8,128)}, u32[]{:S(2)}) copy-start(f32[1,1,2,64,2048]{4,3,2,1,0:T(8,128)} %param.4) | copy-start | bytes 3145732
  4.2 11.3 %copy-start.1 = (f32[1,1,2,64,2048]{4,3,2,1,0:T(8,128)S(1)}, f32[1,1,2,64,2048]{4,3,2,1,0:T(8,128)}, u32[]{:S(2)}) copy-start(f32[1,1,2,64,2048]{4,3,2,1,0:T(8,128)} %param.4) | copy-start | bytes 3145732
  4.8 16.8 %collective-permute-start.3 = (f32[32,32,128]{2,1,0:T(8,128)S(1)}, f32[32,32,128]{2,1,0:T(8,128)S(1)}, u32[]{:S(2)}, u32[]{:S(2)}) collective-permute-start(f32[32,32,128]{2,1,0:T(8,128)S(1)} %get-tuple-element.19.refs_1_), channel_id=1, source_target_pairs={{0,8},{12,4},{1,9},{13,5},{2,10},{14,6},{3,11},{15,7},{16,24},{28,... | collective-permute-start | bytes 1572872 | tf_op jit(solution)/shard_map/ppermute | solution.py:324
  9.3 12.9 %collective-permute-start.2 = (f32[32,32,128]{2,1,0:T(8,128)S(1)}, f32[32,32,128]{2,1,0:T(8,128)S(1)}, u32[]{:S(2)}, u32[]{:S(2)}) collective-permute-start(f32[32,32,128]{2,1,0:T(8,128)S(1)} %get-tuple-element.19.refs_1_), channel_id=1, source_target_pairs={{1,0},{0,1},{3,2},{2,3},{5,4},{4,5},{7,6},{6,7},{9,8},{8,9},{11,10... | collective-permute-start | bytes 1572872 | tf_op jit(solution)/shard_map/ppermute | solution.py:320
  10.9 4.6 %collective-permute-start = (f32[136,128]{1,0:T(8,128)S(1)}, f32[136,128]{1,0:T(8,128)S(1)}, u32[]{:S(2)}, u32[]{:S(2)}) collective-permute-start(f32[136,128]{1,0:T(8,128)S(1)} %get-tuple-element.32), channel_id=1, source_target_pairs={{16,0},{0,16},{17,1},{1,17},{18,2},{2,18},{19,3},{3,19},{20,4},{4,... | collective-permute-start | bytes 208904 | tf_op jit(solution)/shard_map/ppermute | solution.py:305
  17.0 1.2 %collective-permute-start.7 = (f32[8,128]{1,0:T(8,128)S(1)}, f32[8,128]{1,0:T(8,128)S(1)}, u32[]{:S(2)}, u32[]{:S(2)}) collective-permute-start(f32[8,128]{1,0:T(8,128)S(1)} %get-tuple-element.20.refs_1_), channel_id=1, source_target_pairs={{1,0},{0,1},{3,2},{2,3},{5,4},{4,5},{7,6},{6,7},{9,8},{8,9},{11,10... | collective-permute-start | bytes 12296 | tf_op jit(solution)/shard_map/ppermute | solution.py:327
  18.3 15.8 %collective-permute-start.8 = (f32[32,32,128]{2,1,0:T(8,128)S(1)}, f32[32,32,128]{2,1,0:T(8,128)S(1)}, u32[]{:S(2)}, u32[]{:S(2)}) collective-permute-start(f32[32,32,128]{2,1,0:T(8,128)S(1)} %after.4), channel_id=1, source_target_pairs={{0,4},{4,8},{8,12},{12,0},{1,5},{5,9},{9,13},{13,1},{2,6},{6,10},{... | collective-permute-start | bytes 1572872 | tf_op jit(solution)/shard_map/ppermute | solution.py:327
  21.6 1.6 %collective-permute-start.4 = (f32[16,32,128]{2,1,0:T(8,128)S(1)}, f32[16,32,128]{2,1,0:T(8,128)S(1)}, u32[]{:S(2)}, u32[]{:S(2)}) collective-permute-start(f32[16,32,128]{2,1,0:T(8,128)S(1)} %get-tuple-element.21.refs_2_.refs_5_.refs_3_), channel_id=1, source_target_pairs={{1,0},{0,1},{3,2},{2,3},{5,4},{4,5},{7,6},{6,7},{9,8},{8,9},{11,10... | collective-permute-start | bytes 786440 | tf_op jit(solution)/shard_map/ppermute | solution.py:326
  21.7 1.9 %collective-permute-start.5 = (f32[16,32,128]{2,1,0:T(8,128)S(1)}, f32[16,32,128]{2,1,0:T(8,128)S(1)}, u32[]{:S(2)}, u32[]{:S(2)}) collective-permute-start(f32[16,32,128]{2,1,0:T(8,128)S(1)} %get-tuple-element.22.refs_3_.refs_6_.refs_4_), channel_id=1, source_target_pairs={{1,0},{0,1},{3,2},{2,3},{5,4},{4,5},{7,6},{6,7},{9,8},{8,9},{11,10... | collective-permute-start | bytes 786440 | tf_op jit(solution)/shard_map/ppermute | solution.py:326
  23.6 5.7 %collective-permute-start.6 = (f32[2,136,128]{2,1,0:T(8,128)S(1)}, f32[2,136,128]{2,1,0:T(8,128)S(1)}, u32[]{:S(2)}, u32[]{:S(2)}) collective-permute-start(f32[2,136,128]{2,1,0:T(8,128)S(1)} %after.3), channel_id=1, source_target_pairs={{2,1},{3,0},{0,3},{1,2},{6,5},{7,4},{4,7},{5,6},{10,9},{11,8},{8,1... | collective-permute-start | bytes 417800 | tf_op jit(solution)/shard_map/ppermute | solution.py:332
  34.0 2.8 %collective-permute-start.9 = (f32[32,32,128]{2,1,0:T(8,128)S(1)}, f32[32,32,128]{2,1,0:T(8,128)S(1)}, u32[]{:S(2)}, u32[]{:S(2)}) collective-permute-start(f32[32,32,128]{2,1,0:T(8,128)S(1)} %after.5.refs_7_), channel_id=1, source_target_pairs={{1,0},{0,1},{3,2},{2,3},{5,4},{4,5},{7,6},{6,7},{9,8},{8,9},{11,10... | collective-permute-start | bytes 1572872 | tf_op jit(solution)/shard_map/ppermute | solution.py:347
  35.6 6.5 %collective-permute-start.10 = (f32[32,128]{1,0:T(8,128)S(1)}, f32[32,128]{1,0:T(8,128)S(1)}, u32[]{:S(2)}, u32[]{:S(2)}) collective-permute-start(f32[32,128]{1,0:T(8,128)S(1)} %get-tuple-element.29), channel_id=1, source_target_pairs={{8,0},{4,12},{9,1},{5,13},{10,2},{6,14},{11,3},{7,15},{24,16},{20,... | collective-permute-start | bytes 49160 | tf_op jit(solution)/shard_map/ppermute | solution.py:375
  37.6 4.5 %collective-permute-start.11 = (f32[32,128]{1,0:T(8,128)S(1)}, f32[32,128]{1,0:T(8,128)S(1)}, u32[]{:S(2)}, u32[]{:S(2)}) collective-permute-start(f32[32,128]{1,0:T(8,128)S(1)} %get-tuple-element.30), channel_id=1, source_target_pairs={{4,0},{8,4},{12,8},{0,12},{5,1},{9,5},{13,9},{1,13},{6,2},{10,6},{... | collective-permute-start | bytes 49160 | tf_op jit(solution)/shard_map/ppermute | solution.py:375

commit v18 on v16

--- a/solution.py
+++ b/solution.py
@@ -242,19 +242,16 @@
         out_ref[tau] = at_sub(place, jnp.concatenate(here, axis=1), 0)
 
 
-def complete(place, early, *refs):
-    backs, out_ref = refs[:-1], refs[-1]
+def add(place, early, back, out_ref, *, shift, last):
     nt, block, wide = early.shape
-    naux = wide // block
     half = block // 2
     for tau in range(nt):
-        parts = [jnp.zeros((block, block), F32)] * naux
-        for shift, ref in enumerate(backs, 1):
-            upper = ref[:, tau * half : (tau + 1) * half]
-            lower = ref[:, (nt + tau) * half : (nt + tau + 1) * half]
-            parts[shift] = at_sub(place, jnp.concatenate([upper, lower], axis=0), 1)
+        upper = back[:, tau * half : (tau + 1) * half]
+        lower = back[:, (nt + tau) * half : (nt + tau + 1) * half]
+        parts = [jnp.zeros((block, block), F32)] * (wide // block)
+        parts[shift] = at_sub(place, jnp.concatenate([upper, lower], axis=0), 1)
         total = early[tau] + jnp.concatenate(parts, axis=1)
-        out_ref[tau] = pltpu.roll(total, place[3] * block, 1)
+        out_ref[tau] = pltpu.roll(total, place[3] * block, 1) if last else total
 
 
 def local(three_center, occupied_green, virtual_green, block_list, sizes):
@@ -371,12 +368,17 @@
         last_other,
     )
     backs += last_back
-    returned = [lax.ppermute(back, "aux", ring(naux, i)) for i, back in enumerate(backs, 1)]
+    backs[:-1] = [after(back, backs[-1]) for back in backs[:-1]]
+    returned = [
+        lax.ppermute(back, "aux", [(target, source) for source, target in pairs]) for back, pairs in zip(backs, plan)
+    ]
     shape = ((nt, block_aux, nauxf), F32)
     (direct,) = call(
         meet_direct, [shape], [scratch(count)], work, sides, direct, tensor, nt=nt, naux=naux
     )
-    (partial_chi,) = call(complete, [shape], [], 0, direct, *returned)
+    partial_chi = direct
+    for i in range(len(plan), 0, -1):
+        (partial_chi,) = call(add, [shape], [], 0, partial_chi, returned[i - 1], shift=i, last=i == 1)
     owners = nt * nob * nsub
     received = lax.all_to_all(
         partial_chi.reshape(owners, nt * block_aux // owners, nauxf),

time: 52.1 us -> 51.7 us (level)
  waiting for transfers between devices: 16.6 us -> 15.4 us
  starting transfers between devices: 15.5 us -> 16.2 us
    ppermute x2, waiting for transfers between devices: 3.6 us -> 2 us  [local(): lax.ppermute(back, 'aux', [(target, source) for source, target in pairs])]
    ppermute x2, starting transfers between devices: 3.93 us -> 4.59 us  [local(): lax.ppermute(back, 'aux', [(target, source) for source, target in pairs])]
    pallas_call x8 -> x9, Pallas kernels: 7.15 us -> 7.27 us  [call(): pl.pallas_call(here, out_shape=shapes, in_specs=[VMEM] * len(arguments),...]
  transfers between devices with their start and end apart: 12 -> 12, of which waited for: 8 -> 10; matrix products, arithmetic and copies ran while one was open for 3% -> 3% of each run, Pallas kernels for 13% -> 12%
where the time goes in v18:
time: 51.7 us; the launch traced here: 51.4 us
  starting transfers between devices  16.2 us (31%)
  waiting for transfers between devices  15.4 us (30%)
  blocking collectives  9.05 us (18%)
  Pallas kernels  7.28 us (14%)
  other arithmetic  2.07 us (4%)
  local copies, waits for them, and re-layouts  1.27 us (2%)
    all_to_all x1, blocking collectives, local(): lax.all_to_all(partial_chi.reshape(owners, nt * block_aux // owners, naux...  9.05 us
    pallas_call x9, Pallas kernels, call(): pl.pallas_call(here, out_shape=shapes, in_specs=[VMEM] * len(arguments),...  7.27 us
    ppermute x1, waiting for transfers between devices, local(): fars.append(lax.ppermute(late_near, ('orb', 'sub'), pairs))  6.16 us
    ppermute x2, starting transfers between devices, local(): lax.ppermute(back, 'aux', [(target, source) for source, target in pairs])  4.59 us
    ppermute x1, starting transfers between devices, local(): lax.ppermute(after(again, lax.ppermute(token, 'sub', swap)), 'aux', plan[...  4.51 us
    ppermute x1, waiting for transfers between devices, local(): lax.ppermute(small, 'tau', ring(nt, shift))  3.07 us
    ppermute x1, starting transfers between devices, local(): lax.ppermute(tensor, 'orb', ring(nob, shift))  2.94 us
    ppermute x2, waiting for transfers between devices, local(): lax.ppermute(back, 'aux', [(target, source) for source, target in pairs])  2 us
  transfers between devices with their start and end apart: 12, of which 10 were waited for; matrix products, arithmetic and copies ran while one was open for 3% of the time, Pallas kernels for 12%

profile of v18, /device:TPU:0, one launch (start us, length us, event | category | flops | bytes accessed | tf_op | source)
XLA Modules:
  0.0 51.4 jit_solution(15770816317618406500)
XLA Ops:
  0.0 2.9 %collective-permute-start.1 = (f32[128,2048]{1,0:T(8,128)}, f32[128,2048]{1,0:T(8,128)S(1)}, u32[]{:S(2)}, u32[]{:S(2)}) collective-permute-start(f32[128,2048]{1,0:T(8,128)} %bitcast.5), channel_id=1, source_target_pairs={{2,0},{0,2},{3,1},{1,3},{6,4},{4,6},{7,5},{5,7},{10,8},{8,10},{11,... | collective-permute-start | bytes 3145736 | tf_op jit(solution)/shard_map/ppermute | solution.py:289
  2.9 1.3 %copy-done = f32[1,1,2,64,2048]{4,3,2,1,0:T(8,128)S(1)} copy-done((f32[1,1,2,64,2048]{4,3,2,1,0:T(8,128)S(1)}, f32[1,1,2,64,2048]{4,3,2,1,0:T(8,128)}, u32[]{:S(2)}) %copy-start) | copy-done | bytes 1048600
  4.2 0.6 %prepare.1 = (f32[32,32,128]{2,1,0:T(8,128)S(1)}, f32[32,32,128]{2,1,0:T(8,128)S(1)}) custom-call(f32[128,2048]{1,0:T(8,128)S(1)} %bitcast.6), custom_call_target="tpu_custom_call" | custom-call | bytes 1048576 | tf_op jit(solution)/shard_map/prepare/pallas_call | solution.py:278
  4.8 1.6 %collective-permute-start.3 = (f32[32,32,128]{2,1,0:T(8,128)S(1)}, f32[32,32,128]{2,1,0:T(8,128)S(1)}, u32[]{:S(2)}, u32[]{:S(2)}) collective-permute-start(f32[32,32,128]{2,1,0:T(8,128)S(1)} %get-tuple-element.19.refs_1_), channel_id=1, source_target_pairs={{0,4},{4,8},{8,12},{12,0},{1,5},{5,9},{9,13},{13,1},{2,6},{6,10},{... | collective-permute-start | bytes 1572872 | tf_op jit(solution)/shard_map/ppermute | solution.py:321
  6.4 0.7 %convert_element_type.5 = f32[1,2]{1,0:T(1,128)S(1)} convert(s32[1,2]{1,0:T(1,128)} %param.7) | non-fusion elementwise | flops 2 | bytes 16 | tf_op jit(solution)/shard_map/convert_element_type | solution.py:299
  7.1 0.8 %fusion = (f32[1,136,128]{2,1,0:T(8,128)S(1)}, f32[136,128]{1,0:T(8,128)S(1)}) fusion(f32[1,2]{1,0:T(1,128)S(1)} %convert_element_type.5, f32[64,128]{1,0:T(8,128)} %param.6, f32[64,128]{1,0:T(8,128)} %param.5), kind=kLoop, calls=%fused_computation.4 | loop fusion | flops 69632 | bytes 204808 | tf_op jit(solution)/shard_map/stack | solution.py:302
  7.9 1.6 %collective-permute-start = (f32[136,128]{1,0:T(8,128)S(1)}, f32[136,128]{1,0:T(8,128)S(1)}, u32[]{:S(2)}, u32[]{:S(2)}) collective-permute-start(f32[136,128]{1,0:T(8,128)S(1)} %get-tuple-element.32), channel_id=1, source_target_pairs={{16,0},{0,16},{17,1},{1,17},{18,2},{2,18},{19,3},{3,19},{20,4},{4,... | collective-permute-start | bytes 208904 | tf_op jit(solution)/shard_map/ppermute | solution.py:302
  9.5 3.1 %collective-permute-done = f32[136,128]{1,0:T(8,128)S(1)} collective-permute-done((f32[136,128]{1,0:T(8,128)S(1)}, f32[136,128]{1,0:T(8,128)S(1)}, u32[]{:S(2)}, u32[]{:S(2)}) %collective-permute-start) | collective-permute-done | bytes 69664 | tf_op jit(solution)/shard_map/ppermute | solution.py:302
  12.6 1.5 %first.1 = (f32[4,512,256]{2,1,0:T(8,128)S(1)}, f32[8,128]{1,0:T(8,128)S(1)}) custom-call(f32[2,136,128]{2,1,0:T(8,128)S(1)} %pad_maximum_fusion.refs_0_, f32[128,2048]{1,0:T(8,128)S(1)} %bitcast.7), custom_call_target="tpu_custom_call" | custom-call | bytes 1187840 | tf_op jit(solution)/shard_map/first/pallas_call | solution.py:278
  14.0 0.1 collective-permute-start.7
  14.1 1.2 %collective-permute-done.7.refs_1_ = f32[8,128]{1,0:T(8,128)S(1)} collective-permute-done((f32[8,128]{1,0:T(8,128)S(1)}, f32[8,128]{1,0:T(8,128)S(1)}, u32[]{:S(2)}, u32[]{:S(2)}) %collective-permute-start.7) | collective-permute-done | bytes 4128 | tf_op jit(solution)/shard_map/ppermute | solution.py:324
  15.3 4.5 %collective-permute-start.8 = (f32[32,32,128]{2,1,0:T(8,128)S(1)}, f32[32,32,128]{2,1,0:T(8,128)S(1)}, u32[]{:S(2)}, u32[]{:S(2)}) collective-permute-start(f32[32,32,128]{2,1,0:T(8,128)S(1)} %after.5), channel_id=1, source_target_pairs={{0,8},{12,4},{1,9},{13,5},{2,10},{14,6},{3,11},{15,7},{16,24},{28,... | collective-permute-start | bytes 1572872 | tf_op jit(solution)/shard_map/ppermute | solution.py:324
  19.8 0.3 collective-permute-done.3.refs_0_
  20.2 0.5 collective-permute-start.5
  20.7 1.0 %collective-permute-done.4.refs_4_.refs_7_.refs_5_ = f32[16,32,128]{2,1,0:T(8,128)S(1)} collective-permute-done((f32[16,32,128]{2,1,0:T(8,128)S(1)}, f32[16,32,128]{2,1,0:T(8,128)S(1)}, u32[]{:S(2)}, u32[]{:S(2)}) %collective-permute-start.4) | collective-permute-done | bytes 262176 | tf_op jit(solution)/shard_map/ppermute | solution.py:323
  21.7 0.4 collective-permute-done.5.refs_5_.refs_8_.refs_6_
  22.1 0.3 collective-permute-start.6
  22.4 6.2 %collective-permute-done.6.refs_3_ = f32[2,136,128]{2,1,0:T(8,128)S(1)} collective-permute-done((f32[2,136,128]{2,1,0:T(8,128)S(1)}, f32[2,136,128]{2,1,0:T(8,128)S(1)}, u32[]{:S(2)}, u32[]{:S(2)}) %collective-permute-start.6) | collective-permute-done | bytes 139296 | tf_op jit(solution)/shard_map/ppermute | solution.py:329
  28.6 1.8 %second.1 = (bf16[256,4096]{1,0:T(8,128)(2,1)S(1)}, f32[8,128]{1,0:T(8,128)S(1)}) custom-call(f32[2,136,128]{2,1,0:T(8,128)S(1)} %pad_maximum_fusion.refs_0_, f32[4,512,256]{2,1,0:T(8,128)S(1)} %get-tuple-element.18.refs_1_, f32[128,2048]{1,0:T(8,128)S(1)} %collective-permute-done.1.refs_2_, f32[2,136,128]{2,1,0:T(8,128)S(1)} %collective-permute-done.6.refs_3_, ...), custom_call_target="tpu_custom_call" | custom-call | flops 603979776 | bytes 4997120 | tf_op jit(solution)/shard_map/second/pallas_call | solution.py:278
  30.3 0.9 %collective-permute-done.8.refs_0_ = f32[32,32,128]{2,1,0:T(8,128)S(1)} collective-permute-done((f32[32,32,128]{2,1,0:T(8,128)S(1)}, f32[32,32,128]{2,1,0:T(8,128)S(1)}, u32[]{:S(2)}, u32[]{:S(2)}) %collective-permute-start.8) | collective-permute-done | bytes 524320 | tf_op jit(solution)/shard_map/ppermute | solution.py:324
  31.3 1.5 %meet_own.1 = (f32[160,64]{1,0:T(8,128)S(1)}, f32[32,64]{1,0:T(8,128)S(1)}, f32[32,128]{1,0:T(8,128)S(1)}) custom-call(bf16[256,4096]{1,0:T(8,128)(2,1)S(1)} %get-tuple-element.23.refs_0_, f32[32,32,128]{2,1,0:T(8,128)S(1)} %get-tuple-element.19.refs_1_, f32[32,32,128]{2,1,0:T(8,128)S(1)} %collective-permute-done.2.refs_1_.refs_4_.refs_2_, ...), custom_call_target="tpu_custom_call" | custom-call | flops 1342177280 | bytes 6815744 | tf_op jit(solution)/shard_map/meet_own/pallas_call | solution.py:278
  32.8 0.4 collective-permute-done.9.refs_2_
  33.2 0.7 %meet_back.1 = (bf16[64,4096]{1,0:T(8,128)(2,1)S(1)}, f32[32,128]{1,0:T(8,128)S(1)}) custom-call(bf16[256,4096]{1,0:T(8,128)(2,1)S(1)} %get-tuple-element.23.refs_0_, f32[32,64]{1,0:T(8,128)S(1)} %get-tuple-element.27.refs_1_, f32[32,32,128]{2,1,0:T(8,128)S(1)} %collective-permute-done.9.refs_2_), custom_call_target="tpu_custom_call" | custom-call | flops 134217728 | bytes 4726784 | tf_op jit(solution)/shard_map/meet_back/pallas_call | solution.py:278
  33.9 1.3 %collective-permute-start.10 = (f32[32,128]{1,0:T(8,128)S(1)}, f32[32,128]{1,0:T(8,128)S(1)}, u32[]{:S(2)}, u32[]{:S(2)}) collective-permute-start(f32[32,128]{1,0:T(8,128)S(1)} %get-tuple-element.29.refs_1_), channel_id=1, source_target_pairs={{8,0},{4,12},{9,1},{5,13},{10,2},{6,14},{11,3},{7,15},{24,16},{20,... | collective-permute-start | bytes 49160 | tf_op jit(solution)/shard_map/ppermute | solution.py:373
  35.3 3.3 %collective-permute-start.11 = (f32[32,128]{1,0:T(8,128)S(1)}, f32[32,128]{1,0:T(8,128)S(1)}, u32[]{:S(2)}, u32[]{:S(2)}) collective-permute-start(f32[32,128]{1,0:T(8,128)S(1)} %after.7), channel_id=1, source_target_pairs={{4,0},{8,4},{12,8},{0,12},{5,1},{9,5},{13,9},{1,13},{6,2},{10,6},{... | collective-permute-start | bytes 49160 | tf_op jit(solution)/shard_map/ppermute | solution.py:373
  38.5 0.7 %meet_direct.1.refs_0_ = f32[2,64,256]{2,1,0:T(8,128)S(1)} custom-call(bf16[256,4096]{1,0:T(8,128)(2,1)S(1)} %get-tuple-element.23.refs_0_, f32[160,64]{1,0:T(8,128)S(1)} %get-tuple-element.26.refs_1_, bf16[64,4096]{1,0:T(8,128)(2,1)S(1)} %get-tuple-element.28.refs_2_), custom_call_target="tpu_custom_call" | custom-call | flops 134217728 | bytes 5283840 | tf_op jit(solution)/shard_map/meet_direct/pallas_call | solution.py:278
  39.3 1.2 %collective-permute-done.10.refs_1_ = f32[32,128]{1,0:T(8,128)S(1)} collective-permute-done((f32[32,128]{1,0:T(8,128)S(1)}, f32[32,128]{1,0:T(8,128)S(1)}, u32[]{:S(2)}, u32[]{:S(2)}) %collective-permute-start.10) | collective-permute-done | bytes 16416 | tf_op jit(solution)/shard_map/ppermute | solution.py:373
  40.5 0.1 add.4.refs_0_
  40.6 0.8 %collective-permute-done.11.refs_1_ = f32[32,128]{1,0:T(8,128)S(1)} collective-permute-done((f32[32,128]{1,0:T(8,128)S(1)}, f32[32,128]{1,0:T(8,128)S(1)}, u32[]{:S(2)}, u32[]{:S(2)}) %collective-permute-start.11) | collective-permute-done | bytes 16416 | tf_op jit(solution)/shard_map/ppermute | solution.py:373
  41.4 0.3 add.5
  41.7 9.0 %all_to_all.5 = f32[8,16,256]{2,1,0:T(8,128)S(1)} all-to-all(f32[8,16,256]{2,1,0:T(8,128)S(1)} %bitcast.8), channel_id=1, replica_groups=mesh['tau'=2,'aux'=4,'orb'=2,'sub'=2] {'tau','orb','sub'}, dimensions={0} | all-to-all | bytes 262144 | tf_op jit(solution)/shard_map/all_to_all | solution.py:383
  50.8 0.6 %broadcast_multiply_fusion = f32[16,256]{1,0:T(8,128)} fusion(f32[16,256]{1,0:T(8,128)S(1)} %reduce_sum.9), kind=kLoop, calls=%fused_computation.3 | loop fusion | flops 4096 | bytes 32768 | tf_op jit(solution)/shard_map/mul | solution.py:390
  (16 shorter events, 0.2 us)
Async XLA Ops:
  0.0 28.6 %collective-permute-start.1 = (f32[128,2048]{1,0:T(8,128)}, f32[128,2048]{1,0:T(8,128)S(1)}, u32[]{:S(2)}, u32[]{:S(2)}) collective-permute-start(f32[128,2048]{1,0:T(8,128)} %bitcast.5), channel_id=1, source_target_pairs={{2,0},{0,2},{3,1},{1,3},{6,4},{4,6},{7,5},{5,7},{10,8},{8,10},{11,... | collective-permute-start | bytes 3145736 | tf_op jit(solution)/shard_map/ppermute | solution.py:289
  2.9 1.3 %copy-start = (f32[1,1,2,64,2048]{4,3,2,1,0:T(8,128)S(1)}, f32[1,1,2,64,2048]{4,3,2,1,0:T(8,128)}, u32[]{:S(2)}) copy-start(f32[1,1,2,64,2048]{4,3,2,1,0:T(8,128)} %param.4) | copy-start | bytes 3145732
  4.2 8.4 %copy-start.1 = (f32[1,1,2,64,2048]{4,3,2,1,0:T(8,128)S(1)}, f32[1,1,2,64,2048]{4,3,2,1,0:T(8,128)}, u32[]{:S(2)}) copy-start(f32[1,1,2,64,2048]{4,3,2,1,0:T(8,128)} %param.4) | copy-start | bytes 3145732
  4.8 15.3 %collective-permute-start.3 = (f32[32,32,128]{2,1,0:T(8,128)S(1)}, f32[32,32,128]{2,1,0:T(8,128)S(1)}, u32[]{:S(2)}, u32[]{:S(2)}) collective-permute-start(f32[32,32,128]{2,1,0:T(8,128)S(1)} %get-tuple-element.19.refs_1_), channel_id=1, source_target_pairs={{0,4},{4,8},{8,12},{12,0},{1,5},{5,9},{9,13},{13,1},{2,6},{6,10},{... | collective-permute-start | bytes 1572872 | tf_op jit(solution)/shard_map/ppermute | solution.py:321
  6.4 14.3 %collective-permute-start.2 = (f32[32,32,128]{2,1,0:T(8,128)S(1)}, f32[32,32,128]{2,1,0:T(8,128)S(1)}, u32[]{:S(2)}, u32[]{:S(2)}) collective-permute-start(f32[32,32,128]{2,1,0:T(8,128)S(1)} %get-tuple-element.19.refs_1_), channel_id=1, source_target_pairs={{1,0},{0,1},{3,2},{2,3},{5,4},{4,5},{7,6},{6,7},{9,8},{8,9},{11,10... | collective-permute-start | bytes 1572872 | tf_op jit(solution)/shard_map/ppermute | solution.py:317
  7.9 4.7 %collective-permute-start = (f32[136,128]{1,0:T(8,128)S(1)}, f32[136,128]{1,0:T(8,128)S(1)}, u32[]{:S(2)}, u32[]{:S(2)}) collective-permute-start(f32[136,128]{1,0:T(8,128)S(1)} %get-tuple-element.32), channel_id=1, source_target_pairs={{16,0},{0,16},{17,1},{1,17},{18,2},{2,18},{19,3},{3,19},{20,4},{4,... | collective-permute-start | bytes 208904 | tf_op jit(solution)/shard_map/ppermute | solution.py:302
  14.0 1.2 %collective-permute-start.7 = (f32[8,128]{1,0:T(8,128)S(1)}, f32[8,128]{1,0:T(8,128)S(1)}, u32[]{:S(2)}, u32[]{:S(2)}) collective-permute-start(f32[8,128]{1,0:T(8,128)S(1)} %get-tuple-element.20.refs_1_), channel_id=1, source_target_pairs={{1,0},{0,1},{3,2},{2,3},{5,4},{4,5},{7,6},{6,7},{9,8},{8,9},{11,10... | collective-permute-start | bytes 12296 | tf_op jit(solution)/shard_map/ppermute | solution.py:324
  15.3 16.0 %collective-permute-start.8 = (f32[32,32,128]{2,1,0:T(8,128)S(1)}, f32[32,32,128]{2,1,0:T(8,128)S(1)}, u32[]{:S(2)}, u32[]{:S(2)}) collective-permute-start(f32[32,32,128]{2,1,0:T(8,128)S(1)} %after.5), channel_id=1, source_target_pairs={{0,8},{12,4},{1,9},{13,5},{2,10},{14,6},{3,11},{15,7},{16,24},{28,... | collective-permute-start | bytes 1572872 | tf_op jit(solution)/shard_map/ppermute | solution.py:324
  20.1 1.6 %collective-permute-start.4 = (f32[16,32,128]{2,1,0:T(8,128)S(1)}, f32[16,32,128]{2,1,0:T(8,128)S(1)}, u32[]{:S(2)}, u32[]{:S(2)}) collective-permute-start(f32[16,32,128]{2,1,0:T(8,128)S(1)} %get-tuple-element.21.refs_2_.refs_5_.refs_3_), channel_id=1, source_target_pairs={{1,0},{0,1},{3,2},{2,3},{5,4},{4,5},{7,6},{6,7},{9,8},{8,9},{11,10... | collective-permute-start | bytes 786440 | tf_op jit(solution)/shard_map/ppermute | solution.py:323
  20.2 1.9 %collective-permute-start.5 = (f32[16,32,128]{2,1,0:T(8,128)S(1)}, f32[16,32,128]{2,1,0:T(8,128)S(1)}, u32[]{:S(2)}, u32[]{:S(2)}) collective-permute-start(f32[16,32,128]{2,1,0:T(8,128)S(1)} %get-tuple-element.22.refs_3_.refs_6_.refs_4_), channel_id=1, source_target_pairs={{1,0},{0,1},{3,2},{2,3},{5,4},{4,5},{7,6},{6,7},{9,8},{8,9},{11,10... | collective-permute-start | bytes 786440 | tf_op jit(solution)/shard_map/ppermute | solution.py:323
  22.1 6.4 %collective-permute-start.6 = (f32[2,136,128]{2,1,0:T(8,128)S(1)}, f32[2,136,128]{2,1,0:T(8,128)S(1)}, u32[]{:S(2)}, u32[]{:S(2)}) collective-permute-start(f32[2,136,128]{2,1,0:T(8,128)S(1)} %after.4), channel_id=1, source_target_pairs={{2,1},{3,0},{0,3},{1,2},{6,5},{7,4},{4,7},{5,6},{10,9},{11,8},{8,1... | collective-permute-start | bytes 417800 | tf_op jit(solution)/shard_map/ppermute | solution.py:329
  31.3 1.9 %collective-permute-start.9 = (f32[32,32,128]{2,1,0:T(8,128)S(1)}, f32[32,32,128]{2,1,0:T(8,128)S(1)}, u32[]{:S(2)}, u32[]{:S(2)}) collective-permute-start(f32[32,32,128]{2,1,0:T(8,128)S(1)} %after.6.refs_7_), channel_id=1, source_target_pairs={{1,0},{0,1},{3,2},{2,3},{5,4},{4,5},{7,6},{6,7},{9,8},{8,9},{11,10... | collective-permute-start | bytes 1572872 | tf_op jit(solution)/shard_map/ppermute | solution.py:344
  33.9 6.6 %collective-permute-start.10 = (f32[32,128]{1,0:T(8,128)S(1)}, f32[32,128]{1,0:T(8,128)S(1)}, u32[]{:S(2)}, u32[]{:S(2)}) collective-permute-start(f32[32,128]{1,0:T(8,128)S(1)} %get-tuple-element.29.refs_1_), channel_id=1, source_target_pairs={{8,0},{4,12},{9,1},{5,13},{10,2},{6,14},{11,3},{7,15},{24,16},{20,... | collective-permute-start | bytes 49160 | tf_op jit(solution)/shard_map/ppermute | solution.py:373
  35.3 6.1 %collective-permute-start.11 = (f32[32,128]{1,0:T(8,128)S(1)}, f32[32,128]{1,0:T(8,128)S(1)}, u32[]{:S(2)}, u32[]{:S(2)}) collective-permute-start(f32[32,128]{1,0:T(8,128)S(1)} %after.7), channel_id=1, source_target_pairs={{4,0},{8,4},{12,8},{0,12},{5,1},{9,5},{13,9},{1,13},{6,2},{10,6},{... | collective-permute-start | bytes 49160 | tf_op jit(solution)/shard_map/ppermute | solution.py:373

commit v19 on v16

--- a/solution.py
+++ b/solution.py
@@ -68,7 +68,7 @@
         if 2 * shift < naux:
             plan.append([(source, (source + shift) % naux) for source in range(naux)])
         else:
-            plan.append([(z, z + shift) if z % 2 == 0 else (z + shift, z) for z in range(shift)])
+            plan.append([(z, z + shift) if z % 2 else (z + shift, z) for z in range(shift)])
     return plan
 
 
@@ -371,7 +371,9 @@
         last_other,
     )
     backs += last_back
-    returned = [lax.ppermute(back, "aux", ring(naux, i)) for i, back in enumerate(backs, 1)]
+    returned = [
+        lax.ppermute(back, "aux", [(target, source) for source, target in pairs]) for back, pairs in zip(backs, plan)
+    ]
     shape = ((nt, block_aux, nauxf), F32)
     (direct,) = call(
         meet_direct, [shape], [scratch(count)], work, sides, direct, tensor, nt=nt, naux=naux

time: 52.1 us -> 50.5 us (0.969)
  starting transfers between devices: 15.5 us -> 12.8 us
  waiting for transfers between devices: 16.6 us -> 17.7 us
    ppermute x1, starting transfers between devices: 4.51 us -> 1.28 us  [local(): lax.ppermute(after(again, lax.ppermute(token, 'sub', swap)), 'aux', plan[...]
    ppermute x1, waiting for transfers between devices: 0.3 us -> 3.53 us  [local(): lax.ppermute(mine, 'aux', pairs)]
    ppermute x2, waiting for transfers between devices: 3.6 us -> 0.67 us  [local(): lax.ppermute(back, 'aux', [(target, source) for source, target in pairs])]
    ppermute x1, waiting for transfers between devices: 0.95 us -> 1.74 us  [local(): lax.ppermute(after(again, lax.ppermute(token, 'sub', swap)), 'aux', plan[...]
  transfers between devices with their start and end apart: 12 -> 12, of which waited for: 8 -> 8; matrix products, arithmetic and copies ran while one was open for 3% -> 3% of each run, Pallas kernels for 13% -> 14%
where the time goes in v19:
time: 50.5 us; the launch traced here: 50.2 us
  waiting for transfers between devices  17.7 us (35%)
  starting transfers between devices  12.8 us (25%)
  blocking collectives  9.05 us (18%)
  Pallas kernels  7.16 us (14%)
  other arithmetic  2.07 us (4%)
  local copies, waits for them, and re-layouts  1.27 us (3%)
    all_to_all x1, blocking collectives, local(): lax.all_to_all(partial_chi.reshape(owners, nt * block_aux // owners, naux...  9.05 us
    pallas_call x8, Pallas kernels, call(): pl.pallas_call(here, out_shape=shapes, in_specs=[VMEM] * len(arguments),...  7.15 us
    ppermute x1, waiting for transfers between devices, local(): fars.append(lax.ppermute(late_near, ('orb', 'sub'), pairs))  6.16 us
    ppermute x2, starting transfers between devices, local(): lax.ppermute(back, 'aux', [(target, source) for source, target in pairs])  4.41 us
    ppermute x1, waiting for transfers between devices, local(): lax.ppermute(mine, 'aux', pairs)  3.53 us
    ppermute x1, waiting for transfers between devices, local(): lax.ppermute(small, 'tau', ring(nt, shift))  3.07 us
    ppermute x1, starting transfers between devices, local(): lax.ppermute(tensor, 'orb', ring(nob, shift))  2.94 us
    ppermute x1, waiting for transfers between devices, local(): lax.ppermute(after(again, lax.ppermute(token, 'sub', swap)), 'aux', plan[...  1.74 us
  transfers between devices with their start and end apart: 12, of which 8 were waited for; matrix products, arithmetic and copies ran while one was open for 3% of the time, Pallas kernels for 14%

profile of v19, /device:TPU:0, one launch (start us, length us, event | category | flops | bytes accessed | tf_op | source)
XLA Modules:
  0.0 50.2 jit_solution(2416309696893513202)
XLA Ops:
  0.0 2.9 %collective-permute-start.1 = (f32[128,2048]{1,0:T(8,128)}, f32[128,2048]{1,0:T(8,128)S(1)}, u32[]{:S(2)}, u32[]{:S(2)}) collective-permute-start(f32[128,2048]{1,0:T(8,128)} %bitcast.5), channel_id=1, source_target_pairs={{2,0},{0,2},{3,1},{1,3},{6,4},{4,6},{7,5},{5,7},{10,8},{8,10},{11,... | collective-permute-start | bytes 3145736 | tf_op jit(solution)/shard_map/ppermute | solution.py:292
  2.9 1.3 %copy-done = f32[1,1,2,64,2048]{4,3,2,1,0:T(8,128)S(1)} copy-done((f32[1,1,2,64,2048]{4,3,2,1,0:T(8,128)S(1)}, f32[1,1,2,64,2048]{4,3,2,1,0:T(8,128)}, u32[]{:S(2)}) %copy-start) | copy-done | bytes 1048600
  4.2 0.6 %prepare.1 = (f32[32,32,128]{2,1,0:T(8,128)S(1)}, f32[32,32,128]{2,1,0:T(8,128)S(1)}) custom-call(f32[128,2048]{1,0:T(8,128)S(1)} %bitcast.6), custom_call_target="tpu_custom_call" | custom-call | bytes 1048576 | tf_op jit(solution)/shard_map/prepare/pallas_call | solution.py:281
  4.8 1.6 %collective-permute-start.3 = (f32[32,32,128]{2,1,0:T(8,128)S(1)}, f32[32,32,128]{2,1,0:T(8,128)S(1)}, u32[]{:S(2)}, u32[]{:S(2)}) collective-permute-start(f32[32,32,128]{2,1,0:T(8,128)S(1)} %get-tuple-element.19.refs_1_), channel_id=1, source_target_pairs={{0,4},{4,8},{8,12},{12,0},{1,5},{5,9},{9,13},{13,1},{2,6},{6,10},{... | collective-permute-start | bytes 1572872 | tf_op jit(solution)/shard_map/ppermute | solution.py:324
  6.4 0.7 %convert_element_type.5 = f32[1,2]{1,0:T(1,128)S(1)} convert(s32[1,2]{1,0:T(1,128)} %param.7) | non-fusion elementwise | flops 2 | bytes 16 | tf_op jit(solution)/shard_map/convert_element_type | solution.py:302
  7.1 0.8 %fusion = (f32[1,136,128]{2,1,0:T(8,128)S(1)}, f32[136,128]{1,0:T(8,128)S(1)}) fusion(f32[1,2]{1,0:T(1,128)S(1)} %convert_element_type.5, f32[64,128]{1,0:T(8,128)} %param.6, f32[64,128]{1,0:T(8,128)} %param.5), kind=kLoop, calls=%fused_computation.4 | loop fusion | flops 69632 | bytes 204808 | tf_op jit(solution)/shard_map/stack | solution.py:305
  7.9 1.6 %collective-permute-start = (f32[136,128]{1,0:T(8,128)S(1)}, f32[136,128]{1,0:T(8,128)S(1)}, u32[]{:S(2)}, u32[]{:S(2)}) collective-permute-start(f32[136,128]{1,0:T(8,128)S(1)} %get-tuple-element.32), channel_id=1, source_target_pairs={{16,0},{0,16},{17,1},{1,17},{18,2},{2,18},{19,3},{3,19},{20,4},{4,... | collective-permute-start | bytes 208904 | tf_op jit(solution)/shard_map/ppermute | solution.py:305
  9.5 3.1 %collective-permute-done = f32[136,128]{1,0:T(8,128)S(1)} collective-permute-done((f32[136,128]{1,0:T(8,128)S(1)}, f32[136,128]{1,0:T(8,128)S(1)}, u32[]{:S(2)}, u32[]{:S(2)}) %collective-permute-start) | collective-permute-done | bytes 69664 | tf_op jit(solution)/shard_map/ppermute | solution.py:305
  12.6 1.5 %first.1 = (f32[4,512,256]{2,1,0:T(8,128)S(1)}, f32[8,128]{1,0:T(8,128)S(1)}) custom-call(f32[2,136,128]{2,1,0:T(8,128)S(1)} %pad_maximum_fusion.refs_0_, f32[128,2048]{1,0:T(8,128)S(1)} %bitcast.7), custom_call_target="tpu_custom_call" | custom-call | bytes 1187840 | tf_op jit(solution)/shard_map/first/pallas_call | solution.py:281
  14.0 0.1 collective-permute-start.7
  14.1 1.2 %collective-permute-done.7.refs_1_ = f32[8,128]{1,0:T(8,128)S(1)} collective-permute-done((f32[8,128]{1,0:T(8,128)S(1)}, f32[8,128]{1,0:T(8,128)S(1)}, u32[]{:S(2)}, u32[]{:S(2)}) %collective-permute-start.7) | collective-permute-done | bytes 4128 | tf_op jit(solution)/shard_map/ppermute | solution.py:327
  15.3 1.3 %collective-permute-start.8 = (f32[32,32,128]{2,1,0:T(8,128)S(1)}, f32[32,32,128]{2,1,0:T(8,128)S(1)}, u32[]{:S(2)}, u32[]{:S(2)}) collective-permute-start(f32[32,32,128]{2,1,0:T(8,128)S(1)} %after.4), channel_id=1, source_target_pairs={{8,0},{4,12},{9,1},{5,13},{10,2},{6,14},{11,3},{7,15},{24,16},{20,... | collective-permute-start | bytes 1572872 | tf_op jit(solution)/shard_map/ppermute | solution.py:327
  16.6 3.5 %collective-permute-done.3.refs_0_ = f32[32,32,128]{2,1,0:T(8,128)S(1)} collective-permute-done((f32[32,32,128]{2,1,0:T(8,128)S(1)}, f32[32,32,128]{2,1,0:T(8,128)S(1)}, u32[]{:S(2)}, u32[]{:S(2)}) %collective-permute-start.3) | collective-permute-done | bytes 524320 | tf_op jit(solution)/shard_map/ppermute | solution.py:324
  20.1 0.1 collective-permute-start.4
  20.2 0.5 collective-permute-start.5
  20.7 1.0 %collective-permute-done.4.refs_4_.refs_7_.refs_5_ = f32[16,32,128]{2,1,0:T(8,128)S(1)} collective-permute-done((f32[16,32,128]{2,1,0:T(8,128)S(1)}, f32[16,32,128]{2,1,0:T(8,128)S(1)}, u32[]{:S(2)}, u32[]{:S(2)}) %collective-permute-start.4) | collective-permute-done | bytes 262176 | tf_op jit(solution)/shard_map/ppermute | solution.py:326
  21.7 0.4 collective-permute-done.5.refs_5_.refs_8_.refs_6_
  22.1 0.3 collective-permute-start.6
  22.4 6.2 %collective-permute-done.6.refs_3_ = f32[2,136,128]{2,1,0:T(8,128)S(1)} collective-permute-done((f32[2,136,128]{2,1,0:T(8,128)S(1)}, f32[2,136,128]{2,1,0:T(8,128)S(1)}, u32[]{:S(2)}, u32[]{:S(2)}) %collective-permute-start.6) | collective-permute-done | bytes 139296 | tf_op jit(solution)/shard_map/ppermute | solution.py:332
  28.6 0.0 collective-permute-done.1.refs_2_
  28.6 1.8 %second.1 = (bf16[256,4096]{1,0:T(8,128)(2,1)S(1)}, f32[8,128]{1,0:T(8,128)S(1)}) custom-call(f32[2,136,128]{2,1,0:T(8,128)S(1)} %pad_maximum_fusion.refs_0_, f32[4,512,256]{2,1,0:T(8,128)S(1)} %get-tuple-element.18.refs_1_, f32[128,2048]{1,0:T(8,128)S(1)} %collective-permute-done.1.refs_2_, f32[2,136,128]{2,1,0:T(8,128)S(1)} %collective-permute-done.6.refs_3_, ...), custom_call_target="tpu_custom_call" | custom-call | flops 603979776 | bytes 4997120 | tf_op jit(solution)/shard_map/second/pallas_call | solution.py:281
  30.3 1.7 %collective-permute-done.8.refs_0_ = f32[32,32,128]{2,1,0:T(8,128)S(1)} collective-permute-done((f32[32,32,128]{2,1,0:T(8,128)S(1)}, f32[32,32,128]{2,1,0:T(8,128)S(1)}, u32[]{:S(2)}, u32[]{:S(2)}) %collective-permute-start.8) | collective-permute-done | bytes 524320 | tf_op jit(solution)/shard_map/ppermute | solution.py:327
  32.1 1.5 %meet_own.1 = (f32[160,64]{1,0:T(8,128)S(1)}, f32[32,64]{1,0:T(8,128)S(1)}, f32[32,128]{1,0:T(8,128)S(1)}) custom-call(bf16[256,4096]{1,0:T(8,128)(2,1)S(1)} %get-tuple-element.23.refs_0_, f32[32,32,128]{2,1,0:T(8,128)S(1)} %get-tuple-element.19.refs_1_, f32[32,32,128]{2,1,0:T(8,128)S(1)} %collective-permute-done.2.refs_1_.refs_4_.refs_2_, ...), custom_call_target="tpu_custom_call" | custom-call | flops 1342177280 | bytes 6815744 | tf_op jit(solution)/shard_map/meet_own/pallas_call | solution.py:281
  33.6 3.1 %collective-permute-start.10 = (f32[32,128]{1,0:T(8,128)S(1)}, f32[32,128]{1,0:T(8,128)S(1)}, u32[]{:S(2)}, u32[]{:S(2)}) collective-permute-start(f32[32,128]{1,0:T(8,128)S(1)} %get-tuple-element.29), channel_id=1, source_target_pairs={{4,0},{8,4},{12,8},{0,12},{5,1},{9,5},{13,9},{1,13},{6,2},{10,6},{... | collective-permute-start | bytes 49160 | tf_op jit(solution)/shard_map/ppermute | solution.py:375
  36.7 0.0 collective-permute-done.9.refs_2_
  36.7 0.7 %meet_back.1 = (bf16[64,4096]{1,0:T(8,128)(2,1)S(1)}, f32[32,128]{1,0:T(8,128)S(1)}) custom-call(bf16[256,4096]{1,0:T(8,128)(2,1)S(1)} %get-tuple-element.23.refs_0_, f32[32,64]{1,0:T(8,128)S(1)} %get-tuple-element.27.refs_1_, f32[32,32,128]{2,1,0:T(8,128)S(1)} %collective-permute-done.9.refs_2_), custom_call_target="tpu_custom_call" | custom-call | flops 134217728 | bytes 4726784 | tf_op jit(solution)/shard_map/meet_back/pallas_call | solution.py:281
  37.4 1.3 %collective-permute-start.11 = (f32[32,128]{1,0:T(8,128)S(1)}, f32[32,128]{1,0:T(8,128)S(1)}, u32[]{:S(2)}, u32[]{:S(2)}) collective-permute-start(f32[32,128]{1,0:T(8,128)S(1)} %get-tuple-element.30), channel_id=1, source_target_pairs={{0,8},{12,4},{1,9},{13,5},{2,10},{14,6},{3,11},{15,7},{16,24},{28,... | collective-permute-start | bytes 49160 | tf_op jit(solution)/shard_map/ppermute | solution.py:375
  38.7 0.7 %meet_direct.1.refs_0_ = f32[2,64,256]{2,1,0:T(8,128)S(1)} custom-call(bf16[256,4096]{1,0:T(8,128)(2,1)S(1)} %get-tuple-element.23.refs_0_, f32[160,64]{1,0:T(8,128)S(1)} %get-tuple-element.26.refs_1_, bf16[64,4096]{1,0:T(8,128)(2,1)S(1)} %get-tuple-element.28.refs_2_), custom_call_target="tpu_custom_call" | custom-call | flops 134217728 | bytes 5283840 | tf_op jit(solution)/shard_map/meet_direct/pallas_call | solution.py:281
  39.5 0.7 %collective-permute-done.11.refs_2_ = f32[32,128]{1,0:T(8,128)S(1)} collective-permute-done((f32[32,128]{1,0:T(8,128)S(1)}, f32[32,128]{1,0:T(8,128)S(1)}, u32[]{:S(2)}, u32[]{:S(2)}) %collective-permute-start.11) | collective-permute-done | bytes 16416 | tf_op jit(solution)/shard_map/ppermute | solution.py:375
  40.2 0.3 complete.1
  40.5 9.0 %all_to_all.5 = f32[8,16,256]{2,1,0:T(8,128)S(1)} all-to-all(f32[8,16,256]{2,1,0:T(8,128)S(1)} %bitcast.8), channel_id=1, replica_groups=mesh['tau'=2,'aux'=4,'orb'=2,'sub'=2] {'tau','orb','sub'}, dimensions={0} | all-to-all | bytes 262144 | tf_op jit(solution)/shard_map/all_to_all | solution.py:383
  49.5 0.6 %broadcast_multiply_fusion = f32[16,256]{1,0:T(8,128)} fusion(f32[16,256]{1,0:T(8,128)S(1)} %reduce_sum.9), kind=kLoop, calls=%fused_computation.3 | loop fusion | flops 4096 | bytes 32768 | tf_op jit(solution)/shard_map/mul | solution.py:390
  (14 shorter events, 0.1 us)
Async XLA Ops:
  0.0 28.6 %collective-permute-start.1 = (f32[128,2048]{1,0:T(8,128)}, f32[128,2048]{1,0:T(8,128)S(1)}, u32[]{:S(2)}, u32[]{:S(2)}) collective-permute-start(f32[128,2048]{1,0:T(8,128)} %bitcast.5), channel_id=1, source_target_pairs={{2,0},{0,2},{3,1},{1,3},{6,4},{4,6},{7,5},{5,7},{10,8},{8,10},{11,... | collective-permute-start | bytes 3145736 | tf_op jit(solution)/shard_map/ppermute | solution.py:292
  2.9 1.3 %copy-start = (f32[1,1,2,64,2048]{4,3,2,1,0:T(8,128)S(1)}, f32[1,1,2,64,2048]{4,3,2,1,0:T(8,128)}, u32[]{:S(2)}) copy-start(f32[1,1,2,64,2048]{4,3,2,1,0:T(8,128)} %param.4) | copy-start | bytes 3145732
  4.2 8.4 %copy-start.1 = (f32[1,1,2,64,2048]{4,3,2,1,0:T(8,128)S(1)}, f32[1,1,2,64,2048]{4,3,2,1,0:T(8,128)}, u32[]{:S(2)}) copy-start(f32[1,1,2,64,2048]{4,3,2,1,0:T(8,128)} %param.4) | copy-start | bytes 3145732
  4.8 15.3 %collective-permute-start.3 = (f32[32,32,128]{2,1,0:T(8,128)S(1)}, f32[32,32,128]{2,1,0:T(8,128)S(1)}, u32[]{:S(2)}, u32[]{:S(2)}) collective-permute-start(f32[32,32,128]{2,1,0:T(8,128)S(1)} %get-tuple-element.19.refs_1_), channel_id=1, source_target_pairs={{0,4},{4,8},{8,12},{12,0},{1,5},{5,9},{9,13},{13,1},{2,6},{6,10},{... | collective-permute-start | bytes 1572872 | tf_op jit(solution)/shard_map/ppermute | solution.py:324
  6.4 14.3 %collective-permute-start.2 = (f32[32,32,128]{2,1,0:T(8,128)S(1)}, f32[32,32,128]{2,1,0:T(8,128)S(1)}, u32[]{:S(2)}, u32[]{:S(2)}) collective-permute-start(f32[32,32,128]{2,1,0:T(8,128)S(1)} %get-tuple-element.19.refs_1_), channel_id=1, source_target_pairs={{1,0},{0,1},{3,2},{2,3},{5,4},{4,5},{7,6},{6,7},{9,8},{8,9},{11,10... | collective-permute-start | bytes 1572872 | tf_op jit(solution)/shard_map/ppermute | solution.py:320
  7.9 4.7 %collective-permute-start = (f32[136,128]{1,0:T(8,128)S(1)}, f32[136,128]{1,0:T(8,128)S(1)}, u32[]{:S(2)}, u32[]{:S(2)}) collective-permute-start(f32[136,128]{1,0:T(8,128)S(1)} %get-tuple-element.32), channel_id=1, source_target_pairs={{16,0},{0,16},{17,1},{1,17},{18,2},{2,18},{19,3},{3,19},{20,4},{4,... | collective-permute-start | bytes 208904 | tf_op jit(solution)/shard_map/ppermute | solution.py:305
  14.0 1.2 %collective-permute-start.7 = (f32[8,128]{1,0:T(8,128)S(1)}, f32[8,128]{1,0:T(8,128)S(1)}, u32[]{:S(2)}, u32[]{:S(2)}) collective-permute-start(f32[8,128]{1,0:T(8,128)S(1)} %get-tuple-element.20.refs_1_), channel_id=1, source_target_pairs={{1,0},{0,1},{3,2},{2,3},{5,4},{4,5},{7,6},{6,7},{9,8},{8,9},{11,10... | collective-permute-start | bytes 12296 | tf_op jit(solution)/shard_map/ppermute | solution.py:327
  15.3 16.8 %collective-permute-start.8 = (f32[32,32,128]{2,1,0:T(8,128)S(1)}, f32[32,32,128]{2,1,0:T(8,128)S(1)}, u32[]{:S(2)}, u32[]{:S(2)}) collective-permute-start(f32[32,32,128]{2,1,0:T(8,128)S(1)} %after.4), channel_id=1, source_target_pairs={{8,0},{4,12},{9,1},{5,13},{10,2},{6,14},{11,3},{7,15},{24,16},{20,... | collective-permute-start | bytes 1572872 | tf_op jit(solution)/shard_map/ppermute | solution.py:327
  20.1 1.6 %collective-permute-start.4 = (f32[16,32,128]{2,1,0:T(8,128)S(1)}, f32[16,32,128]{2,1,0:T(8,128)S(1)}, u32[]{:S(2)}, u32[]{:S(2)}) collective-permute-start(f32[16,32,128]{2,1,0:T(8,128)S(1)} %get-tuple-element.21.refs_2_.refs_5_.refs_3_), channel_id=1, source_target_pairs={{1,0},{0,1},{3,2},{2,3},{5,4},{4,5},{7,6},{6,7},{9,8},{8,9},{11,10... | collective-permute-start | bytes 786440 | tf_op jit(solution)/shard_map/ppermute | solution.py:326
  20.2 1.9 %collective-permute-start.5 = (f32[16,32,128]{2,1,0:T(8,128)S(1)}, f32[16,32,128]{2,1,0:T(8,128)S(1)}, u32[]{:S(2)}, u32[]{:S(2)}) collective-permute-start(f32[16,32,128]{2,1,0:T(8,128)S(1)} %get-tuple-element.22.refs_3_.refs_6_.refs_4_), channel_id=1, source_target_pairs={{1,0},{0,1},{3,2},{2,3},{5,4},{4,5},{7,6},{6,7},{9,8},{8,9},{11,10... | collective-permute-start | bytes 786440 | tf_op jit(solution)/shard_map/ppermute | solution.py:326
  22.1 6.4 %collective-permute-start.6 = (f32[2,136,128]{2,1,0:T(8,128)S(1)}, f32[2,136,128]{2,1,0:T(8,128)S(1)}, u32[]{:S(2)}, u32[]{:S(2)}) collective-permute-start(f32[2,136,128]{2,1,0:T(8,128)S(1)} %after.3), channel_id=1, source_target_pairs={{2,1},{3,0},{0,3},{1,2},{6,5},{7,4},{4,7},{5,6},{10,9},{11,8},{8,1... | collective-permute-start | bytes 417800 | tf_op jit(solution)/shard_map/ppermute | solution.py:332
  32.1 4.6 %collective-permute-start.9 = (f32[32,32,128]{2,1,0:T(8,128)S(1)}, f32[32,32,128]{2,1,0:T(8,128)S(1)}, u32[]{:S(2)}, u32[]{:S(2)}) collective-permute-start(f32[32,32,128]{2,1,0:T(8,128)S(1)} %after.5.refs_7_), channel_id=1, source_target_pairs={{1,0},{0,1},{3,2},{2,3},{5,4},{4,5},{7,6},{6,7},{9,8},{8,9},{11,10... | collective-permute-start | bytes 1572872 | tf_op jit(solution)/shard_map/ppermute | solution.py:347
  33.6 5.9 %collective-permute-start.10 = (f32[32,128]{1,0:T(8,128)S(1)}, f32[32,128]{1,0:T(8,128)S(1)}, u32[]{:S(2)}, u32[]{:S(2)}) collective-permute-start(f32[32,128]{1,0:T(8,128)S(1)} %get-tuple-element.29), channel_id=1, source_target_pairs={{4,0},{8,4},{12,8},{0,12},{5,1},{9,5},{13,9},{1,13},{6,2},{10,6},{... | collective-permute-start | bytes 49160 | tf_op jit(solution)/shard_map/ppermute | solution.py:375
  37.4 2.8 %collective-permute-start.11 = (f32[32,128]{1,0:T(8,128)S(1)}, f32[32,128]{1,0:T(8,128)S(1)}, u32[]{:S(2)}, u32[]{:S(2)}) collective-permute-start(f32[32,128]{1,0:T(8,128)S(1)} %get-tuple-element.30), channel_id=1, source_target_pairs={{0,8},{12,4},{1,9},{13,5},{2,10},{14,6},{3,11},{15,7},{16,24},{28,... | collective-permute-start | bytes 49160 | tf_op jit(solution)/shard_map/ppermute | solution.py:375

commit v20 on v19

--- a/solution.py
+++ b/solution.py
@@ -205,13 +205,11 @@
 
 
 def meet_own(place, sides, *refs, count):
-    refs, (direct, back, *backs, tensor, ordered) = refs[: 4 * count - 1], refs[4 * count - 1 :]
-    pieces = [refs[:1], refs[1:2]] + [refs[i : i + 2] for i in range(2, 4 * count - 2, 2)] + [refs[-1:]]
+    refs, (tensor, back, *backs, ordered) = refs[: 4 * count - 3], refs[4 * count - 3 :]
+    pieces = [refs[i : i + 2] for i in range(0, 4 * count - 4, 2)] + [refs[-1:]]
     half = refs[0].shape[1]
-    rows = sides.shape[0] // 2
     relay(pieces, tensor)
-    direct[...] = products(tensor[...], sides[:rows, :], half)
-    rest = products(tensor[4 * half :, :], sides[rows:, :], half)
+    rest = products(tensor[...], sides[sides.shape[0] // 2 :, :], half)
     for i, back_ref in enumerate(backs):
         back_ref[...] = fold(
             place, rest[2 * i * half : (2 * i + 1) * half], rest[(2 * i + 1) * half : 2 * (i + 1) * half], ordered
@@ -226,14 +224,19 @@
     back_ref[...] = fold(place, own[...], other, ordered)
 
 
-def meet_direct(place, sides, own, tensor, out_ref, ordered, *, nt, naux):
+def meet_direct(place, sides, mine, mine_other, own, last, out_ref, tensor, ordered, *, nt, naux):
     count = ordered.shape[0]
     block = ordered.shape[2]
     half = block // 2
-    other = products(tensor[...], sides[: sides.shape[0] // 2, :], half)
+    side = sides[: sides.shape[0] // 2, :]
+    relay([[mine], [mine_other]], tensor)
+    tensor[4 * half :, :] = last[...]
+    some = products(tensor[...], side, half)
+    own = jnp.concatenate([some[:block], products(own[...], side, half)], axis=0)
+    other = some[block:]
     for i in range(count):
-        first_half = own[i * block : i * block + half, :]
-        second_half = own[i * block + half : (i + 1) * block, :] if i < count - 1 else other
+        first_half = own[i * block : i * block + half]
+        second_half = own[i * block + half : (i + 1) * block] if i < count - 1 else other
         unfold(by_sub(place, first_half, second_half, 0), ordered, i)
     for tau in range(nt):
         here = [jnp.zeros((half, block), F32)] * naux
@@ -350,14 +353,14 @@
     wide = nt * rows_aux
     shape = ((rows_aux, 2 * wide), F32)
     scratch = lambda count: ((count, wide, block_aux), F32)
-    direct, back, *backs = call(
+    own_rows = 2 * (2 * count - 3) * rows_aux
+    own, back, *backs = call(
         meet_own,
-        [(((2 * count - 1) * rows_aux, wide), F32), ((rows_aux, wide), F32)] + [shape] * (len(plan) - 1),
-        [((2 * (2 * count - 1) * rows_aux, depth), BF16), scratch(1)],
-        work * (2 * count - 1) * 2,
+        [((own_rows, depth), BF16), ((rows_aux, wide), F32)] + [shape] * (len(plan) - 1),
+        [scratch(1)],
+        work * (2 * count - 3),
         sides,
-        mine,
-        *early,
+        *early[1:],
         last,
         count=len(plan),
     )
@@ -376,7 +379,17 @@
     ]
     shape = ((nt, block_aux, nauxf), F32)
     (direct,) = call(
-        meet_direct, [shape], [scratch(count)], work, sides, direct, tensor, nt=nt, naux=naux
+        meet_direct,
+        [shape],
+        [((6 * rows_aux, depth), BF16), ((count, wide, block_aux), F32)],
+        work * (2 * count),
+        sides,
+        mine,
+        mine_other,
+        own,
+        tensor,
+        nt=nt,
+        naux=naux,
     )
     (partial_chi,) = call(complete, [shape], [], 0, direct, *returned)
     owners = nt * nob * nsub

time: 50.5 us -> 49.8 us (0.986)
    ppermute x2, waiting for transfers between devices: 0.67 us -> 0.16 us  [local(): lax.ppermute(back, 'aux', [(target, source) for source, target in pairs])]
  transfers between devices with their start and end apart: 12 -> 12, of which waited for: 8 -> 8; matrix products, arithmetic and copies ran while one was open for 3% -> 3% of each run, Pallas kernels for 14% -> 13%
where the time goes in v20:
time: 49.8 us; the launch traced here: 49.5 us
  waiting for transfers between devices  17.2 us (35%)
  starting transfers between devices  12.8 us (26%)
  blocking collectives  9.05 us (18%)
  Pallas kernels  6.97 us (14%)
  other arithmetic  2.07 us (4%)
  local copies, waits for them, and re-layouts  1.27 us (3%)
    all_to_all x1, blocking collectives, local(): lax.all_to_all(partial_chi.reshape(owners, nt * block_aux // owners, naux...  9.05 us
    pallas_call x8, Pallas kernels, call(): pl.pallas_call(here, out_shape=shapes, in_specs=[VMEM] * len(arguments),...  6.97 us
    ppermute x1, waiting for transfers between devices, local(): fars.append(lax.ppermute(late_near, ('orb', 'sub'), pairs))  6.16 us
    ppermute x2, starting transfers between devices, local(): lax.ppermute(back, 'aux', [(target, source) for source, target in pairs])  4.43 us
    ppermute x1, waiting for transfers between devices, local(): lax.ppermute(mine, 'aux', pairs)  3.53 us
    ppermute x1, waiting for transfers between devices, local(): lax.ppermute(small, 'tau', ring(nt, shift))  3.07 us
    ppermute x1, starting transfers between devices, local(): lax.ppermute(tensor, 'orb', ring(nob, shift))  2.94 us
    ppermute x1, waiting for transfers between devices, local(): lax.ppermute(after(again, lax.ppermute(token, 'sub', swap)), 'aux', plan[...  1.75 us
  transfers between devices with their start and end apart: 12, of which 8 were waited for; matrix products, arithmetic and copies ran while one was open for 3% of the time, Pallas kernels for 13%

profile of v20, /device:TPU:0, one launch (start us, length us, event | category | flops | bytes accessed | tf_op | source)
XLA Modules:
  0.0 49.5 jit_solution(6790051583971900935)
XLA Ops:
  0.0 2.9 %collective-permute-start.1 = (f32[128,2048]{1,0:T(8,128)}, f32[128,2048]{1,0:T(8,128)S(1)}, u32[]{:S(2)}, u32[]{:S(2)}) collective-permute-start(f32[128,2048]{1,0:T(8,128)} %bitcast.5), channel_id=1, source_target_pairs={{2,0},{0,2},{3,1},{1,3},{6,4},{4,6},{7,5},{5,7},{10,8},{8,10},{11,... | collective-permute-start | bytes 3145736 | tf_op jit(solution)/shard_map/ppermute | solution.py:295
  2.9 1.3 %copy-done = f32[1,1,2,64,2048]{4,3,2,1,0:T(8,128)S(1)} copy-done((f32[1,1,2,64,2048]{4,3,2,1,0:T(8,128)S(1)}, f32[1,1,2,64,2048]{4,3,2,1,0:T(8,128)}, u32[]{:S(2)}) %copy-start) | copy-done | bytes 1048600
  4.2 0.6 %prepare.1 = (f32[32,32,128]{2,1,0:T(8,128)S(1)}, f32[32,32,128]{2,1,0:T(8,128)S(1)}) custom-call(f32[128,2048]{1,0:T(8,128)S(1)} %bitcast.6), custom_call_target="tpu_custom_call" | custom-call | bytes 1048576 | tf_op jit(solution)/shard_map/prepare/pallas_call | solution.py:284
  4.8 1.6 %collective-permute-start.3 = (f32[32,32,128]{2,1,0:T(8,128)S(1)}, f32[32,32,128]{2,1,0:T(8,128)S(1)}, u32[]{:S(2)}, u32[]{:S(2)}) collective-permute-start(f32[32,32,128]{2,1,0:T(8,128)S(1)} %get-tuple-element.19.refs_1_), channel_id=1, source_target_pairs={{0,4},{4,8},{8,12},{12,0},{1,5},{5,9},{9,13},{13,1},{2,6},{6,10},{... | collective-permute-start | bytes 1572872 | tf_op jit(solution)/shard_map/ppermute | solution.py:327
  6.4 0.7 %convert_element_type.5 = f32[1,2]{1,0:T(1,128)S(1)} convert(s32[1,2]{1,0:T(1,128)} %param.7) | non-fusion elementwise | flops 2 | bytes 16 | tf_op jit(solution)/shard_map/convert_element_type | solution.py:305
  7.1 0.8 %fusion = (f32[1,136,128]{2,1,0:T(8,128)S(1)}, f32[136,128]{1,0:T(8,128)S(1)}) fusion(f32[1,2]{1,0:T(1,128)S(1)} %convert_element_type.5, f32[64,128]{1,0:T(8,128)} %param.6, f32[64,128]{1,0:T(8,128)} %param.5), kind=kLoop, calls=%fused_computation.4 | loop fusion | flops 69632 | bytes 204808 | tf_op jit(solution)/shard_map/stack | solution.py:308
  7.9 1.6 %collective-permute-start = (f32[136,128]{1,0:T(8,128)S(1)}, f32[136,128]{1,0:T(8,128)S(1)}, u32[]{:S(2)}, u32[]{:S(2)}) collective-permute-start(f32[136,128]{1,0:T(8,128)S(1)} %get-tuple-element.32), channel_id=1, source_target_pairs={{16,0},{0,16},{17,1},{1,17},{18,2},{2,18},{19,3},{3,19},{20,4},{4,... | collective-permute-start | bytes 208904 | tf_op jit(solution)/shard_map/ppermute | solution.py:308
  9.5 3.1 %collective-permute-done = f32[136,128]{1,0:T(8,128)S(1)} collective-permute-done((f32[136,128]{1,0:T(8,128)S(1)}, f32[136,128]{1,0:T(8,128)S(1)}, u32[]{:S(2)}, u32[]{:S(2)}) %collective-permute-start) | collective-permute-done | bytes 69664 | tf_op jit(solution)/shard_map/ppermute | solution.py:308
  12.6 1.5 %first.1 = (f32[4,512,256]{2,1,0:T(8,128)S(1)}, f32[8,128]{1,0:T(8,128)S(1)}) custom-call(f32[2,136,128]{2,1,0:T(8,128)S(1)} %pad_maximum_fusion.refs_0_, f32[128,2048]{1,0:T(8,128)S(1)} %bitcast.7), custom_call_target="tpu_custom_call" | custom-call | bytes 1187840 | tf_op jit(solution)/shard_map/first/pallas_call | solution.py:284
  14.1 0.1 collective-permute-start.7
  14.1 1.2 %collective-permute-done.7.refs_1_ = f32[8,128]{1,0:T(8,128)S(1)} collective-permute-done((f32[8,128]{1,0:T(8,128)S(1)}, f32[8,128]{1,0:T(8,128)S(1)}, u32[]{:S(2)}, u32[]{:S(2)}) %collective-permute-start.7) | collective-permute-done | bytes 4128 | tf_op jit(solution)/shard_map/ppermute | solution.py:330
  15.3 1.3 %collective-permute-start.8 = (f32[32,32,128]{2,1,0:T(8,128)S(1)}, f32[32,32,128]{2,1,0:T(8,128)S(1)}, u32[]{:S(2)}, u32[]{:S(2)}) collective-permute-start(f32[32,32,128]{2,1,0:T(8,128)S(1)} %after.4), channel_id=1, source_target_pairs={{8,0},{4,12},{9,1},{5,13},{10,2},{6,14},{11,3},{7,15},{24,16},{20,... | collective-permute-start | bytes 1572872 | tf_op jit(solution)/shard_map/ppermute | solution.py:330
  16.6 3.5 %collective-permute-done.3.refs_0_ = f32[32,32,128]{2,1,0:T(8,128)S(1)} collective-permute-done((f32[32,32,128]{2,1,0:T(8,128)S(1)}, f32[32,32,128]{2,1,0:T(8,128)S(1)}, u32[]{:S(2)}, u32[]{:S(2)}) %collective-permute-start.3) | collective-permute-done | bytes 524320 | tf_op jit(solution)/shard_map/ppermute | solution.py:327
  20.1 0.1 collective-permute-start.4
  20.2 0.5 %collective-permute-start.5 = (f32[16,32,128]{2,1,0:T(8,128)S(1)}, f32[16,32,128]{2,1,0:T(8,128)S(1)}, u32[]{:S(2)}, u32[]{:S(2)}) collective-permute-start(f32[16,32,128]{2,1,0:T(8,128)S(1)} %get-tuple-element.22.refs_3_.refs_6_.refs_2_), channel_id=1, source_target_pairs={{1,0},{0,1},{3,2},{2,3},{5,4},{4,5},{7,6},{6,7},{9,8},{8,9},{11,10... | collective-permute-start | bytes 786440 | tf_op jit(solution)/shard_map/ppermute | solution.py:329
  20.7 1.0 %collective-permute-done.4.refs_4_.refs_7_.refs_3_ = f32[16,32,128]{2,1,0:T(8,128)S(1)} collective-permute-done((f32[16,32,128]{2,1,0:T(8,128)S(1)}, f32[16,32,128]{2,1,0:T(8,128)S(1)}, u32[]{:S(2)}, u32[]{:S(2)}) %collective-permute-start.4) | collective-permute-done | bytes 262176 | tf_op jit(solution)/shard_map/ppermute | solution.py:329
  21.7 0.4 collective-permute-done.5.refs_5_.refs_8_.refs_4_
  22.1 0.3 collective-permute-start.6
  22.4 6.2 %collective-permute-done.6.refs_3_ = f32[2,136,128]{2,1,0:T(8,128)S(1)} collective-permute-done((f32[2,136,128]{2,1,0:T(8,128)S(1)}, f32[2,136,128]{2,1,0:T(8,128)S(1)}, u32[]{:S(2)}, u32[]{:S(2)}) %collective-permute-start.6) | collective-permute-done | bytes 139296 | tf_op jit(solution)/shard_map/ppermute | solution.py:335
  28.6 0.0 collective-permute-done.1.refs_2_
  28.6 1.7 %second.1 = (bf16[256,4096]{1,0:T(8,128)(2,1)S(1)}, f32[8,128]{1,0:T(8,128)S(1)}) custom-call(f32[2,136,128]{2,1,0:T(8,128)S(1)} %pad_maximum_fusion.refs_0_, f32[4,512,256]{2,1,0:T(8,128)S(1)} %get-tuple-element.18.refs_1_, f32[128,2048]{1,0:T(8,128)S(1)} %collective-permute-done.1.refs_2_, f32[2,136,128]{2,1,0:T(8,128)S(1)} %collective-permute-done.6.refs_3_, ...), custom_call_target="tpu_custom_call" | custom-call | flops 603979776 | bytes 4997120 | tf_op jit(solution)/shard_map/second/pallas_call | solution.py:284
  30.3 1.8 %collective-permute-done.8.refs_0_ = f32[32,32,128]{2,1,0:T(8,128)S(1)} collective-permute-done((f32[32,32,128]{2,1,0:T(8,128)S(1)}, f32[32,32,128]{2,1,0:T(8,128)S(1)}, u32[]{:S(2)}, u32[]{:S(2)}) %collective-permute-start.8) | collective-permute-done | bytes 524320 | tf_op jit(solution)/shard_map/ppermute | solution.py:330
  32.1 0.0 collective-permute-start.9
  32.1 0.8 %meet_own.1 = (bf16[192,4096]{1,0:T(8,128)(2,1)S(1)}, f32[32,64]{1,0:T(8,128)S(1)}, f32[32,128]{1,0:T(8,128)S(1)}) custom-call(bf16[256,4096]{1,0:T(8,128)(2,1)S(1)} %get-tuple-element.23.refs_0_, f32[16,32,128]{2,1,0:T(8,128)S(1)} %get-tuple-element.21.refs_2_.refs_5_.refs_1_, f32[16,32,128]{2,1,0:T(8,128)S(1)} %get-tuple-element.22.refs_3_.refs_6_.refs_2_, ...), custom_call_target="tpu_custom_call" | custom-call | flops 402653184 | bytes 5767168 | tf_op jit(solution)/shard_map/meet_own/pallas_call | solution.py:284
  32.9 3.1 %collective-permute-start.10 = (f32[32,128]{1,0:T(8,128)S(1)}, f32[32,128]{1,0:T(8,128)S(1)}, u32[]{:S(2)}, u32[]{:S(2)}) collective-permute-start(f32[32,128]{1,0:T(8,128)S(1)} %get-tuple-element.29), channel_id=1, source_target_pairs={{4,0},{8,4},{12,8},{0,12},{5,1},{9,5},{13,9},{1,13},{6,2},{10,6},{... | collective-permute-start | bytes 49160 | tf_op jit(solution)/shard_map/ppermute | solution.py:378
  36.0 0.7 %meet_back.1 = (bf16[64,4096]{1,0:T(8,128)(2,1)S(1)}, f32[32,128]{1,0:T(8,128)S(1)}) custom-call(bf16[256,4096]{1,0:T(8,128)(2,1)S(1)} %get-tuple-element.23.refs_0_, f32[32,64]{1,0:T(8,128)S(1)} %get-tuple-element.27.refs_1_, f32[32,32,128]{2,1,0:T(8,128)S(1)} %collective-permute-done.9.refs_2_), custom_call_target="tpu_custom_call" | custom-call | flops 134217728 | bytes 4726784 | tf_op jit(solution)/shard_map/meet_back/pallas_call | solution.py:284
  36.7 1.3 %collective-permute-start.11 = (f32[32,128]{1,0:T(8,128)S(1)}, f32[32,128]{1,0:T(8,128)S(1)}, u32[]{:S(2)}, u32[]{:S(2)}) collective-permute-start(f32[32,128]{1,0:T(8,128)S(1)} %get-tuple-element.30), channel_id=1, source_target_pairs={{0,8},{12,4},{1,9},{13,5},{2,10},{14,6},{3,11},{15,7},{16,24},{28,... | collective-permute-start | bytes 49160 | tf_op jit(solution)/shard_map/ppermute | solution.py:378
  38.1 1.2 %meet_direct.1.refs_0_ = f32[2,64,256]{2,1,0:T(8,128)S(1)} custom-call(bf16[256,4096]{1,0:T(8,128)(2,1)S(1)} %get-tuple-element.23.refs_0_, f32[32,32,128]{2,1,0:T(8,128)S(1)} %get-tuple-element.19.refs_1_, f32[32,32,128]{2,1,0:T(8,128)S(1)} %collective-permute-done.2.refs_1_.refs_4_.refs_2_, bf16[192,4096]{1,0:T(8,128)(2,1)S(1)} %get-tuple-element.26.refs_3_, ...), custom_call_target="tpu_custom_call" | custom-call | flops 805306368 | bytes 9437184 | tf_op jit(solution)/shard_map/meet_direct/pallas_call | solution.py:284
  39.3 0.2 collective-permute-done.11.refs_2_
  39.5 0.3 complete.1
  39.8 9.1 %all_to_all.5 = f32[8,16,256]{2,1,0:T(8,128)S(1)} all-to-all(f32[8,16,256]{2,1,0:T(8,128)S(1)} %bitcast.8), channel_id=1, replica_groups=mesh['tau'=2,'aux'=4,'orb'=2,'sub'=2] {'tau','orb','sub'}, dimensions={0} | all-to-all | bytes 262144 | tf_op jit(solution)/shard_map/all_to_all | solution.py:396
  48.9 0.6 %broadcast_multiply_fusion = f32[16,256]{1,0:T(8,128)} fusion(f32[16,256]{1,0:T(8,128)S(1)} %reduce_sum.9), kind=kLoop, calls=%fused_computation.3 | loop fusion | flops 4096 | bytes 32768 | tf_op jit(solution)/shard_map/mul | solution.py:403
  (14 shorter events, 0.1 us)
Async XLA Ops:
  0.0 28.6 %collective-permute-start.1 = (f32[128,2048]{1,0:T(8,128)}, f32[128,2048]{1,0:T(8,128)S(1)}, u32[]{:S(2)}, u32[]{:S(2)}) collective-permute-start(f32[128,2048]{1,0:T(8,128)} %bitcast.5), channel_id=1, source_target_pairs={{2,0},{0,2},{3,1},{1,3},{6,4},{4,6},{7,5},{5,7},{10,8},{8,10},{11,... | collective-permute-start | bytes 3145736 | tf_op jit(solution)/shard_map/ppermute | solution.py:295
  2.9 1.3 %copy-start = (f32[1,1,2,64,2048]{4,3,2,1,0:T(8,128)S(1)}, f32[1,1,2,64,2048]{4,3,2,1,0:T(8,128)}, u32[]{:S(2)}) copy-start(f32[1,1,2,64,2048]{4,3,2,1,0:T(8,128)} %param.4) | copy-start | bytes 3145732
  4.2 8.4 %copy-start.1 = (f32[1,1,2,64,2048]{4,3,2,1,0:T(8,128)S(1)}, f32[1,1,2,64,2048]{4,3,2,1,0:T(8,128)}, u32[]{:S(2)}) copy-start(f32[1,1,2,64,2048]{4,3,2,1,0:T(8,128)} %param.4) | copy-start | bytes 3145732
  4.8 15.3 %collective-permute-start.3 = (f32[32,32,128]{2,1,0:T(8,128)S(1)}, f32[32,32,128]{2,1,0:T(8,128)S(1)}, u32[]{:S(2)}, u32[]{:S(2)}) collective-permute-start(f32[32,32,128]{2,1,0:T(8,128)S(1)} %get-tuple-element.19.refs_1_), channel_id=1, source_target_pairs={{0,4},{4,8},{8,12},{12,0},{1,5},{5,9},{9,13},{13,1},{2,6},{6,10},{... | collective-permute-start | bytes 1572872 | tf_op jit(solution)/shard_map/ppermute | solution.py:327
  6.4 14.3 %collective-permute-start.2 = (f32[32,32,128]{2,1,0:T(8,128)S(1)}, f32[32,32,128]{2,1,0:T(8,128)S(1)}, u32[]{:S(2)}, u32[]{:S(2)}) collective-permute-start(f32[32,32,128]{2,1,0:T(8,128)S(1)} %get-tuple-element.19.refs_1_), channel_id=1, source_target_pairs={{1,0},{0,1},{3,2},{2,3},{5,4},{4,5},{7,6},{6,7},{9,8},{8,9},{11,10... | collective-permute-start | bytes 1572872 | tf_op jit(solution)/shard_map/ppermute | solution.py:323
  7.9 4.7 %collective-permute-start = (f32[136,128]{1,0:T(8,128)S(1)}, f32[136,128]{1,0:T(8,128)S(1)}, u32[]{:S(2)}, u32[]{:S(2)}) collective-permute-start(f32[136,128]{1,0:T(8,128)S(1)} %get-tuple-element.32), channel_id=1, source_target_pairs={{16,0},{0,16},{17,1},{1,17},{18,2},{2,18},{19,3},{3,19},{20,4},{4,... | collective-permute-start | bytes 208904 | tf_op jit(solution)/shard_map/ppermute | solution.py:308
  14.1 1.2 %collective-permute-start.7 = (f32[8,128]{1,0:T(8,128)S(1)}, f32[8,128]{1,0:T(8,128)S(1)}, u32[]{:S(2)}, u32[]{:S(2)}) collective-permute-start(f32[8,128]{1,0:T(8,128)S(1)} %get-tuple-element.20.refs_1_), channel_id=1, source_target_pairs={{1,0},{0,1},{3,2},{2,3},{5,4},{4,5},{7,6},{6,7},{9,8},{8,9},{11,10... | collective-permute-start | bytes 12296 | tf_op jit(solution)/shard_map/ppermute | solution.py:330
  15.3 16.8 %collective-permute-start.8 = (f32[32,32,128]{2,1,0:T(8,128)S(1)}, f32[32,32,128]{2,1,0:T(8,128)S(1)}, u32[]{:S(2)}, u32[]{:S(2)}) collective-permute-start(f32[32,32,128]{2,1,0:T(8,128)S(1)} %after.4), channel_id=1, source_target_pairs={{8,0},{4,12},{9,1},{5,13},{10,2},{6,14},{11,3},{7,15},{24,16},{20,... | collective-permute-start | bytes 1572872 | tf_op jit(solution)/shard_map/ppermute | solution.py:330
  20.1 1.6 %collective-permute-start.4 = (f32[16,32,128]{2,1,0:T(8,128)S(1)}, f32[16,32,128]{2,1,0:T(8,128)S(1)}, u32[]{:S(2)}, u32[]{:S(2)}) collective-permute-start(f32[16,32,128]{2,1,0:T(8,128)S(1)} %get-tuple-element.21.refs_2_.refs_5_.refs_1_), channel_id=1, source_target_pairs={{1,0},{0,1},{3,2},{2,3},{5,4},{4,5},{7,6},{6,7},{9,8},{8,9},{11,10... | collective-permute-start | bytes 786440 | tf_op jit(solution)/shard_map/ppermute | solution.py:329
  20.2 1.9 %collective-permute-start.5 = (f32[16,32,128]{2,1,0:T(8,128)S(1)}, f32[16,32,128]{2,1,0:T(8,128)S(1)}, u32[]{:S(2)}, u32[]{:S(2)}) collective-permute-start(f32[16,32,128]{2,1,0:T(8,128)S(1)} %get-tuple-element.22.refs_3_.refs_6_.refs_2_), channel_id=1, source_target_pairs={{1,0},{0,1},{3,2},{2,3},{5,4},{4,5},{7,6},{6,7},{9,8},{8,9},{11,10... | collective-permute-start | bytes 786440 | tf_op jit(solution)/shard_map/ppermute | solution.py:329
  22.1 6.4 %collective-permute-start.6 = (f32[2,136,128]{2,1,0:T(8,128)S(1)}, f32[2,136,128]{2,1,0:T(8,128)S(1)}, u32[]{:S(2)}, u32[]{:S(2)}) collective-permute-start(f32[2,136,128]{2,1,0:T(8,128)S(1)} %after.3), channel_id=1, source_target_pairs={{2,1},{3,0},{0,3},{1,2},{6,5},{7,4},{4,7},{5,6},{10,9},{11,8},{8,1... | collective-permute-start | bytes 417800 | tf_op jit(solution)/shard_map/ppermute | solution.py:335
  32.1 3.9 %collective-permute-start.9 = (f32[32,32,128]{2,1,0:T(8,128)S(1)}, f32[32,32,128]{2,1,0:T(8,128)S(1)}, u32[]{:S(2)}, u32[]{:S(2)}) collective-permute-start(f32[32,32,128]{2,1,0:T(8,128)S(1)} %after.5.refs_5_), channel_id=1, source_target_pairs={{1,0},{0,1},{3,2},{2,3},{5,4},{4,5},{7,6},{6,7},{9,8},{8,9},{11,10... | collective-permute-start | bytes 1572872 | tf_op jit(solution)/shard_map/ppermute | solution.py:350
  32.9 6.4 %collective-permute-start.10 = (f32[32,128]{1,0:T(8,128)S(1)}, f32[32,128]{1,0:T(8,128)S(1)}, u32[]{:S(2)}, u32[]{:S(2)}) collective-permute-start(f32[32,128]{1,0:T(8,128)S(1)} %get-tuple-element.29), channel_id=1, source_target_pairs={{4,0},{8,4},{12,8},{0,12},{5,1},{9,5},{13,9},{1,13},{6,2},{10,6},{... | collective-permute-start | bytes 49160 | tf_op jit(solution)/shard_map/ppermute | solution.py:378
  36.7 2.8 %collective-permute-start.11 = (f32[32,128]{1,0:T(8,128)S(1)}, f32[32,128]{1,0:T(8,128)S(1)}, u32[]{:S(2)}, u32[]{:S(2)}) collective-permute-start(f32[32,128]{1,0:T(8,128)S(1)} %get-tuple-element.30), channel_id=1, source_target_pairs={{0,8},{12,4},{1,9},{13,5},{2,10},{14,6},{3,11},{15,7},{16,24},{28,... | collective-permute-start | bytes 49160 | tf_op jit(solution)/shard_map/ppermute | solution.py:378

commit v21 on v20

--- a/solution.py
+++ b/solution.py
@@ -66,7 +66,7 @@
     plan = []
     for shift in range(1, naux // 2 + 1):
         if 2 * shift < naux:
-            plan.append([(source, (source + shift) % naux) for source in range(naux)])
+            plan.append([((target + shift) % naux, target) for target in range(naux)])
         else:
             plan.append([(z, z + shift) if z % 2 else (z + shift, z) for z in range(shift)])
     return plan
@@ -241,7 +241,7 @@
     for tau in range(nt):
         here = [jnp.zeros((half, block), F32)] * naux
         for shift in range(count):
-            here[(naux - shift) % naux] = ordered[shift, tau * half : (tau + 1) * half, :]
+            here[shift] = ordered[shift, tau * half : (tau + 1) * half, :]
         out_ref[tau] = at_sub(place, jnp.concatenate(here, axis=1), 0)
 
 
@@ -255,7 +255,7 @@
         for shift, ref in enumerate(backs, 1):
             upper = ref[:, tau * half : (tau + 1) * half]
             lower = ref[:, (nt + tau) * half : (nt + tau + 1) * half]
-            parts[shift] = at_sub(place, jnp.concatenate([upper, lower], axis=0), 1)
+            parts[naux - shift] = at_sub(place, jnp.concatenate([upper, lower], axis=0), 1)
         total = early[tau] + jnp.concatenate(parts, axis=1)
         out_ref[tau] = pltpu.roll(total, place[3] * block, 1)
 

time: 49.8 us -> 51 us (1.024)
  waiting for transfers between devices: 17.2 us -> 18.2 us
    ppermute x1, waiting for transfers between devices: 3.53 us -> 0.76 us  [local(): lax.ppermute(mine, 'aux', pairs)]
    ppermute x1, starting transfers between devices: 1.63 us -> 3.65 us  [local(): lax.ppermute(mine, 'aux', pairs)]
    ppermute x1, waiting for transfers between devices: 1.75 us -> 3.78 us  [local(): lax.ppermute(after(again, lax.ppermute(token, 'sub', swap)), 'aux', plan[...]
    ppermute x2, starting transfers between devices: 4.43 us -> 2.58 us  [local(): lax.ppermute(back, 'aux', [(target, source) for source, target in pairs])]
    ppermute x1, waiting for transfers between devices: 0.01 us -> 1 us  [local(): last_other = lax.ppermute(last, 'sub', swap)]
    ppermute x1, waiting for transfers between devices: 6.16 us -> 6.9 us  [local(): fars.append(lax.ppermute(late_near, ('orb', 'sub'), pairs))]
  transfers between devices with their start and end apart: 12 -> 12, of which waited for: 8 -> 9; matrix products, arithmetic and copies ran while one was open for 3% -> 3% of each run, Pallas kernels for 13% -> 13%
where the time goes in v21:
time: 51 us; the launch traced here: 50.7 us
  waiting for transfers between devices  18.2 us (36%)
  starting transfers between devices  13 us (25%)
  blocking collectives  9.05 us (18%)
  Pallas kernels  6.95 us (14%)
  other arithmetic  2.07 us (4%)
  local copies, waits for them, and re-layouts  1.27 us (2%)
    all_to_all x1, blocking collectives, local(): lax.all_to_all(partial_chi.reshape(owners, nt * block_aux // owners, naux...  9.05 us
    pallas_call x8, Pallas kernels, call(): pl.pallas_call(here, out_shape=shapes, in_specs=[VMEM] * len(arguments),...  6.95 us
    ppermute x1, waiting for transfers between devices, local(): fars.append(lax.ppermute(late_near, ('orb', 'sub'), pairs))  6.9 us
    ppermute x1, waiting for transfers between devices, local(): lax.ppermute(after(again, lax.ppermute(token, 'sub', swap)), 'aux', plan[...  3.78 us
    ppermute x1, starting transfers between devices, local(): lax.ppermute(mine, 'aux', pairs)  3.65 us
    ppermute x1, waiting for transfers between devices, local(): lax.ppermute(small, 'tau', ring(nt, shift))  3.07 us
    ppermute x1, starting transfers between devices, local(): lax.ppermute(tensor, 'orb', ring(nob, shift))  2.94 us
    ppermute x2, starting transfers between devices, local(): lax.ppermute(back, 'aux', [(target, source) for source, target in pairs])  2.58 us
  transfers between devices with their start and end apart: 12, of which 9 were waited for; matrix products, arithmetic and copies ran while one was open for 3% of the time, Pallas kernels for 13%

profile of v21, /device:TPU:0, one launch (start us, length us, event | category | flops | bytes accessed | tf_op | source)
XLA Modules:
  0.0 50.7 jit_solution(15111301324306597820)
XLA Ops:
  0.0 2.9 %collective-permute-start.1 = (f32[128,2048]{1,0:T(8,128)}, f32[128,2048]{1,0:T(8,128)S(1)}, u32[]{:S(2)}, u32[]{:S(2)}) collective-permute-start(f32[128,2048]{1,0:T(8,128)} %bitcast.5), channel_id=1, source_target_pairs={{2,0},{0,2},{3,1},{1,3},{6,4},{4,6},{7,5},{5,7},{10,8},{8,10},{11,... | collective-permute-start | bytes 3145736 | tf_op jit(solution)/shard_map/ppermute | solution.py:295
  2.9 1.3 %copy-done = f32[1,1,2,64,2048]{4,3,2,1,0:T(8,128)S(1)} copy-done((f32[1,1,2,64,2048]{4,3,2,1,0:T(8,128)S(1)}, f32[1,1,2,64,2048]{4,3,2,1,0:T(8,128)}, u32[]{:S(2)}) %copy-start) | copy-done | bytes 1048600
  4.2 0.6 %prepare.1 = (f32[32,32,128]{2,1,0:T(8,128)S(1)}, f32[32,32,128]{2,1,0:T(8,128)S(1)}) custom-call(f32[128,2048]{1,0:T(8,128)S(1)} %bitcast.6), custom_call_target="tpu_custom_call" | custom-call | bytes 1048576 | tf_op jit(solution)/shard_map/prepare/pallas_call | solution.py:284
  4.8 3.7 %collective-permute-start.3 = (f32[32,32,128]{2,1,0:T(8,128)S(1)}, f32[32,32,128]{2,1,0:T(8,128)S(1)}, u32[]{:S(2)}, u32[]{:S(2)}) collective-permute-start(f32[32,32,128]{2,1,0:T(8,128)S(1)} %get-tuple-element.19.refs_1_), channel_id=1, source_target_pairs={{4,0},{8,4},{12,8},{0,12},{5,1},{9,5},{13,9},{1,13},{6,2},{10,6},{... | collective-permute-start | bytes 1572872 | tf_op jit(solution)/shard_map/ppermute | solution.py:327
  8.5 0.7 %convert_element_type.5 = f32[1,2]{1,0:T(1,128)S(1)} convert(s32[1,2]{1,0:T(1,128)} %param.7) | non-fusion elementwise | flops 2 | bytes 16 | tf_op jit(solution)/shard_map/convert_element_type | solution.py:305
  9.1 0.8 %fusion = (f32[1,136,128]{2,1,0:T(8,128)S(1)}, f32[136,128]{1,0:T(8,128)S(1)}) fusion(f32[1,2]{1,0:T(1,128)S(1)} %convert_element_type.5, f32[64,128]{1,0:T(8,128)} %param.6, f32[64,128]{1,0:T(8,128)} %param.5), kind=kLoop, calls=%fused_computation.4 | loop fusion | flops 69632 | bytes 204808 | tf_op jit(solution)/shard_map/stack | solution.py:308
  9.9 1.6 %collective-permute-start = (f32[136,128]{1,0:T(8,128)S(1)}, f32[136,128]{1,0:T(8,128)S(1)}, u32[]{:S(2)}, u32[]{:S(2)}) collective-permute-start(f32[136,128]{1,0:T(8,128)S(1)} %get-tuple-element.32), channel_id=1, source_target_pairs={{16,0},{0,16},{17,1},{1,17},{18,2},{2,18},{19,3},{3,19},{20,4},{4,... | collective-permute-start | bytes 208904 | tf_op jit(solution)/shard_map/ppermute | solution.py:308
  11.5 3.1 %collective-permute-done = f32[136,128]{1,0:T(8,128)S(1)} collective-permute-done((f32[136,128]{1,0:T(8,128)S(1)}, f32[136,128]{1,0:T(8,128)S(1)}, u32[]{:S(2)}, u32[]{:S(2)}) %collective-permute-start) | collective-permute-done | bytes 69664 | tf_op jit(solution)/shard_map/ppermute | solution.py:308
  14.6 1.5 %first.1 = (f32[4,512,256]{2,1,0:T(8,128)S(1)}, f32[8,128]{1,0:T(8,128)S(1)}) custom-call(f32[2,136,128]{2,1,0:T(8,128)S(1)} %pad_maximum_fusion.refs_0_, f32[128,2048]{1,0:T(8,128)S(1)} %bitcast.7), custom_call_target="tpu_custom_call" | custom-call | bytes 1187840 | tf_op jit(solution)/shard_map/first/pallas_call | solution.py:284
  16.1 0.1 collective-permute-start.7
  16.2 1.2 %collective-permute-done.7.refs_1_ = f32[8,128]{1,0:T(8,128)S(1)} collective-permute-done((f32[8,128]{1,0:T(8,128)S(1)}, f32[8,128]{1,0:T(8,128)S(1)}, u32[]{:S(2)}, u32[]{:S(2)}) %collective-permute-start.7) | collective-permute-done | bytes 4128 | tf_op jit(solution)/shard_map/ppermute | solution.py:330
  17.3 1.3 %collective-permute-start.8 = (f32[32,32,128]{2,1,0:T(8,128)S(1)}, f32[32,32,128]{2,1,0:T(8,128)S(1)}, u32[]{:S(2)}, u32[]{:S(2)}) collective-permute-start(f32[32,32,128]{2,1,0:T(8,128)S(1)} %after.4), channel_id=1, source_target_pairs={{8,0},{4,12},{9,1},{5,13},{10,2},{6,14},{11,3},{7,15},{24,16},{20,... | collective-permute-start | bytes 1572872 | tf_op jit(solution)/shard_map/ppermute | solution.py:330
  18.6 0.8 %collective-permute-done.3.refs_0_ = f32[32,32,128]{2,1,0:T(8,128)S(1)} collective-permute-done((f32[32,32,128]{2,1,0:T(8,128)S(1)}, f32[32,32,128]{2,1,0:T(8,128)S(1)}, u32[]{:S(2)}, u32[]{:S(2)}) %collective-permute-start.3) | collective-permute-done | bytes 524320 | tf_op jit(solution)/shard_map/ppermute | solution.py:327
  19.4 0.1 collective-permute-start.4
  19.5 0.5 collective-permute-start.5
  20.0 1.0 %collective-permute-done.4.refs_4_.refs_7_.refs_3_ = f32[16,32,128]{2,1,0:T(8,128)S(1)} collective-permute-done((f32[16,32,128]{2,1,0:T(8,128)S(1)}, f32[16,32,128]{2,1,0:T(8,128)S(1)}, u32[]{:S(2)}, u32[]{:S(2)}) %collective-permute-start.4) | collective-permute-done | bytes 262176 | tf_op jit(solution)/shard_map/ppermute | solution.py:329
  21.0 0.4 collective-permute-done.5.refs_5_.refs_8_.refs_4_
  21.4 0.3 collective-permute-start.6
  21.7 6.9 %collective-permute-done.6.refs_3_ = f32[2,136,128]{2,1,0:T(8,128)S(1)} collective-permute-done((f32[2,136,128]{2,1,0:T(8,128)S(1)}, f32[2,136,128]{2,1,0:T(8,128)S(1)}, u32[]{:S(2)}, u32[]{:S(2)}) %collective-permute-start.6) | collective-permute-done | bytes 139296 | tf_op jit(solution)/shard_map/ppermute | solution.py:335
  28.6 1.7 %second.1 = (bf16[256,4096]{1,0:T(8,128)(2,1)S(1)}, f32[8,128]{1,0:T(8,128)S(1)}) custom-call(f32[2,136,128]{2,1,0:T(8,128)S(1)} %pad_maximum_fusion.refs_0_, f32[4,512,256]{2,1,0:T(8,128)S(1)} %get-tuple-element.18.refs_1_, f32[128,2048]{1,0:T(8,128)S(1)} %collective-permute-done.1.refs_2_, f32[2,136,128]{2,1,0:T(8,128)S(1)} %collective-permute-done.6.refs_3_, ...), custom_call_target="tpu_custom_call" | custom-call | flops 603979776 | bytes 4997120 | tf_op jit(solution)/shard_map/second/pallas_call | solution.py:284
  30.3 3.8 %collective-permute-done.8.refs_0_ = f32[32,32,128]{2,1,0:T(8,128)S(1)} collective-permute-done((f32[32,32,128]{2,1,0:T(8,128)S(1)}, f32[32,32,128]{2,1,0:T(8,128)S(1)}, u32[]{:S(2)}, u32[]{:S(2)}) %collective-permute-start.8) | collective-permute-done | bytes 524320 | tf_op jit(solution)/shard_map/ppermute | solution.py:330
  34.1 0.8 %meet_own.1 = (bf16[192,4096]{1,0:T(8,128)(2,1)S(1)}, f32[32,64]{1,0:T(8,128)S(1)}, f32[32,128]{1,0:T(8,128)S(1)}) custom-call(bf16[256,4096]{1,0:T(8,128)(2,1)S(1)} %get-tuple-element.23.refs_0_, f32[16,32,128]{2,1,0:T(8,128)S(1)} %get-tuple-element.21.refs_2_.refs_5_.refs_1_, f32[16,32,128]{2,1,0:T(8,128)S(1)} %get-tuple-element.22.refs_3_.refs_6_.refs_2_, ...), custom_call_target="tpu_custom_call" | custom-call | flops 402653184 | bytes 5767168 | tf_op jit(solution)/shard_map/meet_own/pallas_call | solution.py:284
  34.9 0.1 collective-permute-start.10
  35.0 1.0 %collective-permute-done.9.refs_2_ = f32[32,32,128]{2,1,0:T(8,128)S(1)} collective-permute-done((f32[32,32,128]{2,1,0:T(8,128)S(1)}, f32[32,32,128]{2,1,0:T(8,128)S(1)}, u32[]{:S(2)}, u32[]{:S(2)}) %collective-permute-start.9) | collective-permute-done | bytes 524320 | tf_op jit(solution)/shard_map/ppermute | solution.py:350
  36.0 0.7 %meet_back.1 = (bf16[64,4096]{1,0:T(8,128)(2,1)S(1)}, f32[32,128]{1,0:T(8,128)S(1)}) custom-call(bf16[256,4096]{1,0:T(8,128)(2,1)S(1)} %get-tuple-element.23.refs_0_, f32[32,64]{1,0:T(8,128)S(1)} %get-tuple-element.27.refs_1_, f32[32,32,128]{2,1,0:T(8,128)S(1)} %collective-permute-done.9.refs_2_), custom_call_target="tpu_custom_call" | custom-call | flops 134217728 | bytes 4726784 | tf_op jit(solution)/shard_map/meet_back/pallas_call | solution.py:284
  36.7 2.5 %collective-permute-start.11 = (f32[32,128]{1,0:T(8,128)S(1)}, f32[32,128]{1,0:T(8,128)S(1)}, u32[]{:S(2)}, u32[]{:S(2)}) collective-permute-start(f32[32,128]{1,0:T(8,128)S(1)} %get-tuple-element.30), channel_id=1, source_target_pairs={{0,8},{12,4},{1,9},{13,5},{2,10},{14,6},{3,11},{15,7},{16,24},{28,... | collective-permute-start | bytes 49160 | tf_op jit(solution)/shard_map/ppermute | solution.py:378
  39.2 1.2 %meet_direct.1.refs_0_ = f32[2,64,256]{2,1,0:T(8,128)S(1)} custom-call(bf16[256,4096]{1,0:T(8,128)(2,1)S(1)} %get-tuple-element.23.refs_0_, f32[32,32,128]{2,1,0:T(8,128)S(1)} %get-tuple-element.19.refs_1_, f32[32,32,128]{2,1,0:T(8,128)S(1)} %collective-permute-done.2.refs_1_.refs_4_.refs_2_, bf16[192,4096]{1,0:T(8,128)(2,1)S(1)} %get-tuple-element.26.refs_3_, ...), custom_call_target="tpu_custom_call" | custom-call | flops 805306368 | bytes 9437184 | tf_op jit(solution)/shard_map/meet_direct/pallas_call | solution.py:284
  40.5 0.0 collective-permute-done.10.refs_1_
  40.5 0.2 collective-permute-done.11.refs_2_
  40.7 0.3 complete.1
  41.0 9.1 %all_to_all.5 = f32[8,16,256]{2,1,0:T(8,128)S(1)} all-to-all(f32[8,16,256]{2,1,0:T(8,128)S(1)} %bitcast.8), channel_id=1, replica_groups=mesh['tau'=2,'aux'=4,'orb'=2,'sub'=2] {'tau','orb','sub'}, dimensions={0} | all-to-all | bytes 262144 | tf_op jit(solution)/shard_map/all_to_all | solution.py:396
  50.0 0.6 %broadcast_multiply_fusion = f32[16,256]{1,0:T(8,128)} fusion(f32[16,256]{1,0:T(8,128)S(1)} %reduce_sum.9), kind=kLoop, calls=%fused_computation.3 | loop fusion | flops 4096 | bytes 32768 | tf_op jit(solution)/shard_map/mul | solution.py:403
  (14 shorter events, 0.1 us)
Async XLA Ops:
  0.0 28.6 %collective-permute-start.1 = (f32[128,2048]{1,0:T(8,128)}, f32[128,2048]{1,0:T(8,128)S(1)}, u32[]{:S(2)}, u32[]{:S(2)}) collective-permute-start(f32[128,2048]{1,0:T(8,128)} %bitcast.5), channel_id=1, source_target_pairs={{2,0},{0,2},{3,1},{1,3},{6,4},{4,6},{7,5},{5,7},{10,8},{8,10},{11,... | collective-permute-start | bytes 3145736 | tf_op jit(solution)/shard_map/ppermute | solution.py:295
  2.9 1.3 %copy-start = (f32[1,1,2,64,2048]{4,3,2,1,0:T(8,128)S(1)}, f32[1,1,2,64,2048]{4,3,2,1,0:T(8,128)}, u32[]{:S(2)}) copy-start(f32[1,1,2,64,2048]{4,3,2,1,0:T(8,128)} %param.4) | copy-start | bytes 3145732
  4.2 10.4 %copy-start.1 = (f32[1,1,2,64,2048]{4,3,2,1,0:T(8,128)S(1)}, f32[1,1,2,64,2048]{4,3,2,1,0:T(8,128)}, u32[]{:S(2)}) copy-start(f32[1,1,2,64,2048]{4,3,2,1,0:T(8,128)} %param.4) | copy-start | bytes 3145732
  4.8 14.6 %collective-permute-start.3 = (f32[32,32,128]{2,1,0:T(8,128)S(1)}, f32[32,32,128]{2,1,0:T(8,128)S(1)}, u32[]{:S(2)}, u32[]{:S(2)}) collective-permute-start(f32[32,32,128]{2,1,0:T(8,128)S(1)} %get-tuple-element.19.refs_1_), channel_id=1, source_target_pairs={{4,0},{8,4},{12,8},{0,12},{5,1},{9,5},{13,9},{1,13},{6,2},{10,6},{... | collective-permute-start | bytes 1572872 | tf_op jit(solution)/shard_map/ppermute | solution.py:327
  8.5 11.5 %collective-permute-start.2 = (f32[32,32,128]{2,1,0:T(8,128)S(1)}, f32[32,32,128]{2,1,0:T(8,128)S(1)}, u32[]{:S(2)}, u32[]{:S(2)}) collective-permute-start(f32[32,32,128]{2,1,0:T(8,128)S(1)} %get-tuple-element.19.refs_1_), channel_id=1, source_target_pairs={{1,0},{0,1},{3,2},{2,3},{5,4},{4,5},{7,6},{6,7},{9,8},{8,9},{11,10... | collective-permute-start | bytes 1572872 | tf_op jit(solution)/shard_map/ppermute | solution.py:323
  9.9 4.7 %collective-permute-start = (f32[136,128]{1,0:T(8,128)S(1)}, f32[136,128]{1,0:T(8,128)S(1)}, u32[]{:S(2)}, u32[]{:S(2)}) collective-permute-start(f32[136,128]{1,0:T(8,128)S(1)} %get-tuple-element.32), channel_id=1, source_target_pairs={{16,0},{0,16},{17,1},{1,17},{18,2},{2,18},{19,3},{3,19},{20,4},{4,... | collective-permute-start | bytes 208904 | tf_op jit(solution)/shard_map/ppermute | solution.py:308
  16.1 1.2 %collective-permute-start.7 = (f32[8,128]{1,0:T(8,128)S(1)}, f32[8,128]{1,0:T(8,128)S(1)}, u32[]{:S(2)}, u32[]{:S(2)}) collective-permute-start(f32[8,128]{1,0:T(8,128)S(1)} %get-tuple-element.20.refs_1_), channel_id=1, source_target_pairs={{1,0},{0,1},{3,2},{2,3},{5,4},{4,5},{7,6},{6,7},{9,8},{8,9},{11,10... | collective-permute-start | bytes 12296 | tf_op jit(solution)/shard_map/ppermute | solution.py:330
  17.3 16.8 %collective-permute-start.8 = (f32[32,32,128]{2,1,0:T(8,128)S(1)}, f32[32,32,128]{2,1,0:T(8,128)S(1)}, u32[]{:S(2)}, u32[]{:S(2)}) collective-permute-start(f32[32,32,128]{2,1,0:T(8,128)S(1)} %after.4), channel_id=1, source_target_pairs={{8,0},{4,12},{9,1},{5,13},{10,2},{6,14},{11,3},{7,15},{24,16},{20,... | collective-permute-start | bytes 1572872 | tf_op jit(solution)/shard_map/ppermute | solution.py:330
  19.4 1.6 %collective-permute-start.4 = (f32[16,32,128]{2,1,0:T(8,128)S(1)}, f32[16,32,128]{2,1,0:T(8,128)S(1)}, u32[]{:S(2)}, u32[]{:S(2)}) collective-permute-start(f32[16,32,128]{2,1,0:T(8,128)S(1)} %get-tuple-element.21.refs_2_.refs_5_.refs_1_), channel_id=1, source_target_pairs={{1,0},{0,1},{3,2},{2,3},{5,4},{4,5},{7,6},{6,7},{9,8},{8,9},{11,10... | collective-permute-start | bytes 786440 | tf_op jit(solution)/shard_map/ppermute | solution.py:329
  19.5 1.9 %collective-permute-start.5 = (f32[16,32,128]{2,1,0:T(8,128)S(1)}, f32[16,32,128]{2,1,0:T(8,128)S(1)}, u32[]{:S(2)}, u32[]{:S(2)}) collective-permute-start(f32[16,32,128]{2,1,0:T(8,128)S(1)} %get-tuple-element.22.refs_3_.refs_6_.refs_2_), channel_id=1, source_target_pairs={{1,0},{0,1},{3,2},{2,3},{5,4},{4,5},{7,6},{6,7},{9,8},{8,9},{11,10... | collective-permute-start | bytes 786440 | tf_op jit(solution)/shard_map/ppermute | solution.py:329
  21.4 7.2 %collective-permute-start.6 = (f32[2,136,128]{2,1,0:T(8,128)S(1)}, f32[2,136,128]{2,1,0:T(8,128)S(1)}, u32[]{:S(2)}, u32[]{:S(2)}) collective-permute-start(f32[2,136,128]{2,1,0:T(8,128)S(1)} %after.3), channel_id=1, source_target_pairs={{2,1},{3,0},{0,3},{1,2},{6,5},{7,4},{4,7},{5,6},{10,9},{11,8},{8,1... | collective-permute-start | bytes 417800 | tf_op jit(solution)/shard_map/ppermute | solution.py:335
  34.1 1.9 %collective-permute-start.9 = (f32[32,32,128]{2,1,0:T(8,128)S(1)}, f32[32,32,128]{2,1,0:T(8,128)S(1)}, u32[]{:S(2)}, u32[]{:S(2)}) collective-permute-start(f32[32,32,128]{2,1,0:T(8,128)S(1)} %after.5.refs_5_), channel_id=1, source_target_pairs={{1,0},{0,1},{3,2},{2,3},{5,4},{4,5},{7,6},{6,7},{9,8},{8,9},{11,10... | collective-permute-start | bytes 1572872 | tf_op jit(solution)/shard_map/ppermute | solution.py:350
  34.9 5.6 %collective-permute-start.10 = (f32[32,128]{1,0:T(8,128)S(1)}, f32[32,128]{1,0:T(8,128)S(1)}, u32[]{:S(2)}, u32[]{:S(2)}) collective-permute-start(f32[32,128]{1,0:T(8,128)S(1)} %get-tuple-element.29), channel_id=1, source_target_pairs={{0,4},{4,8},{8,12},{12,0},{1,5},{5,9},{9,13},{13,1},{2,6},{6,10},{... | collective-permute-start | bytes 49160 | tf_op jit(solution)/shard_map/ppermute | solution.py:378
  36.7 4.0 %collective-permute-start.11 = (f32[32,128]{1,0:T(8,128)S(1)}, f32[32,128]{1,0:T(8,128)S(1)}, u32[]{:S(2)}, u32[]{:S(2)}) collective-permute-start(f32[32,128]{1,0:T(8,128)S(1)} %get-tuple-element.30), channel_id=1, source_target_pairs={{0,8},{12,4},{1,9},{13,5},{2,10},{14,6},{3,11},{15,7},{16,24},{28,... | collective-permute-start | bytes 49160 | tf_op jit(solution)/shard_map/ppermute | solution.py:378

commit v22 on v20

--- a/solution.py
+++ b/solution.py
@@ -246,7 +246,7 @@
 
 
 def complete(place, early, *refs):
-    backs, out_ref = refs[:-1], refs[-1]
+    backs, keep, give = refs[:-2], refs[-2], refs[-1]
     nt, block, wide = early.shape
     naux = wide // block
     half = block // 2
@@ -257,7 +257,13 @@
             lower = ref[:, (nt + tau) * half : (nt + tau + 1) * half]
             parts[shift] = at_sub(place, jnp.concatenate([upper, lower], axis=0), 1)
         total = early[tau] + jnp.concatenate(parts, axis=1)
-        out_ref[tau] = pltpu.roll(total, place[3] * block, 1)
+        total = pltpu.roll(total, place[3] * block, 1)
+        owners, rows, _ = keep.shape
+        for i in range(owners // nt):
+            first_rows = total[2 * i * rows : (2 * i + 1) * rows]
+            second_rows = total[(2 * i + 1) * rows : 2 * (i + 1) * rows]
+            keep[tau * (owners // nt) + i] = jnp.where(place[2] == 0, first_rows, second_rows)
+            give[tau * (owners // nt) + i] = jnp.where(place[2] == 0, second_rows, first_rows)
 
 
 def local(three_center, occupied_green, virtual_green, block_list, sizes):
@@ -391,14 +397,11 @@
         nt=nt,
         naux=naux,
     )
-    (partial_chi,) = call(complete, [shape], [], 0, direct, *returned)
-    owners = nt * nob * nsub
+    owners = nt * nob
+    shape = ((owners, block_aux // (nob * nsub), nauxf), F32)
+    keep, give = call(complete, [shape] * 2, [], 0, direct, *returned)
     received = lax.all_to_all(
-        partial_chi.reshape(owners, nt * block_aux // owners, nauxf),
-        ("tau", "orb", "sub"),
-        split_axis=0,
-        concat_axis=0,
-        tiled=True,
+        keep + lax.ppermute(give, "sub", swap), ("tau", "orb"), split_axis=0, concat_axis=0, tiled=True
     )
     return received.sum(axis=0) * (-2.0 / math.sqrt(norb * slots * width))
 

time: 49.8 us -> 50.4 us (1.012)
  waiting for transfers between devices: 17.2 us -> 18.5 us
  blocking collectives: 9.05 us -> 8.36 us
    ppermute x0 -> x1, waiting for transfers between devices: none -> 1.24 us  [local(): lax.ppermute(give, 'sub', swap)]
    all_to_all x1, blocking collectives: 9.05 us -> 8.36 us  [local(): lax.all_to_all(keep + lax.ppermute(give, 'sub', swap), ('tau', 'orb'), sp...]
  transfers between devices with their start and end apart: 12 -> 13, of which waited for: 8 -> 9; matrix products, arithmetic and copies ran while one was open for 3% -> 3% of each run, Pallas kernels for 13% -> 13%
where the time goes in v22:
time: 50.4 us; the launch traced here: 50.1 us
  waiting for transfers between devices  18.5 us (37%)
  starting transfers between devices  12.9 us (26%)
  blocking collectives  8.36 us (17%)
  Pallas kernels  6.97 us (14%)
  other arithmetic  2.08 us (4%)
  local copies, waits for them, and re-layouts  1.27 us (3%)
    all_to_all x1, blocking collectives, local(): lax.all_to_all(keep + lax.ppermute(give, 'sub', swap), ('tau', 'orb'), sp...  8.36 us
    pallas_call x8, Pallas kernels, call(): pl.pallas_call(here, out_shape=shapes, in_specs=[VMEM] * len(arguments),...  6.97 us
    ppermute x1, waiting for transfers between devices, local(): fars.append(lax.ppermute(late_near, ('orb', 'sub'), pairs))  6.16 us
    ppermute x2, starting transfers between devices, local(): lax.ppermute(back, 'aux', [(target, source) for source, target in pairs])  4.43 us
    ppermute x1, waiting for transfers between devices, local(): lax.ppermute(mine, 'aux', pairs)  3.53 us
    ppermute x1, waiting for transfers between devices, local(): lax.ppermute(small, 'tau', ring(nt, shift))  3.07 us
    ppermute x1, starting transfers between devices, local(): lax.ppermute(tensor, 'orb', ring(nob, shift))  2.94 us
    ppermute x1, waiting for transfers between devices, local(): lax.ppermute(after(again, lax.ppermute(token, 'sub', swap)), 'aux', plan[...  1.75 us
  transfers between devices with their start and end apart: 13, of which 9 were waited for; matrix products, arithmetic and copies ran while one was open for 3% of the time, Pallas kernels for 13%

profile of v22, /device:TPU:0, one launch (start us, length us, event | category | flops | bytes accessed | tf_op | source)
XLA Modules:
  0.0 50.1 jit_solution(18097489455882809473)
XLA Ops:
  0.0 2.9 %collective-permute-start.1 = (f32[128,2048]{1,0:T(8,128)}, f32[128,2048]{1,0:T(8,128)S(1)}, u32[]{:S(2)}, u32[]{:S(2)}) collective-permute-start(f32[128,2048]{1,0:T(8,128)} %bitcast.4), channel_id=1, source_target_pairs={{2,0},{0,2},{3,1},{1,3},{6,4},{4,6},{7,5},{5,7},{10,8},{8,10},{11,... | collective-permute-start | bytes 3145736 | tf_op jit(solution)/shard_map/ppermute | solution.py:301
  2.9 1.3 %copy-done = f32[1,1,2,64,2048]{4,3,2,1,0:T(8,128)S(1)} copy-done((f32[1,1,2,64,2048]{4,3,2,1,0:T(8,128)S(1)}, f32[1,1,2,64,2048]{4,3,2,1,0:T(8,128)}, u32[]{:S(2)}) %copy-start) | copy-done | bytes 1048600
  4.2 0.6 %prepare.1 = (f32[32,32,128]{2,1,0:T(8,128)S(1)}, f32[32,32,128]{2,1,0:T(8,128)S(1)}) custom-call(f32[128,2048]{1,0:T(8,128)S(1)} %bitcast.5), custom_call_target="tpu_custom_call" | custom-call | bytes 1048576 | tf_op jit(solution)/shard_map/prepare/pallas_call | solution.py:290
  4.8 1.6 %collective-permute-start.3 = (f32[32,32,128]{2,1,0:T(8,128)S(1)}, f32[32,32,128]{2,1,0:T(8,128)S(1)}, u32[]{:S(2)}, u32[]{:S(2)}) collective-permute-start(f32[32,32,128]{2,1,0:T(8,128)S(1)} %get-tuple-element.21.refs_1_), channel_id=1, source_target_pairs={{0,4},{4,8},{8,12},{12,0},{1,5},{5,9},{9,13},{13,1},{2,6},{6,10},{... | collective-permute-start | bytes 1572872 | tf_op jit(solution)/shard_map/ppermute | solution.py:333
  6.4 0.7 %convert_element_type.5 = f32[1,2]{1,0:T(1,128)S(1)} convert(s32[1,2]{1,0:T(1,128)} %param.7) | non-fusion elementwise | flops 2 | bytes 16 | tf_op jit(solution)/shard_map/convert_element_type | solution.py:311
  7.1 0.8 %fusion = (f32[1,136,128]{2,1,0:T(8,128)S(1)}, f32[136,128]{1,0:T(8,128)S(1)}) fusion(f32[1,2]{1,0:T(1,128)S(1)} %convert_element_type.5, f32[64,128]{1,0:T(8,128)} %param.6, f32[64,128]{1,0:T(8,128)} %param.5), kind=kLoop, calls=%fused_computation.4 | loop fusion | flops 69632 | bytes 204808 | tf_op jit(solution)/shard_map/stack | solution.py:314
  7.9 1.6 %collective-permute-start = (f32[136,128]{1,0:T(8,128)S(1)}, f32[136,128]{1,0:T(8,128)S(1)}, u32[]{:S(2)}, u32[]{:S(2)}) collective-permute-start(f32[136,128]{1,0:T(8,128)S(1)} %get-tuple-element.36), channel_id=1, source_target_pairs={{16,0},{0,16},{17,1},{1,17},{18,2},{2,18},{19,3},{3,19},{20,4},{4,... | collective-permute-start | bytes 208904 | tf_op jit(solution)/shard_map/ppermute | solution.py:314
  9.5 3.1 %collective-permute-done = f32[136,128]{1,0:T(8,128)S(1)} collective-permute-done((f32[136,128]{1,0:T(8,128)S(1)}, f32[136,128]{1,0:T(8,128)S(1)}, u32[]{:S(2)}, u32[]{:S(2)}) %collective-permute-start) | collective-permute-done | bytes 69664 | tf_op jit(solution)/shard_map/ppermute | solution.py:314
  12.6 1.5 %first.1 = (f32[4,512,256]{2,1,0:T(8,128)S(1)}, f32[8,128]{1,0:T(8,128)S(1)}) custom-call(f32[2,136,128]{2,1,0:T(8,128)S(1)} %pad_maximum_fusion.refs_0_, f32[128,2048]{1,0:T(8,128)S(1)} %bitcast.6), custom_call_target="tpu_custom_call" | custom-call | bytes 1187840 | tf_op jit(solution)/shard_map/first/pallas_call | solution.py:290
  14.1 0.1 collective-permute-start.7
  14.1 1.2 %collective-permute-done.7.refs_1_ = f32[8,128]{1,0:T(8,128)S(1)} collective-permute-done((f32[8,128]{1,0:T(8,128)S(1)}, f32[8,128]{1,0:T(8,128)S(1)}, u32[]{:S(2)}, u32[]{:S(2)}) %collective-permute-start.7) | collective-permute-done | bytes 4128 | tf_op jit(solution)/shard_map/ppermute | solution.py:336
  15.3 1.3 %collective-permute-start.8 = (f32[32,32,128]{2,1,0:T(8,128)S(1)}, f32[32,32,128]{2,1,0:T(8,128)S(1)}, u32[]{:S(2)}, u32[]{:S(2)}) collective-permute-start(f32[32,32,128]{2,1,0:T(8,128)S(1)} %after.4), channel_id=1, source_target_pairs={{8,0},{4,12},{9,1},{5,13},{10,2},{6,14},{11,3},{7,15},{24,16},{20,... | collective-permute-start | bytes 1572872 | tf_op jit(solution)/shard_map/ppermute | solution.py:336
  16.6 3.5 %collective-permute-done.3.refs_0_ = f32[32,32,128]{2,1,0:T(8,128)S(1)} collective-permute-done((f32[32,32,128]{2,1,0:T(8,128)S(1)}, f32[32,32,128]{2,1,0:T(8,128)S(1)}, u32[]{:S(2)}, u32[]{:S(2)}) %collective-permute-start.3) | collective-permute-done | bytes 524320 | tf_op jit(solution)/shard_map/ppermute | solution.py:333
  20.1 0.1 collective-permute-start.4
  20.2 0.5 collective-permute-start.5
  20.7 1.0 %collective-permute-done.4.refs_4_.refs_7_.refs_3_ = f32[16,32,128]{2,1,0:T(8,128)S(1)} collective-permute-done((f32[16,32,128]{2,1,0:T(8,128)S(1)}, f32[16,32,128]{2,1,0:T(8,128)S(1)}, u32[]{:S(2)}, u32[]{:S(2)}) %collective-permute-start.4) | collective-permute-done | bytes 262176 | tf_op jit(solution)/shard_map/ppermute | solution.py:335
  21.7 0.4 collective-permute-done.5.refs_5_.refs_8_.refs_4_
  22.1 0.3 collective-permute-start.6
  22.4 6.2 %collective-permute-done.6.refs_3_ = f32[2,136,128]{2,1,0:T(8,128)S(1)} collective-permute-done((f32[2,136,128]{2,1,0:T(8,128)S(1)}, f32[2,136,128]{2,1,0:T(8,128)S(1)}, u32[]{:S(2)}, u32[]{:S(2)}) %collective-permute-start.6) | collective-permute-done | bytes 139296 | tf_op jit(solution)/shard_map/ppermute | solution.py:341
  28.6 1.7 %second.1 = (bf16[256,4096]{1,0:T(8,128)(2,1)S(1)}, f32[8,128]{1,0:T(8,128)S(1)}) custom-call(f32[2,136,128]{2,1,0:T(8,128)S(1)} %pad_maximum_fusion.refs_0_, f32[4,512,256]{2,1,0:T(8,128)S(1)} %get-tuple-element.20.refs_1_, f32[128,2048]{1,0:T(8,128)S(1)} %collective-permute-done.1.refs_2_, f32[2,136,128]{2,1,0:T(8,128)S(1)} %collective-permute-done.6.refs_3_, ...), custom_call_target="tpu_custom_call" | custom-call | flops 603979776 | bytes 4997120 | tf_op jit(solution)/shard_map/second/pallas_call | solution.py:290
  30.3 1.8 %collective-permute-done.8.refs_0_ = f32[32,32,128]{2,1,0:T(8,128)S(1)} collective-permute-done((f32[32,32,128]{2,1,0:T(8,128)S(1)}, f32[32,32,128]{2,1,0:T(8,128)S(1)}, u32[]{:S(2)}, u32[]{:S(2)}) %collective-permute-start.8) | collective-permute-done | bytes 524320 | tf_op jit(solution)/shard_map/ppermute | solution.py:336
  32.1 0.8 %meet_own.1 = (bf16[192,4096]{1,0:T(8,128)(2,1)S(1)}, f32[32,64]{1,0:T(8,128)S(1)}, f32[32,128]{1,0:T(8,128)S(1)}) custom-call(bf16[256,4096]{1,0:T(8,128)(2,1)S(1)} %get-tuple-element.25.refs_0_, f32[16,32,128]{2,1,0:T(8,128)S(1)} %get-tuple-element.23.refs_2_.refs_5_.refs_1_, f32[16,32,128]{2,1,0:T(8,128)S(1)} %get-tuple-element.24.refs_3_.refs_6_.refs_2_, ...), custom_call_target="tpu_custom_call" | custom-call | flops 402653184 | bytes 5767168 | tf_op jit(solution)/shard_map/meet_own/pallas_call | solution.py:290
  32.9 3.1 %collective-permute-start.10 = (f32[32,128]{1,0:T(8,128)S(1)}, f32[32,128]{1,0:T(8,128)S(1)}, u32[]{:S(2)}, u32[]{:S(2)}) collective-permute-start(f32[32,128]{1,0:T(8,128)S(1)} %get-tuple-element.31), channel_id=1, source_target_pairs={{4,0},{8,4},{12,8},{0,12},{5,1},{9,5},{13,9},{1,13},{6,2},{10,6},{... | collective-permute-start | bytes 49160 | tf_op jit(solution)/shard_map/ppermute | solution.py:384
  36.0 0.7 %meet_back.1 = (bf16[64,4096]{1,0:T(8,128)(2,1)S(1)}, f32[32,128]{1,0:T(8,128)S(1)}) custom-call(bf16[256,4096]{1,0:T(8,128)(2,1)S(1)} %get-tuple-element.25.refs_0_, f32[32,64]{1,0:T(8,128)S(1)} %get-tuple-element.29.refs_1_, f32[32,32,128]{2,1,0:T(8,128)S(1)} %collective-permute-done.9.refs_2_), custom_call_target="tpu_custom_call" | custom-call | flops 134217728 | bytes 4726784 | tf_op jit(solution)/shard_map/meet_back/pallas_call | solution.py:290
  36.7 1.3 %collective-permute-start.11 = (f32[32,128]{1,0:T(8,128)S(1)}, f32[32,128]{1,0:T(8,128)S(1)}, u32[]{:S(2)}, u32[]{:S(2)}) collective-permute-start(f32[32,128]{1,0:T(8,128)S(1)} %get-tuple-element.32), channel_id=1, source_target_pairs={{0,8},{12,4},{1,9},{13,5},{2,10},{14,6},{3,11},{15,7},{16,24},{28,... | collective-permute-start | bytes 49160 | tf_op jit(solution)/shard_map/ppermute | solution.py:384
  38.1 1.2 %meet_direct.1.refs_0_ = f32[2,64,256]{2,1,0:T(8,128)S(1)} custom-call(bf16[256,4096]{1,0:T(8,128)(2,1)S(1)} %get-tuple-element.25.refs_0_, f32[32,32,128]{2,1,0:T(8,128)S(1)} %get-tuple-element.21.refs_1_, f32[32,32,128]{2,1,0:T(8,128)S(1)} %collective-permute-done.2.refs_1_.refs_4_.refs_2_, bf16[192,4096]{1,0:T(8,128)(2,1)S(1)} %get-tuple-element.28.refs_3_, ...), custom_call_target="tpu_custom_call" | custom-call | flops 805306368 | bytes 9437184 | tf_op jit(solution)/shard_map/meet_direct/pallas_call | solution.py:290
  39.3 0.2 collective-permute-done.11.refs_2_
  39.5 0.3 complete.1
  39.8 0.1 collective-permute-start.12
  39.9 1.2 %collective-permute-done.12 = f32[4,16,256]{2,1,0:T(8,128)S(1)} collective-permute-done((f32[4,16,256]{2,1,0:T(8,128)S(1)}, f32[4,16,256]{2,1,0:T(8,128)S(1)}, u32[]{:S(2)}, u32[]{:S(2)}) %collective-permute-start.12) | collective-permute-done | bytes 65568 | tf_op jit(solution)/shard_map/ppermute | solution.py:404
  41.1 8.4 %all_to_all.5 = f32[4,16,256]{2,1,0:T(8,128)S(1)} all-to-all(f32[4,16,256]{2,1,0:T(8,128)S(1)} %add.5), channel_id=1, replica_groups=mesh['tau'=2,'aux'=4,'orb'=2,'sub'=2] {'tau','orb'}, dimensions={0} | all-to-all | bytes 131072 | tf_op jit(solution)/shard_map/all_to_all | solution.py:403
  49.5 0.6 %broadcast_multiply_fusion = f32[16,256]{1,0:T(8,128)} fusion(f32[16,256]{1,0:T(8,128)S(1)} %reduce_sum.9), kind=kLoop, calls=%fused_computation.3 | loop fusion | flops 4096 | bytes 32768 | tf_op jit(solution)/shard_map/mul | solution.py:406
  (17 shorter events, 0.1 us)
Async XLA Ops:
  0.0 28.6 %collective-permute-start.1 = (f32[128,2048]{1,0:T(8,128)}, f32[128,2048]{1,0:T(8,128)S(1)}, u32[]{:S(2)}, u32[]{:S(2)}) collective-permute-start(f32[128,2048]{1,0:T(8,128)} %bitcast.4), channel_id=1, source_target_pairs={{2,0},{0,2},{3,1},{1,3},{6,4},{4,6},{7,5},{5,7},{10,8},{8,10},{11,... | collective-permute-start | bytes 3145736 | tf_op jit(solution)/shard_map/ppermute | solution.py:301
  2.9 1.3 %copy-start = (f32[1,1,2,64,2048]{4,3,2,1,0:T(8,128)S(1)}, f32[1,1,2,64,2048]{4,3,2,1,0:T(8,128)}, u32[]{:S(2)}) copy-start(f32[1,1,2,64,2048]{4,3,2,1,0:T(8,128)} %param.4) | copy-start | bytes 3145732
  4.2 8.4 %copy-start.1 = (f32[1,1,2,64,2048]{4,3,2,1,0:T(8,128)S(1)}, f32[1,1,2,64,2048]{4,3,2,1,0:T(8,128)}, u32[]{:S(2)}) copy-start(f32[1,1,2,64,2048]{4,3,2,1,0:T(8,128)} %param.4) | copy-start | bytes 3145732
  4.8 15.3 %collective-permute-start.3 = (f32[32,32,128]{2,1,0:T(8,128)S(1)}, f32[32,32,128]{2,1,0:T(8,128)S(1)}, u32[]{:S(2)}, u32[]{:S(2)}) collective-permute-start(f32[32,32,128]{2,1,0:T(8,128)S(1)} %get-tuple-element.21.refs_1_), channel_id=1, source_target_pairs={{0,4},{4,8},{8,12},{12,0},{1,5},{5,9},{9,13},{13,1},{2,6},{6,10},{... | collective-permute-start | bytes 1572872 | tf_op jit(solution)/shard_map/ppermute | solution.py:333
  6.4 14.3 %collective-permute-start.2 = (f32[32,32,128]{2,1,0:T(8,128)S(1)}, f32[32,32,128]{2,1,0:T(8,128)S(1)}, u32[]{:S(2)}, u32[]{:S(2)}) collective-permute-start(f32[32,32,128]{2,1,0:T(8,128)S(1)} %get-tuple-element.21.refs_1_), channel_id=1, source_target_pairs={{1,0},{0,1},{3,2},{2,3},{5,4},{4,5},{7,6},{6,7},{9,8},{8,9},{11,10... | collective-permute-start | bytes 1572872 | tf_op jit(solution)/shard_map/ppermute | solution.py:329
  7.9 4.7 %collective-permute-start = (f32[136,128]{1,0:T(8,128)S(1)}, f32[136,128]{1,0:T(8,128)S(1)}, u32[]{:S(2)}, u32[]{:S(2)}) collective-permute-start(f32[136,128]{1,0:T(8,128)S(1)} %get-tuple-element.36), channel_id=1, source_target_pairs={{16,0},{0,16},{17,1},{1,17},{18,2},{2,18},{19,3},{3,19},{20,4},{4,... | collective-permute-start | bytes 208904 | tf_op jit(solution)/shard_map/ppermute | solution.py:314
  14.1 1.2 %collective-permute-start.7 = (f32[8,128]{1,0:T(8,128)S(1)}, f32[8,128]{1,0:T(8,128)S(1)}, u32[]{:S(2)}, u32[]{:S(2)}) collective-permute-start(f32[8,128]{1,0:T(8,128)S(1)} %get-tuple-element.22.refs_1_), channel_id=1, source_target_pairs={{1,0},{0,1},{3,2},{2,3},{5,4},{4,5},{7,6},{6,7},{9,8},{8,9},{11,10... | collective-permute-start | bytes 12296 | tf_op jit(solution)/shard_map/ppermute | solution.py:336
  15.3 16.8 %collective-permute-start.8 = (f32[32,32,128]{2,1,0:T(8,128)S(1)}, f32[32,32,128]{2,1,0:T(8,128)S(1)}, u32[]{:S(2)}, u32[]{:S(2)}) collective-permute-start(f32[32,32,128]{2,1,0:T(8,128)S(1)} %after.4), channel_id=1, source_target_pairs={{8,0},{4,12},{9,1},{5,13},{10,2},{6,14},{11,3},{7,15},{24,16},{20,... | collective-permute-start | bytes 1572872 | tf_op jit(solution)/shard_map/ppermute | solution.py:336
  20.1 1.6 %collective-permute-start.4 = (f32[16,32,128]{2,1,0:T(8,128)S(1)}, f32[16,32,128]{2,1,0:T(8,128)S(1)}, u32[]{:S(2)}, u32[]{:S(2)}) collective-permute-start(f32[16,32,128]{2,1,0:T(8,128)S(1)} %get-tuple-element.23.refs_2_.refs_5_.refs_1_), channel_id=1, source_target_pairs={{1,0},{0,1},{3,2},{2,3},{5,4},{4,5},{7,6},{6,7},{9,8},{8,9},{11,10... | collective-permute-start | bytes 786440 | tf_op jit(solution)/shard_map/ppermute | solution.py:335
  20.2 1.9 %collective-permute-start.5 = (f32[16,32,128]{2,1,0:T(8,128)S(1)}, f32[16,32,128]{2,1,0:T(8,128)S(1)}, u32[]{:S(2)}, u32[]{:S(2)}) collective-permute-start(f32[16,32,128]{2,1,0:T(8,128)S(1)} %get-tuple-element.24.refs_3_.refs_6_.refs_2_), channel_id=1, source_target_pairs={{1,0},{0,1},{3,2},{2,3},{5,4},{4,5},{7,6},{6,7},{9,8},{8,9},{11,10... | collective-permute-start | bytes 786440 | tf_op jit(solution)/shard_map/ppermute | solution.py:335
  22.1 6.4 %collective-permute-start.6 = (f32[2,136,128]{2,1,0:T(8,128)S(1)}, f32[2,136,128]{2,1,0:T(8,128)S(1)}, u32[]{:S(2)}, u32[]{:S(2)}) collective-permute-start(f32[2,136,128]{2,1,0:T(8,128)S(1)} %after.3), channel_id=1, source_target_pairs={{2,1},{3,0},{0,3},{1,2},{6,5},{7,4},{4,7},{5,6},{10,9},{11,8},{8,1... | collective-permute-start | bytes 417800 | tf_op jit(solution)/shard_map/ppermute | solution.py:341
  32.1 3.9 %collective-permute-start.9 = (f32[32,32,128]{2,1,0:T(8,128)S(1)}, f32[32,32,128]{2,1,0:T(8,128)S(1)}, u32[]{:S(2)}, u32[]{:S(2)}) collective-permute-start(f32[32,32,128]{2,1,0:T(8,128)S(1)} %after.5.refs_5_), channel_id=1, source_target_pairs={{1,0},{0,1},{3,2},{2,3},{5,4},{4,5},{7,6},{6,7},{9,8},{8,9},{11,10... | collective-permute-start | bytes 1572872 | tf_op jit(solution)/shard_map/ppermute | solution.py:356
  32.9 6.4 %collective-permute-start.10 = (f32[32,128]{1,0:T(8,128)S(1)}, f32[32,128]{1,0:T(8,128)S(1)}, u32[]{:S(2)}, u32[]{:S(2)}) collective-permute-start(f32[32,128]{1,0:T(8,128)S(1)} %get-tuple-element.31), channel_id=1, source_target_pairs={{4,0},{8,4},{12,8},{0,12},{5,1},{9,5},{13,9},{1,13},{6,2},{10,6},{... | collective-permute-start | bytes 49160 | tf_op jit(solution)/shard_map/ppermute | solution.py:384
  36.7 2.8 %collective-permute-start.11 = (f32[32,128]{1,0:T(8,128)S(1)}, f32[32,128]{1,0:T(8,128)S(1)}, u32[]{:S(2)}, u32[]{:S(2)}) collective-permute-start(f32[32,128]{1,0:T(8,128)S(1)} %get-tuple-element.32), channel_id=1, source_target_pairs={{0,8},{12,4},{1,9},{13,5},{2,10},{14,6},{3,11},{15,7},{16,24},{28,... | collective-permute-start | bytes 49160 | tf_op jit(solution)/shard_map/ppermute | solution.py:384
  39.8 1.3 %collective-permute-start.12 = (f32[4,16,256]{2,1,0:T(8,128)S(1)}, f32[4,16,256]{2,1,0:T(8,128)S(1)}, u32[]{:S(2)}, u32[]{:S(2)}) collective-permute-start(f32[4,16,256]{2,1,0:T(8,128)S(1)} %get-tuple-element.34), channel_id=1, source_target_pairs={{1,0},{0,1},{3,2},{2,3},{5,4},{4,5},{7,6},{6,7},{9,8},{8,9},{11,10... | collective-permute-start | bytes 196616 | tf_op jit(solution)/shard_map/ppermute | solution.py:404

commit v23 on v20

--- a/solution.py
+++ b/solution.py
@@ -36,10 +36,11 @@
 
 def prepare(place, tensor, mine, again, turned, *, share):
     some = mine.shape[1]
-    turned[...] = tensor[...].T
+    columns = tensor.shape[1]
+    turned[:columns, :] = tensor[...].T
     start = place[1] * share
     for at in range(share):
-        rows = turned[pl.ds(start + at, some, stride=turned.shape[0] // some), :]
+        rows = turned[pl.ds(start + at, some, stride=columns // some), :]
         mine[at] = rows
         again[at] = rows
 
@@ -199,7 +200,7 @@
 
 def fold(place, own, other, ordered):
     unfold(by_sub(place, own, other, 0), ordered, 0)
-    back = ordered[0].T
+    back = ordered[0, : own.shape[1], :].T
     half = own.shape[0]
     return jnp.concatenate([back[:half], back[half:]], axis=1)
 
@@ -294,7 +295,7 @@
 
     tensors = [lax.ppermute(tensor, "orb", ring(nob, shift)) for shift in range(1, nob)]
     mine, again = call(
-        prepare, [((share, rows_aux, listed), F32)] * 2, [((columns, listed), F32)], 0, tensor, share=share
+        prepare, [((share, rows_aux, listed), F32)] * 2, [((columns + width, listed), F32)], 0, tensor, share=share
     )
     plan = shifts_of(naux)
     swap = ring(nsub, 1)
@@ -314,7 +315,7 @@
     acc, token = call(
         first,
         [((groups, rows_aux // 2 * share, 2 * listed), F32), ((8, 128), F32)],
-        [((groups * rows_aux // 2 * share, 2 * width), F32)],
+        [((groups * rows_aux // 2 * share + share, 2 * width), F32)],
         0,
         near,
         tensor,
@@ -336,7 +337,7 @@
     sides, token_late = call(
         second,
         [((2 * rows, depth), BF16), ((8, 128), F32)],
-        [((groups * rows_aux // 2 * share, 2 * width), F32)],
+        [((groups * rows_aux // 2 * share + share, 2 * width), F32)],
         work,
         near,
         acc,
@@ -352,7 +353,7 @@
     work = 8 * rows * depth * rows_aux
     wide = nt * rows_aux
     shape = ((rows_aux, 2 * wide), F32)
-    scratch = lambda count: ((count, wide, block_aux), F32)
+    scratch = lambda count: ((count, wide + 8, block_aux), F32)
     own_rows = 2 * (2 * count - 3) * rows_aux
     own, back, *backs = call(
         meet_own,
@@ -381,7 +382,7 @@
     (direct,) = call(
         meet_direct,
         [shape],
-        [((6 * rows_aux, depth), BF16), ((count, wide, block_aux), F32)],
+        [((6 * rows_aux, depth), BF16), scratch(count)],
         work * (2 * count),
         sides,
         mine,

time: 49.8 us -> 49.8 us (level)
  no operation moved by 1% of the time
where the time goes in v23:
time: 49.8 us; the launch traced here: 49.5 us
  waiting for transfers between devices  17.2 us (35%)
  starting transfers between devices  12.8 us (26%)
  blocking collectives  9.05 us (18%)
  Pallas kernels  6.97 us (14%)
  other arithmetic  2.07 us (4%)
  local copies, waits for them, and re-layouts  1.27 us (3%)
    all_to_all x1, blocking collectives, local(): lax.all_to_all(partial_chi.reshape(owners, nt * block_aux // owners, naux...  9.05 us
    pallas_call x8, Pallas kernels, call(): pl.pallas_call(here, out_shape=shapes, in_specs=[VMEM] * len(arguments),...  6.97 us
    ppermute x1, waiting for transfers between devices, local(): fars.append(lax.ppermute(late_near, ('orb', 'sub'), pairs))  6.16 us
    ppermute x2, starting transfers between devices, local(): lax.ppermute(back, 'aux', [(target, source) for source, target in pairs])  4.43 us
    ppermute x1, waiting for transfers between devices, local(): lax.ppermute(mine, 'aux', pairs)  3.53 us
    ppermute x1, waiting for transfers between devices, local(): lax.ppermute(small, 'tau', ring(nt, shift))  3.07 us
    ppermute x1, starting transfers between devices, local(): lax.ppermute(tensor, 'orb', ring(nob, shift))  2.94 us
    ppermute x1, waiting for transfers between devices, local(): lax.ppermute(after(again, lax.ppermute(token, 'sub', swap)), 'aux', plan[...  1.75 us
  transfers between devices with their start and end apart: 12, of which 8 were waited for; matrix products, arithmetic and copies ran while one was open for 3% of the time, Pallas kernels for 13%

profile of v23, /device:TPU:0, one launch (start us, length us, event | category | flops | bytes accessed | tf_op | source)
XLA Modules:
  0.0 49.5 jit_solution(16554493503008353622)
XLA Ops:
  0.0 2.9 %collective-permute-start.1 = (f32[128,2048]{1,0:T(8,128)}, f32[128,2048]{1,0:T(8,128)S(1)}, u32[]{:S(2)}, u32[]{:S(2)}) collective-permute-start(f32[128,2048]{1,0:T(8,128)} %bitcast.5), channel_id=1, source_target_pairs={{2,0},{0,2},{3,1},{1,3},{6,4},{4,6},{7,5},{5,7},{10,8},{8,10},{11,... | collective-permute-start | bytes 3145736 | tf_op jit(solution)/shard_map/ppermute | solution.py:296
  2.9 1.3 %copy-done = f32[1,1,2,64,2048]{4,3,2,1,0:T(8,128)S(1)} copy-done((f32[1,1,2,64,2048]{4,3,2,1,0:T(8,128)S(1)}, f32[1,1,2,64,2048]{4,3,2,1,0:T(8,128)}, u32[]{:S(2)}) %copy-start) | copy-done | bytes 1048600
  4.2 0.6 %prepare.1 = (f32[32,32,128]{2,1,0:T(8,128)S(1)}, f32[32,32,128]{2,1,0:T(8,128)S(1)}) custom-call(f32[128,2048]{1,0:T(8,128)S(1)} %bitcast.6), custom_call_target="tpu_custom_call" | custom-call | bytes 1048576 | tf_op jit(solution)/shard_map/prepare/pallas_call | solution.py:285
  4.8 1.6 %collective-permute-start.3 = (f32[32,32,128]{2,1,0:T(8,128)S(1)}, f32[32,32,128]{2,1,0:T(8,128)S(1)}, u32[]{:S(2)}, u32[]{:S(2)}) collective-permute-start(f32[32,32,128]{2,1,0:T(8,128)S(1)} %get-tuple-element.19.refs_1_), channel_id=1, source_target_pairs={{0,4},{4,8},{8,12},{12,0},{1,5},{5,9},{9,13},{13,1},{2,6},{6,10},{... | collective-permute-start | bytes 1572872 | tf_op jit(solution)/shard_map/ppermute | solution.py:328
  6.4 0.7 %convert_element_type.5 = f32[1,2]{1,0:T(1,128)S(1)} convert(s32[1,2]{1,0:T(1,128)} %param.7) | non-fusion elementwise | flops 2 | bytes 16 | tf_op jit(solution)/shard_map/convert_element_type | solution.py:306
  7.1 0.8 %fusion = (f32[1,136,128]{2,1,0:T(8,128)S(1)}, f32[136,128]{1,0:T(8,128)S(1)}) fusion(f32[1,2]{1,0:T(1,128)S(1)} %convert_element_type.5, f32[64,128]{1,0:T(8,128)} %param.6, f32[64,128]{1,0:T(8,128)} %param.5), kind=kLoop, calls=%fused_computation.4 | loop fusion | flops 69632 | bytes 204808 | tf_op jit(solution)/shard_map/stack | solution.py:309
  7.9 1.6 %collective-permute-start = (f32[136,128]{1,0:T(8,128)S(1)}, f32[136,128]{1,0:T(8,128)S(1)}, u32[]{:S(2)}, u32[]{:S(2)}) collective-permute-start(f32[136,128]{1,0:T(8,128)S(1)} %get-tuple-element.32), channel_id=1, source_target_pairs={{16,0},{0,16},{17,1},{1,17},{18,2},{2,18},{19,3},{3,19},{20,4},{4,... | collective-permute-start | bytes 208904 | tf_op jit(solution)/shard_map/ppermute | solution.py:309
  9.5 3.1 %collective-permute-done = f32[136,128]{1,0:T(8,128)S(1)} collective-permute-done((f32[136,128]{1,0:T(8,128)S(1)}, f32[136,128]{1,0:T(8,128)S(1)}, u32[]{:S(2)}, u32[]{:S(2)}) %collective-permute-start) | collective-permute-done | bytes 69664 | tf_op jit(solution)/shard_map/ppermute | solution.py:309
  12.6 1.5 %first.1 = (f32[4,512,256]{2,1,0:T(8,128)S(1)}, f32[8,128]{1,0:T(8,128)S(1)}) custom-call(f32[2,136,128]{2,1,0:T(8,128)S(1)} %pad_maximum_fusion.refs_0_, f32[128,2048]{1,0:T(8,128)S(1)} %bitcast.7), custom_call_target="tpu_custom_call" | custom-call | bytes 1187840 | tf_op jit(solution)/shard_map/first/pallas_call | solution.py:285
  14.1 0.1 collective-permute-start.7
  14.1 1.2 %collective-permute-done.7.refs_1_ = f32[8,128]{1,0:T(8,128)S(1)} collective-permute-done((f32[8,128]{1,0:T(8,128)S(1)}, f32[8,128]{1,0:T(8,128)S(1)}, u32[]{:S(2)}, u32[]{:S(2)}) %collective-permute-start.7) | collective-permute-done | bytes 4128 | tf_op jit(solution)/shard_map/ppermute | solution.py:331
  15.3 1.3 %collective-permute-start.8 = (f32[32,32,128]{2,1,0:T(8,128)S(1)}, f32[32,32,128]{2,1,0:T(8,128)S(1)}, u32[]{:S(2)}, u32[]{:S(2)}) collective-permute-start(f32[32,32,128]{2,1,0:T(8,128)S(1)} %after.4), channel_id=1, source_target_pairs={{8,0},{4,12},{9,1},{5,13},{10,2},{6,14},{11,3},{7,15},{24,16},{20,... | collective-permute-start | bytes 1572872 | tf_op jit(solution)/shard_map/ppermute | solution.py:331
  16.6 3.5 %collective-permute-done.3.refs_0_ = f32[32,32,128]{2,1,0:T(8,128)S(1)} collective-permute-done((f32[32,32,128]{2,1,0:T(8,128)S(1)}, f32[32,32,128]{2,1,0:T(8,128)S(1)}, u32[]{:S(2)}, u32[]{:S(2)}) %collective-permute-start.3) | collective-permute-done | bytes 524320 | tf_op jit(solution)/shard_map/ppermute | solution.py:328
  20.1 0.1 collective-permute-start.4
  20.2 0.5 %collective-permute-start.5 = (f32[16,32,128]{2,1,0:T(8,128)S(1)}, f32[16,32,128]{2,1,0:T(8,128)S(1)}, u32[]{:S(2)}, u32[]{:S(2)}) collective-permute-start(f32[16,32,128]{2,1,0:T(8,128)S(1)} %get-tuple-element.22.refs_3_.refs_6_.refs_2_), channel_id=1, source_target_pairs={{1,0},{0,1},{3,2},{2,3},{5,4},{4,5},{7,6},{6,7},{9,8},{8,9},{11,10... | collective-permute-start | bytes 786440 | tf_op jit(solution)/shard_map/ppermute | solution.py:330
  20.7 1.0 %collective-permute-done.4.refs_4_.refs_7_.refs_3_ = f32[16,32,128]{2,1,0:T(8,128)S(1)} collective-permute-done((f32[16,32,128]{2,1,0:T(8,128)S(1)}, f32[16,32,128]{2,1,0:T(8,128)S(1)}, u32[]{:S(2)}, u32[]{:S(2)}) %collective-permute-start.4) | collective-permute-done | bytes 262176 | tf_op jit(solution)/shard_map/ppermute | solution.py:330
  21.7 0.4 collective-permute-done.5.refs_5_.refs_8_.refs_4_
  22.1 0.3 collective-permute-start.6
  22.4 6.2 %collective-permute-done.6.refs_3_ = f32[2,136,128]{2,1,0:T(8,128)S(1)} collective-permute-done((f32[2,136,128]{2,1,0:T(8,128)S(1)}, f32[2,136,128]{2,1,0:T(8,128)S(1)}, u32[]{:S(2)}, u32[]{:S(2)}) %collective-permute-start.6) | collective-permute-done | bytes 139296 | tf_op jit(solution)/shard_map/ppermute | solution.py:336
  28.6 0.0 collective-permute-done.1.refs_2_
  28.6 1.7 %second.1 = (bf16[256,4096]{1,0:T(8,128)(2,1)S(1)}, f32[8,128]{1,0:T(8,128)S(1)}) custom-call(f32[2,136,128]{2,1,0:T(8,128)S(1)} %pad_maximum_fusion.refs_0_, f32[4,512,256]{2,1,0:T(8,128)S(1)} %get-tuple-element.18.refs_1_, f32[128,2048]{1,0:T(8,128)S(1)} %collective-permute-done.1.refs_2_, f32[2,136,128]{2,1,0:T(8,128)S(1)} %collective-permute-done.6.refs_3_, ...), custom_call_target="tpu_custom_call" | custom-call | flops 603979776 | bytes 4997120 | tf_op jit(solution)/shard_map/second/pallas_call | solution.py:285
  30.3 1.8 %collective-permute-done.8.refs_0_ = f32[32,32,128]{2,1,0:T(8,128)S(1)} collective-permute-done((f32[32,32,128]{2,1,0:T(8,128)S(1)}, f32[32,32,128]{2,1,0:T(8,128)S(1)}, u32[]{:S(2)}, u32[]{:S(2)}) %collective-permute-start.8) | collective-permute-done | bytes 524320 | tf_op jit(solution)/shard_map/ppermute | solution.py:331
  32.1 0.0 collective-permute-start.9
  32.1 0.8 %meet_own.1 = (bf16[192,4096]{1,0:T(8,128)(2,1)S(1)}, f32[32,64]{1,0:T(8,128)S(1)}, f32[32,128]{1,0:T(8,128)S(1)}) custom-call(bf16[256,4096]{1,0:T(8,128)(2,1)S(1)} %get-tuple-element.23.refs_0_, f32[16,32,128]{2,1,0:T(8,128)S(1)} %get-tuple-element.21.refs_2_.refs_5_.refs_1_, f32[16,32,128]{2,1,0:T(8,128)S(1)} %get-tuple-element.22.refs_3_.refs_6_.refs_2_, ...), custom_call_target="tpu_custom_call" | custom-call | flops 402653184 | bytes 5767168 | tf_op jit(solution)/shard_map/meet_own/pallas_call | solution.py:285
  32.9 3.1 %collective-permute-start.10 = (f32[32,128]{1,0:T(8,128)S(1)}, f32[32,128]{1,0:T(8,128)S(1)}, u32[]{:S(2)}, u32[]{:S(2)}) collective-permute-start(f32[32,128]{1,0:T(8,128)S(1)} %get-tuple-element.29), channel_id=1, source_target_pairs={{4,0},{8,4},{12,8},{0,12},{5,1},{9,5},{13,9},{1,13},{6,2},{10,6},{... | collective-permute-start | bytes 49160 | tf_op jit(solution)/shard_map/ppermute | solution.py:379
  36.0 0.7 %meet_back.1 = (bf16[64,4096]{1,0:T(8,128)(2,1)S(1)}, f32[32,128]{1,0:T(8,128)S(1)}) custom-call(bf16[256,4096]{1,0:T(8,128)(2,1)S(1)} %get-tuple-element.23.refs_0_, f32[32,64]{1,0:T(8,128)S(1)} %get-tuple-element.27.refs_1_, f32[32,32,128]{2,1,0:T(8,128)S(1)} %collective-permute-done.9.refs_2_), custom_call_target="tpu_custom_call" | custom-call | flops 134217728 | bytes 4726784 | tf_op jit(solution)/shard_map/meet_back/pallas_call | solution.py:285
  36.7 1.3 %collective-permute-start.11 = (f32[32,128]{1,0:T(8,128)S(1)}, f32[32,128]{1,0:T(8,128)S(1)}, u32[]{:S(2)}, u32[]{:S(2)}) collective-permute-start(f32[32,128]{1,0:T(8,128)S(1)} %get-tuple-element.30), channel_id=1, source_target_pairs={{0,8},{12,4},{1,9},{13,5},{2,10},{14,6},{3,11},{15,7},{16,24},{28,... | collective-permute-start | bytes 49160 | tf_op jit(solution)/shard_map/ppermute | solution.py:379
  38.1 1.2 %meet_direct.1.refs_0_ = f32[2,64,256]{2,1,0:T(8,128)S(1)} custom-call(bf16[256,4096]{1,0:T(8,128)(2,1)S(1)} %get-tuple-element.23.refs_0_, f32[32,32,128]{2,1,0:T(8,128)S(1)} %get-tuple-element.19.refs_1_, f32[32,32,128]{2,1,0:T(8,128)S(1)} %collective-permute-done.2.refs_1_.refs_4_.refs_2_, bf16[192,4096]{1,0:T(8,128)(2,1)S(1)} %get-tuple-element.26.refs_3_, ...), custom_call_target="tpu_custom_call" | custom-call | flops 805306368 | bytes 9437184 | tf_op jit(solution)/shard_map/meet_direct/pallas_call | solution.py:285
  39.3 0.2 collective-permute-done.11.refs_2_
  39.5 0.3 complete.1
  39.8 9.1 %all_to_all.5 = f32[8,16,256]{2,1,0:T(8,128)S(1)} all-to-all(f32[8,16,256]{2,1,0:T(8,128)S(1)} %bitcast.8), channel_id=1, replica_groups=mesh['tau'=2,'aux'=4,'orb'=2,'sub'=2] {'tau','orb','sub'}, dimensions={0} | all-to-all | bytes 262144 | tf_op jit(solution)/shard_map/all_to_all | solution.py:397
  48.9 0.6 %broadcast_multiply_fusion = f32[16,256]{1,0:T(8,128)} fusion(f32[16,256]{1,0:T(8,128)S(1)} %reduce_sum.9), kind=kLoop, calls=%fused_computation.3 | loop fusion | flops 4096 | bytes 32768 | tf_op jit(solution)/shard_map/mul | solution.py:404
  (14 shorter events, 0.1 us)
Async XLA Ops:
  0.0 28.6 %collective-permute-start.1 = (f32[128,2048]{1,0:T(8,128)}, f32[128,2048]{1,0:T(8,128)S(1)}, u32[]{:S(2)}, u32[]{:S(2)}) collective-permute-start(f32[128,2048]{1,0:T(8,128)} %bitcast.5), channel_id=1, source_target_pairs={{2,0},{0,2},{3,1},{1,3},{6,4},{4,6},{7,5},{5,7},{10,8},{8,10},{11,... | collective-permute-start | bytes 3145736 | tf_op jit(solution)/shard_map/ppermute | solution.py:296
  2.9 1.3 %copy-start = (f32[1,1,2,64,2048]{4,3,2,1,0:T(8,128)S(1)}, f32[1,1,2,64,2048]{4,3,2,1,0:T(8,128)}, u32[]{:S(2)}) copy-start(f32[1,1,2,64,2048]{4,3,2,1,0:T(8,128)} %param.4) | copy-start | bytes 3145732
  4.2 8.4 %copy-start.1 = (f32[1,1,2,64,2048]{4,3,2,1,0:T(8,128)S(1)}, f32[1,1,2,64,2048]{4,3,2,1,0:T(8,128)}, u32[]{:S(2)}) copy-start(f32[1,1,2,64,2048]{4,3,2,1,0:T(8,128)} %param.4) | copy-start | bytes 3145732
  4.8 15.3 %collective-permute-start.3 = (f32[32,32,128]{2,1,0:T(8,128)S(1)}, f32[32,32,128]{2,1,0:T(8,128)S(1)}, u32[]{:S(2)}, u32[]{:S(2)}) collective-permute-start(f32[32,32,128]{2,1,0:T(8,128)S(1)} %get-tuple-element.19.refs_1_), channel_id=1, source_target_pairs={{0,4},{4,8},{8,12},{12,0},{1,5},{5,9},{9,13},{13,1},{2,6},{6,10},{... | collective-permute-start | bytes 1572872 | tf_op jit(solution)/shard_map/ppermute | solution.py:328
  6.4 14.3 %collective-permute-start.2 = (f32[32,32,128]{2,1,0:T(8,128)S(1)}, f32[32,32,128]{2,1,0:T(8,128)S(1)}, u32[]{:S(2)}, u32[]{:S(2)}) collective-permute-start(f32[32,32,128]{2,1,0:T(8,128)S(1)} %get-tuple-element.19.refs_1_), channel_id=1, source_target_pairs={{1,0},{0,1},{3,2},{2,3},{5,4},{4,5},{7,6},{6,7},{9,8},{8,9},{11,10... | collective-permute-start | bytes 1572872 | tf_op jit(solution)/shard_map/ppermute | solution.py:324
  7.9 4.7 %collective-permute-start = (f32[136,128]{1,0:T(8,128)S(1)}, f32[136,128]{1,0:T(8,128)S(1)}, u32[]{:S(2)}, u32[]{:S(2)}) collective-permute-start(f32[136,128]{1,0:T(8,128)S(1)} %get-tuple-element.32), channel_id=1, source_target_pairs={{16,0},{0,16},{17,1},{1,17},{18,2},{2,18},{19,3},{3,19},{20,4},{4,... | collective-permute-start | bytes 208904 | tf_op jit(solution)/shard_map/ppermute | solution.py:309
  14.1 1.2 %collective-permute-start.7 = (f32[8,128]{1,0:T(8,128)S(1)}, f32[8,128]{1,0:T(8,128)S(1)}, u32[]{:S(2)}, u32[]{:S(2)}) collective-permute-start(f32[8,128]{1,0:T(8,128)S(1)} %get-tuple-element.20.refs_1_), channel_id=1, source_target_pairs={{1,0},{0,1},{3,2},{2,3},{5,4},{4,5},{7,6},{6,7},{9,8},{8,9},{11,10... | collective-permute-start | bytes 12296 | tf_op jit(solution)/shard_map/ppermute | solution.py:331
  15.3 16.8 %collective-permute-start.8 = (f32[32,32,128]{2,1,0:T(8,128)S(1)}, f32[32,32,128]{2,1,0:T(8,128)S(1)}, u32[]{:S(2)}, u32[]{:S(2)}) collective-permute-start(f32[32,32,128]{2,1,0:T(8,128)S(1)} %after.4), channel_id=1, source_target_pairs={{8,0},{4,12},{9,1},{5,13},{10,2},{6,14},{11,3},{7,15},{24,16},{20,... | collective-permute-start | bytes 1572872 | tf_op jit(solution)/shard_map/ppermute | solution.py:331
  20.1 1.6 %collective-permute-start.4 = (f32[16,32,128]{2,1,0:T(8,128)S(1)}, f32[16,32,128]{2,1,0:T(8,128)S(1)}, u32[]{:S(2)}, u32[]{:S(2)}) collective-permute-start(f32[16,32,128]{2,1,0:T(8,128)S(1)} %get-tuple-element.21.refs_2_.refs_5_.refs_1_), channel_id=1, source_target_pairs={{1,0},{0,1},{3,2},{2,3},{5,4},{4,5},{7,6},{6,7},{9,8},{8,9},{11,10... | collective-permute-start | bytes 786440 | tf_op jit(solution)/shard_map/ppermute | solution.py:330
  20.2 1.9 %collective-permute-start.5 = (f32[16,32,128]{2,1,0:T(8,128)S(1)}, f32[16,32,128]{2,1,0:T(8,128)S(1)}, u32[]{:S(2)}, u32[]{:S(2)}) collective-permute-start(f32[16,32,128]{2,1,0:T(8,128)S(1)} %get-tuple-element.22.refs_3_.refs_6_.refs_2_), channel_id=1, source_target_pairs={{1,0},{0,1},{3,2},{2,3},{5,4},{4,5},{7,6},{6,7},{9,8},{8,9},{11,10... | collective-permute-start | bytes 786440 | tf_op jit(solution)/shard_map/ppermute | solution.py:330
  22.1 6.4 %collective-permute-start.6 = (f32[2,136,128]{2,1,0:T(8,128)S(1)}, f32[2,136,128]{2,1,0:T(8,128)S(1)}, u32[]{:S(2)}, u32[]{:S(2)}) collective-permute-start(f32[2,136,128]{2,1,0:T(8,128)S(1)} %after.3), channel_id=1, source_target_pairs={{2,1},{3,0},{0,3},{1,2},{6,5},{7,4},{4,7},{5,6},{10,9},{11,8},{8,1... | collective-permute-start | bytes 417800 | tf_op jit(solution)/shard_map/ppermute | solution.py:336
  32.1 3.9 %collective-permute-start.9 = (f32[32,32,128]{2,1,0:T(8,128)S(1)}, f32[32,32,128]{2,1,0:T(8,128)S(1)}, u32[]{:S(2)}, u32[]{:S(2)}) collective-permute-start(f32[32,32,128]{2,1,0:T(8,128)S(1)} %after.5.refs_5_), channel_id=1, source_target_pairs={{1,0},{0,1},{3,2},{2,3},{5,4},{4,5},{7,6},{6,7},{9,8},{8,9},{11,10... | collective-permute-start | bytes 1572872 | tf_op jit(solution)/shard_map/ppermute | solution.py:351
  32.9 6.4 %collective-permute-start.10 = (f32[32,128]{1,0:T(8,128)S(1)}, f32[32,128]{1,0:T(8,128)S(1)}, u32[]{:S(2)}, u32[]{:S(2)}) collective-permute-start(f32[32,128]{1,0:T(8,128)S(1)} %get-tuple-element.29), channel_id=1, source_target_pairs={{4,0},{8,4},{12,8},{0,12},{5,1},{9,5},{13,9},{1,13},{6,2},{10,6},{... | collective-permute-start | bytes 49160 | tf_op jit(solution)/shard_map/ppermute | solution.py:379
  36.7 2.8 %collective-permute-start.11 = (f32[32,128]{1,0:T(8,128)S(1)}, f32[32,128]{1,0:T(8,128)S(1)}, u32[]{:S(2)}, u32[]{:S(2)}) collective-permute-start(f32[32,128]{1,0:T(8,128)S(1)} %get-tuple-element.30), channel_id=1, source_target_pairs={{0,8},{12,4},{1,9},{13,5},{2,10},{14,6},{3,11},{15,7},{16,24},{28,... | collective-permute-start | bytes 49160 | tf_op jit(solution)/shard_map/ppermute | solution.py:379

commit v24 on v23

--- a/solution.py
+++ b/solution.py
@@ -328,7 +328,7 @@
             halve, [((share // 2, rows_aux, listed), F32)] * 2, [], 0, lax.ppermute(mine, "aux", pairs), token
         )
         early += [*parts, *(lax.ppermute(part, "sub", swap) for part in parts)]
-    last = lax.ppermute(after(again, lax.ppermute(token, "sub", swap)), "aux", plan[-1])
+    last = lax.ppermute(after(again, token), "aux", plan[-1])
     fars = []
     late_near = after(near, *early)
     for shift in range(1, nob):

time: 49.8 us -> 56.5 us (1.13)
  starting transfers between devices: 12.8 us -> 21.1 us
  blocking collectives: 9.05 us -> 8.12 us
  waiting for transfers between devices: 17.2 us -> 16.5 us
    ppermute x2, starting transfers between devices: 4.43 us -> 12.8 us  [local(): lax.ppermute(back, 'aux', [(target, source) for source, target in pairs])]
    ppermute x2 -> x1, waiting for transfers between devices: 2.91 us -> 1.03 us  [local(): last = lax.ppermute(after(again, token), 'aux', plan[-1])]
    ppermute x1, waiting for transfers between devices: 3.53 us -> 4.84 us  [local(): lax.ppermute(mine, 'aux', pairs)]
    all_to_all x1, blocking collectives: 9.05 us -> 8.12 us  [local(): lax.all_to_all(partial_chi.reshape(owners, nt * block_aux // owners, naux...]
    ppermute x2 -> x1, starting transfers between devices: 1.35 us -> 1.29 us  [local(): last = lax.ppermute(after(again, token), 'aux', plan[-1])]
  transfers between devices with their start and end apart: 12 -> 11, of which waited for: 8 -> 7; matrix products, arithmetic and copies ran while one was open for 3% -> 3% of each run, Pallas kernels for 13% -> 12%
where the time goes in v24:
time: 56.5 us; the launch traced here: 56.2 us
  starting transfers between devices  21.1 us (37%)
  waiting for transfers between devices  16.5 us (29%)
  blocking collectives  8.12 us (14%)
  Pallas kernels  6.97 us (12%)
  other arithmetic  2.07 us (4%)
  local copies, waits for them, and re-layouts  1.27 us (2%)
    ppermute x2, starting transfers between devices, local(): lax.ppermute(back, 'aux', [(target, source) for source, target in pairs])  12.8 us
    all_to_all x1, blocking collectives, local(): lax.all_to_all(partial_chi.reshape(owners, nt * block_aux // owners, naux...  8.12 us
    pallas_call x8, Pallas kernels, call(): pl.pallas_call(here, out_shape=shapes, in_specs=[VMEM] * len(arguments),...  6.97 us
    ppermute x1, waiting for transfers between devices, local(): fars.append(lax.ppermute(late_near, ('orb', 'sub'), pairs))  6.06 us
    ppermute x1, waiting for transfers between devices, local(): lax.ppermute(mine, 'aux', pairs)  4.84 us
    ppermute x1, waiting for transfers between devices, local(): lax.ppermute(small, 'tau', ring(nt, shift))  3.07 us
    ppermute x1, starting transfers between devices, local(): lax.ppermute(tensor, 'orb', ring(nob, shift))  2.94 us
    ppermute x1, starting transfers between devices, local(): lax.ppermute(mine, 'aux', pairs)  1.63 us
  transfers between devices with their start and end apart: 11, of which 7 were waited for; matrix products, arithmetic and copies ran while one was open for 3% of the time, Pallas kernels for 12%

profile of v24, /device:TPU:0, one launch (start us, length us, event | category | flops | bytes accessed | tf_op | source)
XLA Modules:
  0.0 56.2 jit_solution(6018188543369406930)
XLA Ops:
  0.0 2.9 %collective-permute-start.1 = (f32[128,2048]{1,0:T(8,128)}, f32[128,2048]{1,0:T(8,128)S(1)}, u32[]{:S(2)}, u32[]{:S(2)}) collective-permute-start(f32[128,2048]{1,0:T(8,128)} %bitcast.5), channel_id=1, source_target_pairs={{2,0},{0,2},{3,1},{1,3},{6,4},{4,6},{7,5},{5,7},{10,8},{8,10},{11,... | collective-permute-start | bytes 3145736 | tf_op jit(solution)/shard_map/ppermute | solution.py:296
  2.9 1.3 %copy-done = f32[1,1,2,64,2048]{4,3,2,1,0:T(8,128)S(1)} copy-done((f32[1,1,2,64,2048]{4,3,2,1,0:T(8,128)S(1)}, f32[1,1,2,64,2048]{4,3,2,1,0:T(8,128)}, u32[]{:S(2)}) %copy-start) | copy-done | bytes 1048600
  4.2 0.6 %prepare.1 = (f32[32,32,128]{2,1,0:T(8,128)S(1)}, f32[32,32,128]{2,1,0:T(8,128)S(1)}) custom-call(f32[128,2048]{1,0:T(8,128)S(1)} %bitcast.6), custom_call_target="tpu_custom_call" | custom-call | bytes 1048576 | tf_op jit(solution)/shard_map/prepare/pallas_call | solution.py:285
  4.8 1.6 %collective-permute-start.3 = (f32[32,32,128]{2,1,0:T(8,128)S(1)}, f32[32,32,128]{2,1,0:T(8,128)S(1)}, u32[]{:S(2)}, u32[]{:S(2)}) collective-permute-start(f32[32,32,128]{2,1,0:T(8,128)S(1)} %get-tuple-element.19.refs_1_), channel_id=1, source_target_pairs={{0,4},{4,8},{8,12},{12,0},{1,5},{5,9},{9,13},{13,1},{2,6},{6,10},{... | collective-permute-start | bytes 1572872 | tf_op jit(solution)/shard_map/ppermute | solution.py:328
  6.4 0.7 %convert_element_type.5 = f32[1,2]{1,0:T(1,128)S(1)} convert(s32[1,2]{1,0:T(1,128)} %param.7) | non-fusion elementwise | flops 2 | bytes 16 | tf_op jit(solution)/shard_map/convert_element_type | solution.py:306
  7.1 0.8 %fusion = (f32[1,136,128]{2,1,0:T(8,128)S(1)}, f32[136,128]{1,0:T(8,128)S(1)}) fusion(f32[1,2]{1,0:T(1,128)S(1)} %convert_element_type.5, f32[64,128]{1,0:T(8,128)} %param.6, f32[64,128]{1,0:T(8,128)} %param.5), kind=kLoop, calls=%fused_computation.4 | loop fusion | flops 69632 | bytes 204808 | tf_op jit(solution)/shard_map/stack | solution.py:309
  7.9 1.6 %collective-permute-start = (f32[136,128]{1,0:T(8,128)S(1)}, f32[136,128]{1,0:T(8,128)S(1)}, u32[]{:S(2)}, u32[]{:S(2)}) collective-permute-start(f32[136,128]{1,0:T(8,128)S(1)} %get-tuple-element.32), channel_id=1, source_target_pairs={{16,0},{0,16},{17,1},{1,17},{18,2},{2,18},{19,3},{3,19},{20,4},{4,... | collective-permute-start | bytes 208904 | tf_op jit(solution)/shard_map/ppermute | solution.py:309
  9.5 3.1 %collective-permute-done = f32[136,128]{1,0:T(8,128)S(1)} collective-permute-done((f32[136,128]{1,0:T(8,128)S(1)}, f32[136,128]{1,0:T(8,128)S(1)}, u32[]{:S(2)}, u32[]{:S(2)}) %collective-permute-start) | collective-permute-done | bytes 69664 | tf_op jit(solution)/shard_map/ppermute | solution.py:309
  12.6 1.5 %first.1 = (f32[4,512,256]{2,1,0:T(8,128)S(1)}, f32[8,128]{1,0:T(8,128)S(1)}) custom-call(f32[2,136,128]{2,1,0:T(8,128)S(1)} %pad_maximum_fusion.refs_0_, f32[128,2048]{1,0:T(8,128)S(1)} %bitcast.7), custom_call_target="tpu_custom_call" | custom-call | bytes 1187840 | tf_op jit(solution)/shard_map/first/pallas_call | solution.py:285
  14.1 1.3 %collective-permute-start.7 = (f32[32,32,128]{2,1,0:T(8,128)S(1)}, f32[32,32,128]{2,1,0:T(8,128)S(1)}, u32[]{:S(2)}, u32[]{:S(2)}) collective-permute-start(f32[32,32,128]{2,1,0:T(8,128)S(1)} %after.4), channel_id=1, source_target_pairs={{8,0},{4,12},{9,1},{5,13},{10,2},{6,14},{11,3},{7,15},{24,16},{20,... | collective-permute-start | bytes 1572872 | tf_op jit(solution)/shard_map/ppermute | solution.py:331
  15.4 4.8 %collective-permute-done.3.refs_0_ = f32[32,32,128]{2,1,0:T(8,128)S(1)} collective-permute-done((f32[32,32,128]{2,1,0:T(8,128)S(1)}, f32[32,32,128]{2,1,0:T(8,128)S(1)}, u32[]{:S(2)}, u32[]{:S(2)}) %collective-permute-start.3) | collective-permute-done | bytes 524320 | tf_op jit(solution)/shard_map/ppermute | solution.py:328
  20.2 0.1 collective-permute-start.4
  20.3 0.5 collective-permute-start.5
  20.8 0.0 collective-permute-done.2.refs_1_.refs_4_.refs_2_
  20.8 1.0 %collective-permute-done.4.refs_4_.refs_7_.refs_3_ = f32[16,32,128]{2,1,0:T(8,128)S(1)} collective-permute-done((f32[16,32,128]{2,1,0:T(8,128)S(1)}, f32[16,32,128]{2,1,0:T(8,128)S(1)}, u32[]{:S(2)}, u32[]{:S(2)}) %collective-permute-start.4) | collective-permute-done | bytes 262176 | tf_op jit(solution)/shard_map/ppermute | solution.py:330
  21.8 0.4 collective-permute-done.5.refs_5_.refs_8_.refs_4_
  22.2 0.3 collective-permute-start.6
  22.5 6.1 %collective-permute-done.6.refs_3_ = f32[2,136,128]{2,1,0:T(8,128)S(1)} collective-permute-done((f32[2,136,128]{2,1,0:T(8,128)S(1)}, f32[2,136,128]{2,1,0:T(8,128)S(1)}, u32[]{:S(2)}, u32[]{:S(2)}) %collective-permute-start.6) | collective-permute-done | bytes 139296 | tf_op jit(solution)/shard_map/ppermute | solution.py:336
  28.6 0.0 collective-permute-done.1.refs_2_
  28.6 1.7 %second.1 = (bf16[256,4096]{1,0:T(8,128)(2,1)S(1)}, f32[8,128]{1,0:T(8,128)S(1)}) custom-call(f32[2,136,128]{2,1,0:T(8,128)S(1)} %pad_maximum_fusion.refs_0_, f32[4,512,256]{2,1,0:T(8,128)S(1)} %get-tuple-element.18.refs_1_, f32[128,2048]{1,0:T(8,128)S(1)} %collective-permute-done.1.refs_2_, f32[2,136,128]{2,1,0:T(8,128)S(1)} %collective-permute-done.6.refs_3_, ...), custom_call_target="tpu_custom_call" | custom-call | flops 603979776 | bytes 4997120 | tf_op jit(solution)/shard_map/second/pallas_call | solution.py:285
  30.3 1.0 %collective-permute-done.7.refs_0_ = f32[32,32,128]{2,1,0:T(8,128)S(1)} collective-permute-done((f32[32,32,128]{2,1,0:T(8,128)S(1)}, f32[32,32,128]{2,1,0:T(8,128)S(1)}, u32[]{:S(2)}, u32[]{:S(2)}) %collective-permute-start.7) | collective-permute-done | bytes 524320 | tf_op jit(solution)/shard_map/ppermute | solution.py:331
  31.3 0.0 collective-permute-start.8
  31.3 0.8 %meet_own.1 = (bf16[192,4096]{1,0:T(8,128)(2,1)S(1)}, f32[32,64]{1,0:T(8,128)S(1)}, f32[32,128]{1,0:T(8,128)S(1)}) custom-call(bf16[256,4096]{1,0:T(8,128)(2,1)S(1)} %get-tuple-element.23.refs_0_, f32[16,32,128]{2,1,0:T(8,128)S(1)} %get-tuple-element.21.refs_2_.refs_5_.refs_1_, f32[16,32,128]{2,1,0:T(8,128)S(1)} %get-tuple-element.22.refs_3_.refs_6_.refs_2_, ...), custom_call_target="tpu_custom_call" | custom-call | flops 402653184 | bytes 5767168 | tf_op jit(solution)/shard_map/meet_own/pallas_call | solution.py:285
  32.2 11.5 %collective-permute-start.9 = (f32[32,128]{1,0:T(8,128)S(1)}, f32[32,128]{1,0:T(8,128)S(1)}, u32[]{:S(2)}, u32[]{:S(2)}) collective-permute-start(f32[32,128]{1,0:T(8,128)S(1)} %get-tuple-element.29), channel_id=1, source_target_pairs={{4,0},{8,4},{12,8},{0,12},{5,1},{9,5},{13,9},{1,13},{6,2},{10,6},{... | collective-permute-start | bytes 49160 | tf_op jit(solution)/shard_map/ppermute | solution.py:379
  43.6 0.7 %meet_back.1 = (bf16[64,4096]{1,0:T(8,128)(2,1)S(1)}, f32[32,128]{1,0:T(8,128)S(1)}) custom-call(bf16[256,4096]{1,0:T(8,128)(2,1)S(1)} %get-tuple-element.23.refs_0_, f32[32,64]{1,0:T(8,128)S(1)} %get-tuple-element.27.refs_1_, f32[32,32,128]{2,1,0:T(8,128)S(1)} %collective-permute-done.8.refs_2_), custom_call_target="tpu_custom_call" | custom-call | flops 134217728 | bytes 4726784 | tf_op jit(solution)/shard_map/meet_back/pallas_call | solution.py:285
  44.4 1.3 %collective-permute-start.10 = (f32[32,128]{1,0:T(8,128)S(1)}, f32[32,128]{1,0:T(8,128)S(1)}, u32[]{:S(2)}, u32[]{:S(2)}) collective-permute-start(f32[32,128]{1,0:T(8,128)S(1)} %get-tuple-element.30), channel_id=1, source_target_pairs={{0,8},{12,4},{1,9},{13,5},{2,10},{14,6},{3,11},{15,7},{16,24},{28,... | collective-permute-start | bytes 49160 | tf_op jit(solution)/shard_map/ppermute | solution.py:379
  45.7 1.2 %meet_direct.1.refs_0_ = f32[2,64,256]{2,1,0:T(8,128)S(1)} custom-call(bf16[256,4096]{1,0:T(8,128)(2,1)S(1)} %get-tuple-element.23.refs_0_, f32[32,32,128]{2,1,0:T(8,128)S(1)} %get-tuple-element.19.refs_1_, f32[32,32,128]{2,1,0:T(8,128)S(1)} %collective-permute-done.2.refs_1_.refs_4_.refs_2_, bf16[192,4096]{1,0:T(8,128)(2,1)S(1)} %get-tuple-element.26.refs_3_, ...), custom_call_target="tpu_custom_call" | custom-call | flops 805306368 | bytes 9437184 | tf_op jit(solution)/shard_map/meet_direct/pallas_call | solution.py:285
  47.0 0.0 collective-permute-done.9.refs_1_
  47.0 0.2 collective-permute-done.10.refs_2_
  47.1 0.3 complete.1
  47.5 8.1 %all_to_all.5 = f32[8,16,256]{2,1,0:T(8,128)S(1)} all-to-all(f32[8,16,256]{2,1,0:T(8,128)S(1)} %bitcast.8), channel_id=1, replica_groups=mesh['tau'=2,'aux'=4,'orb'=2,'sub'=2] {'tau','orb','sub'}, dimensions={0} | all-to-all | bytes 262144 | tf_op jit(solution)/shard_map/all_to_all | solution.py:397
  55.6 0.6 %broadcast_multiply_fusion = f32[16,256]{1,0:T(8,128)} fusion(f32[16,256]{1,0:T(8,128)S(1)} %reduce_sum.9), kind=kLoop, calls=%fused_computation.3 | loop fusion | flops 4096 | bytes 32768 | tf_op jit(solution)/shard_map/mul | solution.py:404
  (12 shorter events, 0.1 us)
Async XLA Ops:
  0.0 28.6 %collective-permute-start.1 = (f32[128,2048]{1,0:T(8,128)}, f32[128,2048]{1,0:T(8,128)S(1)}, u32[]{:S(2)}, u32[]{:S(2)}) collective-permute-start(f32[128,2048]{1,0:T(8,128)} %bitcast.5), channel_id=1, source_target_pairs={{2,0},{0,2},{3,1},{1,3},{6,4},{4,6},{7,5},{5,7},{10,8},{8,10},{11,... | collective-permute-start | bytes 3145736 | tf_op jit(solution)/shard_map/ppermute | solution.py:296
  2.9 1.3 %copy-start = (f32[1,1,2,64,2048]{4,3,2,1,0:T(8,128)S(1)}, f32[1,1,2,64,2048]{4,3,2,1,0:T(8,128)}, u32[]{:S(2)}) copy-start(f32[1,1,2,64,2048]{4,3,2,1,0:T(8,128)} %param.4) | copy-start | bytes 3145732
  4.2 8.4 %copy-start.1 = (f32[1,1,2,64,2048]{4,3,2,1,0:T(8,128)S(1)}, f32[1,1,2,64,2048]{4,3,2,1,0:T(8,128)}, u32[]{:S(2)}) copy-start(f32[1,1,2,64,2048]{4,3,2,1,0:T(8,128)} %param.4) | copy-start | bytes 3145732
  4.8 15.4 %collective-permute-start.3 = (f32[32,32,128]{2,1,0:T(8,128)S(1)}, f32[32,32,128]{2,1,0:T(8,128)S(1)}, u32[]{:S(2)}, u32[]{:S(2)}) collective-permute-start(f32[32,32,128]{2,1,0:T(8,128)S(1)} %get-tuple-element.19.refs_1_), channel_id=1, source_target_pairs={{0,4},{4,8},{8,12},{12,0},{1,5},{5,9},{9,13},{13,1},{2,6},{6,10},{... | collective-permute-start | bytes 1572872 | tf_op jit(solution)/shard_map/ppermute | solution.py:328
  6.4 14.4 %collective-permute-start.2 = (f32[32,32,128]{2,1,0:T(8,128)S(1)}, f32[32,32,128]{2,1,0:T(8,128)S(1)}, u32[]{:S(2)}, u32[]{:S(2)}) collective-permute-start(f32[32,32,128]{2,1,0:T(8,128)S(1)} %get-tuple-element.19.refs_1_), channel_id=1, source_target_pairs={{1,0},{0,1},{3,2},{2,3},{5,4},{4,5},{7,6},{6,7},{9,8},{8,9},{11,10... | collective-permute-start | bytes 1572872 | tf_op jit(solution)/shard_map/ppermute | solution.py:324
  7.9 4.7 %collective-permute-start = (f32[136,128]{1,0:T(8,128)S(1)}, f32[136,128]{1,0:T(8,128)S(1)}, u32[]{:S(2)}, u32[]{:S(2)}) collective-permute-start(f32[136,128]{1,0:T(8,128)S(1)} %get-tuple-element.32), channel_id=1, source_target_pairs={{16,0},{0,16},{17,1},{1,17},{18,2},{2,18},{19,3},{3,19},{20,4},{4,... | collective-permute-start | bytes 208904 | tf_op jit(solution)/shard_map/ppermute | solution.py:309
  14.1 17.3 %collective-permute-start.7 = (f32[32,32,128]{2,1,0:T(8,128)S(1)}, f32[32,32,128]{2,1,0:T(8,128)S(1)}, u32[]{:S(2)}, u32[]{:S(2)}) collective-permute-start(f32[32,32,128]{2,1,0:T(8,128)S(1)} %after.4), channel_id=1, source_target_pairs={{8,0},{4,12},{9,1},{5,13},{10,2},{6,14},{11,3},{7,15},{24,16},{20,... | collective-permute-start | bytes 1572872 | tf_op jit(solution)/shard_map/ppermute | solution.py:331
  20.2 1.6 %collective-permute-start.4 = (f32[16,32,128]{2,1,0:T(8,128)S(1)}, f32[16,32,128]{2,1,0:T(8,128)S(1)}, u32[]{:S(2)}, u32[]{:S(2)}) collective-permute-start(f32[16,32,128]{2,1,0:T(8,128)S(1)} %get-tuple-element.21.refs_2_.refs_5_.refs_1_), channel_id=1, source_target_pairs={{1,0},{0,1},{3,2},{2,3},{5,4},{4,5},{7,6},{6,7},{9,8},{8,9},{11,10... | collective-permute-start | bytes 786440 | tf_op jit(solution)/shard_map/ppermute | solution.py:330
  20.3 1.9 %collective-permute-start.5 = (f32[16,32,128]{2,1,0:T(8,128)S(1)}, f32[16,32,128]{2,1,0:T(8,128)S(1)}, u32[]{:S(2)}, u32[]{:S(2)}) collective-permute-start(f32[16,32,128]{2,1,0:T(8,128)S(1)} %get-tuple-element.22.refs_3_.refs_6_.refs_2_), channel_id=1, source_target_pairs={{1,0},{0,1},{3,2},{2,3},{5,4},{4,5},{7,6},{6,7},{9,8},{8,9},{11,10... | collective-permute-start | bytes 786440 | tf_op jit(solution)/shard_map/ppermute | solution.py:330
  22.2 6.3 %collective-permute-start.6 = (f32[2,136,128]{2,1,0:T(8,128)S(1)}, f32[2,136,128]{2,1,0:T(8,128)S(1)}, u32[]{:S(2)}, u32[]{:S(2)}) collective-permute-start(f32[2,136,128]{2,1,0:T(8,128)S(1)} %after.3), channel_id=1, source_target_pairs={{2,1},{3,0},{0,3},{1,2},{6,5},{7,4},{4,7},{5,6},{10,9},{11,8},{8,1... | collective-permute-start | bytes 417800 | tf_op jit(solution)/shard_map/ppermute | solution.py:336
  31.3 12.3 %collective-permute-start.8 = (f32[32,32,128]{2,1,0:T(8,128)S(1)}, f32[32,32,128]{2,1,0:T(8,128)S(1)}, u32[]{:S(2)}, u32[]{:S(2)}) collective-permute-start(f32[32,32,128]{2,1,0:T(8,128)S(1)} %after.5.refs_5_), channel_id=1, source_target_pairs={{1,0},{0,1},{3,2},{2,3},{5,4},{4,5},{7,6},{6,7},{9,8},{8,9},{11,10... | collective-permute-start | bytes 1572872 | tf_op jit(solution)/shard_map/ppermute | solution.py:351
  32.2 14.8 %collective-permute-start.9 = (f32[32,128]{1,0:T(8,128)S(1)}, f32[32,128]{1,0:T(8,128)S(1)}, u32[]{:S(2)}, u32[]{:S(2)}) collective-permute-start(f32[32,128]{1,0:T(8,128)S(1)} %get-tuple-element.29), channel_id=1, source_target_pairs={{4,0},{8,4},{12,8},{0,12},{5,1},{9,5},{13,9},{1,13},{6,2},{10,6},{... | collective-permute-start | bytes 49160 | tf_op jit(solution)/shard_map/ppermute | solution.py:379
  44.4 2.8 %collective-permute-start.10 = (f32[32,128]{1,0:T(8,128)S(1)}, f32[32,128]{1,0:T(8,128)S(1)}, u32[]{:S(2)}, u32[]{:S(2)}) collective-permute-start(f32[32,128]{1,0:T(8,128)S(1)} %get-tuple-element.30), channel_id=1, source_target_pairs={{0,8},{12,4},{1,9},{13,5},{2,10},{14,6},{3,11},{15,7},{16,24},{28,... | collective-permute-start | bytes 49160 | tf_op jit(solution)/shard_map/ppermute | solution.py:379

commit v25 on v24

--- a/solution.py
+++ b/solution.py
@@ -49,6 +49,10 @@
     some = outs[0].shape[0]
     for i, out in enumerate(outs):
         out[...] = block[i * some : (i + 1) * some]
+
+
+def hold(place, block, token, out):
+    out[...] = block[...]
 
 
 def after(block, *tokens):
@@ -328,7 +332,8 @@
             halve, [((share // 2, rows_aux, listed), F32)] * 2, [], 0, lax.ppermute(mine, "aux", pairs), token
         )
         early += [*parts, *(lax.ppermute(part, "sub", swap) for part in parts)]
-    last = lax.ppermute(after(again, token), "aux", plan[-1])
+    (later,) = call(hold, [(again.shape, F32)], [], 0, again, lax.ppermute(token, "sub", swap))
+    last = lax.ppermute(later, "aux", plan[-1])
     fars = []
     late_near = after(near, *early)
     for shift in range(1, nob):

time: 56.5 us -> 49.8 us (0.88)
  starting transfers between devices: 21.1 us -> 12.7 us
  blocking collectives: 8.12 us -> 9.05 us
  waiting for transfers between devices: 16.5 us -> 17.2 us
    ppermute x2, starting transfers between devices: 12.8 us -> 4.38 us  [local(): lax.ppermute(back, 'aux', [(target, source) for source, target in pairs])]
    ppermute x1 -> x2, waiting for transfers between devices: 1.03 us -> 2.95 us  [the longest x1 1.8 us: local(): last = lax.ppermute(later, 'aux', plan[-1])]
    ppermute x1, waiting for transfers between devices: 4.84 us -> 3.48 us  [local(): lax.ppermute(mine, 'aux', pairs)]
    all_to_all x1, blocking collectives: 8.12 us -> 9.05 us  [local(): lax.all_to_all(partial_chi.reshape(owners, nt * block_aux // owners, naux...]
    ppermute x1 -> x2, starting transfers between devices: 1.29 us -> 1.36 us  [the longest x1 1.29 us: local(): last = lax.ppermute(later, 'aux', plan[-1])]
    pallas_call x8 -> x9, Pallas kernels: 6.97 us -> 7 us  [call(): pl.pallas_call(here, out_shape=shapes, in_specs=[VMEM] * len(arguments),...]
  transfers between devices with their start and end apart: 11 -> 12, of which waited for: 7 -> 8; matrix products, arithmetic and copies ran while one was open for 3% -> 3% of each run, Pallas kernels for 12% -> 14%
where the time goes in v25:
time: 49.8 us; the launch traced here: 49.5 us
  waiting for transfers between devices  17.2 us (35%)
  starting transfers between devices  12.7 us (26%)
  blocking collectives  9.05 us (18%)
  Pallas kernels  7 us (14%)
  other arithmetic  2.07 us (4%)
  local copies, waits for them, and re-layouts  1.27 us (3%)
    all_to_all x1, blocking collectives, local(): lax.all_to_all(partial_chi.reshape(owners, nt * block_aux // owners, naux...  9.05 us
    pallas_call x9, Pallas kernels, call(): pl.pallas_call(here, out_shape=shapes, in_specs=[VMEM] * len(arguments),...  7 us
    ppermute x1, waiting for transfers between devices, local(): fars.append(lax.ppermute(late_near, ('orb', 'sub'), pairs))  6.16 us
    ppermute x2, starting transfers between devices, local(): lax.ppermute(back, 'aux', [(target, source) for source, target in pairs])  4.38 us
    ppermute x1, waiting for transfers between devices, local(): lax.ppermute(mine, 'aux', pairs)  3.48 us
    ppermute x1, waiting for transfers between devices, local(): lax.ppermute(small, 'tau', ring(nt, shift))  3.07 us
    ppermute x1, starting transfers between devices, local(): lax.ppermute(tensor, 'orb', ring(nob, shift))  2.94 us
    ppermute x1, waiting for transfers between devices, local(): last = lax.ppermute(later, 'aux', plan[-1])  1.8 us
  transfers between devices with their start and end apart: 12, of which 8 were waited for; matrix products, arithmetic and copies ran while one was open for 3% of the time, Pallas kernels for 14%

profile of v25, /device:TPU:0, one launch (start us, length us, event | category | flops | bytes accessed | tf_op | source)
XLA Modules:
  0.0 49.5 jit_solution(3257494061272222077)
XLA Ops:
  0.0 2.9 %collective-permute-start.1 = (f32[128,2048]{1,0:T(8,128)}, f32[128,2048]{1,0:T(8,128)S(1)}, u32[]{:S(2)}, u32[]{:S(2)}) collective-permute-start(f32[128,2048]{1,0:T(8,128)} %bitcast.5), channel_id=1, source_target_pairs={{2,0},{0,2},{3,1},{1,3},{6,4},{4,6},{7,5},{5,7},{10,8},{8,10},{11,... | collective-permute-start | bytes 3145736 | tf_op jit(solution)/shard_map/ppermute | solution.py:300
  2.9 1.3 %copy-done = f32[1,1,2,64,2048]{4,3,2,1,0:T(8,128)S(1)} copy-done((f32[1,1,2,64,2048]{4,3,2,1,0:T(8,128)S(1)}, f32[1,1,2,64,2048]{4,3,2,1,0:T(8,128)}, u32[]{:S(2)}) %copy-start) | copy-done | bytes 1048600
  4.2 0.6 %prepare.1 = (f32[32,32,128]{2,1,0:T(8,128)S(1)}, f32[32,32,128]{2,1,0:T(8,128)S(1)}) custom-call(f32[128,2048]{1,0:T(8,128)S(1)} %bitcast.6), custom_call_target="tpu_custom_call" | custom-call | bytes 1048576 | tf_op jit(solution)/shard_map/prepare/pallas_call | solution.py:289
  4.8 1.6 %collective-permute-start.3 = (f32[32,32,128]{2,1,0:T(8,128)S(1)}, f32[32,32,128]{2,1,0:T(8,128)S(1)}, u32[]{:S(2)}, u32[]{:S(2)}) collective-permute-start(f32[32,32,128]{2,1,0:T(8,128)S(1)} %get-tuple-element.19.refs_1_), channel_id=1, source_target_pairs={{0,4},{4,8},{8,12},{12,0},{1,5},{5,9},{9,13},{13,1},{2,6},{6,10},{... | collective-permute-start | bytes 1572872 | tf_op jit(solution)/shard_map/ppermute | solution.py:332
  6.4 0.7 %convert_element_type.5 = f32[1,2]{1,0:T(1,128)S(1)} convert(s32[1,2]{1,0:T(1,128)} %param.7) | non-fusion elementwise | flops 2 | bytes 16 | tf_op jit(solution)/shard_map/convert_element_type | solution.py:310
  7.1 0.8 %fusion = (f32[1,136,128]{2,1,0:T(8,128)S(1)}, f32[136,128]{1,0:T(8,128)S(1)}) fusion(f32[1,2]{1,0:T(1,128)S(1)} %convert_element_type.5, f32[64,128]{1,0:T(8,128)} %param.6, f32[64,128]{1,0:T(8,128)} %param.5), kind=kLoop, calls=%fused_computation.4 | loop fusion | flops 69632 | bytes 204808 | tf_op jit(solution)/shard_map/stack | solution.py:313
  7.9 1.6 %collective-permute-start = (f32[136,128]{1,0:T(8,128)S(1)}, f32[136,128]{1,0:T(8,128)S(1)}, u32[]{:S(2)}, u32[]{:S(2)}) collective-permute-start(f32[136,128]{1,0:T(8,128)S(1)} %get-tuple-element.32), channel_id=1, source_target_pairs={{16,0},{0,16},{17,1},{1,17},{18,2},{2,18},{19,3},{3,19},{20,4},{4,... | collective-permute-start | bytes 208904 | tf_op jit(solution)/shard_map/ppermute | solution.py:313
  9.5 3.1 %collective-permute-done = f32[136,128]{1,0:T(8,128)S(1)} collective-permute-done((f32[136,128]{1,0:T(8,128)S(1)}, f32[136,128]{1,0:T(8,128)S(1)}, u32[]{:S(2)}, u32[]{:S(2)}) %collective-permute-start) | collective-permute-done | bytes 69664 | tf_op jit(solution)/shard_map/ppermute | solution.py:313
  12.6 1.5 %first.1 = (f32[4,512,256]{2,1,0:T(8,128)S(1)}, f32[8,128]{1,0:T(8,128)S(1)}) custom-call(f32[2,136,128]{2,1,0:T(8,128)S(1)} %pad_maximum_fusion.refs_0_, f32[128,2048]{1,0:T(8,128)S(1)} %bitcast.7), custom_call_target="tpu_custom_call" | custom-call | bytes 1187840 | tf_op jit(solution)/shard_map/first/pallas_call | solution.py:289
  14.1 0.1 collective-permute-start.7
  14.1 1.2 %collective-permute-done.7.refs_1_ = f32[8,128]{1,0:T(8,128)S(1)} collective-permute-done((f32[8,128]{1,0:T(8,128)S(1)}, f32[8,128]{1,0:T(8,128)S(1)}, u32[]{:S(2)}, u32[]{:S(2)}) %collective-permute-start.7) | collective-permute-done | bytes 4128 | tf_op jit(solution)/shard_map/ppermute | solution.py:335
  15.3 1.3 %collective-permute-start.8 = (f32[32,32,128]{2,1,0:T(8,128)S(1)}, f32[32,32,128]{2,1,0:T(8,128)S(1)}, u32[]{:S(2)}, u32[]{:S(2)}) collective-permute-start(f32[32,32,128]{2,1,0:T(8,128)S(1)} %hold.1), channel_id=1, source_target_pairs={{8,0},{4,12},{9,1},{5,13},{10,2},{6,14},{11,3},{7,15},{24,16},{20,... | collective-permute-start | bytes 1572872 | tf_op jit(solution)/shard_map/ppermute | solution.py:336
  16.6 3.5 %collective-permute-done.3.refs_0_ = f32[32,32,128]{2,1,0:T(8,128)S(1)} collective-permute-done((f32[32,32,128]{2,1,0:T(8,128)S(1)}, f32[32,32,128]{2,1,0:T(8,128)S(1)}, u32[]{:S(2)}, u32[]{:S(2)}) %collective-permute-start.3) | collective-permute-done | bytes 524320 | tf_op jit(solution)/shard_map/ppermute | solution.py:332
  20.1 0.1 collective-permute-start.4
  20.2 0.5 %collective-permute-start.5 = (f32[16,32,128]{2,1,0:T(8,128)S(1)}, f32[16,32,128]{2,1,0:T(8,128)S(1)}, u32[]{:S(2)}, u32[]{:S(2)}) collective-permute-start(f32[16,32,128]{2,1,0:T(8,128)S(1)} %get-tuple-element.22.refs_3_.refs_6_.refs_2_), channel_id=1, source_target_pairs={{1,0},{0,1},{3,2},{2,3},{5,4},{4,5},{7,6},{6,7},{9,8},{8,9},{11,10... | collective-permute-start | bytes 786440 | tf_op jit(solution)/shard_map/ppermute | solution.py:334
  20.7 1.0 %collective-permute-done.4.refs_4_.refs_7_.refs_3_ = f32[16,32,128]{2,1,0:T(8,128)S(1)} collective-permute-done((f32[16,32,128]{2,1,0:T(8,128)S(1)}, f32[16,32,128]{2,1,0:T(8,128)S(1)}, u32[]{:S(2)}, u32[]{:S(2)}) %collective-permute-start.4) | collective-permute-done | bytes 262176 | tf_op jit(solution)/shard_map/ppermute | solution.py:334
  21.7 0.4 collective-permute-done.5.refs_5_.refs_8_.refs_4_
  22.1 0.3 collective-permute-start.6
  22.4 6.2 %collective-permute-done.6.refs_3_ = f32[2,136,128]{2,1,0:T(8,128)S(1)} collective-permute-done((f32[2,136,128]{2,1,0:T(8,128)S(1)}, f32[2,136,128]{2,1,0:T(8,128)S(1)}, u32[]{:S(2)}, u32[]{:S(2)}) %collective-permute-start.6) | collective-permute-done | bytes 139296 | tf_op jit(solution)/shard_map/ppermute | solution.py:341
  28.6 0.0 collective-permute-done.1.refs_2_
  28.6 1.7 %second.1 = (bf16[256,4096]{1,0:T(8,128)(2,1)S(1)}, f32[8,128]{1,0:T(8,128)S(1)}) custom-call(f32[2,136,128]{2,1,0:T(8,128)S(1)} %pad_maximum_fusion.refs_0_, f32[4,512,256]{2,1,0:T(8,128)S(1)} %get-tuple-element.18.refs_1_, f32[128,2048]{1,0:T(8,128)S(1)} %collective-permute-done.1.refs_2_, f32[2,136,128]{2,1,0:T(8,128)S(1)} %collective-permute-done.6.refs_3_, ...), custom_call_target="tpu_custom_call" | custom-call | flops 603979776 | bytes 4997120 | tf_op jit(solution)/shard_map/second/pallas_call | solution.py:289
  30.3 1.8 %collective-permute-done.8.refs_0_ = f32[32,32,128]{2,1,0:T(8,128)S(1)} collective-permute-done((f32[32,32,128]{2,1,0:T(8,128)S(1)}, f32[32,32,128]{2,1,0:T(8,128)S(1)}, u32[]{:S(2)}, u32[]{:S(2)}) %collective-permute-start.8) | collective-permute-done | bytes 524320 | tf_op jit(solution)/shard_map/ppermute | solution.py:336
  32.1 0.8 %meet_own.1 = (bf16[192,4096]{1,0:T(8,128)(2,1)S(1)}, f32[32,64]{1,0:T(8,128)S(1)}, f32[32,128]{1,0:T(8,128)S(1)}) custom-call(bf16[256,4096]{1,0:T(8,128)(2,1)S(1)} %get-tuple-element.23.refs_0_, f32[16,32,128]{2,1,0:T(8,128)S(1)} %get-tuple-element.21.refs_2_.refs_5_.refs_1_, f32[16,32,128]{2,1,0:T(8,128)S(1)} %get-tuple-element.22.refs_3_.refs_6_.refs_2_, ...), custom_call_target="tpu_custom_call" | custom-call | flops 402653184 | bytes 5767168 | tf_op jit(solution)/shard_map/meet_own/pallas_call | solution.py:289
  33.0 3.0 %collective-permute-start.10 = (f32[32,128]{1,0:T(8,128)S(1)}, f32[32,128]{1,0:T(8,128)S(1)}, u32[]{:S(2)}, u32[]{:S(2)}) collective-permute-start(f32[32,128]{1,0:T(8,128)S(1)} %get-tuple-element.29), channel_id=1, source_target_pairs={{4,0},{8,4},{12,8},{0,12},{5,1},{9,5},{13,9},{1,13},{6,2},{10,6},{... | collective-permute-start | bytes 49160 | tf_op jit(solution)/shard_map/ppermute | solution.py:384
  36.0 0.0 collective-permute-done.9.refs_2_
  36.0 0.7 %meet_back.1 = (bf16[64,4096]{1,0:T(8,128)(2,1)S(1)}, f32[32,128]{1,0:T(8,128)S(1)}) custom-call(bf16[256,4096]{1,0:T(8,128)(2,1)S(1)} %get-tuple-element.23.refs_0_, f32[32,64]{1,0:T(8,128)S(1)} %get-tuple-element.27.refs_1_, f32[32,32,128]{2,1,0:T(8,128)S(1)} %collective-permute-done.9.refs_2_), custom_call_target="tpu_custom_call" | custom-call | flops 134217728 | bytes 4726784 | tf_op jit(solution)/shard_map/meet_back/pallas_call | solution.py:289
  36.7 1.3 %collective-permute-start.11 = (f32[32,128]{1,0:T(8,128)S(1)}, f32[32,128]{1,0:T(8,128)S(1)}, u32[]{:S(2)}, u32[]{:S(2)}) collective-permute-start(f32[32,128]{1,0:T(8,128)S(1)} %get-tuple-element.30), channel_id=1, source_target_pairs={{0,8},{12,4},{1,9},{13,5},{2,10},{14,6},{3,11},{15,7},{16,24},{28,... | collective-permute-start | bytes 49160 | tf_op jit(solution)/shard_map/ppermute | solution.py:384
  38.1 1.2 %meet_direct.1.refs_0_ = f32[2,64,256]{2,1,0:T(8,128)S(1)} custom-call(bf16[256,4096]{1,0:T(8,128)(2,1)S(1)} %get-tuple-element.23.refs_0_, f32[32,32,128]{2,1,0:T(8,128)S(1)} %get-tuple-element.19.refs_1_, f32[32,32,128]{2,1,0:T(8,128)S(1)} %collective-permute-done.2.refs_1_.refs_4_.refs_2_, bf16[192,4096]{1,0:T(8,128)(2,1)S(1)} %get-tuple-element.26.refs_3_, ...), custom_call_target="tpu_custom_call" | custom-call | flops 805306368 | bytes 9437184 | tf_op jit(solution)/shard_map/meet_direct/pallas_call | solution.py:289
  39.3 0.2 collective-permute-done.11.refs_2_
  39.5 0.3 complete.1
  39.8 9.1 %all_to_all.5 = f32[8,16,256]{2,1,0:T(8,128)S(1)} all-to-all(f32[8,16,256]{2,1,0:T(8,128)S(1)} %bitcast.8), channel_id=1, replica_groups=mesh['tau'=2,'aux'=4,'orb'=2,'sub'=2] {'tau','orb','sub'}, dimensions={0} | all-to-all | bytes 262144 | tf_op jit(solution)/shard_map/all_to_all | solution.py:402
  48.9 0.6 %broadcast_multiply_fusion = f32[16,256]{1,0:T(8,128)} fusion(f32[16,256]{1,0:T(8,128)S(1)} %reduce_sum.9), kind=kLoop, calls=%fused_computation.3 | loop fusion | flops 4096 | bytes 32768 | tf_op jit(solution)/shard_map/mul | solution.py:409
  (14 shorter events, 0.1 us)
Async XLA Ops:
  0.0 28.6 %collective-permute-start.1 = (f32[128,2048]{1,0:T(8,128)}, f32[128,2048]{1,0:T(8,128)S(1)}, u32[]{:S(2)}, u32[]{:S(2)}) collective-permute-start(f32[128,2048]{1,0:T(8,128)} %bitcast.5), channel_id=1, source_target_pairs={{2,0},{0,2},{3,1},{1,3},{6,4},{4,6},{7,5},{5,7},{10,8},{8,10},{11,... | collective-permute-start | bytes 3145736 | tf_op jit(solution)/shard_map/ppermute | solution.py:300
  2.9 1.3 %copy-start = (f32[1,1,2,64,2048]{4,3,2,1,0:T(8,128)S(1)}, f32[1,1,2,64,2048]{4,3,2,1,0:T(8,128)}, u32[]{:S(2)}) copy-start(f32[1,1,2,64,2048]{4,3,2,1,0:T(8,128)} %param.4) | copy-start | bytes 3145732
  4.2 8.4 %copy-start.1 = (f32[1,1,2,64,2048]{4,3,2,1,0:T(8,128)S(1)}, f32[1,1,2,64,2048]{4,3,2,1,0:T(8,128)}, u32[]{:S(2)}) copy-start(f32[1,1,2,64,2048]{4,3,2,1,0:T(8,128)} %param.4) | copy-start | bytes 3145732
  4.8 15.3 %collective-permute-start.3 = (f32[32,32,128]{2,1,0:T(8,128)S(1)}, f32[32,32,128]{2,1,0:T(8,128)S(1)}, u32[]{:S(2)}, u32[]{:S(2)}) collective-permute-start(f32[32,32,128]{2,1,0:T(8,128)S(1)} %get-tuple-element.19.refs_1_), channel_id=1, source_target_pairs={{0,4},{4,8},{8,12},{12,0},{1,5},{5,9},{9,13},{13,1},{2,6},{6,10},{... | collective-permute-start | bytes 1572872 | tf_op jit(solution)/shard_map/ppermute | solution.py:332
  6.4 14.3 %collective-permute-start.2 = (f32[32,32,128]{2,1,0:T(8,128)S(1)}, f32[32,32,128]{2,1,0:T(8,128)S(1)}, u32[]{:S(2)}, u32[]{:S(2)}) collective-permute-start(f32[32,32,128]{2,1,0:T(8,128)S(1)} %get-tuple-element.19.refs_1_), channel_id=1, source_target_pairs={{1,0},{0,1},{3,2},{2,3},{5,4},{4,5},{7,6},{6,7},{9,8},{8,9},{11,10... | collective-permute-start | bytes 1572872 | tf_op jit(solution)/shard_map/ppermute | solution.py:328
  7.9 4.7 %collective-permute-start = (f32[136,128]{1,0:T(8,128)S(1)}, f32[136,128]{1,0:T(8,128)S(1)}, u32[]{:S(2)}, u32[]{:S(2)}) collective-permute-start(f32[136,128]{1,0:T(8,128)S(1)} %get-tuple-element.32), channel_id=1, source_target_pairs={{16,0},{0,16},{17,1},{1,17},{18,2},{2,18},{19,3},{3,19},{20,4},{4,... | collective-permute-start | bytes 208904 | tf_op jit(solution)/shard_map/ppermute | solution.py:313
  14.1 1.2 %collective-permute-start.7 = (f32[8,128]{1,0:T(8,128)S(1)}, f32[8,128]{1,0:T(8,128)S(1)}, u32[]{:S(2)}, u32[]{:S(2)}) collective-permute-start(f32[8,128]{1,0:T(8,128)S(1)} %get-tuple-element.20.refs_1_), channel_id=1, source_target_pairs={{1,0},{0,1},{3,2},{2,3},{5,4},{4,5},{7,6},{6,7},{9,8},{8,9},{11,10... | collective-permute-start | bytes 12296 | tf_op jit(solution)/shard_map/ppermute | solution.py:335
  15.3 16.8 %collective-permute-start.8 = (f32[32,32,128]{2,1,0:T(8,128)S(1)}, f32[32,32,128]{2,1,0:T(8,128)S(1)}, u32[]{:S(2)}, u32[]{:S(2)}) collective-permute-start(f32[32,32,128]{2,1,0:T(8,128)S(1)} %hold.1), channel_id=1, source_target_pairs={{8,0},{4,12},{9,1},{5,13},{10,2},{6,14},{11,3},{7,15},{24,16},{20,... | collective-permute-start | bytes 1572872 | tf_op jit(solution)/shard_map/ppermute | solution.py:336
  20.1 1.6 %collective-permute-start.4 = (f32[16,32,128]{2,1,0:T(8,128)S(1)}, f32[16,32,128]{2,1,0:T(8,128)S(1)}, u32[]{:S(2)}, u32[]{:S(2)}) collective-permute-start(f32[16,32,128]{2,1,0:T(8,128)S(1)} %get-tuple-element.21.refs_2_.refs_5_.refs_1_), channel_id=1, source_target_pairs={{1,0},{0,1},{3,2},{2,3},{5,4},{4,5},{7,6},{6,7},{9,8},{8,9},{11,10... | collective-permute-start | bytes 786440 | tf_op jit(solution)/shard_map/ppermute | solution.py:334
  20.2 1.9 %collective-permute-start.5 = (f32[16,32,128]{2,1,0:T(8,128)S(1)}, f32[16,32,128]{2,1,0:T(8,128)S(1)}, u32[]{:S(2)}, u32[]{:S(2)}) collective-permute-start(f32[16,32,128]{2,1,0:T(8,128)S(1)} %get-tuple-element.22.refs_3_.refs_6_.refs_2_), channel_id=1, source_target_pairs={{1,0},{0,1},{3,2},{2,3},{5,4},{4,5},{7,6},{6,7},{9,8},{8,9},{11,10... | collective-permute-start | bytes 786440 | tf_op jit(solution)/shard_map/ppermute | solution.py:334
  22.1 6.4 %collective-permute-start.6 = (f32[2,136,128]{2,1,0:T(8,128)S(1)}, f32[2,136,128]{2,1,0:T(8,128)S(1)}, u32[]{:S(2)}, u32[]{:S(2)}) collective-permute-start(f32[2,136,128]{2,1,0:T(8,128)S(1)} %after.2), channel_id=1, source_target_pairs={{2,1},{3,0},{0,3},{1,2},{6,5},{7,4},{4,7},{5,6},{10,9},{11,8},{8,1... | collective-permute-start | bytes 417800 | tf_op jit(solution)/shard_map/ppermute | solution.py:341
  32.1 3.9 %collective-permute-start.9 = (f32[32,32,128]{2,1,0:T(8,128)S(1)}, f32[32,32,128]{2,1,0:T(8,128)S(1)}, u32[]{:S(2)}, u32[]{:S(2)}) collective-permute-start(f32[32,32,128]{2,1,0:T(8,128)S(1)} %after.3.refs_5_), channel_id=1, source_target_pairs={{1,0},{0,1},{3,2},{2,3},{5,4},{4,5},{7,6},{6,7},{9,8},{8,9},{11,10... | collective-permute-start | bytes 1572872 | tf_op jit(solution)/shard_map/ppermute | solution.py:356
  33.0 6.4 %collective-permute-start.10 = (f32[32,128]{1,0:T(8,128)S(1)}, f32[32,128]{1,0:T(8,128)S(1)}, u32[]{:S(2)}, u32[]{:S(2)}) collective-permute-start(f32[32,128]{1,0:T(8,128)S(1)} %get-tuple-element.29), channel_id=1, source_target_pairs={{4,0},{8,4},{12,8},{0,12},{5,1},{9,5},{13,9},{1,13},{6,2},{10,6},{... | collective-permute-start | bytes 49160 | tf_op jit(solution)/shard_map/ppermute | solution.py:384
  36.7 2.8 %collective-permute-start.11 = (f32[32,128]{1,0:T(8,128)S(1)}, f32[32,128]{1,0:T(8,128)S(1)}, u32[]{:S(2)}, u32[]{:S(2)}) collective-permute-start(f32[32,128]{1,0:T(8,128)S(1)} %get-tuple-element.30), channel_id=1, source_target_pairs={{0,8},{12,4},{1,9},{13,5},{2,10},{14,6},{3,11},{15,7},{16,24},{28,... | collective-permute-start | bytes 49160 | tf_op jit(solution)/shard_map/ppermute | solution.py:384

commit v26 on v23

--- a/solution.py
+++ b/solution.py
@@ -205,11 +205,18 @@
     return jnp.concatenate([back[:half], back[half:]], axis=1)
 
 
-def meet_own(place, sides, *refs, count):
-    refs, (tensor, back, *backs, ordered) = refs[: 4 * count - 3], refs[4 * count - 3 :]
-    pieces = [refs[i : i + 2] for i in range(0, 4 * count - 4, 2)] + [refs[-1:]]
-    half = refs[0].shape[1]
-    relay(pieces, tensor)
+def split(place, *refs):
+    refs, tensor = refs[:-1], refs[-1]
+    relay([refs[:1], refs[1:2]] + [refs[i : i + 2] for i in range(2, len(refs), 2)], tensor)
+
+
+def meet_own(place, sides, ready, last, tensor, back, *refs):
+    backs, ordered = refs[:-1], refs[-1]
+    half = last.shape[1]
+    some = tensor.shape[0] - 2 * half
+    if some:
+        tensor[:some, :] = ready[4 * half :, :]
+    relay([[last]], tensor.at[some:, :])
     rest = products(tensor[...], sides[sides.shape[0] // 2 :, :], half)
     for i, back_ref in enumerate(backs):
         back_ref[...] = fold(
@@ -225,12 +232,12 @@
     back_ref[...] = fold(place, own[...], other, ordered)
 
 
-def meet_direct(place, sides, mine, mine_other, own, last, out_ref, tensor, ordered, *, nt, naux):
+def meet_direct(place, sides, ready, own, last, out_ref, tensor, ordered, *, nt, naux):
     count = ordered.shape[0]
     block = ordered.shape[2]
     half = block // 2
     side = sides[: sides.shape[0] // 2, :]
-    relay([[mine], [mine_other]], tensor)
+    tensor[: 4 * half, :] = ready[: 4 * half, :]
     tensor[4 * half :, :] = last[...]
     some = products(tensor[...], side, half)
     own = jnp.concatenate([some[:block], products(own[...], side, half)], axis=0)
@@ -330,7 +337,8 @@
         early += [*parts, *(lax.ppermute(part, "sub", swap) for part in parts)]
     last = lax.ppermute(after(again, lax.ppermute(token, "sub", swap)), "aux", plan[-1])
     fars = []
-    late_near = after(near, *early)
+    (ready,) = call(split, [((4 * len(plan) * rows_aux, share * listed), BF16)], [], 0, mine, *early)
+    late_near = after(near, ready)
     for shift in range(1, nob):
         pairs = [(a * nsub + c, b * nsub + (c + 1) % nsub) for a, b in ring(nob, shift) for c in range(nsub)]
         fars.append(lax.ppermute(late_near, ("orb", "sub"), pairs))
@@ -361,9 +369,8 @@
         [scratch(1)],
         work * (2 * count - 3),
         sides,
-        *early[1:],
+        ready,
         last,
-        count=len(plan),
     )
     tensor, *last_back = call(
         meet_back,
@@ -385,8 +392,7 @@
         [((6 * rows_aux, depth), BF16), scratch(count)],
         work * (2 * count),
         sides,
-        mine,
-        mine_other,
+        ready,
         own,
         tensor,
         nt=nt,

time: 49.8 us -> 49.8 us (level)
    pallas_call x8 -> x9, Pallas kernels: 6.97 us -> 7.35 us  [call(): pl.pallas_call(here, out_shape=shapes, in_specs=[VMEM] * len(arguments),...]
  transfers between devices with their start and end apart: 12 -> 12, of which waited for: 8 -> 8; matrix products, arithmetic and copies ran while one was open for 3% -> 3% of each run, Pallas kernels for 13% -> 14%
where the time goes in v26:
time: 49.8 us; the launch traced here: 49.5 us
  waiting for transfers between devices  16.8 us (34%)
  starting transfers between devices  12.9 us (26%)
  blocking collectives  9.04 us (18%)
  Pallas kernels  7.35 us (15%)
  other arithmetic  2.07 us (4%)
  local copies, waits for them, and re-layouts  1.27 us (3%)
    all_to_all x1, blocking collectives, local(): lax.all_to_all(partial_chi.reshape(owners, nt * block_aux // owners, naux...  9.04 us
    pallas_call x9, Pallas kernels, call(): pl.pallas_call(here, out_shape=shapes, in_specs=[VMEM] * len(arguments),...  7.35 us
    ppermute x1, waiting for transfers between devices, local(): fars.append(lax.ppermute(late_near, ('orb', 'sub'), pairs))  5.76 us
    ppermute x2, starting transfers between devices, local(): lax.ppermute(back, 'aux', [(target, source) for source, target in pairs])  4.43 us
    ppermute x1, waiting for transfers between devices, local(): lax.ppermute(mine, 'aux', pairs)  3.53 us
    ppermute x1, waiting for transfers between devices, local(): lax.ppermute(small, 'tau', ring(nt, shift))  3.07 us
    ppermute x1, starting transfers between devices, local(): lax.ppermute(tensor, 'orb', ring(nob, shift))  2.94 us
    ppermute x1, waiting for transfers between devices, local(): lax.ppermute(after(again, lax.ppermute(token, 'sub', swap)), 'aux', plan[...  1.73 us
  transfers between devices with their start and end apart: 12, of which 8 were waited for; matrix products, arithmetic and copies ran while one was open for 3% of the time, Pallas kernels for 14%

profile of v26, /device:TPU:0, one launch (start us, length us, event | category | flops | bytes accessed | tf_op | source)
XLA Modules:
  0.0 49.5 jit_solution(15601752734894623615)
XLA Ops:
  0.0 2.9 %collective-permute-start.1 = (f32[128,2048]{1,0:T(8,128)}, f32[128,2048]{1,0:T(8,128)S(1)}, u32[]{:S(2)}, u32[]{:S(2)}) collective-permute-start(f32[128,2048]{1,0:T(8,128)} %bitcast.5), channel_id=1, source_target_pairs={{2,0},{0,2},{3,1},{1,3},{6,4},{4,6},{7,5},{5,7},{10,8},{8,10},{11,... | collective-permute-start | bytes 3145736 | tf_op jit(solution)/shard_map/ppermute | solution.py:303
  2.9 1.3 %copy-done = f32[1,1,2,64,2048]{4,3,2,1,0:T(8,128)S(1)} copy-done((f32[1,1,2,64,2048]{4,3,2,1,0:T(8,128)S(1)}, f32[1,1,2,64,2048]{4,3,2,1,0:T(8,128)}, u32[]{:S(2)}) %copy-start) | copy-done | bytes 1048600
  4.2 0.6 %prepare.1 = (f32[32,32,128]{2,1,0:T(8,128)S(1)}, f32[32,32,128]{2,1,0:T(8,128)S(1)}) custom-call(f32[128,2048]{1,0:T(8,128)S(1)} %bitcast.6), custom_call_target="tpu_custom_call" | custom-call | bytes 1048576 | tf_op jit(solution)/shard_map/prepare/pallas_call | solution.py:292
  4.8 1.6 %collective-permute-start.3 = (f32[32,32,128]{2,1,0:T(8,128)S(1)}, f32[32,32,128]{2,1,0:T(8,128)S(1)}, u32[]{:S(2)}, u32[]{:S(2)}) collective-permute-start(f32[32,32,128]{2,1,0:T(8,128)S(1)} %get-tuple-element.19.refs_0_), channel_id=1, source_target_pairs={{0,4},{4,8},{8,12},{12,0},{1,5},{5,9},{9,13},{13,1},{2,6},{6,10},{... | collective-permute-start | bytes 1572872 | tf_op jit(solution)/shard_map/ppermute | solution.py:335
  6.4 0.7 %convert_element_type.5 = f32[1,2]{1,0:T(1,128)S(1)} convert(s32[1,2]{1,0:T(1,128)} %param.7) | non-fusion elementwise | flops 2 | bytes 16 | tf_op jit(solution)/shard_map/convert_element_type | solution.py:313
  7.1 0.8 %fusion = (f32[1,136,128]{2,1,0:T(8,128)S(1)}, f32[136,128]{1,0:T(8,128)S(1)}) fusion(f32[1,2]{1,0:T(1,128)S(1)} %convert_element_type.5, f32[64,128]{1,0:T(8,128)} %param.6, f32[64,128]{1,0:T(8,128)} %param.5), kind=kLoop, calls=%fused_computation.4 | loop fusion | flops 69632 | bytes 204808 | tf_op jit(solution)/shard_map/stack | solution.py:316
  7.9 1.6 %collective-permute-start = (f32[136,128]{1,0:T(8,128)S(1)}, f32[136,128]{1,0:T(8,128)S(1)}, u32[]{:S(2)}, u32[]{:S(2)}) collective-permute-start(f32[136,128]{1,0:T(8,128)S(1)} %get-tuple-element.32), channel_id=1, source_target_pairs={{16,0},{0,16},{17,1},{1,17},{18,2},{2,18},{19,3},{3,19},{20,4},{4,... | collective-permute-start | bytes 208904 | tf_op jit(solution)/shard_map/ppermute | solution.py:316
  9.5 3.1 %collective-permute-done = f32[136,128]{1,0:T(8,128)S(1)} collective-permute-done((f32[136,128]{1,0:T(8,128)S(1)}, f32[136,128]{1,0:T(8,128)S(1)}, u32[]{:S(2)}, u32[]{:S(2)}) %collective-permute-start) | collective-permute-done | bytes 69664 | tf_op jit(solution)/shard_map/ppermute | solution.py:316
  12.6 1.5 %first.1 = (f32[4,512,256]{2,1,0:T(8,128)S(1)}, f32[8,128]{1,0:T(8,128)S(1)}) custom-call(f32[2,136,128]{2,1,0:T(8,128)S(1)} %pad_maximum_fusion.refs_0_, f32[128,2048]{1,0:T(8,128)S(1)} %bitcast.7), custom_call_target="tpu_custom_call" | custom-call | bytes 1187840 | tf_op jit(solution)/shard_map/first/pallas_call | solution.py:292
  14.1 0.1 collective-permute-start.7
  14.1 1.2 %collective-permute-done.7.refs_1_ = f32[8,128]{1,0:T(8,128)S(1)} collective-permute-done((f32[8,128]{1,0:T(8,128)S(1)}, f32[8,128]{1,0:T(8,128)S(1)}, u32[]{:S(2)}, u32[]{:S(2)}) %collective-permute-start.7) | collective-permute-done | bytes 4128 | tf_op jit(solution)/shard_map/ppermute | solution.py:338
  15.3 1.3 %collective-permute-start.8 = (f32[32,32,128]{2,1,0:T(8,128)S(1)}, f32[32,32,128]{2,1,0:T(8,128)S(1)}, u32[]{:S(2)}, u32[]{:S(2)}) collective-permute-start(f32[32,32,128]{2,1,0:T(8,128)S(1)} %after.4), channel_id=1, source_target_pairs={{8,0},{4,12},{9,1},{5,13},{10,2},{6,14},{11,3},{7,15},{24,16},{20,... | collective-permute-start | bytes 1572872 | tf_op jit(solution)/shard_map/ppermute | solution.py:338
  16.6 3.5 %collective-permute-done.3.refs_0_ = f32[32,32,128]{2,1,0:T(8,128)S(1)} collective-permute-done((f32[32,32,128]{2,1,0:T(8,128)S(1)}, f32[32,32,128]{2,1,0:T(8,128)S(1)}, u32[]{:S(2)}, u32[]{:S(2)}) %collective-permute-start.3) | collective-permute-done | bytes 524320 | tf_op jit(solution)/shard_map/ppermute | solution.py:335
  20.1 0.1 collective-permute-start.4
  20.2 0.5 %collective-permute-start.5 = (f32[16,32,128]{2,1,0:T(8,128)S(1)}, f32[16,32,128]{2,1,0:T(8,128)S(1)}, u32[]{:S(2)}, u32[]{:S(2)}) collective-permute-start(f32[16,32,128]{2,1,0:T(8,128)S(1)} %get-tuple-element.22.refs_3_.refs_6_), channel_id=1, source_target_pairs={{1,0},{0,1},{3,2},{2,3},{5,4},{4,5},{7,6},{6,7},{9,8},{8,9},{11,10... | collective-permute-start | bytes 786440 | tf_op jit(solution)/shard_map/ppermute | solution.py:337
  20.7 1.0 %collective-permute-done.4.refs_4_.refs_7_ = f32[16,32,128]{2,1,0:T(8,128)S(1)} collective-permute-done((f32[16,32,128]{2,1,0:T(8,128)S(1)}, f32[16,32,128]{2,1,0:T(8,128)S(1)}, u32[]{:S(2)}, u32[]{:S(2)}) %collective-permute-start.4) | collective-permute-done | bytes 262176 | tf_op jit(solution)/shard_map/ppermute | solution.py:337
  21.7 0.4 collective-permute-done.5.refs_5_.refs_8_
  22.1 0.3 split.1.refs_1_
  22.5 0.3 collective-permute-start.6
  22.8 5.8 %collective-permute-done.6.refs_3_ = f32[2,136,128]{2,1,0:T(8,128)S(1)} collective-permute-done((f32[2,136,128]{2,1,0:T(8,128)S(1)}, f32[2,136,128]{2,1,0:T(8,128)S(1)}, u32[]{:S(2)}, u32[]{:S(2)}) %collective-permute-start.6) | collective-permute-done | bytes 139296 | tf_op jit(solution)/shard_map/ppermute | solution.py:344
  28.6 0.0 collective-permute-done.1.refs_2_
  28.6 1.8 %second.1 = (bf16[256,4096]{1,0:T(8,128)(2,1)S(1)}, f32[8,128]{1,0:T(8,128)S(1)}) custom-call(f32[2,136,128]{2,1,0:T(8,128)S(1)} %pad_maximum_fusion.refs_0_, f32[4,512,256]{2,1,0:T(8,128)S(1)} %get-tuple-element.18.refs_1_, f32[128,2048]{1,0:T(8,128)S(1)} %collective-permute-done.1.refs_2_, f32[2,136,128]{2,1,0:T(8,128)S(1)} %collective-permute-done.6.refs_3_, ...), custom_call_target="tpu_custom_call" | custom-call | flops 603979776 | bytes 4997120 | tf_op jit(solution)/shard_map/second/pallas_call | solution.py:292
  30.3 1.7 %collective-permute-done.8.refs_0_ = f32[32,32,128]{2,1,0:T(8,128)S(1)} collective-permute-done((f32[32,32,128]{2,1,0:T(8,128)S(1)}, f32[32,32,128]{2,1,0:T(8,128)S(1)}, u32[]{:S(2)}, u32[]{:S(2)}) %collective-permute-start.8) | collective-permute-done | bytes 524320 | tf_op jit(solution)/shard_map/ppermute | solution.py:338
  32.1 0.9 %meet_own.1 = (bf16[192,4096]{1,0:T(8,128)(2,1)S(1)}, f32[32,64]{1,0:T(8,128)S(1)}, f32[32,128]{1,0:T(8,128)S(1)}) custom-call(bf16[256,4096]{1,0:T(8,128)(2,1)S(1)} %get-tuple-element.23.refs_0_, bf16[256,4096]{1,0:T(8,128)(2,1)S(1)} %split.1.refs_1_, f32[32,32,128]{2,1,0:T(8,128)S(1)} %after.5.refs_2_), custom_call_target="tpu_custom_call" | custom-call | flops 402653184 | bytes 8912896 | tf_op jit(solution)/shard_map/meet_own/pallas_call | solution.py:292
  32.9 3.1 %collective-permute-start.10 = (f32[32,128]{1,0:T(8,128)S(1)}, f32[32,128]{1,0:T(8,128)S(1)}, u32[]{:S(2)}, u32[]{:S(2)}) collective-permute-start(f32[32,128]{1,0:T(8,128)S(1)} %get-tuple-element.29), channel_id=1, source_target_pairs={{4,0},{8,4},{12,8},{0,12},{5,1},{9,5},{13,9},{1,13},{6,2},{10,6},{... | collective-permute-start | bytes 49160 | tf_op jit(solution)/shard_map/ppermute | solution.py:386
  36.0 0.7 %meet_back.1 = (bf16[64,4096]{1,0:T(8,128)(2,1)S(1)}, f32[32,128]{1,0:T(8,128)S(1)}) custom-call(bf16[256,4096]{1,0:T(8,128)(2,1)S(1)} %get-tuple-element.23.refs_0_, f32[32,64]{1,0:T(8,128)S(1)} %get-tuple-element.27.refs_1_, f32[32,32,128]{2,1,0:T(8,128)S(1)} %collective-permute-done.9.refs_2_), custom_call_target="tpu_custom_call" | custom-call | flops 134217728 | bytes 4726784 | tf_op jit(solution)/shard_map/meet_back/pallas_call | solution.py:292
  36.7 1.3 %collective-permute-start.11 = (f32[32,128]{1,0:T(8,128)S(1)}, f32[32,128]{1,0:T(8,128)S(1)}, u32[]{:S(2)}, u32[]{:S(2)}) collective-permute-start(f32[32,128]{1,0:T(8,128)S(1)} %get-tuple-element.30), channel_id=1, source_target_pairs={{0,8},{12,4},{1,9},{13,5},{2,10},{14,6},{3,11},{15,7},{16,24},{28,... | collective-permute-start | bytes 49160 | tf_op jit(solution)/shard_map/ppermute | solution.py:386
  38.1 1.3 %meet_direct.1.refs_0_ = f32[2,64,256]{2,1,0:T(8,128)S(1)} custom-call(bf16[256,4096]{1,0:T(8,128)(2,1)S(1)} %get-tuple-element.23.refs_0_, bf16[256,4096]{1,0:T(8,128)(2,1)S(1)} %split.1.refs_1_, bf16[192,4096]{1,0:T(8,128)(2,1)S(1)} %get-tuple-element.26.refs_2_, bf16[64,4096]{1,0:T(8,128)(2,1)S(1)} %get-tuple-element.28.refs_3_), custom_call_target="tpu_custom_call" | custom-call | flops 805306368 | bytes 12582912 | tf_op jit(solution)/shard_map/meet_direct/pallas_call | solution.py:292
  39.4 0.1 collective-permute-done.11.refs_2_
  39.5 0.3 complete.1
  39.8 9.0 %all_to_all.5 = f32[8,16,256]{2,1,0:T(8,128)S(1)} all-to-all(f32[8,16,256]{2,1,0:T(8,128)S(1)} %bitcast.8), channel_id=1, replica_groups=mesh['tau'=2,'aux'=4,'orb'=2,'sub'=2] {'tau','orb','sub'}, dimensions={0} | all-to-all | bytes 262144 | tf_op jit(solution)/shard_map/all_to_all | solution.py:403
  48.9 0.6 %broadcast_multiply_fusion = f32[16,256]{1,0:T(8,128)} fusion(f32[16,256]{1,0:T(8,128)S(1)} %reduce_sum.9), kind=kLoop, calls=%fused_computation.3 | loop fusion | flops 4096 | bytes 32768 | tf_op jit(solution)/shard_map/mul | solution.py:410
  (15 shorter events, 0.1 us)
Async XLA Ops:
  0.0 28.6 %collective-permute-start.1 = (f32[128,2048]{1,0:T(8,128)}, f32[128,2048]{1,0:T(8,128)S(1)}, u32[]{:S(2)}, u32[]{:S(2)}) collective-permute-start(f32[128,2048]{1,0:T(8,128)} %bitcast.5), channel_id=1, source_target_pairs={{2,0},{0,2},{3,1},{1,3},{6,4},{4,6},{7,5},{5,7},{10,8},{8,10},{11,... | collective-permute-start | bytes 3145736 | tf_op jit(solution)/shard_map/ppermute | solution.py:303
  2.9 1.3 %copy-start = (f32[1,1,2,64,2048]{4,3,2,1,0:T(8,128)S(1)}, f32[1,1,2,64,2048]{4,3,2,1,0:T(8,128)}, u32[]{:S(2)}) copy-start(f32[1,1,2,64,2048]{4,3,2,1,0:T(8,128)} %param.4) | copy-start | bytes 3145732
  4.2 8.4 %copy-start.1 = (f32[1,1,2,64,2048]{4,3,2,1,0:T(8,128)S(1)}, f32[1,1,2,64,2048]{4,3,2,1,0:T(8,128)}, u32[]{:S(2)}) copy-start(f32[1,1,2,64,2048]{4,3,2,1,0:T(8,128)} %param.4) | copy-start | bytes 3145732
  4.8 15.3 %collective-permute-start.3 = (f32[32,32,128]{2,1,0:T(8,128)S(1)}, f32[32,32,128]{2,1,0:T(8,128)S(1)}, u32[]{:S(2)}, u32[]{:S(2)}) collective-permute-start(f32[32,32,128]{2,1,0:T(8,128)S(1)} %get-tuple-element.19.refs_0_), channel_id=1, source_target_pairs={{0,4},{4,8},{8,12},{12,0},{1,5},{5,9},{9,13},{13,1},{2,6},{6,10},{... | collective-permute-start | bytes 1572872 | tf_op jit(solution)/shard_map/ppermute | solution.py:335
  6.4 14.3 %collective-permute-start.2 = (f32[32,32,128]{2,1,0:T(8,128)S(1)}, f32[32,32,128]{2,1,0:T(8,128)S(1)}, u32[]{:S(2)}, u32[]{:S(2)}) collective-permute-start(f32[32,32,128]{2,1,0:T(8,128)S(1)} %get-tuple-element.19.refs_0_), channel_id=1, source_target_pairs={{1,0},{0,1},{3,2},{2,3},{5,4},{4,5},{7,6},{6,7},{9,8},{8,9},{11,10... | collective-permute-start | bytes 1572872 | tf_op jit(solution)/shard_map/ppermute | solution.py:331
  7.9 4.7 %collective-permute-start = (f32[136,128]{1,0:T(8,128)S(1)}, f32[136,128]{1,0:T(8,128)S(1)}, u32[]{:S(2)}, u32[]{:S(2)}) collective-permute-start(f32[136,128]{1,0:T(8,128)S(1)} %get-tuple-element.32), channel_id=1, source_target_pairs={{16,0},{0,16},{17,1},{1,17},{18,2},{2,18},{19,3},{3,19},{20,4},{4,... | collective-permute-start | bytes 208904 | tf_op jit(solution)/shard_map/ppermute | solution.py:316
  14.1 1.2 %collective-permute-start.7 = (f32[8,128]{1,0:T(8,128)S(1)}, f32[8,128]{1,0:T(8,128)S(1)}, u32[]{:S(2)}, u32[]{:S(2)}) collective-permute-start(f32[8,128]{1,0:T(8,128)S(1)} %get-tuple-element.20.refs_1_), channel_id=1, source_target_pairs={{1,0},{0,1},{3,2},{2,3},{5,4},{4,5},{7,6},{6,7},{9,8},{8,9},{11,10... | collective-permute-start | bytes 12296 | tf_op jit(solution)/shard_map/ppermute | solution.py:338
  15.3 16.8 %collective-permute-start.8 = (f32[32,32,128]{2,1,0:T(8,128)S(1)}, f32[32,32,128]{2,1,0:T(8,128)S(1)}, u32[]{:S(2)}, u32[]{:S(2)}) collective-permute-start(f32[32,32,128]{2,1,0:T(8,128)S(1)} %after.4), channel_id=1, source_target_pairs={{8,0},{4,12},{9,1},{5,13},{10,2},{6,14},{11,3},{7,15},{24,16},{20,... | collective-permute-start | bytes 1572872 | tf_op jit(solution)/shard_map/ppermute | solution.py:338
  20.1 1.6 %collective-permute-start.4 = (f32[16,32,128]{2,1,0:T(8,128)S(1)}, f32[16,32,128]{2,1,0:T(8,128)S(1)}, u32[]{:S(2)}, u32[]{:S(2)}) collective-permute-start(f32[16,32,128]{2,1,0:T(8,128)S(1)} %get-tuple-element.21.refs_2_.refs_5_), channel_id=1, source_target_pairs={{1,0},{0,1},{3,2},{2,3},{5,4},{4,5},{7,6},{6,7},{9,8},{8,9},{11,10... | collective-permute-start | bytes 786440 | tf_op jit(solution)/shard_map/ppermute | solution.py:337
  20.2 1.9 %collective-permute-start.5 = (f32[16,32,128]{2,1,0:T(8,128)S(1)}, f32[16,32,128]{2,1,0:T(8,128)S(1)}, u32[]{:S(2)}, u32[]{:S(2)}) collective-permute-start(f32[16,32,128]{2,1,0:T(8,128)S(1)} %get-tuple-element.22.refs_3_.refs_6_), channel_id=1, source_target_pairs={{1,0},{0,1},{3,2},{2,3},{5,4},{4,5},{7,6},{6,7},{9,8},{8,9},{11,10... | collective-permute-start | bytes 786440 | tf_op jit(solution)/shard_map/ppermute | solution.py:337
  22.5 6.1 %collective-permute-start.6 = (f32[2,136,128]{2,1,0:T(8,128)S(1)}, f32[2,136,128]{2,1,0:T(8,128)S(1)}, u32[]{:S(2)}, u32[]{:S(2)}) collective-permute-start(f32[2,136,128]{2,1,0:T(8,128)S(1)} %after.3), channel_id=1, source_target_pairs={{2,1},{3,0},{0,3},{1,2},{6,5},{7,4},{4,7},{5,6},{10,9},{11,8},{8,1... | collective-permute-start | bytes 417800 | tf_op jit(solution)/shard_map/ppermute | solution.py:344
  32.1 4.0 %collective-permute-start.9 = (f32[32,32,128]{2,1,0:T(8,128)S(1)}, f32[32,32,128]{2,1,0:T(8,128)S(1)}, u32[]{:S(2)}, u32[]{:S(2)}) collective-permute-start(f32[32,32,128]{2,1,0:T(8,128)S(1)} %after.5.refs_2_), channel_id=1, source_target_pairs={{1,0},{0,1},{3,2},{2,3},{5,4},{4,5},{7,6},{6,7},{9,8},{8,9},{11,10... | collective-permute-start | bytes 1572872 | tf_op jit(solution)/shard_map/ppermute | solution.py:359
  32.9 6.4 %collective-permute-start.10 = (f32[32,128]{1,0:T(8,128)S(1)}, f32[32,128]{1,0:T(8,128)S(1)}, u32[]{:S(2)}, u32[]{:S(2)}) collective-permute-start(f32[32,128]{1,0:T(8,128)S(1)} %get-tuple-element.29), channel_id=1, source_target_pairs={{4,0},{8,4},{12,8},{0,12},{5,1},{9,5},{13,9},{1,13},{6,2},{10,6},{... | collective-permute-start | bytes 49160 | tf_op jit(solution)/shard_map/ppermute | solution.py:386
  36.7 2.8 %collective-permute-start.11 = (f32[32,128]{1,0:T(8,128)S(1)}, f32[32,128]{1,0:T(8,128)S(1)}, u32[]{:S(2)}, u32[]{:S(2)}) collective-permute-start(f32[32,128]{1,0:T(8,128)S(1)} %get-tuple-element.30), channel_id=1, source_target_pairs={{0,8},{12,4},{1,9},{13,5},{2,10},{14,6},{3,11},{15,7},{16,24},{28,... | collective-permute-start | bytes 49160 | tf_op jit(solution)/shard_map/ppermute | solution.py:386

commit v27 on v23

--- a/solution.py
+++ b/solution.py
@@ -246,7 +246,7 @@
         out_ref[tau] = at_sub(place, jnp.concatenate(here, axis=1), 0)
 
 
-def complete(place, early, *refs):
+def complete(place, early, *refs, nsub):
     backs, out_ref = refs[:-1], refs[-1]
     nt, block, wide = early.shape
     naux = wide // block
@@ -258,7 +258,11 @@
             lower = ref[:, (nt + tau) * half : (nt + tau + 1) * half]
             parts[shift] = at_sub(place, jnp.concatenate([upper, lower], axis=0), 1)
         total = early[tau] + jnp.concatenate(parts, axis=1)
-        out_ref[tau] = pltpu.roll(total, place[3] * block, 1)
+        total = pltpu.roll(total, place[3] * block, 1)
+        owners, rows, _ = out_ref.shape
+        nob = owners // (nt * nsub)
+        for i in range(nob * nsub):
+            out_ref[((i % nsub) * nob + i // nsub) * nt + tau] = total[i * rows : (i + 1) * rows]
 
 
 def local(three_center, occupied_green, virtual_green, block_list, sizes):
@@ -392,15 +396,10 @@
         nt=nt,
         naux=naux,
     )
-    (partial_chi,) = call(complete, [shape], [], 0, direct, *returned)
     owners = nt * nob * nsub
-    received = lax.all_to_all(
-        partial_chi.reshape(owners, nt * block_aux // owners, nauxf),
-        ("tau", "orb", "sub"),
-        split_axis=0,
-        concat_axis=0,
-        tiled=True,
-    )
+    shape = ((owners, nt * block_aux // owners, nauxf), F32)
+    (partial_chi,) = call(complete, [shape], [], 0, direct, *returned, nsub=nsub)
+    received = lax.all_to_all(partial_chi, ("sub", "orb", "tau"), split_axis=0, concat_axis=0, tiled=True)
     return received.sum(axis=0) * (-2.0 / math.sqrt(norb * slots * width))
 
 

time: 49.8 us -> 49.6 us (level)
  transfers between devices with their start and end apart: 12 -> 12, of which waited for: 8 -> 8; matrix products, arithmetic and copies ran while one was open for 3% -> 3% of each run, Pallas kernels for 13% -> 14%
where the time goes in v27:
time: 49.6 us; the launch traced here: 49.3 us
  waiting for transfers between devices  17.2 us (35%)
  starting transfers between devices  12.8 us (26%)
  blocking collectives  8.87 us (18%)
  Pallas kernels  6.97 us (14%)
  other arithmetic  2.07 us (4%)
  local copies, waits for them, and re-layouts  1.27 us (3%)
    all_to_all x1, blocking collectives, local(): lax.all_to_all(partial_chi, ('sub', 'orb', 'tau'), split_axis=0, concat_a...  8.87 us
    pallas_call x8, Pallas kernels, call(): pl.pallas_call(here, out_shape=shapes, in_specs=[VMEM] * len(arguments),...  6.97 us
    ppermute x1, waiting for transfers between devices, local(): fars.append(lax.ppermute(late_near, ('orb', 'sub'), pairs))  6.16 us
    ppermute x2, starting transfers between devices, local(): lax.ppermute(back, 'aux', [(target, source) for source, target in pairs])  4.43 us
    ppermute x1, waiting for transfers between devices, local(): lax.ppermute(mine, 'aux', pairs)  3.53 us
    ppermute x1, waiting for transfers between devices, local(): lax.ppermute(small, 'tau', ring(nt, shift))  3.07 us
    ppermute x1, starting transfers between devices, local(): lax.ppermute(tensor, 'orb', ring(nob, shift))  2.94 us
    ppermute x1, waiting for transfers between devices, local(): lax.ppermute(after(again, lax.ppermute(token, 'sub', swap)), 'aux', plan[...  1.75 us
  transfers between devices with their start and end apart: 12, of which 8 were waited for; matrix products, arithmetic and copies ran while one was open for 3% of the time, Pallas kernels for 14%

profile of v27, /device:TPU:0, one launch (start us, length us, event | category | flops | bytes accessed | tf_op | source)
XLA Modules:
  0.0 49.3 jit_solution(16948929918873907221)
XLA Ops:
  0.0 2.9 %collective-permute-start.1 = (f32[128,2048]{1,0:T(8,128)}, f32[128,2048]{1,0:T(8,128)S(1)}, u32[]{:S(2)}, u32[]{:S(2)}) collective-permute-start(f32[128,2048]{1,0:T(8,128)} %bitcast.4), channel_id=1, source_target_pairs={{2,0},{0,2},{3,1},{1,3},{6,4},{4,6},{7,5},{5,7},{10,8},{8,10},{11,... | collective-permute-start | bytes 3145736 | tf_op jit(solution)/shard_map/ppermute | solution.py:300
  2.9 1.3 %copy-done = f32[1,1,2,64,2048]{4,3,2,1,0:T(8,128)S(1)} copy-done((f32[1,1,2,64,2048]{4,3,2,1,0:T(8,128)S(1)}, f32[1,1,2,64,2048]{4,3,2,1,0:T(8,128)}, u32[]{:S(2)}) %copy-start) | copy-done | bytes 1048600
  4.2 0.6 %prepare.1 = (f32[32,32,128]{2,1,0:T(8,128)S(1)}, f32[32,32,128]{2,1,0:T(8,128)S(1)}) custom-call(f32[128,2048]{1,0:T(8,128)S(1)} %bitcast.5), custom_call_target="tpu_custom_call" | custom-call | bytes 1048576 | tf_op jit(solution)/shard_map/prepare/pallas_call | solution.py:289
  4.8 1.6 %collective-permute-start.3 = (f32[32,32,128]{2,1,0:T(8,128)S(1)}, f32[32,32,128]{2,1,0:T(8,128)S(1)}, u32[]{:S(2)}, u32[]{:S(2)}) collective-permute-start(f32[32,32,128]{2,1,0:T(8,128)S(1)} %get-tuple-element.19.refs_1_), channel_id=1, source_target_pairs={{0,4},{4,8},{8,12},{12,0},{1,5},{5,9},{9,13},{13,1},{2,6},{6,10},{... | collective-permute-start | bytes 1572872 | tf_op jit(solution)/shard_map/ppermute | solution.py:332
  6.4 0.7 %convert_element_type.5 = f32[1,2]{1,0:T(1,128)S(1)} convert(s32[1,2]{1,0:T(1,128)} %param.7) | non-fusion elementwise | flops 2 | bytes 16 | tf_op jit(solution)/shard_map/convert_element_type | solution.py:310
  7.1 0.8 %fusion = (f32[1,136,128]{2,1,0:T(8,128)S(1)}, f32[136,128]{1,0:T(8,128)S(1)}) fusion(f32[1,2]{1,0:T(1,128)S(1)} %convert_element_type.5, f32[64,128]{1,0:T(8,128)} %param.6, f32[64,128]{1,0:T(8,128)} %param.5), kind=kLoop, calls=%fused_computation.4 | loop fusion | flops 69632 | bytes 204808 | tf_op jit(solution)/shard_map/stack | solution.py:313
  7.9 1.6 %collective-permute-start = (f32[136,128]{1,0:T(8,128)S(1)}, f32[136,128]{1,0:T(8,128)S(1)}, u32[]{:S(2)}, u32[]{:S(2)}) collective-permute-start(f32[136,128]{1,0:T(8,128)S(1)} %get-tuple-element.32), channel_id=1, source_target_pairs={{16,0},{0,16},{17,1},{1,17},{18,2},{2,18},{19,3},{3,19},{20,4},{4,... | collective-permute-start | bytes 208904 | tf_op jit(solution)/shard_map/ppermute | solution.py:313
  9.5 3.1 %collective-permute-done = f32[136,128]{1,0:T(8,128)S(1)} collective-permute-done((f32[136,128]{1,0:T(8,128)S(1)}, f32[136,128]{1,0:T(8,128)S(1)}, u32[]{:S(2)}, u32[]{:S(2)}) %collective-permute-start) | collective-permute-done | bytes 69664 | tf_op jit(solution)/shard_map/ppermute | solution.py:313
  12.6 1.5 %first.1 = (f32[4,512,256]{2,1,0:T(8,128)S(1)}, f32[8,128]{1,0:T(8,128)S(1)}) custom-call(f32[2,136,128]{2,1,0:T(8,128)S(1)} %pad_maximum_fusion.refs_0_, f32[128,2048]{1,0:T(8,128)S(1)} %bitcast.6), custom_call_target="tpu_custom_call" | custom-call | bytes 1187840 | tf_op jit(solution)/shard_map/first/pallas_call | solution.py:289
  14.1 0.1 collective-permute-start.7
  14.1 1.2 %collective-permute-done.7.refs_1_ = f32[8,128]{1,0:T(8,128)S(1)} collective-permute-done((f32[8,128]{1,0:T(8,128)S(1)}, f32[8,128]{1,0:T(8,128)S(1)}, u32[]{:S(2)}, u32[]{:S(2)}) %collective-permute-start.7) | collective-permute-done | bytes 4128 | tf_op jit(solution)/shard_map/ppermute | solution.py:335
  15.3 1.3 %collective-permute-start.8 = (f32[32,32,128]{2,1,0:T(8,128)S(1)}, f32[32,32,128]{2,1,0:T(8,128)S(1)}, u32[]{:S(2)}, u32[]{:S(2)}) collective-permute-start(f32[32,32,128]{2,1,0:T(8,128)S(1)} %after.4), channel_id=1, source_target_pairs={{8,0},{4,12},{9,1},{5,13},{10,2},{6,14},{11,3},{7,15},{24,16},{20,... | collective-permute-start | bytes 1572872 | tf_op jit(solution)/shard_map/ppermute | solution.py:335
  16.6 3.5 %collective-permute-done.3.refs_0_ = f32[32,32,128]{2,1,0:T(8,128)S(1)} collective-permute-done((f32[32,32,128]{2,1,0:T(8,128)S(1)}, f32[32,32,128]{2,1,0:T(8,128)S(1)}, u32[]{:S(2)}, u32[]{:S(2)}) %collective-permute-start.3) | collective-permute-done | bytes 524320 | tf_op jit(solution)/shard_map/ppermute | solution.py:332
  20.1 0.1 collective-permute-start.4
  20.2 0.5 %collective-permute-start.5 = (f32[16,32,128]{2,1,0:T(8,128)S(1)}, f32[16,32,128]{2,1,0:T(8,128)S(1)}, u32[]{:S(2)}, u32[]{:S(2)}) collective-permute-start(f32[16,32,128]{2,1,0:T(8,128)S(1)} %get-tuple-element.22.refs_3_.refs_6_.refs_2_), channel_id=1, source_target_pairs={{1,0},{0,1},{3,2},{2,3},{5,4},{4,5},{7,6},{6,7},{9,8},{8,9},{11,10... | collective-permute-start | bytes 786440 | tf_op jit(solution)/shard_map/ppermute | solution.py:334
  20.7 1.0 %collective-permute-done.4.refs_4_.refs_7_.refs_3_ = f32[16,32,128]{2,1,0:T(8,128)S(1)} collective-permute-done((f32[16,32,128]{2,1,0:T(8,128)S(1)}, f32[16,32,128]{2,1,0:T(8,128)S(1)}, u32[]{:S(2)}, u32[]{:S(2)}) %collective-permute-start.4) | collective-permute-done | bytes 262176 | tf_op jit(solution)/shard_map/ppermute | solution.py:334
  21.7 0.4 collective-permute-done.5.refs_5_.refs_8_.refs_4_
  22.1 0.3 collective-permute-start.6
  22.4 6.2 %collective-permute-done.6.refs_3_ = f32[2,136,128]{2,1,0:T(8,128)S(1)} collective-permute-done((f32[2,136,128]{2,1,0:T(8,128)S(1)}, f32[2,136,128]{2,1,0:T(8,128)S(1)}, u32[]{:S(2)}, u32[]{:S(2)}) %collective-permute-start.6) | collective-permute-done | bytes 139296 | tf_op jit(solution)/shard_map/ppermute | solution.py:340
  28.6 0.0 collective-permute-done.1.refs_2_
  28.6 1.7 %second.1 = (bf16[256,4096]{1,0:T(8,128)(2,1)S(1)}, f32[8,128]{1,0:T(8,128)S(1)}) custom-call(f32[2,136,128]{2,1,0:T(8,128)S(1)} %pad_maximum_fusion.refs_0_, f32[4,512,256]{2,1,0:T(8,128)S(1)} %get-tuple-element.18.refs_1_, f32[128,2048]{1,0:T(8,128)S(1)} %collective-permute-done.1.refs_2_, f32[2,136,128]{2,1,0:T(8,128)S(1)} %collective-permute-done.6.refs_3_, ...), custom_call_target="tpu_custom_call" | custom-call | flops 603979776 | bytes 4997120 | tf_op jit(solution)/shard_map/second/pallas_call | solution.py:289
  30.3 1.8 %collective-permute-done.8.refs_0_ = f32[32,32,128]{2,1,0:T(8,128)S(1)} collective-permute-done((f32[32,32,128]{2,1,0:T(8,128)S(1)}, f32[32,32,128]{2,1,0:T(8,128)S(1)}, u32[]{:S(2)}, u32[]{:S(2)}) %collective-permute-start.8) | collective-permute-done | bytes 524320 | tf_op jit(solution)/shard_map/ppermute | solution.py:335
  32.1 0.0 collective-permute-start.9
  32.1 0.8 %meet_own.1 = (bf16[192,4096]{1,0:T(8,128)(2,1)S(1)}, f32[32,64]{1,0:T(8,128)S(1)}, f32[32,128]{1,0:T(8,128)S(1)}) custom-call(bf16[256,4096]{1,0:T(8,128)(2,1)S(1)} %get-tuple-element.23.refs_0_, f32[16,32,128]{2,1,0:T(8,128)S(1)} %get-tuple-element.21.refs_2_.refs_5_.refs_1_, f32[16,32,128]{2,1,0:T(8,128)S(1)} %get-tuple-element.22.refs_3_.refs_6_.refs_2_, ...), custom_call_target="tpu_custom_call" | custom-call | flops 402653184 | bytes 5767168 | tf_op jit(solution)/shard_map/meet_own/pallas_call | solution.py:289
  32.9 3.1 %collective-permute-start.10 = (f32[32,128]{1,0:T(8,128)S(1)}, f32[32,128]{1,0:T(8,128)S(1)}, u32[]{:S(2)}, u32[]{:S(2)}) collective-permute-start(f32[32,128]{1,0:T(8,128)S(1)} %get-tuple-element.29), channel_id=1, source_target_pairs={{4,0},{8,4},{12,8},{0,12},{5,1},{9,5},{13,9},{1,13},{6,2},{10,6},{... | collective-permute-start | bytes 49160 | tf_op jit(solution)/shard_map/ppermute | solution.py:383
  36.0 0.7 %meet_back.1 = (bf16[64,4096]{1,0:T(8,128)(2,1)S(1)}, f32[32,128]{1,0:T(8,128)S(1)}) custom-call(bf16[256,4096]{1,0:T(8,128)(2,1)S(1)} %get-tuple-element.23.refs_0_, f32[32,64]{1,0:T(8,128)S(1)} %get-tuple-element.27.refs_1_, f32[32,32,128]{2,1,0:T(8,128)S(1)} %collective-permute-done.9.refs_2_), custom_call_target="tpu_custom_call" | custom-call | flops 134217728 | bytes 4726784 | tf_op jit(solution)/shard_map/meet_back/pallas_call | solution.py:289
  36.7 1.3 %collective-permute-start.11 = (f32[32,128]{1,0:T(8,128)S(1)}, f32[32,128]{1,0:T(8,128)S(1)}, u32[]{:S(2)}, u32[]{:S(2)}) collective-permute-start(f32[32,128]{1,0:T(8,128)S(1)} %get-tuple-element.30), channel_id=1, source_target_pairs={{0,8},{12,4},{1,9},{13,5},{2,10},{14,6},{3,11},{15,7},{16,24},{28,... | collective-permute-start | bytes 49160 | tf_op jit(solution)/shard_map/ppermute | solution.py:383
  38.1 1.2 %meet_direct.1.refs_0_ = f32[2,64,256]{2,1,0:T(8,128)S(1)} custom-call(bf16[256,4096]{1,0:T(8,128)(2,1)S(1)} %get-tuple-element.23.refs_0_, f32[32,32,128]{2,1,0:T(8,128)S(1)} %get-tuple-element.19.refs_1_, f32[32,32,128]{2,1,0:T(8,128)S(1)} %collective-permute-done.2.refs_1_.refs_4_.refs_2_, bf16[192,4096]{1,0:T(8,128)(2,1)S(1)} %get-tuple-element.26.refs_3_, ...), custom_call_target="tpu_custom_call" | custom-call | flops 805306368 | bytes 9437184 | tf_op jit(solution)/shard_map/meet_direct/pallas_call | solution.py:289
  39.3 0.2 collective-permute-done.11.refs_2_
  39.5 0.3 complete.1
  39.8 8.9 %all_to_all.5 = f32[8,16,256]{2,1,0:T(8,128)S(1)} all-to-all(f32[8,16,256]{2,1,0:T(8,128)S(1)} %complete.1), channel_id=1, replica_groups=mesh['tau'=2,'aux'=4,'orb'=2,'sub'=2] {'sub','orb','tau'}, dimensions={0} | all-to-all | bytes 262144 | tf_op jit(solution)/shard_map/all_to_all | solution.py:402
  48.7 0.6 %broadcast_multiply_fusion = f32[16,256]{1,0:T(8,128)} fusion(f32[16,256]{1,0:T(8,128)S(1)} %reduce_sum.9), kind=kLoop, calls=%fused_computation.3 | loop fusion | flops 4096 | bytes 32768 | tf_op jit(solution)/shard_map/mul | solution.py:403
  (14 shorter events, 0.1 us)
Async XLA Ops:
  0.0 28.6 %collective-permute-start.1 = (f32[128,2048]{1,0:T(8,128)}, f32[128,2048]{1,0:T(8,128)S(1)}, u32[]{:S(2)}, u32[]{:S(2)}) collective-permute-start(f32[128,2048]{1,0:T(8,128)} %bitcast.4), channel_id=1, source_target_pairs={{2,0},{0,2},{3,1},{1,3},{6,4},{4,6},{7,5},{5,7},{10,8},{8,10},{11,... | collective-permute-start | bytes 3145736 | tf_op jit(solution)/shard_map/ppermute | solution.py:300
  2.9 1.3 %copy-start = (f32[1,1,2,64,2048]{4,3,2,1,0:T(8,128)S(1)}, f32[1,1,2,64,2048]{4,3,2,1,0:T(8,128)}, u32[]{:S(2)}) copy-start(f32[1,1,2,64,2048]{4,3,2,1,0:T(8,128)} %param.4) | copy-start | bytes 3145732
  4.2 8.4 %copy-start.1 = (f32[1,1,2,64,2048]{4,3,2,1,0:T(8,128)S(1)}, f32[1,1,2,64,2048]{4,3,2,1,0:T(8,128)}, u32[]{:S(2)}) copy-start(f32[1,1,2,64,2048]{4,3,2,1,0:T(8,128)} %param.4) | copy-start | bytes 3145732
  4.8 15.3 %collective-permute-start.3 = (f32[32,32,128]{2,1,0:T(8,128)S(1)}, f32[32,32,128]{2,1,0:T(8,128)S(1)}, u32[]{:S(2)}, u32[]{:S(2)}) collective-permute-start(f32[32,32,128]{2,1,0:T(8,128)S(1)} %get-tuple-element.19.refs_1_), channel_id=1, source_target_pairs={{0,4},{4,8},{8,12},{12,0},{1,5},{5,9},{9,13},{13,1},{2,6},{6,10},{... | collective-permute-start | bytes 1572872 | tf_op jit(solution)/shard_map/ppermute | solution.py:332
  6.4 14.3 %collective-permute-start.2 = (f32[32,32,128]{2,1,0:T(8,128)S(1)}, f32[32,32,128]{2,1,0:T(8,128)S(1)}, u32[]{:S(2)}, u32[]{:S(2)}) collective-permute-start(f32[32,32,128]{2,1,0:T(8,128)S(1)} %get-tuple-element.19.refs_1_), channel_id=1, source_target_pairs={{1,0},{0,1},{3,2},{2,3},{5,4},{4,5},{7,6},{6,7},{9,8},{8,9},{11,10... | collective-permute-start | bytes 1572872 | tf_op jit(solution)/shard_map/ppermute | solution.py:328
  7.9 4.7 %collective-permute-start = (f32[136,128]{1,0:T(8,128)S(1)}, f32[136,128]{1,0:T(8,128)S(1)}, u32[]{:S(2)}, u32[]{:S(2)}) collective-permute-start(f32[136,128]{1,0:T(8,128)S(1)} %get-tuple-element.32), channel_id=1, source_target_pairs={{16,0},{0,16},{17,1},{1,17},{18,2},{2,18},{19,3},{3,19},{20,4},{4,... | collective-permute-start | bytes 208904 | tf_op jit(solution)/shard_map/ppermute | solution.py:313
  14.1 1.2 %collective-permute-start.7 = (f32[8,128]{1,0:T(8,128)S(1)}, f32[8,128]{1,0:T(8,128)S(1)}, u32[]{:S(2)}, u32[]{:S(2)}) collective-permute-start(f32[8,128]{1,0:T(8,128)S(1)} %get-tuple-element.20.refs_1_), channel_id=1, source_target_pairs={{1,0},{0,1},{3,2},{2,3},{5,4},{4,5},{7,6},{6,7},{9,8},{8,9},{11,10... | collective-permute-start | bytes 12296 | tf_op jit(solution)/shard_map/ppermute | solution.py:335
  15.3 16.8 %collective-permute-start.8 = (f32[32,32,128]{2,1,0:T(8,128)S(1)}, f32[32,32,128]{2,1,0:T(8,128)S(1)}, u32[]{:S(2)}, u32[]{:S(2)}) collective-permute-start(f32[32,32,128]{2,1,0:T(8,128)S(1)} %after.4), channel_id=1, source_target_pairs={{8,0},{4,12},{9,1},{5,13},{10,2},{6,14},{11,3},{7,15},{24,16},{20,... | collective-permute-start | bytes 1572872 | tf_op jit(solution)/shard_map/ppermute | solution.py:335
  20.1 1.6 %collective-permute-start.4 = (f32[16,32,128]{2,1,0:T(8,128)S(1)}, f32[16,32,128]{2,1,0:T(8,128)S(1)}, u32[]{:S(2)}, u32[]{:S(2)}) collective-permute-start(f32[16,32,128]{2,1,0:T(8,128)S(1)} %get-tuple-element.21.refs_2_.refs_5_.refs_1_), channel_id=1, source_target_pairs={{1,0},{0,1},{3,2},{2,3},{5,4},{4,5},{7,6},{6,7},{9,8},{8,9},{11,10... | collective-permute-start | bytes 786440 | tf_op jit(solution)/shard_map/ppermute | solution.py:334
  20.2 1.9 %collective-permute-start.5 = (f32[16,32,128]{2,1,0:T(8,128)S(1)}, f32[16,32,128]{2,1,0:T(8,128)S(1)}, u32[]{:S(2)}, u32[]{:S(2)}) collective-permute-start(f32[16,32,128]{2,1,0:T(8,128)S(1)} %get-tuple-element.22.refs_3_.refs_6_.refs_2_), channel_id=1, source_target_pairs={{1,0},{0,1},{3,2},{2,3},{5,4},{4,5},{7,6},{6,7},{9,8},{8,9},{11,10... | collective-permute-start | bytes 786440 | tf_op jit(solution)/shard_map/ppermute | solution.py:334
  22.1 6.4 %collective-permute-start.6 = (f32[2,136,128]{2,1,0:T(8,128)S(1)}, f32[2,136,128]{2,1,0:T(8,128)S(1)}, u32[]{:S(2)}, u32[]{:S(2)}) collective-permute-start(f32[2,136,128]{2,1,0:T(8,128)S(1)} %after.3), channel_id=1, source_target_pairs={{2,1},{3,0},{0,3},{1,2},{6,5},{7,4},{4,7},{5,6},{10,9},{11,8},{8,1... | collective-permute-start | bytes 417800 | tf_op jit(solution)/shard_map/ppermute | solution.py:340
  32.1 3.9 %collective-permute-start.9 = (f32[32,32,128]{2,1,0:T(8,128)S(1)}, f32[32,32,128]{2,1,0:T(8,128)S(1)}, u32[]{:S(2)}, u32[]{:S(2)}) collective-permute-start(f32[32,32,128]{2,1,0:T(8,128)S(1)} %after.5.refs_5_), channel_id=1, source_target_pairs={{1,0},{0,1},{3,2},{2,3},{5,4},{4,5},{7,6},{6,7},{9,8},{8,9},{11,10... | collective-permute-start | bytes 1572872 | tf_op jit(solution)/shard_map/ppermute | solution.py:355
  32.9 6.4 %collective-permute-start.10 = (f32[32,128]{1,0:T(8,128)S(1)}, f32[32,128]{1,0:T(8,128)S(1)}, u32[]{:S(2)}, u32[]{:S(2)}) collective-permute-start(f32[32,128]{1,0:T(8,128)S(1)} %get-tuple-element.29), channel_id=1, source_target_pairs={{4,0},{8,4},{12,8},{0,12},{5,1},{9,5},{13,9},{1,13},{6,2},{10,6},{... | collective-permute-start | bytes 49160 | tf_op jit(solution)/shard_map/ppermute | solution.py:383
  36.7 2.8 %collective-permute-start.11 = (f32[32,128]{1,0:T(8,128)S(1)}, f32[32,128]{1,0:T(8,128)S(1)}, u32[]{:S(2)}, u32[]{:S(2)}) collective-permute-start(f32[32,128]{1,0:T(8,128)S(1)} %get-tuple-element.30), channel_id=1, source_target_pairs={{0,8},{12,4},{1,9},{13,5},{2,10},{14,6},{3,11},{15,7},{16,24},{28,... | collective-permute-start | bytes 49160 | tf_op jit(solution)/shard_map/ppermute | solution.py:383
